TPU v7x, 32 devices: a whole 2x2x4 slice. The times are simulated.
32 devices in a mesh: wide: 16 (over z, y, core), narrow: 2 (over x).
Axes of the slice: x: 2, y: 2, z: 4, core: 2. Of those that a mesh axis runs over, the one named last changes fastest.
Arguments:
- lifted_field: bfloat16 [16, 32, 16, 128], P('wide', None, 'narrow'), may hold values from -6 to 6
- spectral_weight: float32 [256, 16, 2, 32, 32], P('wide', 'narrow'), may hold values from -0.75 to 0.75
- mix_weight: bfloat16 [32, 32], replicated, may hold values from -1 to 1
- mix_bias: float32 [32], replicated, may hold values from -3 to 3
- head_weight: bfloat16 [32, 128], replicated, may hold values from -1 to 1
- head_bias: float32 [128], replicated, may hold values from -3 to 3
- out_weight: bfloat16 [128], replicated, may hold values from -0.5 to 0.5
- cotangent: float32 [16, 16, 128], P('wide', 'narrow'), may hold values from -6 to 6
Outputs:
- prediction: float32 [16, 16, 128], P('wide', 'narrow')
- grad_field: bfloat16 [16, 32, 16, 128], P('wide', None, 'narrow')
- grad_spectral: float32 [256, 16, 2, 32, 32], P('wide', 'narrow')
- grad_mix: float32 [32, 32], replicated
- grad_head: float32 [32, 128], replicated
All inputs are finite; a program needn't handle non-finite values.
Results may differ from a plain program's by a relative error of at most 0.018.
Values may be sent and summed in bfloat16 or wider, within the bound.
No kernel may reach another device: no remote copies, remote signals or barrier semaphores. Data moves between devices by JAX's collectives and lax.ppermute only.
A program may use at most 64 MiB of HBM per device.

v0:
```python
import math

import jax
import jax.numpy as jnp
from jax import lax
from jax.sharding import PartitionSpec as P

MX = 16
MY = 16
MZ = 16


HIGHEST_PRECISION = lax.Precision.HIGHEST


def signed_freq(indices, kept_count):
    return jnp.where(indices < kept_count // 2, indices, indices - kept_count)


def phases(positions, frequency, length):
    turned = jnp.mod(positions[:, None] * frequency[None, :], length)
    return turned.astype(jnp.float32) * (2.0 * math.pi / length)


def real_forward(positions, length, kept_count, doubled):
    indices = jnp.arange(kept_count, dtype=jnp.int32)
    angles = phases(positions, indices, length)
    if doubled:
        scaling = 1.0 + (indices > 0).astype(jnp.float32)
    else:
        scaling = jnp.ones((kept_count,), jnp.float32)
    scaling = scaling * (1.0 / math.sqrt(length))
    return jnp.stack([jnp.cos(angles) * scaling, -jnp.sin(angles) * scaling], axis=1)


def real_inverse(positions, length, kept_count, doubled):
    return jnp.transpose(real_forward(positions, length, kept_count, doubled), (2, 1, 0))


def complex_forward(positions, frequency, length):
    angles = phases(positions, frequency, length)
    cosine = jnp.cos(angles) * (1.0 / math.sqrt(length))
    sine = jnp.sin(angles) * (1.0 / math.sqrt(length))
    return jnp.stack([jnp.stack([cosine, sine]), jnp.stack([-sine, cosine])])


def complex_inverse(positions, frequency, length):
    angles = phases(positions, frequency, length)
    cosine = jnp.transpose(jnp.cos(angles)) * (1.0 / math.sqrt(length))
    sine = jnp.transpose(jnp.sin(angles)) * (1.0 / math.sqrt(length))
    return jnp.stack([jnp.stack([cosine, -sine]), jnp.stack([sine, cosine])])


def activation(values):
    return jax.nn.gelu(values, approximate=False)


def activation_slope(values):
    cumulative = 0.5 * (1.0 + lax.erf(values * (1.0 / math.sqrt(2.0))))
    return cumulative + values * jnp.exp(-0.5 * values * values) * (1.0 / math.sqrt(2.0 * math.pi))


def mode_forward(spectrum, weights):
    real_part = spectrum[:, :, 0]
    imag_part = spectrum[:, :, 1]
    real_weight = weights[:, :, 0]
    imag_weight = weights[:, :, 1]

    def combine(spectrum_part, weight_part):
        return jnp.einsum("mki,mkio->mko", spectrum_part, weight_part, precision=HIGHEST_PRECISION)

    out_real = combine(real_part, real_weight) - combine(imag_part, imag_weight)
    out_imag = combine(imag_part, real_weight) + combine(real_part, imag_weight)
    return jnp.stack([out_real, out_imag], axis=2)


def mode_backward(spectrum, weights, gradient):
    real_part = spectrum[:, :, 0]
    imag_part = spectrum[:, :, 1]
    real_weight = weights[:, :, 0]
    imag_weight = weights[:, :, 1]
    real_grad = gradient[:, :, 0]
    imag_grad = gradient[:, :, 1]

    def pulled(weight_part, grad_part):
        return jnp.einsum("mkio,mko->mki", weight_part, grad_part, precision=HIGHEST_PRECISION)

    def product(spectrum_part, grad_part):
        return jnp.einsum("mki,mko->mkio", spectrum_part, grad_part, precision=HIGHEST_PRECISION)

    back_real = pulled(real_weight, real_grad) + pulled(imag_weight, imag_grad)
    back_imag = pulled(real_weight, imag_grad) - pulled(imag_weight, real_grad)
    weight_real = product(real_part, real_grad) + product(imag_part, imag_grad)
    weight_imag = product(real_part, imag_grad) - product(imag_part, real_grad)
    return (
        jnp.stack([back_real, back_imag], axis=2),
        jnp.stack([weight_real, weight_imag], axis=2),
    )


def body(
    lifted_field,
    spectral_weight,
    mix_weight,
    mix_bias,
    head_weight,
    head_bias,
    out_weight,
    cotangent,
):
    wide_count = lax.axis_size("wide")
    narrow_count = lax.axis_size("narrow")
    rows_x, channels, rows_y, z_count = lifted_field.shape
    total_x = rows_x * wide_count
    total_y = rows_y * narrow_count
    wide_index = lax.axis_index("wide")
    x_cells = wide_index * rows_x + jnp.arange(rows_x, dtype=jnp.int32)
    y_every = jnp.arange(total_y, dtype=jnp.int32)
    z_cells = jnp.arange(z_count, dtype=jnp.int32)
    y_freq = signed_freq(jnp.arange(MY, dtype=jnp.int32), MY)
    column_ids = jnp.arange(MY, dtype=jnp.int32)
    mode_rows = MX * MY // wide_count

    def mode_tables(row_count):
        mode_ids = jnp.arange(row_count, dtype=jnp.int32)
        selector = (mode_ids[:, None] % MY == column_ids[None, :]).astype(jnp.float32)
        return (signed_freq(mode_ids // MY, MX), selector)

    def analysis(values, doubled):
        z_table = real_forward(z_cells, z_count, MZ, doubled).astype(jnp.bfloat16)
        spectra = jnp.einsum(
            "xcyz,zrk->krcxy", values, z_table, preferred_element_type=jnp.float32
        ).astype(jnp.bfloat16)
        regrouped = lax.all_to_all(spectra, "narrow", split_axis=0, concat_axis=4, tiled=True)
        y_table = complex_forward(y_every, y_freq, total_y).astype(jnp.bfloat16)
        planes = jnp.einsum(
            "krcxn,srnj->kscxj", regrouped, y_table, preferred_element_type=jnp.float32
        )
        kz_here = planes.shape[0]
        laid_planes = jnp.transpose(planes, (0, 1, 3, 4, 2)).reshape(
            kz_here, 2, rows_x, MY * channels
        )
        columns = lax.all_to_all(laid_planes, "wide", split_axis=3, concat_axis=2, tiled=True)
        x_every = jnp.arange(total_x, dtype=jnp.int32)
        x_table = complex_forward(
            x_every, signed_freq(jnp.arange(MX, dtype=jnp.int32), MX), total_x
        )
        turned = jnp.einsum("ksxq,tsxi->iktq", columns, x_table, precision=HIGHEST_PRECISION)
        owner_ids = jnp.arange(wide_count, dtype=jnp.int32)
        block_ids = jnp.arange(MX, dtype=jnp.int32) * wide_count + wide_index
        routing = (block_ids[None, :] // MX == owner_ids[:, None]).astype(jnp.float32)
        outgoing = jnp.einsum("vi,iktq->vktq", routing, turned, precision=HIGHEST_PRECISION)
        incoming = lax.all_to_all(outgoing, "wide", split_axis=0, concat_axis=0, tiled=True)
        senders = (wide_index * MX + jnp.arange(MX, dtype=jnp.int32)) % wide_count
        chooser = (senders[:, None] == owner_ids[None, :]).astype(jnp.float32)
        assembled = jnp.einsum("lw,wktq->ktlq", chooser, incoming, precision=HIGHEST_PRECISION)
        return jnp.transpose(assembled.reshape(kz_here, 2, mode_rows, channels), (2, 0, 1, 3))

    def synthesis(spectrum, doubled):
        shard_piece = lax.all_gather(spectrum, "wide", axis=0, tiled=True)
        frequency, selector = mode_tables(shard_piece.shape[0])
        x_table = complex_inverse(x_cells, frequency, total_x).astype(jnp.bfloat16)
        turned = jnp.einsum(
            "mkrc,srmx->mkscx", shard_piece, x_table, preferred_element_type=jnp.float32
        )
        planes = jnp.einsum(
            "mkscx,mj->kscxj", turned, selector, precision=HIGHEST_PRECISION
        ).astype(jnp.bfloat16)
        y_table = complex_inverse(y_every, y_freq, total_y).astype(jnp.bfloat16)
        line_data = jnp.einsum(
            "krcxj,srjn->kscxn", planes, y_table, preferred_element_type=jnp.float32
        ).astype(jnp.bfloat16)
        line_data = lax.all_to_all(line_data, "narrow", split_axis=4, concat_axis=0, tiled=True)
        z_table = real_inverse(z_cells, z_count, MZ, doubled).astype(jnp.bfloat16)
        return jnp.einsum("krcxy,krz->xcyz", line_data, z_table, preferred_element_type=jnp.float32)

    spectrum = analysis(lifted_field, False)
    mode = mode_forward(spectrum, spectral_weight).astype(jnp.bfloat16)
    mixed = jnp.einsum(
        "xcyz,cd->xdyz", lifted_field, mix_weight, preferred_element_type=jnp.float32
    )
    pre_act = synthesis(mode, True) + mixed + mix_bias[None, :, None, None]

    def head_row(row_items):
        pre_row, target_row = row_items
        hidden = activation(pre_row).astype(jnp.bfloat16)
        head_pre = (
            jnp.einsum("cyz,cj->jyz", hidden, head_weight, preferred_element_type=jnp.float32)
            + head_bias[:, None, None]
        )
        active = activation(head_pre).astype(jnp.bfloat16)
        predicted = jnp.einsum("jyz,j->yz", active, out_weight, preferred_element_type=jnp.float32)
        head_slope = (
            target_row[None]
            * out_weight.astype(jnp.float32)[:, None, None]
            * activation_slope(head_pre)
        ).astype(jnp.bfloat16)
        returned = jnp.einsum(
            "jyz,cj->cyz", head_slope, head_weight, preferred_element_type=jnp.float32
        )
        grad_row = (returned * activation_slope(pre_row)).astype(jnp.bfloat16)
        head_grad = jnp.einsum(
            "cyz,jyz->cj", hidden, head_slope, preferred_element_type=jnp.float32
        )
        return (predicted, grad_row, head_grad)

    prediction, grad_pre, head_parts = lax.map(head_row, (pre_act, cotangent))
    adjoint = analysis(grad_pre, True)
    back_modes, grad_spectral = mode_backward(spectrum, spectral_weight, adjoint)
    field_back = synthesis(back_modes.astype(jnp.bfloat16), False) + jnp.einsum(
        "xdyz,cd->xcyz", grad_pre, mix_weight, preferred_element_type=jnp.float32
    )
    grad_field = field_back.astype(jnp.bfloat16)
    mix_terms = jnp.einsum(
        "xcyz,xdyz->cd", lifted_field, grad_pre, preferred_element_type=jnp.float32
    )
    grad_mix, grad_head = lax.psum((mix_terms, jnp.sum(head_parts, axis=0)), ("wide", "narrow"))
    return (prediction, grad_field, grad_spectral, grad_mix, grad_head)


def solution(mesh):
    return jax.shard_map(
        body,
        mesh=mesh,
        in_specs=(
            P("wide", None, "narrow", None),
            P("wide", "narrow", None, None, None),
            P(),
            P(),
            P(),
            P(),
            P(),
            P("wide", "narrow", None),
        ),
        out_specs=(
            P("wide", "narrow", None),
            P("wide", None, "narrow", None),
            P("wide", "narrow", None, None, None),
            P(),
            P(),
        ),
        check_vma=False,
    )
```

profile of v0, /device:TPU:1, one launch (start us, length us, event | category | flops | bytes accessed | tf_op | source)
XLA Modules:
  0.0 206.1 jit_solution(14237890492756025355)
XLA Ops:
  0.7 1.0 fusion.44
  1.8 0.7 reshape.761
  2.5 3.3 %all-to-all-start = ((bf16[2,2,2048]{2,1,0:T(2,128)(2,1)}), bf16[2,2,2048]{2,1,0:T(2,128)(2,1)S(1)}, u32[]{:S(2)}, u32[]{:S(2)}) async-start(bf16[2,2,2048]{2,1,0:T(2,128)(2,1)} %reshape.761), calls=%async_computation | async-start | bytes 32768 | tf_op jit(solution)/shard_map/all_to_all | solution.py:134
  6.4 2.6 %all-to-all-done = bf16[2,2,2048]{2,1,0:T(2,128)(2,1)S(1)} async-done(((bf16[2,2,2048]{2,1,0:T(2,128)(2,1)}), bf16[2,2,2048]{2,1,0:T(2,128)(2,1)S(1)}, u32[]{:S(2)}, u32[]{:S(2)}) %all-to-all-start) | async-done | bytes 16416 | tf_op jit(solution)/shard_map/all_to_all | solution.py:134
  9.3 0.3 copy.158
  9.6 1.4 reshape.763
  11.0 7.9 %all-to-all-start.1 = ((f32[16,1,512]{2,1,0:T(1,128)}), f32[16,1,512]{2,1,0:T(1,128)S(1)}, u32[]{:S(2)}, u32[]{:S(2)}) async-start(f32[16,1,512]{2,1,0:T(1,128)} %reshape.763), calls=%async_computation.1 | async-start | bytes 65536 | tf_op jit(solution)/shard_map/all_to_all | solution.py:143
  19.0 5.9 %all-to-all-done.1 = f32[16,1,512]{2,1,0:T(1,128)S(1)} async-done(((f32[16,1,512]{2,1,0:T(1,128)}), f32[16,1,512]{2,1,0:T(1,128)S(1)}, u32[]{:S(2)}, u32[]{:S(2)}) %all-to-all-start.1) | async-done | bytes 32800 | tf_op jit(solution)/shard_map/all_to_all | solution.py:143
  24.9 0.5 broadcast.1609
  25.4 0.7 reduce
  26.1 0.8 reshape.764
  26.9 0.2 copy.159
  27.2 0.3 convolution_bitcast_fusion.4
  27.8 0.8 reshape.765
  28.5 4.1 %all-to-all-start.2 = ((f32[16,1,512]{2,1,0:T(1,128)}), f32[16,1,512]{2,1,0:T(1,128)S(1)}, u32[]{:S(2)}, u32[]{:S(2)}) async-start(f32[16,1,512]{2,1,0:T(1,128)} %reshape.765), calls=%async_computation.2 | async-start | bytes 65536 | tf_op jit(solution)/shard_map/all_to_all | solution.py:153
  32.7 6.0 %all-to-all-done.2 = f32[16,1,512]{2,1,0:T(1,128)S(1)} async-done(((f32[16,1,512]{2,1,0:T(1,128)}), f32[16,1,512]{2,1,0:T(1,128)S(1)}, u32[]{:S(2)}, u32[]{:S(2)}) %all-to-all-start.2) | async-done | bytes 32800 | tf_op jit(solution)/shard_map/all_to_all | solution.py:153
  38.6 0.7 reduce.1
  39.5 0.3 fusion.87
  39.8 3.5 %fusion.4 = f32[16,8,1,32]{3,2,1,0:T(1,128)S(1)} fusion(f32[16,8,2,32,32]{4,3,2,1,0:T(8,128)} %param.9, f32[16,8,32,1]{2,0,1,3:T(8,128)S(1)} %get-tuple-element.57), kind=kOutput, calls=%fused_computation.5 | convolution fusion | flops 1572864 | bytes 2129920 | tf_op jit(solution)/shard_map/mki,mkio->mko/dot_general | solution.py:70
  43.4 3.4 %fusion.14 = f32[16,8,1,32]{3,2,1,0:T(1,128)S(1)} fusion(f32[16,8,2,32,32]{4,3,2,1,0:T(8,128)} %param.9, f32[16,8,32,1]{2,0,1,3:T(8,128)S(1)} %get-tuple-element.57), kind=kOutput, calls=%fused_computation.15 | convolution fusion | flops 1572864 | bytes 2129920 | tf_op jit(solution)/shard_map/mki,mkio->mko/dot_general | solution.py:70
  46.7 1.8 fusion.12
  48.5 1.8 fusion.6
  50.4 21.6 %all_gather.6 = bf16[256,8,2,32]{3,1,2,0:T(8,128)(2,1)S(1)} all-gather(bf16[16,8,2,32]{3,1,2,0:T(8,128)(2,1)S(1)} %copy.91), channel_id=1, replica_groups=mesh['wide'=16,'narrow'=2] {'wide'}, dimensions={0}, use_global_device_ids=true | all-gather | bytes 278528 | tf_op jit(solution)/shard_map/all_gather | solution.py:160
  71.9 1.2 convolution_bitcast_fusion.1
  73.2 1.3 fusion.49
  74.6 0.2 fusion.53
  74.8 0.7 reshape.767
  75.5 3.2 %all-to-all-start.3 = ((bf16[2,2,2048]{2,1,0:T(2,128)(2,1)}), bf16[2,2,2048]{2,1,0:T(2,128)(2,1)S(1)}, u32[]{:S(2)}, u32[]{:S(2)}) async-start(bf16[2,2,2048]{2,1,0:T(2,128)(2,1)} %reshape.767), calls=%async_computation.3 | async-start | bytes 32768 | tf_op jit(solution)/shard_map/all_to_all | solution.py:173
  79.1 2.4 %all-to-all-done.3 = bf16[2,2,2048]{2,1,0:T(2,128)(2,1)S(1)} async-done(((bf16[2,2,2048]{2,1,0:T(2,128)(2,1)}), bf16[2,2,2048]{2,1,0:T(2,128)(2,1)S(1)}, u32[]{:S(2)}, u32[]{:S(2)}) %all-to-all-start.3) | async-done | bytes 16416 | tf_op jit(solution)/shard_map/all_to_all | solution.py:173
  81.6 0.5 fusion.76
  82.1 0.5 fusion.64
  82.6 1.9 fusion.72
  84.9 0.7 reshape.769
  85.6 3.2 %all-to-all-start.4 = ((bf16[2,2,2048]{2,1,0:T(2,128)(2,1)}), bf16[2,2,2048]{2,1,0:T(2,128)(2,1)S(1)}, u32[]{:S(2)}, u32[]{:S(2)}) async-start(bf16[2,2,2048]{2,1,0:T(2,128)(2,1)} %reshape.769), calls=%async_computation.4 | async-start | bytes 32768 | tf_op jit(solution)/shard_map/all_to_all | solution.py:134
  89.0 2.5 %all-to-all-done.4 = bf16[2,2,2048]{2,1,0:T(2,128)(2,1)S(1)} async-done(((bf16[2,2,2048]{2,1,0:T(2,128)(2,1)}), bf16[2,2,2048]{2,1,0:T(2,128)(2,1)S(1)}, u32[]{:S(2)}, u32[]{:S(2)}) %all-to-all-start.4) | async-done | bytes 16416 | tf_op jit(solution)/shard_map/all_to_all | solution.py:134
  91.9 0.3 copy.163
  92.2 1.4 reshape.771
  93.6 5.7 %all-to-all-start.5 = ((f32[16,1,512]{2,1,0:T(1,128)}), f32[16,1,512]{2,1,0:T(1,128)S(1)}, u32[]{:S(2)}, u32[]{:S(2)}) async-start(f32[16,1,512]{2,1,0:T(1,128)} %reshape.771), calls=%async_computation.5 | async-start | bytes 65536 | tf_op jit(solution)/shard_map/all_to_all | solution.py:143
  99.4 39.2 %all-reduce = (f32[32,32]{0,1:T(8,128)S(1)}, f32[32,128]{1,0:T(8,128)}) all-reduce(f32[32,32]{0,1:T(8,128)S(1)} %convolution_bitcast_fusion.14, f32[32,128]{1,0:T(8,128)S(1)} %convolution_bitcast_fusion.13), channel_id=1, replica_groups=mesh['wide'=16,'narrow'=2] {'wide','narrow'}, use_global_device_ids=true, to_apply=%region_0.1 | all-reduce | flops 5120 | bytes 40960 | tf_op jit(solution)/shard_map/psum | solution.py:217
  138.6 0.7 copy.121
  139.3 0.7 reduce.2
  140.0 0.8 reshape.772
  140.9 0.2 copy.164
  141.1 0.3 convolution_bitcast_fusion.2
  141.4 0.2 fusion.85
  141.7 0.8 reshape.773
  142.5 6.2 %all-to-all-start.6 = ((f32[16,1,512]{2,1,0:T(1,128)}), f32[16,1,512]{2,1,0:T(1,128)S(1)}, u32[]{:S(2)}, u32[]{:S(2)}) async-start(f32[16,1,512]{2,1,0:T(1,128)} %reshape.773), calls=%async_computation.6 | async-start | bytes 65536 | tf_op jit(solution)/shard_map/all_to_all | solution.py:153
  148.8 5.8 %all-to-all-done.6 = f32[16,1,512]{2,1,0:T(1,128)S(1)} async-done(((f32[16,1,512]{2,1,0:T(1,128)}), f32[16,1,512]{2,1,0:T(1,128)S(1)}, u32[]{:S(2)}, u32[]{:S(2)}) %all-to-all-start.6) | async-done | bytes 32800 | tf_op jit(solution)/shard_map/all_to_all | solution.py:153
  154.6 0.7 reduce.3
  155.5 0.3 fusion.83
  155.8 5.1 %fusion = f32[16,8,1,32]{3,2,1,0:T(1,128)S(1)} fusion(f32[16,8,2,32,32]{4,3,2,1,0:T(8,128)} %param.9, f32[16,8,32,1]{2,0,1,3:T(8,128)S(1)} %get-tuple-element.61), kind=kOutput, calls=%fused_computation.1 | convolution fusion | flops 1572864 | bytes 2129920 | tf_op jit(solution)/shard_map/mkio,mko->mki/dot_general | solution.py:86
  160.9 5.0 %fusion.10 = f32[16,8,1,32]{3,2,1,0:T(1,128)S(1)} fusion(f32[16,8,2,32,32]{4,3,2,1,0:T(8,128)} %param.9, f32[16,8,32,1]{2,0,1,3:T(8,128)S(1)} %get-tuple-element.61), kind=kOutput, calls=%fused_computation.11 | convolution fusion | flops 1572864 | bytes 2129920 | tf_op jit(solution)/shard_map/mkio,mko->mki/dot_general | solution.py:86
  165.9 3.4 %fusion.8 = f32[16,8,1,32]{3,2,1,0:T(1,128)S(1)} fusion(f32[16,8,2,32,32]{4,3,2,1,0:T(8,128)S(1)} %copy-done.2, f32[16,8,32,1]{2,0,1,3:T(8,128)S(1)} %get-tuple-element.62), kind=kOutput, calls=%fused_computation.9 | convolution fusion | flops 1572864 | bytes 2179072 | tf_op jit(solution)/shard_map/mkio,mko->mki/dot_general | solution.py:86
  169.3 3.4 %fusion.2 = f32[16,8,1,32]{3,2,1,0:T(1,128)S(1)} fusion(f32[16,8,2,32,32]{4,3,2,1,0:T(8,128)S(1)} %copy-done.2, f32[16,8,32,1]{2,0,1,3:T(8,128)S(1)} %get-tuple-element.62), kind=kOutput, calls=%fused_computation.3 | convolution fusion | flops 1572864 | bytes 2179072 | tf_op jit(solution)/shard_map/mkio,mko->mki/dot_general | solution.py:86
  172.8 21.6 %all_gather.7 = bf16[256,8,2,32]{3,1,2,0:T(8,128)(2,1)S(1)} all-gather(bf16[16,8,2,32]{3,1,2,0:T(8,128)(2,1)S(1)} %copy.107), channel_id=1, replica_groups=mesh['wide'=16,'narrow'=2] {'wide'}, dimensions={0}, use_global_device_ids=true | all-gather | bytes 278528 | tf_op jit(solution)/shard_map/all_gather | solution.py:160
  194.5 1.2 convolution_bitcast_fusion
  195.7 1.3 fusion.46
  197.0 0.2 fusion.52
  197.2 0.7 reshape.775
  198.0 3.2 %all-to-all-start.7 = ((bf16[2,2,2048]{2,1,0:T(2,128)(2,1)}), bf16[2,2,2048]{2,1,0:T(2,128)(2,1)S(1)}, u32[]{:S(2)}, u32[]{:S(2)}) async-start(bf16[2,2,2048]{2,1,0:T(2,128)(2,1)} %reshape.775), calls=%async_computation.7 | async-start | bytes 32768 | tf_op jit(solution)/shard_map/all_to_all | solution.py:173
  201.2 1.1 add_bitcast_fusion
  202.4 2.8 %pad_maximum_fusion = f32[16,8,2,32,32]{4,3,2,1,0:T(8,128)} fusion(f32[16,8,1,32,32]{4,3,2,1,0:T(8,128)S(1)} %get-tuple-element.55, f32[16,8,1,32,32]{4,3,2,1,0:T(8,128)S(1)} %get-tuple-element.54), kind=kLoop, calls=%fused_computation | loop fusion | flops 262144 | bytes 2097152 | tf_op jit(solution)/shard_map/stack | solution.py:97
  205.2 0.2 fusion.43
  205.4 0.7 copy.120
  (71 shorter events, 3.5 us)
Async XLA Ops:
  0.6 81.4 %copy-start = (bf16[32,128]{1,0:T(8,128)(2,1)S(1)}, bf16[32,128]{1,0:T(8,128)(2,1)}, u32[]{:S(2)}) copy-start(bf16[32,128]{1,0:T(8,128)(2,1)} %param.12) | copy-start | bytes 24580
  2.5 6.5 %all-to-all-start = ((bf16[2,2,2048]{2,1,0:T(2,128)(2,1)}), bf16[2,2,2048]{2,1,0:T(2,128)(2,1)S(1)}, u32[]{:S(2)}, u32[]{:S(2)}) async-start(bf16[2,2,2048]{2,1,0:T(2,128)(2,1)} %reshape.761), calls=%async_computation | async-start | bytes 32768 | tf_op jit(solution)/shard_map/all_to_all | solution.py:134
  11.0 13.8 %all-to-all-start.1 = ((f32[16,1,512]{2,1,0:T(1,128)}), f32[16,1,512]{2,1,0:T(1,128)S(1)}, u32[]{:S(2)}, u32[]{:S(2)}) async-start(f32[16,1,512]{2,1,0:T(1,128)} %reshape.763), calls=%async_computation.1 | async-start | bytes 65536 | tf_op jit(solution)/shard_map/all_to_all | solution.py:143
  28.5 10.1 %all-to-all-start.2 = ((f32[16,1,512]{2,1,0:T(1,128)}), f32[16,1,512]{2,1,0:T(1,128)S(1)}, u32[]{:S(2)}, u32[]{:S(2)}) async-start(f32[16,1,512]{2,1,0:T(1,128)} %reshape.765), calls=%async_computation.2 | async-start | bytes 65536 | tf_op jit(solution)/shard_map/all_to_all | solution.py:153
  39.8 6.9 %copy-start.1 = (f32[16,8,2,32,32]{4,3,2,1,0:T(8,128)S(1)}, f32[16,8,2,32,32]{4,3,2,1,0:T(8,128)}, u32[]{:S(2)}) copy-start(f32[16,8,2,32,32]{4,3,2,1,0:T(8,128)} %param.9) | copy-start | bytes 3145732
  73.2 5.6 %copy-start.3 = (bf16[1,32,8,128]{3,2,1,0:T(8,128)(2,1)S(1)}, bf16[1,32,8,128]{3,2,1,0:T(8,128)(2,1)}, u32[]{:S(2)}) copy-start(bf16[1,32,8,128]{3,2,1,0:T(8,128)(2,1)} %param.8) | copy-start | bytes 196612
  73.2 5.6 %copy-start.4 = (bf16[32,32]{1,0:T(8,128)(2,1)S(1)}, bf16[32,32]{1,0:T(8,128)(2,1)}, u32[]{:S(2)}) copy-start(bf16[32,32]{1,0:T(8,128)(2,1)} %param.10) | copy-start | bytes 6148
  73.2 5.8 %copy-start.8 = (bf16[128]{0:T(256)(128)(2,1)S(1)}, bf16[128]{0:T(256)(128)(2,1)}, u32[]{:S(2)}) copy-start(bf16[128]{0:T(256)(128)(2,1)} %param.14) | copy-start | bytes 772
  73.2 8.4 %copy-start.6 = (f32[32]{0:T(128)S(1)}, f32[32]{0:T(128)}, u32[]{:S(2)}) copy-start(f32[32]{0:T(128)} %param.11) | copy-start | bytes 388
  74.5 7.5 %copy-start.5 = (f32[1,8,128]{2,1,0:T(8,128)S(1)}, f32[1,8,128]{2,1,0:T(8,128)}, u32[]{:S(2)}) copy-start(f32[1,8,128]{2,1,0:T(8,128)} %param.15) | copy-start | bytes 12292
  74.5 7.5 %copy-start.7 = (f32[128]{0:T(128)S(1)}, f32[128]{0:T(128)}, u32[]{:S(2)}) copy-start(f32[128]{0:T(128)} %param.13) | copy-start | bytes 1540
  75.5 5.9 %all-to-all-start.3 = ((bf16[2,2,2048]{2,1,0:T(2,128)(2,1)}), bf16[2,2,2048]{2,1,0:T(2,128)(2,1)S(1)}, u32[]{:S(2)}, u32[]{:S(2)}) async-start(bf16[2,2,2048]{2,1,0:T(2,128)(2,1)} %reshape.767), calls=%async_computation.3 | async-start | bytes 32768 | tf_op jit(solution)/shard_map/all_to_all | solution.py:173
  85.6 5.9 %all-to-all-start.4 = ((bf16[2,2,2048]{2,1,0:T(2,128)(2,1)}), bf16[2,2,2048]{2,1,0:T(2,128)(2,1)S(1)}, u32[]{:S(2)}, u32[]{:S(2)}) async-start(bf16[2,2,2048]{2,1,0:T(2,128)(2,1)} %reshape.769), calls=%async_computation.4 | async-start | bytes 32768 | tf_op jit(solution)/shard_map/all_to_all | solution.py:134
  93.6 45.8 %all-to-all-start.5 = ((f32[16,1,512]{2,1,0:T(1,128)}), f32[16,1,512]{2,1,0:T(1,128)S(1)}, u32[]{:S(2)}, u32[]{:S(2)}) async-start(f32[16,1,512]{2,1,0:T(1,128)} %reshape.771), calls=%async_computation.5 | async-start | bytes 65536 | tf_op jit(solution)/shard_map/all_to_all | solution.py:143
  142.5 12.1 %all-to-all-start.6 = ((f32[16,1,512]{2,1,0:T(1,128)}), f32[16,1,512]{2,1,0:T(1,128)S(1)}, u32[]{:S(2)}, u32[]{:S(2)}) async-start(f32[16,1,512]{2,1,0:T(1,128)} %reshape.773), calls=%async_computation.6 | async-start | bytes 65536 | tf_op jit(solution)/shard_map/all_to_all | solution.py:153
  155.8 10.1 %copy-start.2 = (f32[16,8,2,32,32]{4,3,2,1,0:T(8,128)S(1)}, f32[16,8,2,32,32]{4,3,2,1,0:T(8,128)}, u32[]{:S(2)}) copy-start(f32[16,8,2,32,32]{4,3,2,1,0:T(8,128)} %param.9) | copy-start | bytes 3145732
  198.0 7.1 %all-to-all-start.7 = ((bf16[2,2,2048]{2,1,0:T(2,128)(2,1)}), bf16[2,2,2048]{2,1,0:T(2,128)(2,1)S(1)}, u32[]{:S(2)}, u32[]{:S(2)}) async-start(bf16[2,2,2048]{2,1,0:T(2,128)(2,1)} %reshape.775), calls=%async_computation.7 | async-start | bytes 32768 | tf_op jit(solution)/shard_map/all_to_all | solution.py:173
where the time goes:
time: 207 us; the launch traced here: 206 us
  blocking collectives  82.4 us (40%)
  matrix products  39.8 us (19%)
  starting transfers between devices  37 us (18%)
  waiting for transfers between devices  25.2 us (12%)
  local copies, waits for them, and re-layouts  13.1 us (6%)
  other arithmetic  7.32 us (4%)
    all_gather x2, blocking collectives, synthesis(): shard_piece = lax.all_gather(spectrum, 'wide', axis=0, tiled=True)  43.2 us
    psum x1, blocking collectives, body(): lax.psum((mix_terms, jnp.sum(head_parts, axis=0)), ('wide', 'narrow'))  39.2 us
    dot_general x4, matrix products, pulled(): jnp.einsum('mkio,mko->mki', weight_part, grad_part, precision=HIGHEST_PRE...  16.9 us
    all_to_all x2, starting transfers between devices, analysis(): lax.all_to_all(laid_planes, 'wide', split_axis=3, concat_axis=2, tiled=True)  13.7 us
    all_to_all x2, waiting for transfers between devices, analysis(): lax.all_to_all(outgoing, 'wide', split_axis=0, concat_axis=0, tiled=True)  11.8 us
    unnamed x36, local copies, waits for them, and re-layouts  11 us
    dot_general x4, matrix products, combine(): jnp.einsum('mki,mkio->mko', spectrum_part, weight_part, precision=HIGHEST...  10.5 us
    all_to_all x2, starting transfers between devices, analysis(): lax.all_to_all(outgoing, 'wide', split_axis=0, concat_axis=0, tiled=True)  10.3 us
  transfers between devices with their start and end apart: 8, of which 6 were waited for; matrix products, arithmetic and copies ran while one was open for 3% of the time, Pallas kernels for 0%

commit v1 on v0

v1 whole, which is shorter than its diff:
```python
import functools
import math

import jax
import jax.numpy as jnp
import numpy as np
from jax import lax
from jax.experimental import pallas as pl
from jax.experimental.pallas import tpu as pltpu
from jax.sharding import PartitionSpec as P

MX = 16
MY = 16
MZ = 16
F32 = jnp.float32
BF16 = jnp.bfloat16
VMEM_LIMIT = 32 * 1024 * 1024


def signed(indices, count):
    return np.where(indices < count // 2, indices, indices - count)


def wave(positions, frequency, length):
    turned = np.mod(np.multiply.outer(positions, frequency), length)
    angles = turned.astype(np.float32) * np.float32(2.0 * math.pi / length)
    scale = np.float32(1.0 / math.sqrt(length))
    return np.cos(angles) * scale, np.sin(angles) * scale


def z_table(length, doubled):
    cosine, sine = wave(np.arange(length), np.arange(MZ), length)
    table = np.stack([cosine.T, -sine.T], axis=1)
    if doubled:
        table[1:] *= 2.0
    return table.reshape(2 * MZ, length).astype(BF16)


def pair(cosine, sine, sign):
    return np.stack(
        [np.stack([cosine, -sign * sine], -1), np.stack([sign * sine, cosine], -1)], -2
    )


def y_tables(total_y, rows_y, kz, modes):
    cosine, sine = wave(np.arange(total_y), signed(np.arange(MY), MY), total_y)
    narrow = total_y // rows_y
    same = np.eye(kz, dtype=np.float32)
    forward = pair(cosine, sine, -1.0).reshape(narrow, rows_y, MY // modes, modes, 2, 2)
    inverse = pair(cosine, sine, 1.0).reshape(narrow, rows_y, MY // modes, modes, 2, 2)
    forward = np.einsum("nybjtr,kl->bjtkynlr", forward, same)
    inverse = np.einsum("nybjst,kl->bnyksjtl", inverse, same)
    blocks = MY // modes
    forward = forward.reshape(blocks, modes * 2 * kz, rows_y * narrow * kz * 2)
    inverse = inverse.reshape(blocks, narrow * rows_y * kz * 2, modes * 2 * kz)
    return forward.astype(BF16), inverse.astype(BF16)


def x_rows(total_x, wide, modes):
    cosine, sine = wave(np.arange(total_x), signed(np.arange(MX), MX), total_x)
    owner_freq = np.arange(wide) * modes // MY
    forward = pair(cosine, sine, -1.0)[:, owner_freq]
    inverse = pair(cosine, sine, 1.0)[:, owner_freq]
    forward = np.transpose(forward, (1, 2, 0, 3))
    inverse = np.transpose(inverse, (0, 2, 1, 3))

    def spread(table):
        shape = (wide, 2, wide, MZ, 2)
        return np.broadcast_to(table[:, :, :, None, :], shape).reshape(wide, 2, wide * MZ * 2)

    return spread(forward).astype(np.float32), spread(inverse).astype(np.float32)


def dot(a, b):
    return jnp.dot(a, b, preferred_element_type=F32)


def dot_nt(a, b):
    return lax.dot_general(a, b, (((1,), (1,)), ((), ())), preferred_element_type=F32)


def dot_tn(a, b):
    return lax.dot_general(a, b, (((0,), (0,)), ((), ())), preferred_element_type=F32)


def iota(shape, axis):
    return lax.broadcasted_iota(jnp.int32, shape, axis)


def halves(values):
    high = values.astype(BF16)
    return high, (values - high.astype(F32)).astype(BF16)


def x_matrix(rows):
    shape = (2 * MZ, rows.shape[1])
    row, column = iota(shape, 0), iota(shape, 1)
    same = (row >> 1) == ((column >> 1) & (MZ - 1))
    value = jnp.where((row & 1) == 0, rows[0:1], rows[1:2])
    return jnp.where(same, value, 0.0)


def analysed(pieces, rows, y_forward, copies, channels):
    high, low = halves(x_matrix(rows))
    turned = dot(high, pieces) + dot(low, pieces)
    rows_y = turned.shape[1] // channels
    lines = jnp.concatenate(
        [turned[:, y * channels : (y + 1) * channels] for y in range(rows_y)], axis=0
    )
    high, low = halves(jnp.concatenate([lines] * copies, axis=1))
    return dot(y_forward, high) + dot(y_forward, low)


def spread_lines(modes, y_inverse, narrow, rows_y):
    lines = dot(y_inverse, modes)
    step = lines.shape[0] // (narrow * rows_y)
    blocks = []
    for n in range(narrow):
        parts = [
            lines[(n * rows_y + y) * step : (n * rows_y + y + 1) * step] for y in range(rows_y)
        ]
        blocks.append(jnp.concatenate(parts, axis=1))
    return jnp.concatenate(blocks, axis=0).astype(BF16)


def repeat_rows(out_ref, block, lanes):
    height = block.shape[0]
    for w in range(out_ref.shape[0] // height):
        out_ref[w * height : (w + 1) * height, :lanes] = block


def selector(shape, condition):
    return jnp.where(condition(iota(shape, 0), iota(shape, 1)), 1.0, 0.0).astype(BF16)


def start_kernel(field_ref, turn_ref, table_ref, send_ref, field_out_ref):
    turned = dot(turn_ref[...], field_ref[...]).astype(BF16)
    field_out_ref[...] = turned
    spectra = dot_nt(table_ref[...], turned).astype(BF16)
    repeat_rows(send_ref, spectra, spectra.shape[1])


def weight_kernel(weight_ref, out_ref):
    _, kz, _, channels, _ = weight_ref.shape
    both = jnp.concatenate([weight_ref[0, :, 0], weight_ref[0, :, 1]], axis=-1)
    out_ref[0] = both.reshape(kz * channels, 2 * channels).astype(BF16)


def mode_kernel(
    narrow, pieces_ref, rows_ref, y_forward_ref, y_inverse_ref, weight_ref, spectrum_ref, send_ref
):
    modes, depth, width = weight_ref.shape
    channels = width // 2
    kz = depth // channels
    rows_y = pieces_ref.shape[1] // channels
    spectrum = analysed(pieces_ref[...], rows_ref[...], y_forward_ref[...], kz, channels)
    spectrum_ref[...] = spectrum[:, :channels]
    row, lane = iota(spectrum.shape, 0), iota(spectrum.shape, 1)
    blocked = jnp.where(row % kz == lane // channels, spectrum, 0.0)
    mixed = []
    for j in range(modes):
        left = blocked[j * 2 * kz : (j + 1) * 2 * kz].astype(BF16)
        product = dot(left, weight_ref[j])
        real, imag = product[:, :channels], product[:, channels:]
        mixed.append(real[:kz] - imag[kz:])
        mixed.append(imag[:kz] + real[kz:])
    mode = jnp.concatenate(mixed, axis=0).astype(BF16)
    block = spread_lines(mode, y_inverse_ref[...], narrow, rows_y)
    repeat_rows(send_ref, block, block.shape[1])


def cell_kernel(
    kz,
    pieces_ref,
    rows_ref,
    z_doubled_ref,
    field_ref,
    mix_ref,
    mix_bias_ref,
    head_ref,
    head_bias_ref,
    out_weight_ref,
    cotangent_ref,
    prediction_ref,
    grad_pre_ref,
    send_ref,
):
    channels = mix_ref.shape[0]
    hidden_units = head_ref.shape[1]
    rows_y = cotangent_ref.shape[0]
    lines = dot(x_matrix(rows_ref[...]).astype(BF16), pieces_ref[...]).astype(BF16)
    branch = dot_tn(lines, z_doubled_ref[...])
    mix, head = mix_ref[...], head_ref[...]
    mix_bias, head_bias = mix_bias_ref[...], head_bias_ref[...]
    out_weight = out_weight_ref[...]
    grad_mix = jnp.zeros((channels, channels), F32)
    grad_head = jnp.zeros((channels, hidden_units), F32)
    gradients = []

    def normal(values):
        cumulative = 0.5 * (1.0 + lax.erf(values * (1.0 / math.sqrt(2.0))))
        density = jnp.exp(-0.5 * values * values) * (1.0 / math.sqrt(2.0 * math.pi))
        return values * cumulative, cumulative + values * density

    for y in range(rows_y):
        cells = slice(y * channels, (y + 1) * channels)
        field = field_ref[cells]
        pre_act = branch[cells] + dot_tn(mix, field) + mix_bias
        hidden, pre_slope = normal(pre_act)
        hidden = hidden.astype(BF16)
        head_pre = dot_tn(head, hidden) + head_bias
        active, slope = normal(head_pre)
        active = active.astype(BF16).astype(F32)
        prediction_ref[y : y + 1] = jnp.sum(active * out_weight, axis=0, keepdims=True)
        head_slope = (cotangent_ref[y : y + 1] * out_weight * slope).astype(BF16)
        grad_pre = (dot(head, head_slope) * pre_slope).astype(BF16)
        grad_head += dot_nt(hidden, head_slope)
        grad_mix += dot_nt(field, grad_pre)
        gradients.append(grad_pre)

    gradient = jnp.concatenate(gradients, axis=0)
    grad_pre_ref[...] = gradient
    spectra = dot_nt(z_doubled_ref[...], gradient).astype(BF16)
    width = spectra.shape[1]
    repeat_rows(send_ref, spectra, width)
    wide_mix = jnp.concatenate(
        [grad_mix, jnp.zeros((channels, hidden_units - channels), F32)], axis=1
    )
    shares = jnp.concatenate([*halves(grad_head), *halves(wide_mix)], axis=0)
    piece = 2 * kz
    place = selector(
        (send_ref.shape[0], 4 * channels),
        lambda row, column: (row // piece == column % channels)
        & (row % piece == column // channels),
    )
    send_ref[:, width:] = dot(place, shares).astype(BF16)


def back_kernel(
    narrow,
    pieces_ref,
    rows_ref,
    y_forward_ref,
    y_inverse_ref,
    weight_ref,
    adjoint_ref,
    send_ref,
):
    modes, depth, width = weight_ref.shape
    channels = width // 2
    kz = depth // channels
    lanes = pieces_ref.shape[1] - 4 * channels
    rows_y = lanes // channels
    pieces = pieces_ref[:, :lanes]
    adjoint = analysed(pieces, rows_ref[...], y_forward_ref[...], 1, channels)
    adjoint_ref[...] = adjoint
    pulled = []
    for j in range(modes):
        real = adjoint[j * 2 * kz : j * 2 * kz + kz]
        imag = adjoint[j * 2 * kz + kz : (j + 1) * 2 * kz]
        left = jnp.concatenate(
            [jnp.concatenate([real, imag], axis=1), jnp.concatenate([imag, -real], axis=1)], axis=0
        )
        pulled.append(dot_nt(left.astype(BF16), weight_ref[j]))
    pulled = jnp.concatenate(pulled, axis=0)
    row, lane = iota(pulled.shape, 0), iota(pulled.shape, 1)
    pulled = jnp.where(row % kz == lane // channels, pulled, 0.0).astype(BF16)
    fold = selector((depth, channels), lambda row, column: row % channels == column)
    modes_back = dot(pulled, fold).astype(BF16)
    block = spread_lines(modes_back, y_inverse_ref[...], narrow, rows_y)
    repeat_rows(send_ref, block, lanes)
    piece = 2 * kz
    add = selector(
        (8, pieces_ref.shape[0]),
        lambda row, column: (row < 2) & ((column % piece) // 2 == row),
    )
    total = dot(add, pieces_ref[:, lanes:])
    total_high, total_low = halves(total[0:2])
    share = jnp.concatenate([total_high.astype(F32), total_low.astype(F32)], axis=0)
    if piece > 4:
        share = jnp.concatenate([share, jnp.zeros((piece - 4, share.shape[1]), F32)], axis=0)
    share = share.astype(BF16)
    for p in range(send_ref.shape[0] // piece):
        send_ref[p * piece : (p + 1) * piece, lanes:] = share


def outer_kernel(spectrum_ref, adjoint_ref, out_ref):
    kz = out_ref.shape[1]
    columns = jnp.transpose(spectrum_ref[0])
    adjoint = adjoint_ref[0]
    for k in range(kz):
        s_real, s_imag = columns[:, k : k + 1], columns[:, kz + k : kz + k + 1]
        a_real, a_imag = adjoint[k : k + 1], adjoint[kz + k : kz + k + 1]
        out_ref[0, k, 0] = s_real * a_real + s_imag * a_imag
        out_ref[0, k, 1] = s_real * a_imag - s_imag * a_real


def finish_kernel(
    kz,
    pieces_ref,
    rows_ref,
    z_table_ref,
    grad_pre_ref,
    mix_ref,
    turn_ref,
    grad_field_ref,
    grad_mix_ref,
    grad_head_ref,
):
    channels = mix_ref.shape[0]
    lanes = pieces_ref.shape[1] - 4 * channels
    rows_y = lanes // channels
    lines = dot(x_matrix(rows_ref[...]).astype(BF16), pieces_ref[:, :lanes]).astype(BF16)
    branch = dot_tn(lines, z_table_ref[...])
    parts = []
    for y in range(rows_y):
        cells = slice(y * channels, (y + 1) * channels)
        parts.append((branch[cells] + dot(mix_ref[...], grad_pre_ref[cells])).astype(BF16))
    grad_field_ref[...] = dot_tn(turn_ref[...], jnp.concatenate(parts, axis=0)).astype(BF16)
    piece = 2 * kz
    shares = pieces_ref[:, lanes:]

    def picked(first):
        shape = (channels, shares.shape[0])
        return dot(
            selector(
                shape,
                lambda row, column: (column // piece == row)
                & ((column % piece == first) | (column % piece == first + 2)),
            ),
            shares,
        )

    grad_head_ref[...] = picked(0)
    grad_mix_ref[...] = picked(1)[:, :channels]


def call(kernel, outs, name, flops=1 << 22):
    return pl.pallas_call(
        kernel,
        out_shape=[jax.ShapeDtypeStruct(shape, dtype) for shape, dtype in outs],
        compiler_params=pltpu.CompilerParams(vmem_limit_bytes=VMEM_LIMIT),
        cost_estimate=pl.CostEstimate(flops=flops, bytes_accessed=1 << 19, transcendentals=0),
        name=name,
    )


def body(
    lifted_field,
    spectral_weight,
    mix_weight,
    mix_bias,
    head_weight,
    head_bias,
    out_weight,
    cotangent,
):
    wide = lax.axis_size("wide")
    narrow = lax.axis_size("narrow")
    _, channels, rows_y, z_count = lifted_field.shape
    modes, kz = spectral_weight.shape[:2]
    hidden_units = head_weight.shape[1]
    total_x, total_y = wide, rows_y * narrow
    index = lax.axis_index("wide")
    cells = channels * rows_y
    extra = 4 * channels
    height = wide * 2 * MZ
    mode_lines = modes * 2 * kz

    z_plain = jnp.asarray(z_table(z_count, False))
    z_doubled = jnp.asarray(z_table(z_count, True))
    y_forward, y_inverse = y_tables(total_y, rows_y, kz, modes)
    block = index % (MY // modes)
    y_forward = lax.dynamic_index_in_dim(jnp.asarray(y_forward), block, 0, False)
    y_inverse = lax.dynamic_index_in_dim(jnp.asarray(y_inverse), block, 0, False)
    rows_forward, rows_inverse = x_rows(total_x, wide, modes)
    rows_forward = lax.dynamic_index_in_dim(jnp.asarray(rows_forward), index, 0, False)
    rows_inverse = lax.dynamic_index_in_dim(jnp.asarray(rows_inverse), index, 0, False)
    order = np.arange(cells).reshape(channels, rows_y).T.reshape(-1)
    turn = jnp.asarray(np.eye(cells, dtype=np.float32)[order].astype(BF16))

    def exchange(send):
        lanes = send.shape[1]
        pieces = send.reshape(wide * narrow, 2 * kz, lanes)
        got = lax.all_to_all(pieces, ("wide", "narrow"), split_axis=0, concat_axis=0, tiled=True)
        return got.reshape(height, lanes)

    send, field = call(
        start_kernel, [((height, cells), BF16), ((cells, z_count), BF16)], "start"
    )(lifted_field.reshape(cells, z_count), turn, z_plain)
    weight = pl.pallas_call(
        weight_kernel,
        grid=(modes,),
        in_specs=[pl.BlockSpec((1, kz, 2, channels, channels), lambda j: (j, 0, 0, 0, 0))],
        out_specs=pl.BlockSpec((1, kz * channels, 2 * channels), lambda j: (j, 0, 0)),
        out_shape=jax.ShapeDtypeStruct((modes, kz * channels, 2 * channels), BF16),
        cost_estimate=pl.CostEstimate(flops=1 << 20, bytes_accessed=5 << 20, transcendentals=0),
        name="weights",
    )(spectral_weight)
    pieces = exchange(send)
    spectrum, send = call(
        functools.partial(mode_kernel, narrow),
        [((mode_lines, channels), F32), ((height, cells), BF16)],
        "mode",
    )(pieces, rows_forward, y_forward, y_inverse, weight)
    pieces = exchange(send)
    prediction, grad_pre, send = call(
        functools.partial(cell_kernel, kz),
        [
            ((rows_y, z_count), F32),
            ((cells, z_count), BF16),
            ((height, cells + extra), BF16),
        ],
        "cell",
    )(
        pieces,
        rows_inverse,
        z_doubled,
        field,
        mix_weight,
        mix_bias[:, None],
        head_weight,
        head_bias[:, None],
        out_weight.astype(F32)[:, None],
        cotangent[0],
    )
    pieces = exchange(send)
    adjoint, send = call(
        functools.partial(back_kernel, narrow),
        [((mode_lines, channels), F32), ((height, cells + extra), BF16)],
        "back",
    )(pieces, rows_forward, y_forward, y_inverse, weight)
    pieces = exchange(send)
    grad_spectral = pl.pallas_call(
        outer_kernel,
        grid=(modes,),
        in_specs=[pl.BlockSpec((1, 2 * kz, channels), lambda j: (j, 0, 0))] * 2,
        out_specs=pl.BlockSpec((1, kz, 2, channels, channels), lambda j: (j, 0, 0, 0, 0)),
        out_shape=jax.ShapeDtypeStruct(spectral_weight.shape, F32),
        cost_estimate=pl.CostEstimate(flops=1 << 22, bytes_accessed=5 << 20, transcendentals=0),
        name="outer",
    )(spectrum.reshape(modes, 2 * kz, channels), adjoint.reshape(modes, 2 * kz, channels))
    grad_field, grad_mix, grad_head = call(
        functools.partial(finish_kernel, kz),
        [
            ((cells, z_count), BF16),
            ((channels, channels), F32),
            ((channels, hidden_units), F32),
        ],
        "finish",
    )(pieces, rows_inverse, z_plain, grad_pre, mix_weight, turn)
    return (
        prediction[None],
        grad_field.reshape(lifted_field.shape),
        grad_spectral,
        grad_mix,
        grad_head,
    )


def solution(mesh):
    return jax.shard_map(
        body,
        mesh=mesh,
        in_specs=(
            P("wide", None, "narrow", None),
            P("wide", "narrow", None, None, None),
            P(),
            P(),
            P(),
            P(),
            P(),
            P("wide", "narrow", None),
        ),
        out_specs=(
            P("wide", "narrow", None),
            P("wide", None, "narrow", None),
            P("wide", "narrow", None, None, None),
            P(),
            P(),
        ),
        check_vma=False,
    )
```

time: 207 us -> 81.9 us (0.40)
  blocking collectives: 82.4 us -> 15.4 us
  matrix products: 39.8 us -> 0 us
  Pallas kernels: 0 us -> 29.9 us
  starting transfers between devices: 37 us -> 15.5 us
  waiting for transfers between devices: 25.2 us -> 12.7 us
  other arithmetic: 7.32 us -> 0.01 us
  local copies, waits for them, and re-layouts: 13.1 us -> 6.08 us
    all_gather x2 -> x0, blocking collectives: 43.2 us -> none  [synthesis(): shard_piece = lax.all_gather(spectrum, 'wide', axis=0, tiled=True)]
    dot_general x33 -> x0, matrix products: 39.8 us -> none  [the longest x4 16.9 us: pulled(): jnp.einsum('mkio,mko->mki', weight_part, grad_part, precision=HIGHEST_PRE...]
    psum x1 -> x0, blocking collectives: 39.2 us -> none  [body(): lax.psum((mix_terms, jnp.sum(head_parts, axis=0)), ('wide', 'narrow'))]
    pallas_call x0 -> x7, Pallas kernels: none -> 29.9 us  [the longest x1 10.1 us: body(): pl.pallas_call(weight_kernel, grid=(modes,), in_specs=[pl.BlockSpec((1, k...]
    all_to_all x8 -> x3, starting transfers between devices: 37 us -> 15.5 us  [exchange(): lax.all_to_all(pieces, ('wide', 'narrow'), split_axis=0, concat_axis=0, t...]
    all_to_all x0 -> x1, blocking collectives: none -> 15.4 us  [exchange(): lax.all_to_all(pieces, ('wide', 'narrow'), split_axis=0, concat_axis=0, t...]
    all_to_all x8 -> x3, waiting for transfers between devices: 25.2 us -> 12.7 us  [exchange(): lax.all_to_all(pieces, ('wide', 'narrow'), split_axis=0, concat_axis=0, t...]
    unnamed x36, local copies, waits for them, and re-layouts: 11 us -> 4.39 us
  transfers between devices with their start and end apart: 8 -> 3, of which waited for: 6 -> 2; matrix products, arithmetic and copies ran while one was open for 3% -> 2% of each run, Pallas kernels for 0% -> 25%
where the time goes in v1:
time: 81.9 us; the launch traced here: 80.4 us
  Pallas kernels  29.9 us (37%)
  starting transfers between devices  15.5 us (19%)
  blocking collectives  15.4 us (19%)
  waiting for transfers between devices  12.7 us (16%)
  local copies, waits for them, and re-layouts  6.08 us (7%)
    all_to_all x3, starting transfers between devices, exchange(): lax.all_to_all(pieces, ('wide', 'narrow'), split_axis=0, concat_axis=0, t...  15.5 us
    all_to_all x1, blocking collectives, exchange(): lax.all_to_all(pieces, ('wide', 'narrow'), split_axis=0, concat_axis=0, t...  15.4 us
    all_to_all x3, waiting for transfers between devices, exchange(): lax.all_to_all(pieces, ('wide', 'narrow'), split_axis=0, concat_axis=0, t...  12.7 us
    pallas_call x1, Pallas kernels, body(): pl.pallas_call(weight_kernel, grid=(modes,), in_specs=[pl.BlockSpec((1, k...  10.1 us
    pallas_call x1, Pallas kernels, body(): pl.pallas_call(outer_kernel, grid=(modes,), in_specs=[pl.BlockSpec((1, 2...  9.97 us
    unnamed x36, local copies, waits for them, and re-layouts  4.39 us
    pallas_call x1, Pallas kernels, body(): call(functools.partial(cell_kernel, kz), [((rows_y, z_count), F32), ((cel...  3.39 us
    pallas_call x1, Pallas kernels, body(): call(functools.partial(back_kernel, narrow), [((mode_lines, channels), F3...  2.1 us
  transfers between devices with their start and end apart: 3, of which 2 were waited for; matrix products, arithmetic and copies ran while one was open for 2% of the time, Pallas kernels for 25%

profile of v1, /device:TPU:1, one launch (start us, length us, event | category | flops | bytes accessed | tf_op | source)
XLA Modules:
  0.0 80.4 jit_solution(141975506411077791)
XLA Ops:
  0.6 0.0 copy-start.16
  0.6 0.0 copy-start.17
  0.7 0.0 copy-start.15
  0.7 0.0 copy-start.2
  0.7 0.9 %copy-done.2 = bf16[256,256]{1,0:T(8,128)(2,1)S(1)} copy-done((bf16[256,256]{1,0:T(8,128)(2,1)S(1)}, bf16[256,256]{1,0:T(8,128)(2,1)}, u32[]{:S(2)}) %copy-start.2) | copy-done | bytes 131096
  1.6 0.0 copy-start.8
  1.6 0.8 %copy-done.8 = bf16[1,32,8,128]{3,2,1,0:T(8,128)(2,1)S(1)} copy-done((bf16[1,32,8,128]{3,2,1,0:T(8,128)(2,1)S(1)}, bf16[1,32,8,128]{3,2,1,0:T(8,128)(2,1)}, u32[]{:S(2)}) %copy-start.8) | copy-done | bytes 65560
  2.4 0.0 copy-start.10
  2.4 0.7 copy-done.10
  3.1 0.0 copy-start.4
  3.1 0.0 copy-start.5
  3.1 0.0 copy-start.9
  3.1 0.0 copy-start.12
  3.1 0.0 copy-start.13
  3.1 0.0 copy-start.14
  3.2 1.1 %start.1 = (bf16[512,256]{1,0:T(8,128)(2,1)}, bf16[256,128]{1,0:T(8,128)(2,1)S(1)}) custom-call(bf16[256,128]{1,0:T(8,128)(2,1)S(1)} %bitcast.30, bf16[256,256]{1,0:T(8,128)(2,1)S(1)} %copy-done.2, bf16[32,128]{1,0:T(8,128)(2,1)S(1)} %copy-done.10), custom_call_target="tpu_custom_call" | custom-call | flops 4194304 | bytes 524288 | tf_op jit(solution)/shard_map/start/pallas_call | solution.py:388
  4.2 7.1 %all-to-all-start = ((bf16[32,16,256]{2,1,0:T(8,128)(2,1)}), bf16[32,16,256]{2,1,0:T(8,128)(2,1)S(1)}, u32[]{:S(2)}, u32[]{:S(2)}) async-start(bf16[32,16,256]{2,1,0:T(8,128)(2,1)} %bitcast.1), calls=%async_computation | async-start | bytes 524288 | tf_op jit(solution)/shard_map/all_to_all | solution.py:385
  11.3 10.1 %weights.1.weight_ref = bf16[16,256,64]{2,1,0:T(8,128)(2,1)} custom-call(f32[16,8,2,32,32]{4,3,2,1,0:T(8,128)} %weight_ref.1), custom_call_target="tpu_custom_call" | custom-call | flops 1048576 | bytes 5242880 | tf_op jit(solution)/shard_map/weights/pallas_call | solution.py:391
  21.4 0.7 dynamic-slice_bitcast_fusion.1.rows_ref
  22.1 0.0 all-to-all-done
  22.1 0.0 copy-done.4
  22.1 0.0 copy-done.5
  22.1 0.0 copy-start
  22.1 1.2 %copy-done = bf16[16,256,64]{2,1,0:T(8,128)(2,1)S(1)} copy-done((bf16[16,256,64]{2,1,0:T(8,128)(2,1)S(1)}, bf16[16,256,64]{2,1,0:T(8,128)(2,1)}, u32[]{:S(2)}) %copy-start) | copy-done | bytes 524312
  23.3 0.0 copy-start.1
  23.3 2.0 %mode.1 = (f32[256,32]{1,0:T(8,128)S(1)}, bf16[512,256]{1,0:T(8,128)(2,1)}) custom-call(bf16[512,256]{1,0:T(8,128)(2,1)S(1)} %bitcast.26, f32[2,512]{1,0:T(2,128)S(1)} %dynamic-slice_bitcast_fusion.1.rows_ref, bf16[256,256]{1,0:T(8,128)(2,1)S(1)} %copy-done.5, bf16[256,256]{1,0:T(8,128)(2,1)S(1)} %copy-done.4, bf16[16,256,64]{2,1,0:T(8,128)(2,1)S(1)} %copy-done), custom_call_target="tpu_custom_call" | custom-call | flops 4194304 | bytes 524288 | tf_op jit(solution)/shard_map/mode/pallas_call | solution.py:401
  25.4 0.0 copy-start.6
  25.4 5.8 %all-to-all-start.1 = ((bf16[32,16,256]{2,1,0:T(8,128)(2,1)}), bf16[32,16,256]{2,1,0:T(8,128)(2,1)S(1)}, u32[]{:S(2)}, u32[]{:S(2)}) async-start(bf16[32,16,256]{2,1,0:T(8,128)(2,1)} %bitcast.4), calls=%async_computation.1 | async-start | bytes 524288 | tf_op jit(solution)/shard_map/all_to_all | solution.py:385
  31.2 0.0 copy-done.16
  31.2 0.1 copy.20.mix_bias_ref
  31.3 0.0 copy-done.6
  31.3 0.0 copy-done.17
  31.3 0.0 copy-start.3
  31.3 0.0 copy-start.11
  31.3 0.1 copy.22.out_weight_ref
  31.4 0.0 copy-done.15
  31.5 0.1 copy.21.head_bias_ref
  31.6 0.7 dynamic-slice_bitcast_fusion.rows_ref
  32.3 9.5 %all-to-all-done.1 = bf16[32,16,256]{2,1,0:T(8,128)(2,1)S(1)} async-done(((bf16[32,16,256]{2,1,0:T(8,128)(2,1)}), bf16[32,16,256]{2,1,0:T(8,128)(2,1)S(1)}, u32[]{:S(2)}, u32[]{:S(2)}) %all-to-all-start.1) | async-done | bytes 262176 | tf_op jit(solution)/shard_map/all_to_all | solution.py:385
  41.8 0.0 copy-done.9
  41.8 0.0 copy-done.12
  41.8 0.0 copy-done.13
  41.8 0.0 copy-done.14
  41.8 3.4 %cell.1 = (f32[8,128]{1,0:T(8,128)}, bf16[256,128]{1,0:T(8,128)(2,1)S(1)}, bf16[512,384]{1,0:T(8,128)(2,1)S(1)}) custom-call(bf16[512,256]{1,0:T(8,128)(2,1)S(1)} %bitcast.25, f32[2,512]{1,0:T(2,128)S(1)} %dynamic-slice_bitcast_fusion.rows_ref, bf16[32,128]{1,0:T(8,128)(2,1)S(1)} %copy-done.13, bf16[256,128]{1,0:T(8,128)(2,1)S(1)} %get-tuple-element.19.field_ref, ...), custom_call_target="tpu_custom_call" | custom-call | flops 4194304 | bytes 524288 | tf_op jit(solution)/shard_map/cell/pallas_call | solution.py:407
  45.2 15.4 %all_to_all.20 = bf16[32,16,384]{2,1,0:T(8,128)(2,1)S(1)} all-to-all(bf16[32,16,384]{2,1,0:T(8,128)(2,1)S(1)} %bitcast.27), channel_id=1, replica_groups=mesh['wide'=16,'narrow'=2] {'wide','narrow'}, dimensions={0} | all-to-all | bytes 786432 | tf_op jit(solution)/shard_map/all_to_all | solution.py:385
  60.6 0.0 copy-done.1
  60.6 2.1 %back.1 = (f32[256,32]{1,0:T(8,128)S(1)}, bf16[512,384]{1,0:T(8,128)(2,1)}) custom-call(bf16[512,384]{1,0:T(8,128)(2,1)S(1)} %bitcast.24, f32[2,512]{1,0:T(2,128)S(1)} %dynamic-slice_bitcast_fusion.1.rows_ref, bf16[256,256]{1,0:T(8,128)(2,1)S(1)} %copy-done.5, bf16[256,256]{1,0:T(8,128)(2,1)S(1)} %copy-done.4, bf16[16,256,64]{2,1,0:T(8,128)(2,1)S(1)} %copy-done.1), custom_call_target="tpu_custom_call" | custom-call | flops 4194304 | bytes 524288 | tf_op jit(solution)/shard_map/back/pallas_call | solution.py:428
  62.7 0.0 copy-start.7
  62.7 0.7 copy-done.7
  63.4 2.6 %all-to-all-start.3 = ((bf16[32,16,384]{2,1,0:T(8,128)(2,1)}), bf16[32,16,384]{2,1,0:T(8,128)(2,1)S(1)}, u32[]{:S(2)}, u32[]{:S(2)}) async-start(bf16[32,16,384]{2,1,0:T(8,128)(2,1)} %bitcast.14), calls=%async_computation.3 | async-start | bytes 786432 | tf_op jit(solution)/shard_map/all_to_all | solution.py:385
  66.0 10.0 %outer.1 = f32[16,8,2,32,32]{4,3,2,1,0:T(8,128)} custom-call(f32[16,16,32]{2,1,0:T(8,128)} %bitcast.28, f32[16,16,32]{2,1,0:T(8,128)} %bitcast.29), custom_call_target="tpu_custom_call" | custom-call | flops 4194304 | bytes 5242880 | tf_op jit(solution)/shard_map/outer/pallas_call | solution.py:434
  76.0 3.2 %all-to-all-done.3 = bf16[32,16,384]{2,1,0:T(8,128)(2,1)S(1)} async-done(((bf16[32,16,384]{2,1,0:T(8,128)(2,1)}), bf16[32,16,384]{2,1,0:T(8,128)(2,1)S(1)}, u32[]{:S(2)}, u32[]{:S(2)}) %all-to-all-start.3) | async-done | bytes 393248 | tf_op jit(solution)/shard_map/all_to_all | solution.py:385
  79.2 0.0 copy-done.3
  79.2 0.0 copy-done.11
  79.2 1.2 %finish.1 = (bf16[256,128]{1,0:T(8,128)(2,1)}, f32[32,32]{1,0:T(8,128)}, f32[32,128]{1,0:T(8,128)}) custom-call(bf16[512,384]{1,0:T(8,128)(2,1)S(1)} %bitcast.23, f32[2,512]{1,0:T(2,128)S(1)} %dynamic-slice_bitcast_fusion.rows_ref, bf16[32,128]{1,0:T(8,128)(2,1)S(1)} %copy-done.11, bf16[256,128]{1,0:T(8,128)(2,1)S(1)} %get-tuple-element.23.grad_pre_ref, ...), custom_call_target="tpu_custom_call" | custom-call | flops 4194304 | bytes 524288 | tf_op jit(solution)/shard_map/finish/pallas_call | solution.py:443
  (1 shorter events, 0.0 us)
Async XLA Ops:
  0.6 30.6 %copy-start.16 = (f32[32]{0:T(128)S(1)}, f32[32]{0:T(128)}, u32[]{:S(2)}) copy-start(f32[32]{0:T(128)} %param.18) | copy-start | bytes 388
  0.6 30.7 %copy-start.17 = (bf16[128]{0:T(256)(128)(2,1)S(1)}, bf16[128]{0:T(256)(128)(2,1)}, u32[]{:S(2)}) copy-start(bf16[128]{0:T(256)(128)(2,1)} %param.21) | copy-start | bytes 772
  0.7 30.8 %copy-start.15 = (f32[128]{0:T(128)S(1)}, f32[128]{0:T(128)}, u32[]{:S(2)}) copy-start(f32[128]{0:T(128)} %param.20) | copy-start | bytes 1540
  0.7 0.9 %copy-start.2 = (bf16[256,256]{1,0:T(8,128)(2,1)S(1)}, bf16[256,256]{1,0:T(8,128)(2,1)}, u32[]{:S(2)}) copy-start(bf16[256,256]{1,0:T(8,128)(2,1)} %constant.48.clone.turn_ref) | copy-start | bytes 393220
  1.6 0.8 %copy-start.8 = (bf16[1,32,8,128]{3,2,1,0:T(8,128)(2,1)S(1)}, bf16[1,32,8,128]{3,2,1,0:T(8,128)(2,1)}, u32[]{:S(2)}) copy-start(bf16[1,32,8,128]{3,2,1,0:T(8,128)(2,1)} %param.15) | copy-start | bytes 196612
  2.4 0.7 copy-start.10
  3.1 19.0 %copy-start.4 = (bf16[256,256]{1,0:T(8,128)(2,1)S(1)}, bf16[256,256]{1,0:T(8,128)(2,1)}, u32[]{:S(2)}) copy-start(bf16[256,256]{1,0:T(8,128)(2,1)} %constant.52.y_inverse_ref) | copy-start | bytes 393220
  3.1 19.0 %copy-start.5 = (bf16[256,256]{1,0:T(8,128)(2,1)S(1)}, bf16[256,256]{1,0:T(8,128)(2,1)}, u32[]{:S(2)}) copy-start(bf16[256,256]{1,0:T(8,128)(2,1)} %constant.51.y_forward_ref) | copy-start | bytes 393220
  3.1 38.6 %copy-start.9 = (bf16[32,32]{1,0:T(8,128)(2,1)S(1)}, bf16[32,32]{1,0:T(8,128)(2,1)}, u32[]{:S(2)}) copy-start(bf16[32,32]{1,0:T(8,128)(2,1)} %mix_ref.3) | copy-start | bytes 6148
  3.1 38.6 %copy-start.12 = (bf16[32,128]{1,0:T(8,128)(2,1)S(1)}, bf16[32,128]{1,0:T(8,128)(2,1)}, u32[]{:S(2)}) copy-start(bf16[32,128]{1,0:T(8,128)(2,1)} %head_ref.1) | copy-start | bytes 24580
  3.1 38.6 %copy-start.13 = (bf16[32,128]{1,0:T(8,128)(2,1)S(1)}, bf16[32,128]{1,0:T(8,128)(2,1)}, u32[]{:S(2)}) copy-start(bf16[32,128]{1,0:T(8,128)(2,1)} %constant.43.clone.z_doubled_ref) | copy-start | bytes 24580
  3.1 38.6 %copy-start.14 = (f32[1,8,128]{2,1,0:T(8,128)S(1)}, f32[1,8,128]{2,1,0:T(8,128)}, u32[]{:S(2)}) copy-start(f32[1,8,128]{2,1,0:T(8,128)} %param.22) | copy-start | bytes 12292
  4.2 17.9 %all-to-all-start = ((bf16[32,16,256]{2,1,0:T(8,128)(2,1)}), bf16[32,16,256]{2,1,0:T(8,128)(2,1)S(1)}, u32[]{:S(2)}, u32[]{:S(2)}) async-start(bf16[32,16,256]{2,1,0:T(8,128)(2,1)} %bitcast.1), calls=%async_computation | async-start | bytes 524288 | tf_op jit(solution)/shard_map/all_to_all | solution.py:385
  22.1 1.2 %copy-start = (bf16[16,256,64]{2,1,0:T(8,128)(2,1)S(1)}, bf16[16,256,64]{2,1,0:T(8,128)(2,1)}, u32[]{:S(2)}) copy-start(bf16[16,256,64]{2,1,0:T(8,128)(2,1)} %weights.1.weight_ref) | copy-start | bytes 1572868
  23.3 37.3 %copy-start.1 = (bf16[16,256,64]{2,1,0:T(8,128)(2,1)S(1)}, bf16[16,256,64]{2,1,0:T(8,128)(2,1)}, u32[]{:S(2)}) copy-start(bf16[16,256,64]{2,1,0:T(8,128)(2,1)} %weights.1.weight_ref) | copy-start | bytes 1572868
  25.4 5.9 %copy-start.6 = (f32[256,32]{1,0:T(8,128)}, f32[256,32]{1,0:T(8,128)S(1)}, u32[]{:S(2)}) copy-start(f32[256,32]{1,0:T(8,128)S(1)} %get-tuple-element.25) | copy-start | bytes 98308
  25.4 16.4 %all-to-all-start.1 = ((bf16[32,16,256]{2,1,0:T(8,128)(2,1)}), bf16[32,16,256]{2,1,0:T(8,128)(2,1)S(1)}, u32[]{:S(2)}, u32[]{:S(2)}) async-start(bf16[32,16,256]{2,1,0:T(8,128)(2,1)} %bitcast.4), calls=%async_computation.1 | async-start | bytes 524288 | tf_op jit(solution)/shard_map/all_to_all | solution.py:385
  31.3 47.9 %copy-start.3 = (bf16[256,256]{1,0:T(8,128)(2,1)S(1)}, bf16[256,256]{1,0:T(8,128)(2,1)}, u32[]{:S(2)}) copy-start(bf16[256,256]{1,0:T(8,128)(2,1)} %constant.48.clone.turn_ref) | copy-start | bytes 393220
  31.3 47.9 %copy-start.11 = (bf16[32,128]{1,0:T(8,128)(2,1)S(1)}, bf16[32,128]{1,0:T(8,128)(2,1)}, u32[]{:S(2)}) copy-start(bf16[32,128]{1,0:T(8,128)(2,1)} %constant.42.clone.table_ref.z_table_ref) | copy-start | bytes 24580
  62.7 0.7 copy-start.7
  63.4 15.8 %all-to-all-start.3 = ((bf16[32,16,384]{2,1,0:T(8,128)(2,1)}), bf16[32,16,384]{2,1,0:T(8,128)(2,1)S(1)}, u32[]{:S(2)}, u32[]{:S(2)}) async-start(bf16[32,16,384]{2,1,0:T(8,128)(2,1)} %bitcast.14), calls=%async_computation.3 | async-start | bytes 786432 | tf_op jit(solution)/shard_map/all_to_all | solution.py:385

commit v2 on v1

v2 whole, which is shorter than its diff:
```python
import functools
import math

import jax
import jax.numpy as jnp
import numpy as np
from jax import lax
from jax.experimental import pallas as pl
from jax.experimental.pallas import tpu as pltpu
from jax.sharding import PartitionSpec as P

MX = 16
MY = 16
MZ = 16
F32 = jnp.float32
BF16 = jnp.bfloat16
VMEM_LIMIT = 32 * 1024 * 1024


def signed(indices, count):
    return np.where(indices < count // 2, indices, indices - count)


def wave(positions, frequency, length):
    turned = np.mod(np.multiply.outer(positions, frequency), length)
    angles = turned.astype(np.float32) * np.float32(2.0 * math.pi / length)
    scale = np.float32(1.0 / math.sqrt(length))
    return np.cos(angles) * scale, np.sin(angles) * scale


def pair(cosine, sine, sign):
    return np.stack(
        [np.stack([cosine, -sign * sine], -1), np.stack([sign * sine, cosine], -1)], -2
    )


def y_tables(total_y, rows_y, kz, modes):
    cosine, sine = wave(np.arange(total_y), signed(np.arange(MY), MY), total_y)
    narrow = total_y // rows_y
    same = np.eye(kz, dtype=np.float32)
    forward = pair(cosine, sine, -1.0).reshape(narrow, rows_y, MY // modes, modes, 2, 2)
    inverse = pair(cosine, sine, 1.0).reshape(narrow, rows_y, MY // modes, modes, 2, 2)
    forward = np.einsum("nybjtr,kl->bjtkynlr", forward, same)
    inverse = np.einsum("nybjst,kl->bnyksjtl", inverse, same)
    blocks = MY // modes
    forward = forward.reshape(blocks, modes * 2 * kz, rows_y * narrow * kz * 2)
    inverse = inverse.reshape(blocks, narrow * rows_y * kz * 2, modes * 2 * kz)
    return forward.astype(BF16), inverse.astype(BF16)


def dot(a, b):
    return jnp.dot(a, b, preferred_element_type=F32)


def dot_nt(a, b):
    return lax.dot_general(a, b, (((1,), (1,)), ((), ())), preferred_element_type=F32)


def dot_tn(a, b):
    return lax.dot_general(a, b, (((0,), (0,)), ((), ())), preferred_element_type=F32)


def grid_of(rows, columns):
    shape = (rows, columns)
    return lax.broadcasted_iota(jnp.int32, shape, 0), lax.broadcasted_iota(jnp.int32, shape, 1)


def selector(rows, columns, condition):
    return jnp.where(condition(*grid_of(rows, columns)), 1.0, 0.0).astype(BF16)


def halves(values):
    high = values.astype(BF16)
    return high, (values - high.astype(F32)).astype(BF16)


def stacked(refs, lanes=slice(None)):
    return jnp.concatenate([ref[:, lanes] for ref in refs], axis=0)


def cosine_of(phase, length):
    angles = (phase & (length - 1)).astype(F32) * (2.0 * math.pi / length)
    return jnp.cos(angles) * (1.0 / math.sqrt(length))


class Place:
    def __init__(self, wide, narrow, kz, modes, rows_y, channels, z_count, fold):
        self.wide, self.narrow, self.kz, self.modes = wide, narrow, kz, modes
        self.rows_y, self.channels, self.z_count, self.fold = rows_y, channels, z_count, fold
        self.inner = 1 << ((wide.bit_length() - 1) // 2)
        self.outer = wide // self.inner
        self.plane = self.inner * narrow
        self.lanes = rows_y * channels

    def here(self):
        wide, narrow = lax.axis_index("wide"), lax.axis_index("narrow")
        return wide // self.inner, wide % self.inner, narrow

    def frequency(self, wide):
        index = (wide * self.modes) // MY
        return jnp.where(index < MX // 2, index, index - MX)

    def z_table(self, doubled):
        row, z = grid_of(2 * MZ, self.z_count)
        _, _, narrow = self.here()
        part = row & 1
        line = row >> 1
        frequency = ((line // self.kz) ^ narrow) * self.kz + line % self.kz
        value = cosine_of(z * frequency + part * (self.z_count // 4), self.z_count)
        if doubled:
            value = jnp.where(frequency > 0, 2.0 * value, value)
        return value.astype(BF16)

    def expanded(self, small, same):
        rows, columns = grid_of(2 * MZ, small.shape[1])
        blocks = []
        for g in range(small.shape[0] // 2):
            value = jnp.where((rows & 1) == 0, small[2 * g : 2 * g + 1], small[2 * g + 1 : 2 * g + 2])
            blocks.append(jnp.where(same(rows >> 1, columns, g), value, 0.0))
        return jnp.concatenate(blocks, axis=0)

    def forward_x(self):
        outer, inner, narrow = self.here()
        plane = inner * self.narrow + narrow
        row, column = grid_of(2 * self.outer, self.plane * 2 * self.kz)
        source = plane ^ (column // (2 * self.kz))
        x = outer * self.inner + source // self.narrow
        frequency = self.frequency((outer ^ (row >> 1)) * self.inner + inner)
        quarter = self.wide // 4
        small = cosine_of(x * frequency + quarter * ((row & 1) - (column & 1)), self.wide)

        def same(line, column, _):
            source = plane ^ (column // (2 * self.kz))
            half, k = source % self.narrow, (column >> 1) % self.kz
            return line == half * self.kz + k

        return self.expanded(small, same)

    def inverse_x(self):
        outer, inner, narrow = self.here()
        row, column = grid_of(2 * self.inner, self.outer * 2 * MZ)
        source = outer ^ (column // (2 * MZ))
        x = outer * self.inner + (inner ^ (row >> 1))
        frequency = self.frequency(source * self.inner + inner)
        quarter = self.wide // 4
        small = cosine_of(x * frequency + quarter * ((column & 1) - (row & 1)), self.wide)

        def same(line, column, _):
            line = ((line // self.kz) ^ narrow) * self.kz + line % self.kz
            return line == (column >> 1) % MZ

        return self.expanded(small, same).astype(BF16)


def analysed(place, pieces, y_forward, copies):
    turned = sum(ref[:, : place.lanes].astype(F32) for ref in pieces)
    channels = place.channels
    lines = jnp.concatenate(
        [turned[:, y * channels : (y + 1) * channels] for y in range(place.rows_y)], axis=0
    )
    high, low = halves(jnp.concatenate([lines] * copies, axis=1))
    return dot(y_forward, high) + dot(y_forward, low)


def spread_lines(place, modes, y_inverse):
    lines = dot(y_inverse, modes)
    step = 2 * place.kz
    blocks = []
    for n in range(place.narrow):
        first = n * place.rows_y
        parts = [lines[(first + y) * step : (first + y + 1) * step] for y in range(place.rows_y)]
        blocks.append(jnp.concatenate(parts, axis=1))
    return jnp.concatenate(blocks, axis=0).astype(BF16)


def received_lines(place, pieces, z_table):
    blocks = []
    for half in range(place.narrow):
        own = [pieces[s][:, : place.lanes].astype(F32) for s in range(half, place.plane, place.narrow)]
        blocks.append(sum(own[1:], own[0]))
    return dot_tn(jnp.concatenate(blocks, axis=0).astype(BF16), z_table)


def start_kernel(place, field_ref, field_out_ref, *send_refs):
    channels, rows_y = place.channels, place.rows_y
    turn = selector(
        place.lanes,
        place.lanes,
        lambda row, column: (row % channels == column // rows_y)
        & (row // channels == column % rows_y),
    )
    turned = dot(turn, field_ref[...]).astype(BF16)
    field_out_ref[...] = turned
    spectra = dot_nt(place.z_table(False), turned)
    step = 2 * place.kz
    for t, ref in enumerate(send_refs):
        ref[...] = spectra[t * step : (t + 1) * step].astype(BF16)


def weight_kernel(weight_ref, out_ref):
    modes, kz, _, channels, _ = weight_ref.shape
    for j in range(modes):
        both = jnp.concatenate([weight_ref[j, :, 0], weight_ref[j, :, 1]], axis=-1)
        out_ref[j] = both.reshape(kz * channels, 2 * channels).astype(BF16)


def fold_kernel(place, *refs):
    pieces, sends = refs[: place.plane], refs[place.plane :]
    high, low = halves(place.forward_x())
    values = stacked(pieces, slice(0, place.lanes))
    partial = (dot(high, values) + dot(low, values)).astype(BF16)
    for s, ref in enumerate(sends):
        ref[:, : place.lanes] = partial[s * 2 * MZ : (s + 1) * 2 * MZ]
    if pieces[0].shape[1] > place.lanes:
        outer, _, _ = place.here()
        shares = sum(ref[:, place.lanes :].astype(F32) for ref in pieces)
        count = 2 * place.outer
        high, low = halves(shares[:count] + shares[count : 2 * count])
        split = jnp.concatenate([high, low], axis=0)
        place_of = selector(
            place.outer * 2 * MZ,
            2 * count,
            lambda row, column: (row % (2 * MZ) == column // place.outer)
            & ((row // (2 * MZ)) ^ outer == column % place.outer),
        )
        chosen = dot(place_of, split).astype(BF16)
        for s, ref in enumerate(sends):
            ref[:, place.lanes :] = chosen[s * 2 * MZ : (s + 1) * 2 * MZ]


def mode_kernel(place, *refs):
    pieces = refs[: place.outer]
    y_forward_ref, y_inverse_ref, weight_ref, spectrum_ref, send_ref = refs[place.outer :]
    kz, channels = place.kz, place.channels
    spectrum = analysed(place, pieces, y_forward_ref[...], kz)
    spectrum_ref[...] = spectrum[:, :channels]
    row, lane = grid_of(*spectrum.shape)
    blocked = jnp.where(row % kz == lane // channels, spectrum, 0.0)
    mixed = []
    for j in range(place.modes):
        left = blocked[j * 2 * kz : (j + 1) * 2 * kz].astype(BF16)
        product = dot(left, weight_ref[j])
        real, imag = product[:, :channels], product[:, channels:]
        mixed.append(real[:kz] - imag[kz:])
        mixed.append(imag[:kz] + real[kz:])
    mode = jnp.concatenate(mixed, axis=0).astype(BF16)
    send_ref[...] = spread_lines(place, mode, y_inverse_ref[...])


def part_kernel(place, *refs):
    pieces, sends = refs[: place.outer], refs[place.outer :]
    lines = dot(place.inverse_x(), stacked(pieces, slice(0, place.lanes))).astype(BF16)
    step = 2 * place.kz
    for s, ref in enumerate(sends):
        ref[:, : place.lanes] = lines[s * step : (s + 1) * step]
    if pieces[0].shape[1] > place.lanes:
        outer, _, _ = place.here()
        shares = stacked(pieces, slice(place.lanes, None))
        gather = selector(
            step,
            shares.shape[0],
            lambda row, column: (column % (2 * MZ) == row // place.outer)
            & ((column // (2 * MZ)) ^ outer == row % place.outer),
        )
        chosen = dot(gather, shares).astype(BF16)
        for ref in sends:
            ref[:, place.lanes :] = chosen


def normal(values):
    cumulative = 0.5 * (1.0 + lax.erf(values * (1.0 / math.sqrt(2.0))))
    density = jnp.exp(-0.5 * values * values) * (1.0 / math.sqrt(2.0 * math.pi))
    return values * cumulative, cumulative + values * density


def cell_kernel(place, *refs):
    pieces, refs = refs[: place.plane], refs[place.plane :]
    field_ref, mix_ref, mix_bias_ref, head_ref, head_bias_ref, out_weight_ref, cotangent_ref = refs[:7]
    prediction_ref, grad_pre_ref = refs[7:9]
    sends = refs[9 : 9 + (place.plane if place.fold else place.narrow)]
    channels, hidden_units = head_ref.shape
    z_table = place.z_table(True)
    branch = received_lines(place, pieces, z_table)
    mix, head = mix_ref[...], head_ref[...]
    mix_bias, head_bias = mix_bias_ref[...], head_bias_ref[...]
    out_weight = out_weight_ref[...]
    grad_mix = jnp.zeros((channels, channels), F32)
    grad_head = jnp.zeros((channels, hidden_units), F32)
    gradients = []
    for y in range(place.rows_y):
        cells = slice(y * channels, (y + 1) * channels)
        field = field_ref[cells]
        pre_act = branch[cells] + dot_tn(mix, field) + mix_bias
        hidden, pre_slope = normal(pre_act)
        hidden = hidden.astype(BF16)
        head_pre = dot_tn(head, hidden) + head_bias
        active, slope = normal(head_pre)
        active = active.astype(BF16).astype(F32)
        prediction_ref[y : y + 1] = jnp.sum(active * out_weight, axis=0, keepdims=True)
        head_slope = (cotangent_ref[y : y + 1] * out_weight * slope).astype(BF16)
        grad_pre = (dot(head, head_slope) * pre_slope).astype(BF16)
        grad_head += dot_nt(hidden, head_slope)
        grad_mix += dot_nt(field, grad_pre)
        gradients.append(grad_pre)

    gradient = jnp.concatenate(gradients, axis=0)
    grad_pre_ref[...] = gradient
    spectra = dot_nt(z_table, gradient)
    step = 2 * place.kz
    for s, ref in enumerate(sends):
        t = s % place.narrow
        ref[:, : place.lanes] = spectra[t * step : (t + 1) * step].astype(BF16)
    if not place.fold:
        refs[-2][...] = grad_mix
        refs[-1][...] = grad_head
        return
    wide_mix = jnp.concatenate(
        [grad_mix, jnp.zeros((channels, hidden_units - channels), F32)], axis=1
    )
    head_high, head_low = halves(grad_head)
    mix_high, mix_low = halves(wide_mix)
    shares = jnp.concatenate([head_high, mix_high, head_low, mix_low], axis=0)
    _, inner, narrow = place.here()
    plane = inner * place.narrow + narrow

    def chosen(row, column):
        kind, owner = (row % step) // place.outer, row % place.outer
        target = owner * place.plane + ((row // step) ^ plane)
        return column == kind * channels + target

    split = dot(selector(place.plane * step, 4 * channels, chosen), shares).astype(BF16)
    for s, ref in enumerate(sends):
        ref[:, place.lanes :] = split[s * step : (s + 1) * step]


def back_kernel(place, *refs):
    pieces = refs[: place.outer]
    y_forward_ref, y_inverse_ref, weight_ref, adjoint_ref, send_ref = refs[place.outer :]
    kz, channels = place.kz, place.channels
    adjoint = analysed(place, pieces, y_forward_ref[...], 1)
    adjoint_ref[...] = adjoint
    pulled = []
    for j in range(place.modes):
        real = adjoint[j * 2 * kz : j * 2 * kz + kz]
        imag = adjoint[j * 2 * kz + kz : (j + 1) * 2 * kz]
        left = jnp.concatenate(
            [jnp.concatenate([real, imag], axis=1), jnp.concatenate([imag, -real], axis=1)], axis=0
        )
        pulled.append(dot_nt(left.astype(BF16), weight_ref[j]))
    pulled = jnp.concatenate(pulled, axis=0)
    row, lane = grid_of(*pulled.shape)
    pulled = jnp.where(row % kz == lane // channels, pulled, 0.0).astype(BF16)
    gather = selector(
        kz * channels, channels, lambda row, column: row % channels == column
    )
    modes_back = dot(pulled, gather).astype(BF16)
    send_ref[:, : place.lanes] = spread_lines(place, modes_back, y_inverse_ref[...])
    if place.fold:
        shares = sum(ref[:, place.lanes :].astype(F32) for ref in pieces)
        high, low = halves(shares[0:2] + shares[2:4])
        rest = jnp.zeros((2 * MZ - 4, shares.shape[1]), F32)
        split = jnp.concatenate([high.astype(F32), low.astype(F32), rest], axis=0)
        send_ref[:, place.lanes :] = split.astype(BF16)


def outer_kernel(spectrum_ref, adjoint_ref, out_ref):
    modes, kz = out_ref.shape[:2]
    for j in range(modes):
        columns = jnp.transpose(spectrum_ref[j])
        adjoint = adjoint_ref[j]
        for k in range(kz):
            s_real, s_imag = columns[:, k : k + 1], columns[:, kz + k : kz + k + 1]
            a_real, a_imag = adjoint[k : k + 1], adjoint[kz + k : kz + k + 1]
            out_ref[j, k, 0] = s_real * a_real + s_imag * a_imag
            out_ref[j, k, 1] = s_real * a_imag - s_imag * a_real


def finish_kernel(place, *refs):
    pieces, refs = refs[: place.plane], refs[place.plane :]
    grad_pre_ref, mix_ref, grad_field_ref = refs[:3]
    channels, rows_y = place.channels, place.rows_y
    branch = received_lines(place, pieces, place.z_table(False))
    parts = []
    for y in range(rows_y):
        cells = slice(y * channels, (y + 1) * channels)
        parts.append((branch[cells] + dot(mix_ref[...], grad_pre_ref[cells])).astype(BF16))
    turn = selector(
        place.lanes,
        place.lanes,
        lambda row, column: (row // rows_y == column % channels)
        & (row % rows_y == column // channels),
    )
    grad_field_ref[...] = dot(turn, jnp.concatenate(parts, axis=0)).astype(BF16)
    if not place.fold:
        return
    grad_mix_ref, grad_head_ref = refs[3:]
    _, inner, narrow = place.here()
    plane = inner * place.narrow + narrow
    step = 2 * place.kz
    shares = stacked(pieces, slice(place.lanes, None))

    def picked(first):
        def condition(row, column):
            kind, owner = (column % step) // place.outer, column % place.outer
            target = owner * place.plane + ((column // step) ^ plane)
            return (target == row) & (kind % 2 == first)

        return dot(selector(channels, shares.shape[0], condition), shares)

    grad_head_ref[...] = picked(0)
    grad_mix_ref[...] = picked(1)[:, :channels]


def call(kernel, outs, name):
    return pl.pallas_call(
        kernel,
        out_shape=[jax.ShapeDtypeStruct(shape, dtype) for shape, dtype in outs],
        compiler_params=pltpu.CompilerParams(vmem_limit_bytes=VMEM_LIMIT),
        cost_estimate=pl.CostEstimate(flops=1 << 22, bytes_accessed=1 << 19, transcendentals=0),
        name=name,
    )


def body(
    lifted_field,
    spectral_weight,
    mix_weight,
    mix_bias,
    head_weight,
    head_bias,
    out_weight,
    cotangent,
):
    wide = lax.axis_size("wide")
    narrow = lax.axis_size("narrow")
    devices = wide * narrow
    _, channels, rows_y, z_count = lifted_field.shape
    modes, kz = spectral_weight.shape[:2]
    hidden_units = head_weight.shape[1]
    cells = channels * rows_y
    place = Place(wide, narrow, kz, modes, rows_y, channels, z_count, False)
    place.fold = devices == channels and 4 * place.outer == 2 * kz and hidden_units % 128 == 0
    extra = hidden_units if place.fold else 0
    step = 2 * kz
    mode_lines = modes * 2 * kz

    y_forward, y_inverse = y_tables(rows_y * narrow, rows_y, kz, modes)
    if len(y_forward) > 1:
        block = lax.axis_index("wide") % len(y_forward)
        y_forward = lax.dynamic_index_in_dim(jnp.asarray(y_forward), block, 0, False)
        y_inverse = lax.dynamic_index_in_dim(jnp.asarray(y_inverse), block, 0, False)
    else:
        y_forward, y_inverse = jnp.asarray(y_forward[0]), jnp.asarray(y_inverse[0])

    def moved(sends, stride):
        got = [sends[0]]
        for s in range(1, len(sends)):
            pairs = [(p, p ^ (s * stride)) for p in range(devices)]
            got.append(lax.ppermute(sends[s], ("wide", "narrow"), pairs))
        return got

    def along_plane(sends):
        return moved([sends[s % len(sends)] for s in range(place.plane)], 1)

    def along_outer(sends):
        return moved([sends[s % len(sends)] for s in range(place.outer)], place.plane)

    def fold(pieces, lanes):
        kernel = functools.partial(fold_kernel, place)
        return call(kernel, [((2 * MZ, lanes), BF16)] * place.outer, "fold")(*pieces)

    def part(pieces, lanes):
        kernel = functools.partial(part_kernel, place)
        return call(kernel, [((step, lanes), BF16)] * place.plane, "part")(*pieces)

    field, *sends = call(
        functools.partial(start_kernel, place),
        [((cells, z_count), BF16)] + [((step, cells), BF16)] * narrow,
        "start",
    )(lifted_field.reshape(cells, z_count))
    some = max(1, modes // 4)
    weight = pl.pallas_call(
        weight_kernel,
        grid=(modes // some,),
        in_specs=[pl.BlockSpec((some, kz, 2, channels, channels), lambda j: (j, 0, 0, 0, 0))],
        out_specs=pl.BlockSpec((some, kz * channels, 2 * channels), lambda j: (j, 0, 0)),
        out_shape=jax.ShapeDtypeStruct((modes, kz * channels, 2 * channels), BF16),
        compiler_params=pltpu.CompilerParams(vmem_limit_bytes=VMEM_LIMIT),
        cost_estimate=pl.CostEstimate(flops=1 << 20, bytes_accessed=5 << 20, transcendentals=0),
        name="weights",
    )(spectral_weight)
    pieces = along_outer(fold(along_plane(sends), cells))
    spectrum, send = call(
        functools.partial(mode_kernel, place),
        [((mode_lines, channels), F32), ((2 * MZ, cells), BF16)],
        "mode",
    )(*pieces, y_forward, y_inverse, weight)
    pieces = along_plane(part(along_outer([send]), cells))
    outs = [((rows_y, z_count), F32), ((cells, z_count), BF16)]
    if place.fold:
        outs += [((step, cells + extra), BF16)] * place.plane
    else:
        outs += [((step, cells), BF16)] * narrow
        outs += [((channels, channels), F32), ((channels, hidden_units), F32)]
    prediction, grad_pre, *sends = call(functools.partial(cell_kernel, place), outs, "cell")(
        *pieces,
        field,
        mix_weight,
        mix_bias[:, None],
        head_weight,
        head_bias[:, None],
        out_weight.astype(F32)[:, None],
        cotangent[0],
    )
    sums = ()
    if not place.fold:
        sums = lax.psum(tuple(sends[-2:]), ("wide", "narrow"))
        sends = sends[:-2]
    pieces = along_outer(fold(along_plane(sends), cells + extra))
    adjoint, send = call(
        functools.partial(back_kernel, place),
        [((mode_lines, channels), F32), ((2 * MZ, cells + extra), BF16)],
        "back",
    )(*pieces, y_forward, y_inverse, weight)
    pieces = along_plane(part(along_outer([send]), cells + extra))
    grad_spectral = pl.pallas_call(
        outer_kernel,
        grid=(modes // some,),
        in_specs=[pl.BlockSpec((some, 2 * kz, channels), lambda j: (j, 0, 0))] * 2,
        out_specs=pl.BlockSpec((some, kz, 2, channels, channels), lambda j: (j, 0, 0, 0, 0)),
        out_shape=jax.ShapeDtypeStruct(spectral_weight.shape, F32),
        compiler_params=pltpu.CompilerParams(vmem_limit_bytes=VMEM_LIMIT),
        cost_estimate=pl.CostEstimate(flops=1 << 22, bytes_accessed=5 << 20, transcendentals=0),
        name="outer",
    )(spectrum.reshape(modes, 2 * kz, channels), adjoint.reshape(modes, 2 * kz, channels))
    outs = [((cells, z_count), BF16)]
    if place.fold:
        outs += [((channels, channels), F32), ((channels, hidden_units), F32)]
    grad_field, *totals = call(functools.partial(finish_kernel, place), outs, "finish")(
        *pieces, grad_pre, mix_weight
    )
    grad_mix, grad_head = totals if place.fold else sums
    return (
        prediction[None],
        grad_field.reshape(lifted_field.shape),
        grad_spectral,
        grad_mix,
        grad_head,
    )


def solution(mesh):
    return jax.shard_map(
        body,
        mesh=mesh,
        in_specs=(
            P("wide", None, "narrow", None),
            P("wide", "narrow", None, None, None),
            P(),
            P(),
            P(),
            P(),
            P(),
            P("wide", "narrow", None),
        ),
        out_specs=(
            P("wide", "narrow", None),
            P("wide", None, "narrow", None),
            P("wide", "narrow", None, None, None),
            P(),
            P(),
        ),
        check_vma=False,
    )
```

time: 81.9 us -> 82.7 us (level)
  starting transfers between devices: 15.5 us -> 45 us
  Pallas kernels: 29.9 us -> 11.7 us
  blocking collectives: 15.4 us -> 0 us
  waiting for transfers between devices: 12.7 us -> 20.6 us
  local copies, waits for them, and re-layouts: 6.08 us -> 3.41 us
    ppermute x0 -> x40, starting transfers between devices: none -> 45 us  [moved(): got.append(lax.ppermute(sends[s], ('wide', 'narrow'), pairs))]
    ppermute x0 -> x40, waiting for transfers between devices: none -> 20.6 us  [moved(): got.append(lax.ppermute(sends[s], ('wide', 'narrow'), pairs))]
    pallas_call x7 -> x11, Pallas kernels: 29.9 us -> 11.7 us  [the longest x1 3.53 us: body(): pl.pallas_call(outer_kernel, grid=(modes // some,), in_specs=[pl.BlockSpe...]
    all_to_all x3 -> x0, starting transfers between devices: 15.5 us -> none  [exchange(): lax.all_to_all(pieces, ('wide', 'narrow'), split_axis=0, concat_axis=0, t...]
    all_to_all x1 -> x0, blocking collectives: 15.4 us -> none  [exchange(): lax.all_to_all(pieces, ('wide', 'narrow'), split_axis=0, concat_axis=0, t...]
    all_to_all x3 -> x0, waiting for transfers between devices: 12.7 us -> none  [exchange(): lax.all_to_all(pieces, ('wide', 'narrow'), split_axis=0, concat_axis=0, t...]
    squeeze x2 -> x0, local copies, waits for them, and re-layouts: 1.38 us -> none  [the longest x1 0.69 us: body(): lax.dynamic_index_in_dim(jnp.asarray(rows_inverse), index, 0, False)]
    unnamed x36 -> x20, local copies, waits for them, and re-layouts: 4.39 us -> 3.09 us
  transfers between devices with their start and end apart: 3 -> 40, of which waited for: 2 -> 11; matrix products, arithmetic and copies ran while one was open for 2% -> 0% of each run, Pallas kernels for 25% -> 5%
where the time goes in v2:
time: 82.7 us; the launch traced here: 81.6 us
  starting transfers between devices  45 us (54%)
  waiting for transfers between devices  20.6 us (25%)
  Pallas kernels  11.7 us (14%)
  local copies, waits for them, and re-layouts  3.41 us (4%)
    ppermute x40, starting transfers between devices, moved(): got.append(lax.ppermute(sends[s], ('wide', 'narrow'), pairs))  45 us
    ppermute x40, waiting for transfers between devices, moved(): got.append(lax.ppermute(sends[s], ('wide', 'narrow'), pairs))  20.6 us
    pallas_call x1, Pallas kernels, body(): pl.pallas_call(outer_kernel, grid=(modes // some,), in_specs=[pl.BlockSpe...  3.53 us
    pallas_call x1, Pallas kernels, body(): call(functools.partial(cell_kernel, place), outs, 'cell')  3.11 us
    unnamed x20, local copies, waits for them, and re-layouts  3.09 us
  transfers between devices with their start and end apart: 40, of which 11 were waited for; matrix products, arithmetic and copies ran while one was open for 0% of the time, Pallas kernels for 5%

profile of v2, /device:TPU:1, one launch (start us, length us, event | category | flops | bytes accessed | tf_op | source)
XLA Modules:
  0.0 81.6 jit_solution(13411648682375872690)
XLA Ops:
  0.7 0.9 %copy-done.3 = bf16[1,32,8,128]{3,2,1,0:T(8,128)(2,1)S(1)} copy-done((bf16[1,32,8,128]{3,2,1,0:T(8,128)(2,1)S(1)}, bf16[1,32,8,128]{3,2,1,0:T(8,128)(2,1)}, u32[]{:S(2)}) %copy-start.3) | copy-done | bytes 65560
  1.5 0.3 start.1
  1.8 2.1 %collective-permute-start = (bf16[16,256]{1,0:T(8,128)(2,1)S(1)}, bf16[16,256]{1,0:T(8,128)(2,1)S(1)}, u32[]{:S(2)}, u32[]{:S(2)}) collective-permute-start(bf16[16,256]{1,0:T(8,128)(2,1)S(1)} %get-tuple-element.50), channel_id=1, source_target_pairs={{0,1},{1,0},{2,3},{3,2},{4,5},{5,4},{6,7},{7,6},{8,9},{9,8},{10,11... | collective-permute-start | bytes 24584 | tf_op jit(solution)/shard_map/ppermute | solution.py:459
  3.9 1.0 %collective-permute-start.1 = (bf16[16,256]{1,0:T(8,128)(2,1)S(1)}, bf16[16,256]{1,0:T(8,128)(2,1)S(1)}, u32[]{:S(2)}, u32[]{:S(2)}) collective-permute-start(bf16[16,256]{1,0:T(8,128)(2,1)S(1)} %get-tuple-element.49.refs_0_), channel_id=1, source_target_pairs={{0,2},{1,3},{2,0},{3,1},{4,6},{5,7},{6,4},{7,5},{8,10},{9,11},{10,... | collective-permute-start | bytes 24584 | tf_op jit(solution)/shard_map/ppermute | solution.py:459
  4.9 1.4 %collective-permute-start.3 = (bf16[16,256]{1,0:T(8,128)(2,1)S(1)}, bf16[16,256]{1,0:T(8,128)(2,1)S(1)}, u32[]{:S(2)}, u32[]{:S(2)}) collective-permute-start(bf16[16,256]{1,0:T(8,128)(2,1)S(1)} %get-tuple-element.49.refs_0_), channel_id=1, source_target_pairs={{0,4},{1,5},{2,6},{3,7},{4,0},{5,1},{6,2},{7,3},{8,12},{9,13},{10,... | collective-permute-start | bytes 24584 | tf_op jit(solution)/shard_map/ppermute | solution.py:459
  6.2 1.2 %collective-permute-start.4 = (bf16[16,256]{1,0:T(8,128)(2,1)S(1)}, bf16[16,256]{1,0:T(8,128)(2,1)S(1)}, u32[]{:S(2)}, u32[]{:S(2)}) collective-permute-start(bf16[16,256]{1,0:T(8,128)(2,1)S(1)} %get-tuple-element.50), channel_id=1, source_target_pairs={{0,5},{1,4},{2,7},{3,6},{4,1},{5,0},{6,3},{7,2},{8,13},{9,12},{10,... | collective-permute-start | bytes 24584 | tf_op jit(solution)/shard_map/ppermute | solution.py:459
  7.4 2.2 %collective-permute-start.5 = (bf16[16,256]{1,0:T(8,128)(2,1)S(1)}, bf16[16,256]{1,0:T(8,128)(2,1)S(1)}, u32[]{:S(2)}, u32[]{:S(2)}) collective-permute-start(bf16[16,256]{1,0:T(8,128)(2,1)S(1)} %get-tuple-element.49.refs_0_), channel_id=1, source_target_pairs={{0,6},{1,7},{2,4},{3,5},{4,2},{5,3},{6,0},{7,1},{8,14},{9,15},{10,... | collective-permute-start | bytes 24584 | tf_op jit(solution)/shard_map/ppermute | solution.py:459
  9.6 1.5 %collective-permute-done.5.refs_6_ = bf16[16,256]{1,0:T(8,128)(2,1)S(1)} collective-permute-done((bf16[16,256]{1,0:T(8,128)(2,1)S(1)}, bf16[16,256]{1,0:T(8,128)(2,1)S(1)}, u32[]{:S(2)}, u32[]{:S(2)}) %collective-permute-start.5) | collective-permute-done | bytes 8224 | tf_op jit(solution)/shard_map/ppermute | solution.py:459
  11.2 2.4 %collective-permute-done.6.refs_7_ = bf16[16,256]{1,0:T(8,128)(2,1)S(1)} collective-permute-done((bf16[16,256]{1,0:T(8,128)(2,1)S(1)}, bf16[16,256]{1,0:T(8,128)(2,1)S(1)}, u32[]{:S(2)}, u32[]{:S(2)}) %collective-permute-start.6) | collective-permute-done | bytes 8224 | tf_op jit(solution)/shard_map/ppermute | solution.py:459
  13.6 0.2 fold.2
  13.8 1.4 %collective-permute-start.7 = (bf16[32,256]{1,0:T(8,128)(2,1)S(1)}, bf16[32,256]{1,0:T(8,128)(2,1)S(1)}, u32[]{:S(2)}, u32[]{:S(2)}) collective-permute-start(bf16[32,256]{1,0:T(8,128)(2,1)S(1)} %get-tuple-element.52), channel_id=1, source_target_pairs={{0,8},{1,9},{2,10},{3,11},{4,12},{5,13},{6,14},{7,15},{8,0},{9,1},... | collective-permute-start | bytes 49160 | tf_op jit(solution)/shard_map/ppermute | solution.py:459
  15.2 2.3 %collective-permute-start.8 = (bf16[32,256]{1,0:T(8,128)(2,1)S(1)}, bf16[32,256]{1,0:T(8,128)(2,1)S(1)}, u32[]{:S(2)}, u32[]{:S(2)}) collective-permute-start(bf16[32,256]{1,0:T(8,128)(2,1)S(1)} %get-tuple-element.53), channel_id=1, source_target_pairs={{0,16},{1,17},{2,18},{3,19},{4,20},{5,21},{6,22},{7,23},{8,24},{9,... | collective-permute-start | bytes 49160 | tf_op jit(solution)/shard_map/ppermute | solution.py:459
  17.5 2.2 %copy-done = f32[16,8,2,32,32]{4,3,2,1,0:T(8,128)S(1)} copy-done((f32[16,8,2,32,32]{4,3,2,1,0:T(8,128)S(1)}, f32[16,8,2,32,32]{4,3,2,1,0:T(8,128)}, u32[]{:S(2)}) %copy-start) | copy-done | bytes 1048600
  19.7 0.6 weights.1.refs_6_
  20.3 1.6 %collective-permute-done.9.refs_3_ = bf16[32,256]{1,0:T(8,128)(2,1)S(1)} collective-permute-done((bf16[32,256]{1,0:T(8,128)(2,1)S(1)}, bf16[32,256]{1,0:T(8,128)(2,1)S(1)}, u32[]{:S(2)}, u32[]{:S(2)}) %collective-permute-start.9) | collective-permute-done | bytes 16416 | tf_op jit(solution)/shard_map/ppermute | solution.py:459
  21.9 1.1 %mode.1 = (f32[256,32]{1,0:T(8,128)S(1)}, bf16[32,256]{1,0:T(8,128)(2,1)S(1)}) custom-call(bf16[32,256]{1,0:T(8,128)(2,1)S(1)} %get-tuple-element.51.refs_0_, bf16[32,256]{1,0:T(8,128)(2,1)S(1)} %collective-permute-done.7.refs_1_, bf16[32,256]{1,0:T(8,128)(2,1)S(1)} %collective-permute-done.8.refs_2_, bf16[32,256]{1,0:T(8,128)(2,1)S(1)} %collective-permute-done.9.refs_3_, ...), custom_call_target="tpu_custom_call" | custom-call | flops 4194304 | bytes 524288 | tf_op jit(solution)/shard_map/mode/pallas_call | solution.py:493
  23.0 0.1 collective-permute-start.10
  23.0 2.2 %collective-permute-start.11 = (bf16[32,256]{1,0:T(8,128)(2,1)S(1)}, bf16[32,256]{1,0:T(8,128)(2,1)S(1)}, u32[]{:S(2)}, u32[]{:S(2)}) collective-permute-start(bf16[32,256]{1,0:T(8,128)(2,1)S(1)} %get-tuple-element.55.refs_0_), channel_id=1, source_target_pairs={{0,16},{1,17},{2,18},{3,19},{4,20},{5,21},{6,22},{7,23},{8,24},{9,... | collective-permute-start | bytes 49160 | tf_op jit(solution)/shard_map/ppermute | solution.py:459
  25.3 1.3 %collective-permute-start.12 = (bf16[32,256]{1,0:T(8,128)(2,1)S(1)}, bf16[32,256]{1,0:T(8,128)(2,1)S(1)}, u32[]{:S(2)}, u32[]{:S(2)}) collective-permute-start(bf16[32,256]{1,0:T(8,128)(2,1)S(1)} %get-tuple-element.55.refs_0_), channel_id=1, source_target_pairs={{0,24},{1,25},{2,26},{3,27},{4,28},{5,29},{6,30},{7,31},{8,16},{9,... | collective-permute-start | bytes 49160 | tf_op jit(solution)/shard_map/ppermute | solution.py:459
  26.6 3.2 %collective-permute-done.12.refs_3_ = bf16[32,256]{1,0:T(8,128)(2,1)S(1)} collective-permute-done((bf16[32,256]{1,0:T(8,128)(2,1)S(1)}, bf16[32,256]{1,0:T(8,128)(2,1)S(1)}, u32[]{:S(2)}, u32[]{:S(2)}) %collective-permute-start.12) | collective-permute-done | bytes 16416 | tf_op jit(solution)/shard_map/ppermute | solution.py:459
  29.8 0.2 part.2
  30.0 0.3 collective-permute-start.13
  30.3 2.2 %collective-permute-start.14 = (bf16[16,256]{1,0:T(8,128)(2,1)S(1)}, bf16[16,256]{1,0:T(8,128)(2,1)S(1)}, u32[]{:S(2)}, u32[]{:S(2)}) collective-permute-start(bf16[16,256]{1,0:T(8,128)(2,1)S(1)} %get-tuple-element.58), channel_id=1, source_target_pairs={{0,2},{1,3},{2,0},{3,1},{4,6},{5,7},{6,4},{7,5},{8,10},{9,11},{10,... | collective-permute-start | bytes 24584 | tf_op jit(solution)/shard_map/ppermute | solution.py:459
  32.5 1.1 %collective-permute-start.15 = (bf16[16,256]{1,0:T(8,128)(2,1)S(1)}, bf16[16,256]{1,0:T(8,128)(2,1)S(1)}, u32[]{:S(2)}, u32[]{:S(2)}) collective-permute-start(bf16[16,256]{1,0:T(8,128)(2,1)S(1)} %get-tuple-element.59), channel_id=1, source_target_pairs={{0,3},{1,2},{2,1},{3,0},{4,7},{5,6},{6,5},{7,4},{8,11},{9,10},{10,... | collective-permute-start | bytes 24584 | tf_op jit(solution)/shard_map/ppermute | solution.py:459
  33.6 0.7 collective-permute-start.16
  34.3 0.7 collective-permute-start.17
  35.0 1.7 %collective-permute-start.18 = (bf16[16,256]{1,0:T(8,128)(2,1)S(1)}, bf16[16,256]{1,0:T(8,128)(2,1)S(1)}, u32[]{:S(2)}, u32[]{:S(2)}) collective-permute-start(bf16[16,256]{1,0:T(8,128)(2,1)S(1)} %get-tuple-element.62), channel_id=1, source_target_pairs={{0,6},{1,7},{2,4},{3,5},{4,2},{5,3},{6,0},{7,1},{8,14},{9,15},{10,... | collective-permute-start | bytes 24584 | tf_op jit(solution)/shard_map/ppermute | solution.py:459
  36.7 1.0 %collective-permute-start.19 = (bf16[16,256]{1,0:T(8,128)(2,1)S(1)}, bf16[16,256]{1,0:T(8,128)(2,1)S(1)}, u32[]{:S(2)}, u32[]{:S(2)}) collective-permute-start(bf16[16,256]{1,0:T(8,128)(2,1)S(1)} %get-tuple-element.63), channel_id=1, source_target_pairs={{0,7},{1,6},{2,5},{3,4},{4,3},{5,2},{6,1},{7,0},{8,15},{9,14},{10,... | collective-permute-start | bytes 24584 | tf_op jit(solution)/shard_map/ppermute | solution.py:459
  37.7 0.1 copy.17.refs_13_
  37.8 0.1 copy.16.refs_12_
  37.9 0.1 copy.15.refs_10_
  38.1 2.6 %collective-permute-done.19.refs_7_ = bf16[16,256]{1,0:T(8,128)(2,1)S(1)} collective-permute-done((bf16[16,256]{1,0:T(8,128)(2,1)S(1)}, bf16[16,256]{1,0:T(8,128)(2,1)S(1)}, u32[]{:S(2)}, u32[]{:S(2)}) %collective-permute-start.19) | collective-permute-done | bytes 8224 | tf_op jit(solution)/shard_map/ppermute | solution.py:459
  40.7 3.1 %cell.1 = (f32[8,128]{1,0:T(8,128)}, bf16[256,128]{1,0:T(8,128)(2,1)S(1)}, bf16[16,384]{1,0:T(8,128)(2,1)S(1)}, bf16[16,384]{1,0:T(8,128)(2,1)S(1)}, bf16[16,384...) custom-call(bf16[16,256]{1,0:T(8,128)(2,1)S(1)} %get-tuple-element.5, ...), custom_call_target="tpu_custom_call" | custom-call | flops 4194304 | bytes 524288 | tf_op jit(solution)/shard_map/cell/pallas_call | solution.py:505
  43.8 1.2 %collective-permute-start.20 = (bf16[16,384]{1,0:T(8,128)(2,1)S(1)}, bf16[16,384]{1,0:T(8,128)(2,1)S(1)}, u32[]{:S(2)}, u32[]{:S(2)}) collective-permute-start(bf16[16,384]{1,0:T(8,128)(2,1)S(1)} %get-tuple-element.67), channel_id=1, source_target_pairs={{0,1},{1,0},{2,3},{3,2},{4,5},{5,4},{6,7},{7,6},{8,9},{9,8},{10,11... | collective-permute-start | bytes 36872 | tf_op jit(solution)/shard_map/ppermute | solution.py:459
  45.0 0.6 collective-permute-start.22
  45.7 0.7 collective-permute-start.23
  46.4 1.7 %collective-permute-start.24 = (bf16[16,384]{1,0:T(8,128)(2,1)S(1)}, bf16[16,384]{1,0:T(8,128)(2,1)S(1)}, u32[]{:S(2)}, u32[]{:S(2)}) collective-permute-start(bf16[16,384]{1,0:T(8,128)(2,1)S(1)} %get-tuple-element.71), channel_id=1, source_target_pairs={{0,5},{1,4},{2,7},{3,6},{4,1},{5,0},{6,3},{7,2},{8,13},{9,12},{10,... | collective-permute-start | bytes 36872 | tf_op jit(solution)/shard_map/ppermute | solution.py:459
  48.1 1.2 %collective-permute-start.25 = (bf16[16,384]{1,0:T(8,128)(2,1)S(1)}, bf16[16,384]{1,0:T(8,128)(2,1)S(1)}, u32[]{:S(2)}, u32[]{:S(2)}) collective-permute-start(bf16[16,384]{1,0:T(8,128)(2,1)S(1)} %get-tuple-element.72), channel_id=1, source_target_pairs={{0,6},{1,7},{2,4},{3,5},{4,2},{5,3},{6,0},{7,1},{8,14},{9,15},{10,... | collective-permute-start | bytes 36872 | tf_op jit(solution)/shard_map/ppermute | solution.py:459
  49.2 0.5 collective-permute-start.26
  49.8 0.0 collective-permute-done.24.refs_5_
  49.8 1.5 %collective-permute-done.25.refs_6_ = bf16[16,384]{1,0:T(8,128)(2,1)S(1)} collective-permute-done((bf16[16,384]{1,0:T(8,128)(2,1)S(1)}, bf16[16,384]{1,0:T(8,128)(2,1)S(1)}, u32[]{:S(2)}, u32[]{:S(2)}) %collective-permute-start.25) | collective-permute-done | bytes 12320 | tf_op jit(solution)/shard_map/ppermute | solution.py:459
  51.4 1.9 %collective-permute-done.26.refs_7_ = bf16[16,384]{1,0:T(8,128)(2,1)S(1)} collective-permute-done((bf16[16,384]{1,0:T(8,128)(2,1)S(1)}, bf16[16,384]{1,0:T(8,128)(2,1)S(1)}, u32[]{:S(2)}, u32[]{:S(2)}) %collective-permute-start.26) | collective-permute-done | bytes 12320 | tf_op jit(solution)/shard_map/ppermute | solution.py:459
  53.3 0.2 fold.3
  53.5 0.1 collective-permute-start.27
  53.6 2.4 %collective-permute-start.28 = (bf16[32,384]{1,0:T(8,128)(2,1)S(1)}, bf16[32,384]{1,0:T(8,128)(2,1)S(1)}, u32[]{:S(2)}, u32[]{:S(2)}) collective-permute-start(bf16[32,384]{1,0:T(8,128)(2,1)S(1)} %get-tuple-element.76), channel_id=1, source_target_pairs={{0,16},{1,17},{2,18},{3,19},{4,20},{5,21},{6,22},{7,23},{8,24},{9,... | collective-permute-start | bytes 73736 | tf_op jit(solution)/shard_map/ppermute | solution.py:459
  56.0 1.1 %collective-permute-start.29 = (bf16[32,384]{1,0:T(8,128)(2,1)S(1)}, bf16[32,384]{1,0:T(8,128)(2,1)S(1)}, u32[]{:S(2)}, u32[]{:S(2)}) collective-permute-start(bf16[32,384]{1,0:T(8,128)(2,1)S(1)} %get-tuple-element.77), channel_id=1, source_target_pairs={{0,24},{1,25},{2,26},{3,27},{4,28},{5,29},{6,30},{7,31},{8,16},{9,... | collective-permute-start | bytes 73736 | tf_op jit(solution)/shard_map/ppermute | solution.py:459
  57.1 0.1 collective-permute-done.28.refs_2_
  57.3 3.3 %collective-permute-done.29.refs_3_ = bf16[32,384]{1,0:T(8,128)(2,1)S(1)} collective-permute-done((bf16[32,384]{1,0:T(8,128)(2,1)S(1)}, bf16[32,384]{1,0:T(8,128)(2,1)S(1)}, u32[]{:S(2)}, u32[]{:S(2)}) %collective-permute-start.29) | collective-permute-done | bytes 24608 | tf_op jit(solution)/shard_map/ppermute | solution.py:459
  60.5 1.0 %back.1 = (f32[256,32]{1,0:T(8,128)S(1)}, bf16[32,384]{1,0:T(8,128)(2,1)S(1)}) custom-call(bf16[32,384]{1,0:T(8,128)(2,1)S(1)} %get-tuple-element.74.refs_0_, bf16[32,384]{1,0:T(8,128)(2,1)S(1)} %collective-permute-done.27.refs_1_, bf16[32,384]{1,0:T(8,128)(2,1)S(1)} %collective-permute-done.28.refs_2_, bf16[32,384]{1,0:T(8,128)(2,1)S(1)} %collective-permute-done.29.refs_3_, ...), custom_call_target="tpu_custom_call" | custom-call | flops 4194304 | bytes 524288 | tf_op jit(solution)/shard_map/back/pallas_call | solution.py:520
  61.5 0.1 collective-permute-start.30
  61.6 1.4 %collective-permute-start.31 = (bf16[32,384]{1,0:T(8,128)(2,1)S(1)}, bf16[32,384]{1,0:T(8,128)(2,1)S(1)}, u32[]{:S(2)}, u32[]{:S(2)}) collective-permute-start(bf16[32,384]{1,0:T(8,128)(2,1)S(1)} %get-tuple-element.78.refs_0_), channel_id=1, source_target_pairs={{0,16},{1,17},{2,18},{3,19},{4,20},{5,21},{6,22},{7,23},{8,24},{9,... | collective-permute-start | bytes 73736 | tf_op jit(solution)/shard_map/ppermute | solution.py:459
  63.0 2.2 %collective-permute-start.32 = (bf16[32,384]{1,0:T(8,128)(2,1)S(1)}, bf16[32,384]{1,0:T(8,128)(2,1)S(1)}, u32[]{:S(2)}, u32[]{:S(2)}) collective-permute-start(bf16[32,384]{1,0:T(8,128)(2,1)S(1)} %get-tuple-element.78.refs_0_), channel_id=1, source_target_pairs={{0,24},{1,25},{2,26},{3,27},{4,28},{5,29},{6,30},{7,31},{8,16},{9,... | collective-permute-start | bytes 73736 | tf_op jit(solution)/shard_map/ppermute | solution.py:459
  65.2 0.1 collective-permute-done.31.refs_2_
  65.3 2.3 %collective-permute-done.32.refs_3_ = bf16[32,384]{1,0:T(8,128)(2,1)S(1)} collective-permute-done((bf16[32,384]{1,0:T(8,128)(2,1)S(1)}, bf16[32,384]{1,0:T(8,128)(2,1)S(1)}, u32[]{:S(2)}, u32[]{:S(2)}) %collective-permute-start.32) | collective-permute-done | bytes 24608 | tf_op jit(solution)/shard_map/ppermute | solution.py:459
  67.6 0.2 part.3
  67.8 0.3 collective-permute-start.33
  68.1 3.5 %collective-permute-start.34 = (bf16[16,384]{1,0:T(8,128)(2,1)S(1)}, bf16[16,384]{1,0:T(8,128)(2,1)S(1)}, u32[]{:S(2)}, u32[]{:S(2)}) collective-permute-start(bf16[16,384]{1,0:T(8,128)(2,1)S(1)} %get-tuple-element.81), channel_id=1, source_target_pairs={{0,2},{1,3},{2,0},{3,1},{4,6},{5,7},{6,4},{7,5},{8,10},{9,11},{10,... | collective-permute-start | bytes 36872 | tf_op jit(solution)/shard_map/ppermute | solution.py:459
  71.6 1.1 %collective-permute-start.35 = (bf16[16,384]{1,0:T(8,128)(2,1)S(1)}, bf16[16,384]{1,0:T(8,128)(2,1)S(1)}, u32[]{:S(2)}, u32[]{:S(2)}) collective-permute-start(bf16[16,384]{1,0:T(8,128)(2,1)S(1)} %get-tuple-element.82), channel_id=1, source_target_pairs={{0,3},{1,2},{2,1},{3,0},{4,7},{5,6},{6,5},{7,4},{8,11},{9,10},{10,... | collective-permute-start | bytes 36872 | tf_op jit(solution)/shard_map/ppermute | solution.py:459
  72.8 0.7 collective-permute-start.36
  73.5 0.7 collective-permute-start.37
  74.2 1.7 %collective-permute-start.38 = (bf16[16,384]{1,0:T(8,128)(2,1)S(1)}, bf16[16,384]{1,0:T(8,128)(2,1)S(1)}, u32[]{:S(2)}, u32[]{:S(2)}) collective-permute-start(bf16[16,384]{1,0:T(8,128)(2,1)S(1)} %get-tuple-element.85), channel_id=1, source_target_pairs={{0,6},{1,7},{2,4},{3,5},{4,2},{5,3},{6,0},{7,1},{8,14},{9,15},{10,... | collective-permute-start | bytes 36872 | tf_op jit(solution)/shard_map/ppermute | solution.py:459
  75.9 1.0 %collective-permute-start.39 = (bf16[16,384]{1,0:T(8,128)(2,1)S(1)}, bf16[16,384]{1,0:T(8,128)(2,1)S(1)}, u32[]{:S(2)}, u32[]{:S(2)}) collective-permute-start(bf16[16,384]{1,0:T(8,128)(2,1)S(1)} %get-tuple-element.86), channel_id=1, source_target_pairs={{0,7},{1,6},{2,5},{3,4},{4,3},{5,2},{6,1},{7,0},{8,15},{9,14},{10,... | collective-permute-start | bytes 36872 | tf_op jit(solution)/shard_map/ppermute | solution.py:459
  76.9 3.5 %outer.1 = f32[16,8,2,32,32]{4,3,2,1,0:T(8,128)} custom-call(f32[16,16,32]{2,1,0:T(8,128)S(1)} %bitcast.11, f32[16,16,32]{2,1,0:T(8,128)S(1)} %bitcast.12), custom_call_target="tpu_custom_call" | custom-call | flops 4194304 | bytes 5242880 | tf_op jit(solution)/shard_map/outer/pallas_call | solution.py:526
  80.5 1.1 %finish.1 = (bf16[256,128]{1,0:T(8,128)(2,1)}, f32[32,32]{1,0:T(8,128)}, f32[32,128]{1,0:T(8,128)}) custom-call(bf16[16,384]{1,0:T(8,128)(2,1)S(1)} %get-tuple-element.79.refs_0_, bf16[16,384]{1,0:T(8,128)(2,1)S(1)} %collective-permute-done.33.refs_1_, bf16[16,384]{1,0:T(8,128)(2,1)S(1)} %collective-permute-done.34.refs_2_, ...), custom_call_target="tpu_custom_call" | custom-call | flops 4194304 | bytes 524288 | tf_op jit(solution)/shard_map/finish/pallas_call | solution.py:539
  (51 shorter events, 0.2 us)
Async XLA Ops:
  0.6 21.2 %copy-start.1 = (bf16[256,256]{1,0:T(8,128)(2,1)S(1)}, bf16[256,256]{1,0:T(8,128)(2,1)}, u32[]{:S(2)}) copy-start(bf16[256,256]{1,0:T(8,128)(2,1)} %constant.4.clone.refs_4_) | copy-start | bytes 393220
  0.6 0.9 %copy-start.3 = (bf16[1,32,8,128]{3,2,1,0:T(8,128)(2,1)S(1)}, bf16[1,32,8,128]{3,2,1,0:T(8,128)(2,1)}, u32[]{:S(2)}) copy-start(bf16[1,32,8,128]{3,2,1,0:T(8,128)(2,1)} %param.10) | copy-start | bytes 196612
  1.5 36.3 %copy-start.7 = (f32[128]{0:T(128)S(1)}, f32[128]{0:T(128)}, u32[]{:S(2)}) copy-start(f32[128]{0:T(128)} %param.15) | copy-start | bytes 1540
  1.5 36.4 %copy-start.8 = (f32[32]{0:T(128)S(1)}, f32[32]{0:T(128)}, u32[]{:S(2)}) copy-start(f32[32]{0:T(128)} %param.13) | copy-start | bytes 388
  1.5 39.2 %copy-start.4 = (bf16[32,32]{1,0:T(8,128)(2,1)S(1)}, bf16[32,32]{1,0:T(8,128)(2,1)}, u32[]{:S(2)}) copy-start(bf16[32,32]{1,0:T(8,128)(2,1)} %refs_9_.3) | copy-start | bytes 6148
  1.5 39.2 %copy-start.6 = (f32[1,8,128]{2,1,0:T(8,128)S(1)}, f32[1,8,128]{2,1,0:T(8,128)}, u32[]{:S(2)}) copy-start(f32[1,8,128]{2,1,0:T(8,128)} %param.17) | copy-start | bytes 12292
  1.8 5.5 %collective-permute-start = (bf16[16,256]{1,0:T(8,128)(2,1)S(1)}, bf16[16,256]{1,0:T(8,128)(2,1)S(1)}, u32[]{:S(2)}, u32[]{:S(2)}) collective-permute-start(bf16[16,256]{1,0:T(8,128)(2,1)S(1)} %get-tuple-element.50), channel_id=1, source_target_pairs={{0,1},{1,0},{2,3},{3,2},{4,5},{5,4},{6,7},{7,6},{8,9},{9,8},{10,11... | collective-permute-start | bytes 24584 | tf_op jit(solution)/shard_map/ppermute | solution.py:459
  3.9 5.7 %collective-permute-start.1 = (bf16[16,256]{1,0:T(8,128)(2,1)S(1)}, bf16[16,256]{1,0:T(8,128)(2,1)S(1)}, u32[]{:S(2)}, u32[]{:S(2)}) collective-permute-start(bf16[16,256]{1,0:T(8,128)(2,1)S(1)} %get-tuple-element.49.refs_0_), channel_id=1, source_target_pairs={{0,2},{1,3},{2,0},{3,1},{4,6},{5,7},{6,4},{7,5},{8,10},{9,11},{10,... | collective-permute-start | bytes 24584 | tf_op jit(solution)/shard_map/ppermute | solution.py:459
  4.9 4.8 %collective-permute-start.2 = (bf16[16,256]{1,0:T(8,128)(2,1)S(1)}, bf16[16,256]{1,0:T(8,128)(2,1)S(1)}, u32[]{:S(2)}, u32[]{:S(2)}) collective-permute-start(bf16[16,256]{1,0:T(8,128)(2,1)S(1)} %get-tuple-element.50), channel_id=1, source_target_pairs={{0,3},{1,2},{2,1},{3,0},{4,7},{5,6},{6,5},{7,4},{8,11},{9,10},{10,... | collective-permute-start | bytes 24584 | tf_op jit(solution)/shard_map/ppermute | solution.py:459
  4.9 4.8 %collective-permute-start.3 = (bf16[16,256]{1,0:T(8,128)(2,1)S(1)}, bf16[16,256]{1,0:T(8,128)(2,1)S(1)}, u32[]{:S(2)}, u32[]{:S(2)}) collective-permute-start(bf16[16,256]{1,0:T(8,128)(2,1)S(1)} %get-tuple-element.49.refs_0_), channel_id=1, source_target_pairs={{0,4},{1,5},{2,6},{3,7},{4,0},{5,1},{6,2},{7,3},{8,12},{9,13},{10,... | collective-permute-start | bytes 24584 | tf_op jit(solution)/shard_map/ppermute | solution.py:459
  6.2 3.4 %collective-permute-start.4 = (bf16[16,256]{1,0:T(8,128)(2,1)S(1)}, bf16[16,256]{1,0:T(8,128)(2,1)S(1)}, u32[]{:S(2)}, u32[]{:S(2)}) collective-permute-start(bf16[16,256]{1,0:T(8,128)(2,1)S(1)} %get-tuple-element.50), channel_id=1, source_target_pairs={{0,5},{1,4},{2,7},{3,6},{4,1},{5,0},{6,3},{7,2},{8,13},{9,12},{10,... | collective-permute-start | bytes 24584 | tf_op jit(solution)/shard_map/ppermute | solution.py:459
  7.4 3.8 %collective-permute-start.5 = (bf16[16,256]{1,0:T(8,128)(2,1)S(1)}, bf16[16,256]{1,0:T(8,128)(2,1)S(1)}, u32[]{:S(2)}, u32[]{:S(2)}) collective-permute-start(bf16[16,256]{1,0:T(8,128)(2,1)S(1)} %get-tuple-element.49.refs_0_), channel_id=1, source_target_pairs={{0,6},{1,7},{2,4},{3,5},{4,2},{5,3},{6,0},{7,1},{8,14},{9,15},{10,... | collective-permute-start | bytes 24584 | tf_op jit(solution)/shard_map/ppermute | solution.py:459
  9.6 4.0 %collective-permute-start.6 = (bf16[16,256]{1,0:T(8,128)(2,1)S(1)}, bf16[16,256]{1,0:T(8,128)(2,1)S(1)}, u32[]{:S(2)}, u32[]{:S(2)}) collective-permute-start(bf16[16,256]{1,0:T(8,128)(2,1)S(1)} %get-tuple-element.50), channel_id=1, source_target_pairs={{0,7},{1,6},{2,5},{3,4},{4,3},{5,2},{6,1},{7,0},{8,15},{9,14},{10,... | collective-permute-start | bytes 24584 | tf_op jit(solution)/shard_map/ppermute | solution.py:459
  13.8 6.5 %collective-permute-start.7 = (bf16[32,256]{1,0:T(8,128)(2,1)S(1)}, bf16[32,256]{1,0:T(8,128)(2,1)S(1)}, u32[]{:S(2)}, u32[]{:S(2)}) collective-permute-start(bf16[32,256]{1,0:T(8,128)(2,1)S(1)} %get-tuple-element.52), channel_id=1, source_target_pairs={{0,8},{1,9},{2,10},{3,11},{4,12},{5,13},{6,14},{7,15},{8,0},{9,1},... | collective-permute-start | bytes 49160 | tf_op jit(solution)/shard_map/ppermute | solution.py:459
  15.2 5.1 %collective-permute-start.8 = (bf16[32,256]{1,0:T(8,128)(2,1)S(1)}, bf16[32,256]{1,0:T(8,128)(2,1)S(1)}, u32[]{:S(2)}, u32[]{:S(2)}) collective-permute-start(bf16[32,256]{1,0:T(8,128)(2,1)S(1)} %get-tuple-element.53), channel_id=1, source_target_pairs={{0,16},{1,17},{2,18},{3,19},{4,20},{5,21},{6,22},{7,23},{8,24},{9,... | collective-permute-start | bytes 49160 | tf_op jit(solution)/shard_map/ppermute | solution.py:459
  17.5 4.4 %collective-permute-start.9 = (bf16[32,256]{1,0:T(8,128)(2,1)S(1)}, bf16[32,256]{1,0:T(8,128)(2,1)S(1)}, u32[]{:S(2)}, u32[]{:S(2)}) collective-permute-start(bf16[32,256]{1,0:T(8,128)(2,1)S(1)} %get-tuple-element.54), channel_id=1, source_target_pairs={{0,24},{1,25},{2,26},{3,27},{4,28},{5,29},{6,30},{7,31},{8,16},{9,... | collective-permute-start | bytes 49160 | tf_op jit(solution)/shard_map/ppermute | solution.py:459
  17.5 2.2 %copy-start = (f32[16,8,2,32,32]{4,3,2,1,0:T(8,128)S(1)}, f32[16,8,2,32,32]{4,3,2,1,0:T(8,128)}, u32[]{:S(2)}) copy-start(f32[16,8,2,32,32]{4,3,2,1,0:T(8,128)} %weight_ref.1) | copy-start | bytes 3145732
  19.7 2.2 %copy-start.2 = (bf16[256,256]{1,0:T(8,128)(2,1)S(1)}, bf16[256,256]{1,0:T(8,128)(2,1)}, u32[]{:S(2)}) copy-start(bf16[256,256]{1,0:T(8,128)(2,1)} %constant.5.clone.refs_5_) | copy-start | bytes 393220
  19.7 18.0 %copy-start.9 = (bf16[128]{0:T(256)(128)(2,1)S(1)}, bf16[128]{0:T(256)(128)(2,1)}, u32[]{:S(2)}) copy-start(bf16[128]{0:T(256)(128)(2,1)} %param.16) | copy-start | bytes 772
  19.7 21.0 %copy-start.5 = (bf16[32,128]{1,0:T(8,128)(2,1)S(1)}, bf16[32,128]{1,0:T(8,128)(2,1)}, u32[]{:S(2)}) copy-start(bf16[32,128]{1,0:T(8,128)(2,1)} %refs_11_.1) | copy-start | bytes 24580
  23.0 3.6 %collective-permute-start.10 = (bf16[32,256]{1,0:T(8,128)(2,1)S(1)}, bf16[32,256]{1,0:T(8,128)(2,1)S(1)}, u32[]{:S(2)}, u32[]{:S(2)}) collective-permute-start(bf16[32,256]{1,0:T(8,128)(2,1)S(1)} %get-tuple-element.55.refs_0_), channel_id=1, source_target_pairs={{0,8},{1,9},{2,10},{3,11},{4,12},{5,13},{6,14},{7,15},{8,0},{9,1},... | collective-permute-start | bytes 49160 | tf_op jit(solution)/shard_map/ppermute | solution.py:459
  23.0 3.6 %collective-permute-start.11 = (bf16[32,256]{1,0:T(8,128)(2,1)S(1)}, bf16[32,256]{1,0:T(8,128)(2,1)S(1)}, u32[]{:S(2)}, u32[]{:S(2)}) collective-permute-start(bf16[32,256]{1,0:T(8,128)(2,1)S(1)} %get-tuple-element.55.refs_0_), channel_id=1, source_target_pairs={{0,16},{1,17},{2,18},{3,19},{4,20},{5,21},{6,22},{7,23},{8,24},{9,... | collective-permute-start | bytes 49160 | tf_op jit(solution)/shard_map/ppermute | solution.py:459
  25.3 4.5 %collective-permute-start.12 = (bf16[32,256]{1,0:T(8,128)(2,1)S(1)}, bf16[32,256]{1,0:T(8,128)(2,1)S(1)}, u32[]{:S(2)}, u32[]{:S(2)}) collective-permute-start(bf16[32,256]{1,0:T(8,128)(2,1)S(1)} %get-tuple-element.55.refs_0_), channel_id=1, source_target_pairs={{0,24},{1,25},{2,26},{3,27},{4,28},{5,29},{6,30},{7,31},{8,16},{9,... | collective-permute-start | bytes 49160 | tf_op jit(solution)/shard_map/ppermute | solution.py:459
  30.0 5.0 %collective-permute-start.13 = (bf16[16,256]{1,0:T(8,128)(2,1)S(1)}, bf16[16,256]{1,0:T(8,128)(2,1)S(1)}, u32[]{:S(2)}, u32[]{:S(2)}) collective-permute-start(bf16[16,256]{1,0:T(8,128)(2,1)S(1)} %get-tuple-element.57), channel_id=1, source_target_pairs={{0,1},{1,0},{2,3},{3,2},{4,5},{5,4},{6,7},{7,6},{8,9},{9,8},{10,11... | collective-permute-start | bytes 24584 | tf_op jit(solution)/shard_map/ppermute | solution.py:459
  30.3 6.4 %collective-permute-start.14 = (bf16[16,256]{1,0:T(8,128)(2,1)S(1)}, bf16[16,256]{1,0:T(8,128)(2,1)S(1)}, u32[]{:S(2)}, u32[]{:S(2)}) collective-permute-start(bf16[16,256]{1,0:T(8,128)(2,1)S(1)} %get-tuple-element.58), channel_id=1, source_target_pairs={{0,2},{1,3},{2,0},{3,1},{4,6},{5,7},{6,4},{7,5},{8,10},{9,11},{10,... | collective-permute-start | bytes 24584 | tf_op jit(solution)/shard_map/ppermute | solution.py:459
  32.5 5.6 %collective-permute-start.15 = (bf16[16,256]{1,0:T(8,128)(2,1)S(1)}, bf16[16,256]{1,0:T(8,128)(2,1)S(1)}, u32[]{:S(2)}, u32[]{:S(2)}) collective-permute-start(bf16[16,256]{1,0:T(8,128)(2,1)S(1)} %get-tuple-element.59), channel_id=1, source_target_pairs={{0,3},{1,2},{2,1},{3,0},{4,7},{5,6},{6,5},{7,4},{8,11},{9,10},{10,... | collective-permute-start | bytes 24584 | tf_op jit(solution)/shard_map/ppermute | solution.py:459
  33.6 4.5 %collective-permute-start.16 = (bf16[16,256]{1,0:T(8,128)(2,1)S(1)}, bf16[16,256]{1,0:T(8,128)(2,1)S(1)}, u32[]{:S(2)}, u32[]{:S(2)}) collective-permute-start(bf16[16,256]{1,0:T(8,128)(2,1)S(1)} %get-tuple-element.60), channel_id=1, source_target_pairs={{0,4},{1,5},{2,6},{3,7},{4,0},{5,1},{6,2},{7,3},{8,12},{9,13},{10,... | collective-permute-start | bytes 24584 | tf_op jit(solution)/shard_map/ppermute | solution.py:459
  34.3 3.7 %collective-permute-start.17 = (bf16[16,256]{1,0:T(8,128)(2,1)S(1)}, bf16[16,256]{1,0:T(8,128)(2,1)S(1)}, u32[]{:S(2)}, u32[]{:S(2)}) collective-permute-start(bf16[16,256]{1,0:T(8,128)(2,1)S(1)} %get-tuple-element.61), channel_id=1, source_target_pairs={{0,5},{1,4},{2,7},{3,6},{4,1},{5,0},{6,3},{7,2},{8,13},{9,12},{10,... | collective-permute-start | bytes 24584 | tf_op jit(solution)/shard_map/ppermute | solution.py:459
  35.0 3.1 %collective-permute-start.18 = (bf16[16,256]{1,0:T(8,128)(2,1)S(1)}, bf16[16,256]{1,0:T(8,128)(2,1)S(1)}, u32[]{:S(2)}, u32[]{:S(2)}) collective-permute-start(bf16[16,256]{1,0:T(8,128)(2,1)S(1)} %get-tuple-element.62), channel_id=1, source_target_pairs={{0,6},{1,7},{2,4},{3,5},{4,2},{5,3},{6,0},{7,1},{8,14},{9,15},{10,... | collective-permute-start | bytes 24584 | tf_op jit(solution)/shard_map/ppermute | solution.py:459
  36.7 4.0 %collective-permute-start.19 = (bf16[16,256]{1,0:T(8,128)(2,1)S(1)}, bf16[16,256]{1,0:T(8,128)(2,1)S(1)}, u32[]{:S(2)}, u32[]{:S(2)}) collective-permute-start(bf16[16,256]{1,0:T(8,128)(2,1)S(1)} %get-tuple-element.63), channel_id=1, source_target_pairs={{0,7},{1,6},{2,5},{3,4},{4,3},{5,2},{6,1},{7,0},{8,15},{9,14},{10,... | collective-permute-start | bytes 24584 | tf_op jit(solution)/shard_map/ppermute | solution.py:459
  43.8 4.3 %collective-permute-start.20 = (bf16[16,384]{1,0:T(8,128)(2,1)S(1)}, bf16[16,384]{1,0:T(8,128)(2,1)S(1)}, u32[]{:S(2)}, u32[]{:S(2)}) collective-permute-start(bf16[16,384]{1,0:T(8,128)(2,1)S(1)} %get-tuple-element.67), channel_id=1, source_target_pairs={{0,1},{1,0},{2,3},{3,2},{4,5},{5,4},{6,7},{7,6},{8,9},{9,8},{10,11... | collective-permute-start | bytes 36872 | tf_op jit(solution)/shard_map/ppermute | solution.py:459
  45.0 4.2 %collective-permute-start.21 = (bf16[16,384]{1,0:T(8,128)(2,1)S(1)}, bf16[16,384]{1,0:T(8,128)(2,1)S(1)}, u32[]{:S(2)}, u32[]{:S(2)}) collective-permute-start(bf16[16,384]{1,0:T(8,128)(2,1)S(1)} %get-tuple-element.68), channel_id=1, source_target_pairs={{0,2},{1,3},{2,0},{3,1},{4,6},{5,7},{6,4},{7,5},{8,10},{9,11},{10,... | collective-permute-start | bytes 36872 | tf_op jit(solution)/shard_map/ppermute | solution.py:459
  45.0 4.8 %collective-permute-start.22 = (bf16[16,384]{1,0:T(8,128)(2,1)S(1)}, bf16[16,384]{1,0:T(8,128)(2,1)S(1)}, u32[]{:S(2)}, u32[]{:S(2)}) collective-permute-start(bf16[16,384]{1,0:T(8,128)(2,1)S(1)} %get-tuple-element.69), channel_id=1, source_target_pairs={{0,3},{1,2},{2,1},{3,0},{4,7},{5,6},{6,5},{7,4},{8,11},{9,10},{10,... | collective-permute-start | bytes 36872 | tf_op jit(solution)/shard_map/ppermute | solution.py:459
  45.7 4.1 %collective-permute-start.23 = (bf16[16,384]{1,0:T(8,128)(2,1)S(1)}, bf16[16,384]{1,0:T(8,128)(2,1)S(1)}, u32[]{:S(2)}, u32[]{:S(2)}) collective-permute-start(bf16[16,384]{1,0:T(8,128)(2,1)S(1)} %get-tuple-element.70), channel_id=1, source_target_pairs={{0,4},{1,5},{2,6},{3,7},{4,0},{5,1},{6,2},{7,3},{8,12},{9,13},{10,... | collective-permute-start | bytes 36872 | tf_op jit(solution)/shard_map/ppermute | solution.py:459
  46.4 3.4 %collective-permute-start.24 = (bf16[16,384]{1,0:T(8,128)(2,1)S(1)}, bf16[16,384]{1,0:T(8,128)(2,1)S(1)}, u32[]{:S(2)}, u32[]{:S(2)}) collective-permute-start(bf16[16,384]{1,0:T(8,128)(2,1)S(1)} %get-tuple-element.71), channel_id=1, source_target_pairs={{0,5},{1,4},{2,7},{3,6},{4,1},{5,0},{6,3},{7,2},{8,13},{9,12},{10,... | collective-permute-start | bytes 36872 | tf_op jit(solution)/shard_map/ppermute | solution.py:459
  48.1 3.3 %collective-permute-start.25 = (bf16[16,384]{1,0:T(8,128)(2,1)S(1)}, bf16[16,384]{1,0:T(8,128)(2,1)S(1)}, u32[]{:S(2)}, u32[]{:S(2)}) collective-permute-start(bf16[16,384]{1,0:T(8,128)(2,1)S(1)} %get-tuple-element.72), channel_id=1, source_target_pairs={{0,6},{1,7},{2,4},{3,5},{4,2},{5,3},{6,0},{7,1},{8,14},{9,15},{10,... | collective-permute-start | bytes 36872 | tf_op jit(solution)/shard_map/ppermute | solution.py:459
  49.2 4.0 %collective-permute-start.26 = (bf16[16,384]{1,0:T(8,128)(2,1)S(1)}, bf16[16,384]{1,0:T(8,128)(2,1)S(1)}, u32[]{:S(2)}, u32[]{:S(2)}) collective-permute-start(bf16[16,384]{1,0:T(8,128)(2,1)S(1)} %get-tuple-element.73), channel_id=1, source_target_pairs={{0,7},{1,6},{2,5},{3,4},{4,3},{5,2},{6,1},{7,0},{8,15},{9,14},{10,... | collective-permute-start | bytes 36872 | tf_op jit(solution)/shard_map/ppermute | solution.py:459
  53.5 3.6 %collective-permute-start.27 = (bf16[32,384]{1,0:T(8,128)(2,1)S(1)}, bf16[32,384]{1,0:T(8,128)(2,1)S(1)}, u32[]{:S(2)}, u32[]{:S(2)}) collective-permute-start(bf16[32,384]{1,0:T(8,128)(2,1)S(1)} %get-tuple-element.75), channel_id=1, source_target_pairs={{0,8},{1,9},{2,10},{3,11},{4,12},{5,13},{6,14},{7,15},{8,0},{9,1},... | collective-permute-start | bytes 73736 | tf_op jit(solution)/shard_map/ppermute | solution.py:459
  53.6 3.7 %collective-permute-start.28 = (bf16[32,384]{1,0:T(8,128)(2,1)S(1)}, bf16[32,384]{1,0:T(8,128)(2,1)S(1)}, u32[]{:S(2)}, u32[]{:S(2)}) collective-permute-start(bf16[32,384]{1,0:T(8,128)(2,1)S(1)} %get-tuple-element.76), channel_id=1, source_target_pairs={{0,16},{1,17},{2,18},{3,19},{4,20},{5,21},{6,22},{7,23},{8,24},{9,... | collective-permute-start | bytes 73736 | tf_op jit(solution)/shard_map/ppermute | solution.py:459
  56.0 4.5 %collective-permute-start.29 = (bf16[32,384]{1,0:T(8,128)(2,1)S(1)}, bf16[32,384]{1,0:T(8,128)(2,1)S(1)}, u32[]{:S(2)}, u32[]{:S(2)}) collective-permute-start(bf16[32,384]{1,0:T(8,128)(2,1)S(1)} %get-tuple-element.77), channel_id=1, source_target_pairs={{0,24},{1,25},{2,26},{3,27},{4,28},{5,29},{6,30},{7,31},{8,16},{9,... | collective-permute-start | bytes 73736 | tf_op jit(solution)/shard_map/ppermute | solution.py:459
  61.5 3.6 %collective-permute-start.30 = (bf16[32,384]{1,0:T(8,128)(2,1)S(1)}, bf16[32,384]{1,0:T(8,128)(2,1)S(1)}, u32[]{:S(2)}, u32[]{:S(2)}) collective-permute-start(bf16[32,384]{1,0:T(8,128)(2,1)S(1)} %get-tuple-element.78.refs_0_), channel_id=1, source_target_pairs={{0,8},{1,9},{2,10},{3,11},{4,12},{5,13},{6,14},{7,15},{8,0},{9,1},... | collective-permute-start | bytes 73736 | tf_op jit(solution)/shard_map/ppermute | solution.py:459
  61.6 3.6 %collective-permute-start.31 = (bf16[32,384]{1,0:T(8,128)(2,1)S(1)}, bf16[32,384]{1,0:T(8,128)(2,1)S(1)}, u32[]{:S(2)}, u32[]{:S(2)}) collective-permute-start(bf16[32,384]{1,0:T(8,128)(2,1)S(1)} %get-tuple-element.78.refs_0_), channel_id=1, source_target_pairs={{0,16},{1,17},{2,18},{3,19},{4,20},{5,21},{6,22},{7,23},{8,24},{9,... | collective-permute-start | bytes 73736 | tf_op jit(solution)/shard_map/ppermute | solution.py:459
  63.0 4.6 %collective-permute-start.32 = (bf16[32,384]{1,0:T(8,128)(2,1)S(1)}, bf16[32,384]{1,0:T(8,128)(2,1)S(1)}, u32[]{:S(2)}, u32[]{:S(2)}) collective-permute-start(bf16[32,384]{1,0:T(8,128)(2,1)S(1)} %get-tuple-element.78.refs_0_), channel_id=1, source_target_pairs={{0,24},{1,25},{2,26},{3,27},{4,28},{5,29},{6,30},{7,31},{8,16},{9,... | collective-permute-start | bytes 73736 | tf_op jit(solution)/shard_map/ppermute | solution.py:459
  67.8 6.4 %collective-permute-start.33 = (bf16[16,384]{1,0:T(8,128)(2,1)S(1)}, bf16[16,384]{1,0:T(8,128)(2,1)S(1)}, u32[]{:S(2)}, u32[]{:S(2)}) collective-permute-start(bf16[16,384]{1,0:T(8,128)(2,1)S(1)} %get-tuple-element.80), channel_id=1, source_target_pairs={{0,1},{1,0},{2,3},{3,2},{4,5},{5,4},{6,7},{7,6},{8,9},{9,8},{10,11... | collective-permute-start | bytes 36872 | tf_op jit(solution)/shard_map/ppermute | solution.py:459
  68.1 7.8 %collective-permute-start.34 = (bf16[16,384]{1,0:T(8,128)(2,1)S(1)}, bf16[16,384]{1,0:T(8,128)(2,1)S(1)}, u32[]{:S(2)}, u32[]{:S(2)}) collective-permute-start(bf16[16,384]{1,0:T(8,128)(2,1)S(1)} %get-tuple-element.81), channel_id=1, source_target_pairs={{0,2},{1,3},{2,0},{3,1},{4,6},{5,7},{6,4},{7,5},{8,10},{9,11},{10,... | collective-permute-start | bytes 36872 | tf_op jit(solution)/shard_map/ppermute | solution.py:459
  71.6 8.8 %collective-permute-start.35 = (bf16[16,384]{1,0:T(8,128)(2,1)S(1)}, bf16[16,384]{1,0:T(8,128)(2,1)S(1)}, u32[]{:S(2)}, u32[]{:S(2)}) collective-permute-start(bf16[16,384]{1,0:T(8,128)(2,1)S(1)} %get-tuple-element.82), channel_id=1, source_target_pairs={{0,3},{1,2},{2,1},{3,0},{4,7},{5,6},{6,5},{7,4},{8,11},{9,10},{10,... | collective-permute-start | bytes 36872 | tf_op jit(solution)/shard_map/ppermute | solution.py:459
  72.8 7.7 %collective-permute-start.36 = (bf16[16,384]{1,0:T(8,128)(2,1)S(1)}, bf16[16,384]{1,0:T(8,128)(2,1)S(1)}, u32[]{:S(2)}, u32[]{:S(2)}) collective-permute-start(bf16[16,384]{1,0:T(8,128)(2,1)S(1)} %get-tuple-element.83), channel_id=1, source_target_pairs={{0,4},{1,5},{2,6},{3,7},{4,0},{5,1},{6,2},{7,3},{8,12},{9,13},{10,... | collective-permute-start | bytes 36872 | tf_op jit(solution)/shard_map/ppermute | solution.py:459
  73.5 6.9 %collective-permute-start.37 = (bf16[16,384]{1,0:T(8,128)(2,1)S(1)}, bf16[16,384]{1,0:T(8,128)(2,1)S(1)}, u32[]{:S(2)}, u32[]{:S(2)}) collective-permute-start(bf16[16,384]{1,0:T(8,128)(2,1)S(1)} %get-tuple-element.84), channel_id=1, source_target_pairs={{0,5},{1,4},{2,7},{3,6},{4,1},{5,0},{6,3},{7,2},{8,13},{9,12},{10,... | collective-permute-start | bytes 36872 | tf_op jit(solution)/shard_map/ppermute | solution.py:459
  74.2 6.2 %collective-permute-start.38 = (bf16[16,384]{1,0:T(8,128)(2,1)S(1)}, bf16[16,384]{1,0:T(8,128)(2,1)S(1)}, u32[]{:S(2)}, u32[]{:S(2)}) collective-permute-start(bf16[16,384]{1,0:T(8,128)(2,1)S(1)} %get-tuple-element.85), channel_id=1, source_target_pairs={{0,6},{1,7},{2,4},{3,5},{4,2},{5,3},{6,0},{7,1},{8,14},{9,15},{10,... | collective-permute-start | bytes 36872 | tf_op jit(solution)/shard_map/ppermute | solution.py:459
  75.9 4.6 %collective-permute-start.39 = (bf16[16,384]{1,0:T(8,128)(2,1)S(1)}, bf16[16,384]{1,0:T(8,128)(2,1)S(1)}, u32[]{:S(2)}, u32[]{:S(2)}) collective-permute-start(bf16[16,384]{1,0:T(8,128)(2,1)S(1)} %get-tuple-element.86), channel_id=1, source_target_pairs={{0,7},{1,6},{2,5},{3,4},{4,3},{5,2},{6,1},{7,0},{8,15},{9,14},{10,... | collective-permute-start | bytes 36872 | tf_op jit(solution)/shard_map/ppermute | solution.py:459

commit v3 on v2

v3 whole, which is shorter than its diff:
```python
import functools
import math

import jax
import jax.numpy as jnp
import numpy as np
from jax import lax
from jax.experimental import pallas as pl
from jax.experimental.pallas import tpu as pltpu
from jax.sharding import PartitionSpec as P

MX = 16
MY = 16
MZ = 16
F32 = jnp.float32
BF16 = jnp.bfloat16
VMEM_LIMIT = 32 * 1024 * 1024


def signed(indices, count):
    return np.where(indices < count // 2, indices, indices - count)


def wave(positions, frequency, length):
    turned = np.mod(np.multiply.outer(positions, frequency), length)
    angles = turned.astype(np.float32) * np.float32(2.0 * math.pi / length)
    scale = np.float32(1.0 / math.sqrt(length))
    return np.cos(angles) * scale, np.sin(angles) * scale


def pair(cosine, sine, sign):
    return np.stack(
        [np.stack([cosine, -sign * sine], -1), np.stack([sign * sine, cosine], -1)], -2
    )


def y_tables(total_y, rows_y, kz, modes):
    cosine, sine = wave(np.arange(total_y), signed(np.arange(MY), MY), total_y)
    narrow = total_y // rows_y
    same = np.eye(kz, dtype=np.float32)
    forward = pair(cosine, sine, -1.0).reshape(narrow, rows_y, MY // modes, modes, 2, 2)
    inverse = pair(cosine, sine, 1.0).reshape(narrow, rows_y, MY // modes, modes, 2, 2)
    forward = np.einsum("nybjtr,kl->bjtkynlr", forward, same)
    inverse = np.einsum("nybjst,kl->bnyksjtl", inverse, same)
    blocks = MY // modes
    forward = forward.reshape(blocks, modes * 2 * kz, rows_y * narrow * kz * 2)
    inverse = inverse.reshape(blocks, narrow * rows_y * kz * 2, modes * 2 * kz)
    return forward.astype(BF16), inverse.astype(BF16)


def dot(a, b):
    return jnp.dot(a, b, preferred_element_type=F32)


def dot_nt(a, b):
    return lax.dot_general(a, b, (((1,), (1,)), ((), ())), preferred_element_type=F32)


def dot_tn(a, b):
    return lax.dot_general(a, b, (((0,), (0,)), ((), ())), preferred_element_type=F32)


def grid_of(rows, columns):
    shape = (rows, columns)
    return lax.broadcasted_iota(jnp.int32, shape, 0), lax.broadcasted_iota(jnp.int32, shape, 1)


def selector(rows, columns, condition):
    return jnp.where(condition(*grid_of(rows, columns)), 1.0, 0.0).astype(BF16)


def halves(values):
    high = values.astype(BF16)
    return high, (values - high.astype(F32)).astype(BF16)


def stacked(refs, lanes=slice(None)):
    return jnp.concatenate([ref[:, lanes] for ref in refs], axis=0)


def cosine_of(phase, length):
    angles = (phase & (length - 1)).astype(F32) * (2.0 * math.pi / length)
    return jnp.cos(angles) * (1.0 / math.sqrt(length))


class Place:
    def __init__(self, wide, narrow, kz, modes, rows_y, channels, z_count, fold):
        self.wide, self.narrow, self.kz, self.modes = wide, narrow, kz, modes
        self.rows_y, self.channels, self.z_count, self.fold = rows_y, channels, z_count, fold
        self.outer = wide // 2
        self.partners = self.outer * narrow
        self.lanes = rows_y * channels

    def here(self):
        wide = lax.axis_index("wide")
        return wide // 2, wide % 2

    def frequency(self, wide):
        index = (wide * self.modes) // MY
        return jnp.where(index < MX // 2, index, index - MX)

    def z_table(self, doubled):
        row, z = grid_of(2 * MZ, self.z_count)
        frequency = row >> 1
        value = cosine_of(z * frequency + (row & 1) * (self.z_count // 4), self.z_count)
        if doubled:
            value = jnp.where(frequency > 0, 2.0 * value, value)
        return value.astype(BF16)

    def expanded(self, small):
        row, column = grid_of(2 * MZ, small.shape[1])
        same = (row >> 1) == ((column >> 1) & (MZ - 1))
        blocks = []
        for g in range(small.shape[0] // 2):
            value = jnp.where((row & 1) == 0, small[2 * g : 2 * g + 1], small[2 * g + 1 : 2 * g + 2])
            blocks.append(jnp.where(same, value, 0.0))
        return jnp.concatenate(blocks, axis=0)

    def forward_x(self):
        outer, inner = self.here()
        row, column = grid_of(2 * self.outer, 4 * MZ)
        x = 2 * outer + (inner ^ (column // (2 * MZ)))
        frequency = self.frequency(2 * (row >> 1) + inner)
        quarter = self.wide // 4
        small = cosine_of(x * frequency + quarter * ((row & 1) - (column & 1)), self.wide)
        return self.expanded(small)

    def inverse_x(self):
        outer, inner = self.here()
        row, column = grid_of(4, self.outer * 2 * MZ)
        x = 2 * outer + (inner ^ (row >> 1))
        frequency = self.frequency(2 * (column // (2 * MZ)) + inner)
        quarter = self.wide // 4
        small = cosine_of(x * frequency + quarter * ((column & 1) - (row & 1)), self.wide)
        return self.expanded(small).astype(BF16)

    def sum_owner(self, index, inner):
        return ((index // self.narrow) * 2 + inner) * self.narrow + index % self.narrow


def repeat_rows(out_ref, block):
    height = block.shape[0]
    for first in range(0, out_ref.shape[0], height):
        out_ref[first : first + height] = block


def write_pieces(place, send_ref, block, shares):
    step, half = 2 * place.kz, place.lanes // 2
    height = send_ref.shape[0] // place.partners
    for p in range(place.partners):
        own = block[p * step % block.shape[0] :][:step]
        first = p * height
        send_ref[first : first + step] = own[:, :half]
        send_ref[first + step : first + 2 * step] = own[:, half:]
        send_ref[first + 2 * step : first + height] = shares[p * 8 % shares.shape[0] :][:8]


def read_pieces(place, pieces_ref):
    step = 2 * place.kz
    if pieces_ref.shape[1] == place.lanes:
        return pieces_ref[...], None
    height = pieces_ref.shape[0] // place.partners
    blocks, shares = [], []
    for p in range(place.partners):
        first = p * height
        left = pieces_ref[first : first + step]
        right = pieces_ref[first + step : first + 2 * step]
        blocks.append(jnp.concatenate([left, right], axis=1))
        shares.append(pieces_ref[first + 2 * step : first + height].astype(F32))
    return jnp.concatenate(blocks, axis=0), shares


def analysed(place, pieces, y_forward, copies):
    height = 2 * MZ
    turned = sum(
        pieces[first : first + height].astype(F32) for first in range(0, pieces.shape[0], height)
    )
    channels = place.channels
    lines = jnp.concatenate(
        [turned[:, y * channels : (y + 1) * channels] for y in range(place.rows_y)], axis=0
    )
    high, low = halves(jnp.concatenate([lines] * copies, axis=1))
    return dot(y_forward, high) + dot(y_forward, low)


def spread_lines(place, modes, y_inverse):
    lines = dot(y_inverse, modes)
    step = 2 * place.kz
    blocks = []
    for n in range(place.narrow):
        first = n * place.rows_y
        parts = [lines[(first + y) * step : (first + y + 1) * step] for y in range(place.rows_y)]
        blocks.append(jnp.concatenate(parts, axis=1))
    return jnp.concatenate(blocks, axis=0).astype(BF16)


def start_kernel(place, field_ref, field_out_ref, send_ref):
    channels, rows_y = place.channels, place.rows_y
    turn = selector(
        place.lanes,
        place.lanes,
        lambda row, column: (row % channels == column // rows_y)
        & (row // channels == column % rows_y),
    )
    turned = dot(turn, field_ref[...]).astype(BF16)
    field_out_ref[...] = turned
    send_ref[...] = dot_nt(place.z_table(False), turned).astype(BF16)


def weight_kernel(weight_ref, out_ref):
    modes, kz, _, channels, _ = weight_ref.shape
    for j in range(modes):
        both = jnp.concatenate([weight_ref[j, :, 0], weight_ref[j, :, 1]], axis=-1)
        out_ref[j] = both.reshape(kz * channels, 2 * channels).astype(BF16)


def fold_kernel(place, *refs):
    own_ref, got_ref = refs[:2]
    high, low = halves(place.forward_x())
    height = 2 * MZ
    values = jnp.concatenate([own_ref[:height], got_ref[:height]], axis=0)
    partial = (dot(high, values) + dot(low, values)).astype(BF16)
    if got_ref.shape[0] == height:
        refs[2][...] = partial
        return
    sums_ref, send_ref = refs[2:]
    got = got_ref[height:].astype(F32)
    width = sums_ref.shape[1]
    high, low = halves(sums_ref[...] + got[:, :width] + got[:, width:])
    count = place.partners
    place_of = selector(
        8 * count,
        4 * count,
        lambda row, column: (row % 8 == column // count) & (row // 8 == column % count),
    )
    shares = dot(place_of, jnp.concatenate([high, low], axis=0)).astype(BF16)
    write_pieces(place, send_ref, partial, shares)


def mode_kernel(
    place, pieces_ref, y_forward_ref, y_inverse_ref, weight_ref, spectrum_ref, send_ref
):
    kz, channels = place.kz, place.channels
    spectrum = analysed(place, pieces_ref[...], y_forward_ref[...], kz)
    spectrum_ref[...] = spectrum[:, :channels]
    row, lane = grid_of(*spectrum.shape)
    blocked = jnp.where(row % kz == lane // channels, spectrum, 0.0)
    mixed = []
    for j in range(place.modes):
        left = blocked[j * 2 * kz : (j + 1) * 2 * kz].astype(BF16)
        product = dot(left, weight_ref[j])
        real, imag = product[:, :channels], product[:, channels:]
        mixed.append(real[:kz] - imag[kz:])
        mixed.append(imag[:kz] + real[kz:])
    mode = jnp.concatenate(mixed, axis=0).astype(BF16)
    repeat_rows(send_ref, spread_lines(place, mode, y_inverse_ref[...]))


def part_kernel(place, *refs):
    pieces, shares = read_pieces(place, refs[0])
    lines = dot(place.inverse_x(), pieces)
    height = 2 * MZ
    own_ref, send_ref = refs[1:3]
    own_ref[...] = lines[:height]
    if shares is None:
        send_ref[...] = lines[height:].astype(BF16)
        return
    sums_ref = refs[3]
    count = place.partners
    got = jnp.concatenate(shares, axis=0).astype(BF16)

    def chosen(part):
        return dot(
            selector(
                2 * count,
                8 * count,
                lambda row, column: (row // count + 2 * part == column % 8)
                & (row % count == column // 8),
            ),
            got,
        )

    high, low = chosen(0), chosen(1)
    sums_ref[...] = high + low
    send_ref[:height] = lines[height:].astype(BF16)
    send_ref[height:] = jnp.concatenate([high, low], axis=1).astype(BF16)


def normal(values):
    cumulative = 0.5 * (1.0 + lax.erf(values * (1.0 / math.sqrt(2.0))))
    density = jnp.exp(-0.5 * values * values) * (1.0 / math.sqrt(2.0 * math.pi))
    return values * cumulative, cumulative + values * density


def cell_kernel(place, *refs):
    own_ref, got_ref, refs = refs[0], refs[1], refs[2:]
    field_ref, mix_ref, mix_bias_ref, head_ref, head_bias_ref, out_weight_ref, cotangent_ref = refs[:7]
    prediction_ref, grad_pre_ref, send_ref = refs[7:10]
    channels, hidden_units = head_ref.shape
    z_table = place.z_table(True)
    lines = (own_ref[...] + got_ref[...].astype(F32)).astype(BF16)
    branch = dot_tn(lines, z_table)
    mix, head = mix_ref[...], head_ref[...]
    mix_bias, head_bias = mix_bias_ref[...], head_bias_ref[...]
    out_weight = out_weight_ref[...]
    grad_mix = jnp.zeros((channels, channels), F32)
    grad_head = jnp.zeros((channels, hidden_units), F32)
    gradients = []
    for y in range(place.rows_y):
        cells = slice(y * channels, (y + 1) * channels)
        field = field_ref[cells]
        pre_act = branch[cells] + dot_tn(mix, field) + mix_bias
        hidden, pre_slope = normal(pre_act)
        hidden = hidden.astype(BF16)
        head_pre = dot_tn(head, hidden) + head_bias
        active, slope = normal(head_pre)
        active = active.astype(BF16).astype(F32)
        prediction_ref[y : y + 1] = jnp.sum(active * out_weight, axis=0, keepdims=True)
        head_slope = (cotangent_ref[y : y + 1] * out_weight * slope).astype(BF16)
        grad_pre = (dot(head, head_slope) * pre_slope).astype(BF16)
        grad_head += dot_nt(hidden, head_slope)
        grad_mix += dot_nt(field, grad_pre)
        gradients.append(grad_pre)

    gradient = jnp.concatenate(gradients, axis=0)
    grad_pre_ref[...] = gradient
    height = 2 * MZ
    send_ref[:height] = dot_nt(z_table, gradient).astype(BF16)
    if not place.fold:
        refs[-2][...] = grad_mix
        refs[-1][...] = grad_head
        return
    wide_mix = jnp.concatenate(
        [grad_mix, jnp.zeros((channels, hidden_units - channels), F32)], axis=1
    )
    high, low = halves(jnp.concatenate([grad_head, wide_mix], axis=0))
    count = place.partners
    _, inner = place.here()

    def chosen(owner):
        def condition(row, column):
            target = place.sum_owner(row % count, owner)
            return column == (row // count) * channels + target

        picked = selector(2 * count, 2 * channels, condition)
        return dot(picked, high), dot(picked, low)

    refs[10][...] = sum(chosen(inner))
    send_ref[height:] = jnp.concatenate(chosen(1 - inner), axis=1).astype(BF16)


def back_kernel(
    place, pieces_ref, y_forward_ref, y_inverse_ref, weight_ref, adjoint_ref, send_ref
):
    kz, channels = place.kz, place.channels
    pieces, shares = read_pieces(place, pieces_ref)
    adjoint = analysed(place, pieces, y_forward_ref[...], 1)
    adjoint_ref[...] = adjoint
    pulled = []
    for j in range(place.modes):
        real = adjoint[j * 2 * kz : j * 2 * kz + kz]
        imag = adjoint[j * 2 * kz + kz : (j + 1) * 2 * kz]
        left = jnp.concatenate(
            [jnp.concatenate([real, imag], axis=1), jnp.concatenate([imag, -real], axis=1)], axis=0
        )
        pulled.append(dot_nt(left.astype(BF16), weight_ref[j]))
    pulled = jnp.concatenate(pulled, axis=0)
    row, lane = grid_of(*pulled.shape)
    pulled = jnp.where(row % kz == lane // channels, pulled, 0.0).astype(BF16)
    gather = selector(
        kz * channels, channels, lambda row, column: row % channels == column
    )
    modes_back = dot(pulled, gather).astype(BF16)
    block = spread_lines(place, modes_back, y_inverse_ref[...])
    if shares is None:
        repeat_rows(send_ref, block)
        return
    total = sum(shares[1:], shares[0])
    high, low = halves(total[0:2] + total[2:4])
    rest = jnp.zeros((4, total.shape[1]), F32)
    split = jnp.concatenate([high.astype(F32), low.astype(F32), rest], axis=0)
    write_pieces(place, send_ref, block, split.astype(BF16))


def outer_kernel(spectrum_ref, adjoint_ref, out_ref):
    modes, kz = out_ref.shape[:2]
    for j in range(modes):
        columns = jnp.transpose(spectrum_ref[j])
        adjoint = adjoint_ref[j]
        for k in range(kz):
            s_real, s_imag = columns[:, k : k + 1], columns[:, kz + k : kz + k + 1]
            a_real, a_imag = adjoint[k : k + 1], adjoint[kz + k : kz + k + 1]
            out_ref[j, k, 0] = s_real * a_real + s_imag * a_imag
            out_ref[j, k, 1] = s_real * a_imag - s_imag * a_real


def finish_kernel(place, *refs):
    own_ref, got_ref, grad_pre_ref, mix_ref = refs[:4]
    refs = refs[4:]
    height = 2 * MZ
    channels, rows_y = place.channels, place.rows_y
    lines = (own_ref[...] + got_ref[:height].astype(F32)).astype(BF16)
    branch = dot_tn(lines, place.z_table(False))
    parts = []
    for y in range(rows_y):
        cells = slice(y * channels, (y + 1) * channels)
        parts.append((branch[cells] + dot(mix_ref[...], grad_pre_ref[cells])).astype(BF16))
    turn = selector(
        place.lanes,
        place.lanes,
        lambda row, column: (row // rows_y == column % channels)
        & (row % rows_y == column // channels),
    )
    if not place.fold:
        refs[0][...] = dot(turn, jnp.concatenate(parts, axis=0)).astype(BF16)
        return
    sums_ref, grad_field_ref, grad_mix_ref, grad_head_ref = refs
    grad_field_ref[...] = dot(turn, jnp.concatenate(parts, axis=0)).astype(BF16)
    _, inner = place.here()
    count = place.partners
    width = sums_ref.shape[1]
    own_high, own_low = halves(sums_ref[...])
    got = got_ref[height:]

    def picked(kind):
        def choose(owner):
            def condition(row, column):
                target = place.sum_owner(column % count, owner)
                return (column // count == kind) & (target == row)

            return selector(channels, 2 * count, condition)

        own, twin = choose(inner), choose(1 - inner)
        both = dot(twin, got)
        return dot(own, own_high) + dot(own, own_low) + both[:, :width] + both[:, width:]

    grad_head_ref[...] = picked(0)
    grad_mix_ref[...] = picked(1)[:, :channels]


def call(kernel, outs, name):
    return pl.pallas_call(
        kernel,
        out_shape=[jax.ShapeDtypeStruct(shape, dtype) for shape, dtype in outs],
        compiler_params=pltpu.CompilerParams(vmem_limit_bytes=VMEM_LIMIT),
        cost_estimate=pl.CostEstimate(flops=1 << 22, bytes_accessed=1 << 19, transcendentals=0),
        name=name,
    )


def body(
    lifted_field,
    spectral_weight,
    mix_weight,
    mix_bias,
    head_weight,
    head_bias,
    out_weight,
    cotangent,
):
    wide = lax.axis_size("wide")
    narrow = lax.axis_size("narrow")
    devices = wide * narrow
    _, channels, rows_y, z_count = lifted_field.shape
    modes, kz = spectral_weight.shape[:2]
    hidden_units = head_weight.shape[1]
    cells = channels * rows_y
    place = Place(wide, narrow, kz, modes, rows_y, channels, z_count, False)
    place.fold = devices == channels and hidden_units == 128 and place.lanes == 256 and kz % 8 == 0
    height = 2 * MZ
    step = 2 * kz
    partners = place.partners
    mode_lines = modes * 2 * kz

    y_forward, y_inverse = y_tables(rows_y * narrow, rows_y, kz, modes)
    if len(y_forward) > 1:
        block = lax.axis_index("wide") % len(y_forward)
        y_forward = lax.dynamic_index_in_dim(jnp.asarray(y_forward), block, 0, False)
        y_inverse = lax.dynamic_index_in_dim(jnp.asarray(y_inverse), block, 0, False)
    else:
        y_forward, y_inverse = jnp.asarray(y_forward[0]), jnp.asarray(y_inverse[0])

    def to_twin(send):
        pairs = [(p, p ^ narrow) for p in range(devices)]
        return lax.ppermute(send, ("wide", "narrow"), pairs)

    groups = [
        [(2 * outer + inner) * narrow + n for outer in range(wide // 2) for n in range(narrow)]
        for inner in range(2)
    ]

    def exchange(send):
        pieces = send.reshape(partners, -1, send.shape[1])
        got = lax.all_to_all(
            pieces, ("wide", "narrow"), 0, 0, axis_index_groups=groups, tiled=True
        )
        return got.reshape(send.shape)

    plain = ((partners * step, cells), BF16)
    shared = ((partners * (2 * step + 8), cells // 2), BF16) if place.fold else plain
    twin_plain = ((height, cells), BF16)
    twin_shared = ((2 * height, cells), BF16) if place.fold else twin_plain
    sums_shape = ((2 * partners, hidden_units), F32)
    own_lines = ((height, cells), F32)

    field, send = call(
        functools.partial(start_kernel, place),
        [((cells, z_count), BF16), twin_plain],
        "start",
    )(lifted_field.reshape(cells, z_count))
    some = max(1, modes // 4)
    weight = pl.pallas_call(
        weight_kernel,
        grid=(modes // some,),
        in_specs=[pl.BlockSpec((some, kz, 2, channels, channels), lambda j: (j, 0, 0, 0, 0))],
        out_specs=pl.BlockSpec((some, kz * channels, 2 * channels), lambda j: (j, 0, 0)),
        out_shape=jax.ShapeDtypeStruct((modes, kz * channels, 2 * channels), BF16),
        compiler_params=pltpu.CompilerParams(vmem_limit_bytes=VMEM_LIMIT),
        cost_estimate=pl.CostEstimate(flops=1 << 20, bytes_accessed=5 << 20, transcendentals=0),
        name="weights",
    )(spectral_weight)
    (send,) = call(functools.partial(fold_kernel, place), [plain], "fold")(send, to_twin(send))
    spectrum, send = call(
        functools.partial(mode_kernel, place),
        [((mode_lines, channels), F32), plain],
        "mode",
    )(exchange(send), y_forward, y_inverse, weight)
    own, send = call(functools.partial(part_kernel, place), [own_lines, twin_plain], "part")(
        exchange(send)
    )
    outs = [((rows_y, z_count), F32), ((cells, z_count), BF16), twin_shared]
    if place.fold:
        outs += [sums_shape]
    else:
        outs += [((channels, channels), F32), ((channels, hidden_units), F32)]
    prediction, grad_pre, send, *sums = call(functools.partial(cell_kernel, place), outs, "cell")(
        own,
        to_twin(send),
        field,
        mix_weight,
        mix_bias[:, None],
        head_weight,
        head_bias[:, None],
        out_weight.astype(F32)[:, None],
        cotangent[0],
    )
    if not place.fold:
        totals = lax.psum(tuple(sums), ("wide", "narrow"))
        sums = []
    (send,) = call(functools.partial(fold_kernel, place), [shared], "fold")(
        send, to_twin(send), *sums
    )
    adjoint, send = call(
        functools.partial(back_kernel, place),
        [((mode_lines, channels), F32), shared],
        "back",
    )(exchange(send), y_forward, y_inverse, weight)
    outs = [own_lines, twin_shared] + ([sums_shape] if place.fold else [])
    own, send, *sums = call(functools.partial(part_kernel, place), outs, "part")(exchange(send))
    grad_spectral = pl.pallas_call(
        outer_kernel,
        grid=(modes // some,),
        in_specs=[pl.BlockSpec((some, 2 * kz, channels), lambda j: (j, 0, 0))] * 2,
        out_specs=pl.BlockSpec((some, kz, 2, channels, channels), lambda j: (j, 0, 0, 0, 0)),
        out_shape=jax.ShapeDtypeStruct(spectral_weight.shape, F32),
        compiler_params=pltpu.CompilerParams(vmem_limit_bytes=VMEM_LIMIT),
        cost_estimate=pl.CostEstimate(flops=1 << 22, bytes_accessed=5 << 20, transcendentals=0),
        name="outer",
    )(spectrum.reshape(modes, 2 * kz, channels), adjoint.reshape(modes, 2 * kz, channels))
    outs = [((cells, z_count), BF16)]
    if place.fold:
        outs += [((channels, channels), F32), ((channels, hidden_units), F32)]
    grad_field, *summed = call(functools.partial(finish_kernel, place), outs, "finish")(
        own, to_twin(send), grad_pre, mix_weight, *sums
    )
    grad_mix, grad_head = summed if place.fold else totals
    return (
        prediction[None],
        grad_field.reshape(lifted_field.shape),
        grad_spectral,
        grad_mix,
        grad_head,
    )


def solution(mesh):
    return jax.shard_map(
        body,
        mesh=mesh,
        in_specs=(
            P("wide", None, "narrow", None),
            P("wide", "narrow", None, None, None),
            P(),
            P(),
            P(),
            P(),
            P(),
            P("wide", "narrow", None),
        ),
        out_specs=(
            P("wide", "narrow", None),
            P("wide", None, "narrow", None),
            P("wide", "narrow", None, None, None),
            P(),
            P(),
        ),
        check_vma=False,
    )
```

time: 82.7 us -> 66.5 us (0.80)
  starting transfers between devices: 45 us -> 13.1 us
  blocking collectives: 0 us -> 30.2 us
  waiting for transfers between devices: 20.6 us -> 6.36 us
    ppermute x40 -> x4, starting transfers between devices: 45 us -> 5.33 us  [to_twin(): return lax.ppermute(send, ('wide', 'narrow'), pairs)]
    all_to_all x0 -> x3, blocking collectives: none -> 30.2 us  [exchange(): lax.all_to_all(pieces, ('wide', 'narrow'), 0, 0, axis_index_groups=groups...]
    ppermute x40 -> x4, waiting for transfers between devices: 20.6 us -> 2.5 us  [to_twin(): return lax.ppermute(send, ('wide', 'narrow'), pairs)]
    all_to_all x0 -> x1, starting transfers between devices: none -> 7.74 us  [exchange(): lax.all_to_all(pieces, ('wide', 'narrow'), 0, 0, axis_index_groups=groups...]
    all_to_all x0 -> x1, waiting for transfers between devices: none -> 3.86 us  [exchange(): lax.all_to_all(pieces, ('wide', 'narrow'), 0, 0, axis_index_groups=groups...]
  transfers between devices with their start and end apart: 40 -> 5, of which waited for: 11 -> 4; matrix products, arithmetic and copies ran while one was open for 0% -> 0% of each run, Pallas kernels for 5% -> 6%
where the time goes in v3:
time: 66.5 us; the launch traced here: 66.1 us
  blocking collectives  30.2 us (45%)
  starting transfers between devices  13.1 us (20%)
  Pallas kernels  12.4 us (19%)
  waiting for transfers between devices  6.36 us (10%)
  local copies, waits for them, and re-layouts  3.41 us (5%)
  between operations  0.74 us (1%)
    all_to_all x3, blocking collectives, exchange(): lax.all_to_all(pieces, ('wide', 'narrow'), 0, 0, axis_index_groups=groups...  30.2 us
    all_to_all x1, starting transfers between devices, exchange(): lax.all_to_all(pieces, ('wide', 'narrow'), 0, 0, axis_index_groups=groups...  7.74 us
    ppermute x4, starting transfers between devices, to_twin(): return lax.ppermute(send, ('wide', 'narrow'), pairs)  5.33 us
    all_to_all x1, waiting for transfers between devices, exchange(): lax.all_to_all(pieces, ('wide', 'narrow'), 0, 0, axis_index_groups=groups...  3.86 us
    pallas_call x1, Pallas kernels, body(): pl.pallas_call(outer_kernel, grid=(modes // some,), in_specs=[pl.BlockSpe...  3.53 us
    unnamed x20, local copies, waits for them, and re-layouts  3.09 us
    pallas_call x1, Pallas kernels, body(): call(functools.partial(cell_kernel, place), outs, 'cell')  3.09 us
    ppermute x4, waiting for transfers between devices, to_twin(): return lax.ppermute(send, ('wide', 'narrow'), pairs)  2.5 us
  transfers between devices with their start and end apart: 5, of which 4 were waited for; matrix products, arithmetic and copies ran while one was open for 0% of the time, Pallas kernels for 6%

profile of v3, /device:TPU:1, one launch (start us, length us, event | category | flops | bytes accessed | tf_op | source)
XLA Modules:
  0.0 66.1 jit_solution(6495017421656105920)
XLA Ops:
  0.6 0.0 copy-start.1
  0.6 0.0 copy-start.2
  0.7 0.0 copy-start.3
  0.7 0.9 %copy-done.3 = bf16[1,32,8,128]{3,2,1,0:T(8,128)(2,1)S(1)} copy-done((bf16[1,32,8,128]{3,2,1,0:T(8,128)(2,1)S(1)}, bf16[1,32,8,128]{3,2,1,0:T(8,128)(2,1)}, u32[]{:S(2)}) %copy-start.3) | copy-done | bytes 65560
  1.5 0.0 copy-start.9
  1.5 0.0 copy-start.8
  1.5 0.0 copy-start.7
  1.5 0.0 copy-start.4
  1.6 0.0 copy-start.5
  1.6 0.0 copy-start.6
  1.6 0.3 start.1
  1.9 0.1 collective-permute-start
  2.0 1.1 %collective-permute-done.refs_1_ = bf16[32,256]{1,0:T(8,128)(2,1)S(1)} collective-permute-done((bf16[32,256]{1,0:T(8,128)(2,1)S(1)}, bf16[32,256]{1,0:T(8,128)(2,1)S(1)}, u32[]{:S(2)}, u32[]{:S(2)}) %collective-permute-start) | collective-permute-done | bytes 16416 | tf_op jit(solution)/shard_map/ppermute | solution.py:485
  3.1 0.9 %fold.2 = bf16[256,256]{1,0:T(8,128)(2,1)} custom-call(bf16[32,256]{1,0:T(8,128)(2,1)S(1)} %get-tuple-element.23.refs_0_, bf16[32,256]{1,0:T(8,128)(2,1)S(1)} %collective-permute-done.refs_1_), custom_call_target="tpu_custom_call" | custom-call | flops 4194304 | bytes 524288 | tf_op jit(solution)/shard_map/fold/pallas_call | solution.py:522
  4.0 7.7 %all-to-all-start = ((bf16[16,16,256]{2,1,0:T(8,128)(2,1)}), bf16[16,16,256]{2,1,0:T(8,128)(2,1)S(1)}, u32[]{:S(2)}, u32[]{:S(2)}) async-start(bf16[16,16,256]{2,1,0:T(8,128)(2,1)} %bitcast.1), calls=%async_computation | async-start | bytes 262144 | tf_op jit(solution)/shard_map/all_to_all | solution.py:494
  11.8 0.0 copy-start
  11.8 2.2 %copy-done = f32[16,8,2,32,32]{4,3,2,1,0:T(8,128)S(1)} copy-done((f32[16,8,2,32,32]{4,3,2,1,0:T(8,128)S(1)}, f32[16,8,2,32,32]{4,3,2,1,0:T(8,128)}, u32[]{:S(2)}) %copy-start) | copy-done | bytes 1048600
  14.0 0.6 weights.1.weight_ref
  14.6 3.9 %all-to-all-done = bf16[16,16,256]{2,1,0:T(8,128)(2,1)S(1)} async-done(((bf16[16,16,256]{2,1,0:T(8,128)(2,1)}), bf16[16,16,256]{2,1,0:T(8,128)(2,1)S(1)}, u32[]{:S(2)}, u32[]{:S(2)}) %all-to-all-start) | async-done | bytes 131104 | tf_op jit(solution)/shard_map/all_to_all | solution.py:494
  18.4 0.0 copy-done.1
  18.4 0.0 copy-done.2
  18.4 1.1 %mode.1 = (f32[256,32]{1,0:T(8,128)S(1)}, bf16[256,256]{1,0:T(8,128)(2,1)S(1)}) custom-call(bf16[256,256]{1,0:T(8,128)(2,1)S(1)} %bitcast.23, bf16[256,256]{1,0:T(8,128)(2,1)S(1)} %copy-done.2, bf16[256,256]{1,0:T(8,128)(2,1)S(1)} %copy-done.1, bf16[16,256,64]{2,1,0:T(8,128)(2,1)S(1)} %weights.1.weight_ref), custom_call_target="tpu_custom_call" | custom-call | flops 4194304 | bytes 524288 | tf_op jit(solution)/shard_map/mode/pallas_call | solution.py:523
  19.5 10.0 %all_to_all.20 = bf16[16,16,256]{2,1,0:T(8,128)(2,1)S(1)} all-to-all(bf16[16,16,256]{2,1,0:T(8,128)(2,1)S(1)} %bitcast.27), channel_id=1, replica_groups={{0,1,4,5,8,9,12,13,16,17,20,21,24,25,28,29},{2,3,6,7,10,11,14,15,18,19,..., dimensions={0} | all-to-all | bytes 262144 | tf_op jit(solution)/shard_map/all_to_all | solution.py:494
  29.5 0.2 part.2
  29.7 2.5 %collective-permute-start.1 = (bf16[32,256]{1,0:T(8,128)(2,1)S(1)}, bf16[32,256]{1,0:T(8,128)(2,1)S(1)}, u32[]{:S(2)}, u32[]{:S(2)}) collective-permute-start(bf16[32,256]{1,0:T(8,128)(2,1)S(1)} %get-tuple-element.26), channel_id=1, source_target_pairs={{0,2},{1,3},{2,0},{3,1},{4,6},{5,7},{6,4},{7,5},{8,10},{9,11},{10,... | collective-permute-start | bytes 49160 | tf_op jit(solution)/shard_map/ppermute | solution.py:485
  32.2 0.0 copy-done.9
  32.2 0.0 copy-done.8
  32.2 0.1 copy.15.refs_4_
  32.3 0.1 copy.17.refs_7_
  32.4 0.0 copy-done.7
  32.4 0.1 copy.16.refs_6_
  32.6 0.5 collective-permute-done.1.refs_1_
  33.1 0.0 copy-done.4
  33.1 0.0 copy-done.5
  33.1 0.0 copy-done.6
  33.1 3.1 %cell.1 = (f32[8,128]{1,0:T(8,128)}, bf16[256,128]{1,0:T(8,128)(2,1)S(1)}, bf16[64,256]{1,0:T(8,128)(2,1)S(1)}, f32[32,128]{1,0:T(8,128)S(1)}) custom-call(f32[32,256]{1,0:T(8,128)S(1)} %get-tuple-element.25.refs_0_, bf16[32,256]{1,0:T(8,128)(2,1)S(1)} %collective-permute-done.1.refs_1_, bf16[256,128]{1,0:T(8,128)(2,1)S(1)} %get-tuple-element.27.refs_2_, ...), custom_call_target="tpu_custom_call" | custom-call | flops 4194304 | bytes 524288 | tf_op jit(solution)/shard_map/cell/pallas_call | solution.py:536
  36.2 0.3 collective-permute-start.2
  36.5 0.9 %collective-permute-done.2.refs_1_ = bf16[64,256]{1,0:T(8,128)(2,1)S(1)} collective-permute-done((bf16[64,256]{1,0:T(8,128)(2,1)S(1)}, bf16[64,256]{1,0:T(8,128)(2,1)S(1)}, u32[]{:S(2)}, u32[]{:S(2)}) %collective-permute-start.2) | collective-permute-done | bytes 32800 | tf_op jit(solution)/shard_map/ppermute | solution.py:485
  37.4 0.3 fold.3
  37.7 9.6 %all_to_all.21 = bf16[16,40,128]{2,1,0:T(8,128)(2,1)S(1)} all-to-all(bf16[16,40,128]{2,1,0:T(8,128)(2,1)S(1)} %bitcast.20), channel_id=1, replica_groups={{0,1,4,5,8,9,12,13,16,17,20,21,24,25,28,29},{2,3,6,7,10,11,14,15,18,19,..., dimensions={0} | all-to-all | bytes 327680 | tf_op jit(solution)/shard_map/all_to_all | solution.py:494
  47.3 1.0 %back.1 = (f32[256,32]{1,0:T(8,128)S(1)}, bf16[640,128]{1,0:T(8,128)(2,1)S(1)}) custom-call(bf16[640,128]{1,0:T(8,128)(2,1)S(1)} %bitcast.21, bf16[256,256]{1,0:T(8,128)(2,1)S(1)} %copy-done.2, bf16[256,256]{1,0:T(8,128)(2,1)S(1)} %copy-done.1, bf16[16,256,64]{2,1,0:T(8,128)(2,1)S(1)} %weights.1.weight_ref), custom_call_target="tpu_custom_call" | custom-call | flops 4194304 | bytes 524288 | tf_op jit(solution)/shard_map/back/pallas_call | solution.py:553
  48.3 10.5 %all_to_all.22 = bf16[16,40,128]{2,1,0:T(8,128)(2,1)S(1)} all-to-all(bf16[16,40,128]{2,1,0:T(8,128)(2,1)S(1)} %bitcast.24), channel_id=1, replica_groups={{0,1,4,5,8,9,12,13,16,17,20,21,24,25,28,29},{2,3,6,7,10,11,14,15,18,19,..., dimensions={0} | all-to-all | bytes 327680 | tf_op jit(solution)/shard_map/all_to_all | solution.py:494
  58.9 0.2 part.3
  59.1 2.4 %collective-permute-start.3 = (bf16[64,256]{1,0:T(8,128)(2,1)S(1)}, bf16[64,256]{1,0:T(8,128)(2,1)S(1)}, u32[]{:S(2)}, u32[]{:S(2)}) collective-permute-start(bf16[64,256]{1,0:T(8,128)(2,1)S(1)} %get-tuple-element.33), channel_id=1, source_target_pairs={{0,2},{1,3},{2,0},{3,1},{4,6},{5,7},{6,4},{7,5},{8,10},{9,11},{10,... | collective-permute-start | bytes 98312 | tf_op jit(solution)/shard_map/ppermute | solution.py:485
  61.5 3.5 %outer.1 = f32[16,8,2,32,32]{4,3,2,1,0:T(8,128)} custom-call(f32[16,16,32]{2,1,0:T(8,128)S(1)} %bitcast.25, f32[16,16,32]{2,1,0:T(8,128)S(1)} %bitcast.26), custom_call_target="tpu_custom_call" | custom-call | flops 4194304 | bytes 5242880 | tf_op jit(solution)/shard_map/outer/pallas_call | solution.py:560
  65.0 0.0 collective-permute-done.3.refs_1_
  65.1 1.1 %finish.1 = (bf16[256,128]{1,0:T(8,128)(2,1)}, f32[32,32]{1,0:T(8,128)}, f32[32,128]{1,0:T(8,128)}) custom-call(f32[32,256]{1,0:T(8,128)S(1)} %get-tuple-element.32.refs_0_, bf16[64,256]{1,0:T(8,128)(2,1)S(1)} %collective-permute-done.3.refs_1_, bf16[256,128]{1,0:T(8,128)(2,1)S(1)} %get-tuple-element.34.refs_2_, bf16[32,32]{1,0:T(8,128)(2,1)S(1)} %copy-done.4, ...), custom_call_target="tpu_custom_call" | custom-call | flops 4194304 | bytes 524288 | tf_op jit(solution)/shard_map/finish/pallas_call | solution.py:573
  (1 shorter events, 0.0 us)
Async XLA Ops:
  0.6 17.8 %copy-start.1 = (bf16[256,256]{1,0:T(8,128)(2,1)S(1)}, bf16[256,256]{1,0:T(8,128)(2,1)}, u32[]{:S(2)}) copy-start(bf16[256,256]{1,0:T(8,128)(2,1)} %constant.5.clone.y_inverse_ref) | copy-start | bytes 393220
  0.6 17.8 %copy-start.2 = (bf16[256,256]{1,0:T(8,128)(2,1)S(1)}, bf16[256,256]{1,0:T(8,128)(2,1)}, u32[]{:S(2)}) copy-start(bf16[256,256]{1,0:T(8,128)(2,1)} %constant.4.clone.y_forward_ref) | copy-start | bytes 393220
  0.7 0.9 %copy-start.3 = (bf16[1,32,8,128]{3,2,1,0:T(8,128)(2,1)S(1)}, bf16[1,32,8,128]{3,2,1,0:T(8,128)(2,1)}, u32[]{:S(2)}) copy-start(bf16[1,32,8,128]{3,2,1,0:T(8,128)(2,1)} %param.10) | copy-start | bytes 196612
  1.5 30.7 %copy-start.9 = (bf16[128]{0:T(256)(128)(2,1)S(1)}, bf16[128]{0:T(256)(128)(2,1)}, u32[]{:S(2)}) copy-start(bf16[128]{0:T(256)(128)(2,1)} %param.16) | copy-start | bytes 772
  1.5 30.7 %copy-start.8 = (f32[32]{0:T(128)S(1)}, f32[32]{0:T(128)}, u32[]{:S(2)}) copy-start(f32[32]{0:T(128)} %param.13) | copy-start | bytes 388
  1.5 30.9 %copy-start.7 = (f32[128]{0:T(128)S(1)}, f32[128]{0:T(128)}, u32[]{:S(2)}) copy-start(f32[128]{0:T(128)} %param.15) | copy-start | bytes 1540
  1.5 31.5 %copy-start.4 = (bf16[32,32]{1,0:T(8,128)(2,1)S(1)}, bf16[32,32]{1,0:T(8,128)(2,1)}, u32[]{:S(2)}) copy-start(bf16[32,32]{1,0:T(8,128)(2,1)} %refs_3_.3) | copy-start | bytes 6148
  1.6 31.5 %copy-start.5 = (bf16[32,128]{1,0:T(8,128)(2,1)S(1)}, bf16[32,128]{1,0:T(8,128)(2,1)}, u32[]{:S(2)}) copy-start(bf16[32,128]{1,0:T(8,128)(2,1)} %refs_5_.1) | copy-start | bytes 24580
  1.6 31.5 %copy-start.6 = (f32[1,8,128]{2,1,0:T(8,128)S(1)}, f32[1,8,128]{2,1,0:T(8,128)}, u32[]{:S(2)}) copy-start(f32[1,8,128]{2,1,0:T(8,128)} %param.17) | copy-start | bytes 12292
  1.9 1.2 %collective-permute-start = (bf16[32,256]{1,0:T(8,128)(2,1)S(1)}, bf16[32,256]{1,0:T(8,128)(2,1)S(1)}, u32[]{:S(2)}, u32[]{:S(2)}) collective-permute-start(bf16[32,256]{1,0:T(8,128)(2,1)S(1)} %get-tuple-element.23.refs_0_), channel_id=1, source_target_pairs={{0,2},{1,3},{2,0},{3,1},{4,6},{5,7},{6,4},{7,5},{8,10},{9,11},{10,... | collective-permute-start | bytes 49160 | tf_op jit(solution)/shard_map/ppermute | solution.py:485
  4.0 14.4 %all-to-all-start = ((bf16[16,16,256]{2,1,0:T(8,128)(2,1)}), bf16[16,16,256]{2,1,0:T(8,128)(2,1)S(1)}, u32[]{:S(2)}, u32[]{:S(2)}) async-start(bf16[16,16,256]{2,1,0:T(8,128)(2,1)} %bitcast.1), calls=%async_computation | async-start | bytes 262144 | tf_op jit(solution)/shard_map/all_to_all | solution.py:494
  11.8 2.2 %copy-start = (f32[16,8,2,32,32]{4,3,2,1,0:T(8,128)S(1)}, f32[16,8,2,32,32]{4,3,2,1,0:T(8,128)}, u32[]{:S(2)}) copy-start(f32[16,8,2,32,32]{4,3,2,1,0:T(8,128)} %weight_ref.1) | copy-start | bytes 3145732
  29.7 3.3 %collective-permute-start.1 = (bf16[32,256]{1,0:T(8,128)(2,1)S(1)}, bf16[32,256]{1,0:T(8,128)(2,1)S(1)}, u32[]{:S(2)}, u32[]{:S(2)}) collective-permute-start(bf16[32,256]{1,0:T(8,128)(2,1)S(1)} %get-tuple-element.26), channel_id=1, source_target_pairs={{0,2},{1,3},{2,0},{3,1},{4,6},{5,7},{6,4},{7,5},{8,10},{9,11},{10,... | collective-permute-start | bytes 49160 | tf_op jit(solution)/shard_map/ppermute | solution.py:485
  36.2 1.2 %collective-permute-start.2 = (bf16[64,256]{1,0:T(8,128)(2,1)S(1)}, bf16[64,256]{1,0:T(8,128)(2,1)S(1)}, u32[]{:S(2)}, u32[]{:S(2)}) collective-permute-start(bf16[64,256]{1,0:T(8,128)(2,1)S(1)} %get-tuple-element.29.refs_0_), channel_id=1, source_target_pairs={{0,2},{1,3},{2,0},{3,1},{4,6},{5,7},{6,4},{7,5},{8,10},{9,11},{10,... | collective-permute-start | bytes 98312 | tf_op jit(solution)/shard_map/ppermute | solution.py:485
  59.1 5.9 %collective-permute-start.3 = (bf16[64,256]{1,0:T(8,128)(2,1)S(1)}, bf16[64,256]{1,0:T(8,128)(2,1)S(1)}, u32[]{:S(2)}, u32[]{:S(2)}) collective-permute-start(bf16[64,256]{1,0:T(8,128)(2,1)S(1)} %get-tuple-element.33), channel_id=1, source_target_pairs={{0,2},{1,3},{2,0},{3,1},{4,6},{5,7},{6,4},{7,5},{8,10},{9,11},{10,... | collective-permute-start | bytes 98312 | tf_op jit(solution)/shard_map/ppermute | solution.py:485

commit v4 on v3

--- a/solution.py
+++ b/solution.py
@@ -15,6 +15,16 @@
 F32 = jnp.float32
 BF16 = jnp.bfloat16
 VMEM_LIMIT = 32 * 1024 * 1024
+
+TAIL_SLOPE = 0.275
+TAIL = (
+    0.11780925840139389,
+    0.04211147502064705,
+    0.3339323103427887,
+    -0.3309934139251709,
+    0.4519987106323242,
+    -0.11485832929611206,
+)
 
 
 def signed(indices, count):
@@ -194,32 +204,56 @@
     return jnp.concatenate(blocks, axis=0).astype(BF16)
 
 
-def start_kernel(place, field_ref, field_out_ref, send_ref):
+def turn_matrix(place):
     channels, rows_y = place.channels, place.rows_y
-    turn = selector(
+    return selector(
         place.lanes,
         place.lanes,
         lambda row, column: (row % channels == column // rows_y)
         & (row // channels == column % rows_y),
     )
-    turned = dot(turn, field_ref[...]).astype(BF16)
-    field_out_ref[...] = turned
+
+
+def side_by_side(values, count):
+    height = values.shape[0] // count
+    return jnp.concatenate([values[y * height : (y + 1) * height] for y in range(count)], axis=1)
+
+
+def one_below_other(values, count):
+    width = values.shape[1] // count
+    return jnp.concatenate([values[:, y * width : (y + 1) * width] for y in range(count)], axis=0)
+
+
+def start_kernel(place, field_ref, field_out_ref, send_ref):
+    turned = dot(turn_matrix(place), field_ref[...]).astype(BF16)
+    field_out_ref[...] = side_by_side(turned, place.rows_y)
     send_ref[...] = dot_nt(place.z_table(False), turned).astype(BF16)
 
 
-def weight_kernel(weight_ref, out_ref):
+def prepare_kernel(
+    place, weight_ref, packed_ref, z_plain_ref, z_doubled_ref, turn_ref, forward_ref, inverse_ref
+):
     modes, kz, _, channels, _ = weight_ref.shape
-    for j in range(modes):
-        both = jnp.concatenate([weight_ref[j, :, 0], weight_ref[j, :, 1]], axis=-1)
-        out_ref[j] = both.reshape(kz * channels, 2 * channels).astype(BF16)
+    for q in range(modes // 4):
+        parts = [weight_ref[4 * q + j // 2, :, j % 2] for j in range(8)]
+        packed = jnp.concatenate(parts, axis=-1).reshape(kz * channels, 8 * channels)
+        packed_ref[q] = packed.astype(BF16)
+    z_plain_ref[...] = place.z_table(False)
+    z_doubled_ref[...] = place.z_table(True)
+    turn_ref[...] = turn_matrix(place)
+    forward_ref[...] = jnp.concatenate(halves(place.forward_x()), axis=1)
+    inverse_ref[...] = place.inverse_x()
 
 
 def fold_kernel(place, *refs):
     own_ref, got_ref = refs[:2]
-    high, low = halves(place.forward_x())
     height = 2 * MZ
     values = jnp.concatenate([own_ref[:height], got_ref[:height]], axis=0)
-    partial = (dot(high, values) + dot(low, values)).astype(BF16)
+    if len(refs) > 3:
+        tables, refs = refs[2][...], refs[:2] + refs[3:]
+    else:
+        tables = jnp.concatenate(halves(place.forward_x()), axis=1)
+    partial = dot(tables, jnp.concatenate([values, values], axis=0)).astype(BF16)
     if got_ref.shape[0] == height:
         refs[2][...] = partial
         return
@@ -246,26 +280,29 @@
     row, lane = grid_of(*spectrum.shape)
     blocked = jnp.where(row % kz == lane // channels, spectrum, 0.0)
     mixed = []
-    for j in range(place.modes):
-        left = blocked[j * 2 * kz : (j + 1) * 2 * kz].astype(BF16)
-        product = dot(left, weight_ref[j])
-        real, imag = product[:, :channels], product[:, channels:]
-        mixed.append(real[:kz] - imag[kz:])
-        mixed.append(imag[:kz] + real[kz:])
+    for q in range(place.modes // 4):
+        left = blocked[q * 8 * kz : (q + 1) * 8 * kz].astype(BF16)
+        product = dot(left, weight_ref[q])
+        for j in range(4):
+            own = product[j * 2 * kz : (j + 1) * 2 * kz, j * 2 * channels : (j + 1) * 2 * channels]
+            real, imag = own[:, :channels], own[:, channels:]
+            mixed.append(real[:kz] - imag[kz:])
+            mixed.append(imag[:kz] + real[kz:])
     mode = jnp.concatenate(mixed, axis=0).astype(BF16)
     repeat_rows(send_ref, spread_lines(place, mode, y_inverse_ref[...]))
 
 
 def part_kernel(place, *refs):
     pieces, shares = read_pieces(place, refs[0])
-    lines = dot(place.inverse_x(), pieces)
+    lines = dot(refs[1][...], pieces)
     height = 2 * MZ
-    own_ref, send_ref = refs[1:3]
+    refs = refs[3:] if place.fold and shares is not None else refs[2:]
+    own_ref, send_ref = refs[:2]
     own_ref[...] = lines[:height]
     if shares is None:
         send_ref[...] = lines[height:].astype(BF16)
         return
-    sums_ref = refs[3]
+    sums_ref = refs[2]
     count = place.partners
     got = jnp.concatenate(shares, axis=0).astype(BF16)
 
@@ -287,45 +324,55 @@
 
 
 def normal(values):
-    cumulative = 0.5 * (1.0 + lax.erf(values * (1.0 / math.sqrt(2.0))))
-    density = jnp.exp(-0.5 * values * values) * (1.0 / math.sqrt(2.0 * math.pi))
-    return values * cumulative, cumulative + values * density
+    scaled = 1.0 / (1.0 + TAIL_SLOPE * jnp.abs(values))
+    decay = jnp.exp(-0.5 * values * values)
+    tail = TAIL[-1]
+    for factor in TAIL[-2::-1]:
+        tail = tail * scaled + factor
+    tail = tail * (scaled * decay)
+    cumulative = jnp.where(values > 0.0, 1.0 - tail, tail)
+    return values * cumulative, cumulative + values * (decay * (1.0 / math.sqrt(2.0 * math.pi)))
 
 
 def cell_kernel(place, *refs):
-    own_ref, got_ref, refs = refs[0], refs[1], refs[2:]
-    field_ref, mix_ref, mix_bias_ref, head_ref, head_bias_ref, out_weight_ref, cotangent_ref = refs[:7]
-    prediction_ref, grad_pre_ref, send_ref = refs[7:10]
+    own_ref, got_ref, z_table_ref, refs = refs[0], refs[1], refs[2], refs[3:]
+    field_ref, mix_ref, mix_bias_ref, head_ref, head_bias_ref = refs[:5]
+    out_row_ref, out_column_ref, cotangent_ref = refs[5:8]
+    prediction_ref, grad_pre_ref, send_ref = refs[8:11]
     channels, hidden_units = head_ref.shape
-    z_table = place.z_table(True)
+    rows_y, z_count = place.rows_y, place.z_count
+    z_table = z_table_ref[...]
     lines = (own_ref[...] + got_ref[...].astype(F32)).astype(BF16)
-    branch = dot_tn(lines, z_table)
-    mix, head = mix_ref[...], head_ref[...]
-    mix_bias, head_bias = mix_bias_ref[...], head_bias_ref[...]
-    out_weight = out_weight_ref[...]
-    grad_mix = jnp.zeros((channels, channels), F32)
-    grad_head = jnp.zeros((channels, hidden_units), F32)
-    gradients = []
-    for y in range(place.rows_y):
-        cells = slice(y * channels, (y + 1) * channels)
-        field = field_ref[cells]
-        pre_act = branch[cells] + dot_tn(mix, field) + mix_bias
-        hidden, pre_slope = normal(pre_act)
-        hidden = hidden.astype(BF16)
-        head_pre = dot_tn(head, hidden) + head_bias
-        active, slope = normal(head_pre)
-        active = active.astype(BF16).astype(F32)
-        prediction_ref[y : y + 1] = jnp.sum(active * out_weight, axis=0, keepdims=True)
-        head_slope = (cotangent_ref[y : y + 1] * out_weight * slope).astype(BF16)
-        grad_pre = (dot(head, head_slope) * pre_slope).astype(BF16)
-        grad_head += dot_nt(hidden, head_slope)
-        grad_mix += dot_nt(field, grad_pre)
-        gradients.append(grad_pre)
-
-    gradient = jnp.concatenate(gradients, axis=0)
+    branch = side_by_side(dot_tn(lines, z_table), rows_y)
+    field, head = field_ref[...], head_ref[...]
+    head_turned = jnp.transpose(head.astype(F32)).astype(BF16)
+    pre_act = branch + dot_tn(mix_ref[...], field) + mix_bias_ref[...]
+    head_bias, out_row, out_column = head_bias_ref[...], out_row_ref[...], out_column_ref[...]
+    width = 2 * z_count
+    hidden, slopes, head_pre = [], [], []
+    for first in range(0, rows_y * z_count, width):
+        value, slope = normal(pre_act[:, first : first + width])
+        hidden.append(value.astype(BF16))
+        slopes.append(slope)
+        head_pre.append(dot(head_turned, hidden[-1]))
+    head_slopes, gradients = [], []
+    for index, first in enumerate(range(0, rows_y, 2)):
+        target = jnp.concatenate(
+            [cotangent_ref[y : y + 1] for y in range(first, first + 2)], axis=1
+        )
+        active, slope = normal(head_pre[index] + head_bias)
+        predicted = dot(out_row, active.astype(BF16))
+        prediction_ref[first : first + 1] = predicted[:, :z_count]
+        prediction_ref[first + 1 : first + 2] = predicted[:, z_count:]
+        head_slope = (target * out_column * slope).astype(BF16)
+        gradients.append((dot(head, head_slope) * slopes[index]).astype(BF16))
+        head_slopes.append(head_slope)
+    gradient = jnp.concatenate(gradients, axis=1)
     grad_pre_ref[...] = gradient
     height = 2 * MZ
-    send_ref[:height] = dot_nt(z_table, gradient).astype(BF16)
+    send_ref[:height] = dot_nt(z_table, one_below_other(gradient, rows_y)).astype(BF16)
+    grad_mix = dot_nt(field, gradient)
+    grad_head = dot_nt(jnp.concatenate(hidden, axis=1), jnp.concatenate(head_slopes, axis=1))
     if not place.fold:
         refs[-2][...] = grad_mix
         refs[-1][...] = grad_head
@@ -345,7 +392,7 @@
         picked = selector(2 * count, 2 * channels, condition)
         return dot(picked, high), dot(picked, low)
 
-    refs[10][...] = sum(chosen(inner))
+    refs[11][...] = sum(chosen(inner))
     send_ref[height:] = jnp.concatenate(chosen(1 - inner), axis=1).astype(BF16)
 
 
@@ -356,14 +403,18 @@
     pieces, shares = read_pieces(place, pieces_ref)
     adjoint = analysed(place, pieces, y_forward_ref[...], 1)
     adjoint_ref[...] = adjoint
-    pulled = []
-    for j in range(place.modes):
-        real = adjoint[j * 2 * kz : j * 2 * kz + kz]
-        imag = adjoint[j * 2 * kz + kz : (j + 1) * 2 * kz]
-        left = jnp.concatenate(
-            [jnp.concatenate([real, imag], axis=1), jnp.concatenate([imag, -real], axis=1)], axis=0
-        )
-        pulled.append(dot_nt(left.astype(BF16), weight_ref[j]))
+    turned = []
+    for first in range(0, adjoint.shape[0], 2 * kz):
+        turned += [adjoint[first + kz : first + 2 * kz], -adjoint[first : first + kz]]
+    left = jnp.concatenate([adjoint, jnp.concatenate(turned, axis=0)], axis=1)
+    left = jnp.concatenate([left] * 4, axis=1)
+    row, lane = grid_of(*left.shape)
+    same = (row // (2 * kz)) % 4 == lane // (2 * channels)
+    left = jnp.where(same, left, 0.0).astype(BF16)
+    block = 8 * kz
+    pulled = [
+        dot_nt(left[q * block : (q + 1) * block], weight_ref[q]) for q in range(place.modes // 4)
+    ]
     pulled = jnp.concatenate(pulled, axis=0)
     row, lane = grid_of(*pulled.shape)
     pulled = jnp.where(row % kz == lane // channels, pulled, 0.0).astype(BF16)
@@ -382,7 +433,8 @@
     write_pieces(place, send_ref, block, split.astype(BF16))
 
 
-def outer_kernel(spectrum_ref, adjoint_ref, out_ref):
+def outer_kernel(spectrum_ref, adjoint_ref, out_ref, done_ref):
+    done_ref[...] = jnp.zeros(done_ref.shape, F32)
     modes, kz = out_ref.shape[:2]
     for j in range(modes):
         columns = jnp.transpose(spectrum_ref[j])
@@ -395,27 +447,19 @@
 
 
 def finish_kernel(place, *refs):
-    own_ref, got_ref, grad_pre_ref, mix_ref = refs[:4]
-    refs = refs[4:]
+    own_ref, got_ref, z_table_ref, turn_ref, grad_pre_ref, mix_ref = refs[:6]
+    refs = refs[6:]
     height = 2 * MZ
     channels, rows_y = place.channels, place.rows_y
     lines = (own_ref[...] + got_ref[:height].astype(F32)).astype(BF16)
-    branch = dot_tn(lines, place.z_table(False))
-    parts = []
-    for y in range(rows_y):
-        cells = slice(y * channels, (y + 1) * channels)
-        parts.append((branch[cells] + dot(mix_ref[...], grad_pre_ref[cells])).astype(BF16))
-    turn = selector(
-        place.lanes,
-        place.lanes,
-        lambda row, column: (row // rows_y == column % channels)
-        & (row % rows_y == column // channels),
-    )
+    branch = dot_tn(lines, z_table_ref[...])
+    pointwise = one_below_other(dot(mix_ref[...], grad_pre_ref[...]), rows_y)
+    grad_field = dot_tn(turn_ref[...], (branch + pointwise).astype(BF16)).astype(BF16)
     if not place.fold:
-        refs[0][...] = dot(turn, jnp.concatenate(parts, axis=0)).astype(BF16)
+        refs[0][...] = grad_field
         return
     sums_ref, grad_field_ref, grad_mix_ref, grad_head_ref = refs
-    grad_field_ref[...] = dot(turn, jnp.concatenate(parts, axis=0)).astype(BF16)
+    grad_field_ref[...] = grad_field
     _, inner = place.here()
     count = place.partners
     width = sums_ref.shape[1]
@@ -505,19 +549,21 @@
 
     field, send = call(
         functools.partial(start_kernel, place),
-        [((cells, z_count), BF16), twin_plain],
+        [((channels, rows_y * z_count), BF16), twin_plain],
         "start",
     )(lifted_field.reshape(cells, z_count))
     some = max(1, modes // 4)
-    weight = pl.pallas_call(
-        weight_kernel,
-        grid=(modes // some,),
-        in_specs=[pl.BlockSpec((some, kz, 2, channels, channels), lambda j: (j, 0, 0, 0, 0))],
-        out_specs=pl.BlockSpec((some, kz * channels, 2 * channels), lambda j: (j, 0, 0)),
-        out_shape=jax.ShapeDtypeStruct((modes, kz * channels, 2 * channels), BF16),
-        compiler_params=pltpu.CompilerParams(vmem_limit_bytes=VMEM_LIMIT),
-        cost_estimate=pl.CostEstimate(flops=1 << 20, bytes_accessed=5 << 20, transcendentals=0),
-        name="weights",
+    weight, z_plain, z_doubled, turn, forward, inverse = call(
+        functools.partial(prepare_kernel, place),
+        [
+            ((modes // 4, kz * channels, 8 * channels), BF16),
+            ((height, z_count), BF16),
+            ((height, z_count), BF16),
+            ((cells, cells), BF16),
+            ((wide // 2 * height, 4 * height), BF16),
+            ((2 * height, wide // 2 * height), BF16),
+        ],
+        "prepare",
     )(spectral_weight)
     (send,) = call(functools.partial(fold_kernel, place), [plain], "fold")(send, to_twin(send))
     spectrum, send = call(
@@ -526,9 +572,9 @@
         "mode",
     )(exchange(send), y_forward, y_inverse, weight)
     own, send = call(functools.partial(part_kernel, place), [own_lines, twin_plain], "part")(
-        exchange(send)
-    )
-    outs = [((rows_y, z_count), F32), ((cells, z_count), BF16), twin_shared]
+        exchange(send), inverse
+    )
+    outs = [((rows_y, z_count), F32), ((channels, rows_y * z_count), BF16), twin_shared]
     if place.fold:
         outs += [sums_shape]
     else:
@@ -536,11 +582,13 @@
     prediction, grad_pre, send, *sums = call(functools.partial(cell_kernel, place), outs, "cell")(
         own,
         to_twin(send),
+        z_doubled,
         field,
         mix_weight,
         mix_bias[:, None],
         head_weight,
         head_bias[:, None],
+        out_weight[None],
         out_weight.astype(F32)[:, None],
         cotangent[0],
     )
@@ -548,30 +596,38 @@
         totals = lax.psum(tuple(sums), ("wide", "narrow"))
         sums = []
     (send,) = call(functools.partial(fold_kernel, place), [shared], "fold")(
-        send, to_twin(send), *sums
+        send, to_twin(send), forward, *sums
     )
     adjoint, send = call(
         functools.partial(back_kernel, place),
         [((mode_lines, channels), F32), shared],
         "back",
     )(exchange(send), y_forward, y_inverse, weight)
-    outs = [own_lines, twin_shared] + ([sums_shape] if place.fold else [])
-    own, send, *sums = call(functools.partial(part_kernel, place), outs, "part")(exchange(send))
-    grad_spectral = pl.pallas_call(
+    grad_spectral, done = pl.pallas_call(
         outer_kernel,
         grid=(modes // some,),
         in_specs=[pl.BlockSpec((some, 2 * kz, channels), lambda j: (j, 0, 0))] * 2,
-        out_specs=pl.BlockSpec((some, kz, 2, channels, channels), lambda j: (j, 0, 0, 0, 0)),
-        out_shape=jax.ShapeDtypeStruct(spectral_weight.shape, F32),
+        out_specs=[
+            pl.BlockSpec((some, kz, 2, channels, channels), lambda j: (j, 0, 0, 0, 0)),
+            pl.BlockSpec((8, 128), lambda j: (0, 0)),
+        ],
+        out_shape=[
+            jax.ShapeDtypeStruct(spectral_weight.shape, F32),
+            jax.ShapeDtypeStruct((8, 128), F32),
+        ],
         compiler_params=pltpu.CompilerParams(vmem_limit_bytes=VMEM_LIMIT),
         cost_estimate=pl.CostEstimate(flops=1 << 22, bytes_accessed=5 << 20, transcendentals=0),
         name="outer",
     )(spectrum.reshape(modes, 2 * kz, channels), adjoint.reshape(modes, 2 * kz, channels))
+    pieces = exchange(send)
+    outs = [own_lines, twin_shared] + ([sums_shape] if place.fold else [])
+    operands = (pieces, inverse, done) if place.fold else (pieces, inverse)
+    own, send, *sums = call(functools.partial(part_kernel, place), outs, "part")(*operands)
     outs = [((cells, z_count), BF16)]
     if place.fold:
         outs += [((channels, channels), F32), ((channels, hidden_units), F32)]
     grad_field, *summed = call(functools.partial(finish_kernel, place), outs, "finish")(
-        own, to_twin(send), grad_pre, mix_weight, *sums
+        own, to_twin(send), z_plain, turn, grad_pre, mix_weight, *sums
     )
     grad_mix, grad_head = summed if place.fold else totals
     return (

time: 66.5 us -> 63.3 us (0.952)
  blocking collectives: 30.2 us -> 19.6 us
  starting transfers between devices: 13.1 us -> 17.1 us
  waiting for transfers between devices: 6.36 us -> 10.3 us
  Pallas kernels: 12.4 us -> 11.4 us
    all_to_all x3 -> x2, blocking collectives: 30.2 us -> 19.6 us  [exchange(): lax.all_to_all(pieces, ('wide', 'narrow'), 0, 0, axis_index_groups=groups...]
    all_to_all x1 -> x2, starting transfers between devices: 7.74 us -> 11.7 us  [exchange(): lax.all_to_all(pieces, ('wide', 'narrow'), 0, 0, axis_index_groups=groups...]
    all_to_all x1 -> x2, waiting for transfers between devices: 3.86 us -> 6.93 us  [exchange(): lax.all_to_all(pieces, ('wide', 'narrow'), 0, 0, axis_index_groups=groups...]
    pallas_call x1, Pallas kernels: 3.09 us -> 1.62 us  [body(): call(functools.partial(cell_kernel, place), outs, 'cell')]
    ppermute x4, waiting for transfers between devices: 2.5 us -> 3.36 us  [to_twin(): return lax.ppermute(send, ('wide', 'narrow'), pairs)]
  transfers between devices with their start and end apart: 5 -> 6, of which waited for: 4 -> 6; matrix products, arithmetic and copies ran while one was open for 0% -> 1% of each run, Pallas kernels for 6% -> 7%
where the time goes in v4:
time: 63.3 us; the launch traced here: 62.6 us
  blocking collectives  19.6 us (31%)
  starting transfers between devices  17.1 us (27%)
  Pallas kernels  11.4 us (18%)
  waiting for transfers between devices  10.3 us (16%)
  local copies, waits for them, and re-layouts  3.41 us (5%)
  between operations  0.74 us (1%)
    all_to_all x2, blocking collectives, exchange(): lax.all_to_all(pieces, ('wide', 'narrow'), 0, 0, axis_index_groups=groups...  19.6 us
    all_to_all x2, starting transfers between devices, exchange(): lax.all_to_all(pieces, ('wide', 'narrow'), 0, 0, axis_index_groups=groups...  11.7 us
    all_to_all x2, waiting for transfers between devices, exchange(): lax.all_to_all(pieces, ('wide', 'narrow'), 0, 0, axis_index_groups=groups...  6.93 us
    ppermute x4, starting transfers between devices, to_twin(): return lax.ppermute(send, ('wide', 'narrow'), pairs)  5.42 us
    pallas_call x1, Pallas kernels, body(): pl.pallas_call(outer_kernel, grid=(modes // some,), in_specs=[pl.BlockSpe...  3.55 us
    ppermute x4, waiting for transfers between devices, to_twin(): return lax.ppermute(send, ('wide', 'narrow'), pairs)  3.36 us
    unnamed x20, local copies, waits for them, and re-layouts  3.09 us
    pallas_call x1, Pallas kernels, body(): call(functools.partial(back_kernel, place), [((mode_lines, channels), F32...  1.7 us
  transfers between devices with their start and end apart: 6, of which 6 were waited for; matrix products, arithmetic and copies ran while one was open for 1% of the time, Pallas kernels for 7%

profile of v4, /device:TPU:1, one launch (start us, length us, event | category | flops | bytes accessed | tf_op | source)
XLA Modules:
  0.0 62.6 jit_solution(7636519457748864251)
XLA Ops:
  0.6 0.0 copy-start.1
  0.6 0.0 copy-start.2
  0.7 0.0 copy-start.3
  0.7 0.9 %copy-done.3 = bf16[1,32,8,128]{3,2,1,0:T(8,128)(2,1)S(1)} copy-done((bf16[1,32,8,128]{3,2,1,0:T(8,128)(2,1)S(1)}, bf16[1,32,8,128]{3,2,1,0:T(8,128)(2,1)}, u32[]{:S(2)}) %copy-start.3) | copy-done | bytes 65560
  1.5 0.0 copy-start.7
  1.5 0.0 copy-start.9
  1.5 0.0 copy-start.8
  1.5 0.0 copy-start.4
  1.6 0.0 copy-start.5
  1.6 0.0 copy-start.6
  1.6 0.3 start.1
  1.9 0.1 collective-permute-start
  2.0 1.1 %collective-permute-done.refs_1_ = bf16[32,256]{1,0:T(8,128)(2,1)S(1)} collective-permute-done((bf16[32,256]{1,0:T(8,128)(2,1)S(1)}, bf16[32,256]{1,0:T(8,128)(2,1)S(1)}, u32[]{:S(2)}, u32[]{:S(2)}) %collective-permute-start) | collective-permute-done | bytes 16416 | tf_op jit(solution)/shard_map/ppermute | solution.py:529
  3.1 1.0 %fold.2 = bf16[256,256]{1,0:T(8,128)(2,1)} custom-call(bf16[32,256]{1,0:T(8,128)(2,1)S(1)} %get-tuple-element.31.refs_0_, bf16[32,256]{1,0:T(8,128)(2,1)S(1)} %collective-permute-done.refs_1_), custom_call_target="tpu_custom_call" | custom-call | flops 4194304 | bytes 524288 | tf_op jit(solution)/shard_map/fold/pallas_call | solution.py:568
  4.0 7.7 %all-to-all-start = ((bf16[16,16,256]{2,1,0:T(8,128)(2,1)}), bf16[16,16,256]{2,1,0:T(8,128)(2,1)S(1)}, u32[]{:S(2)}, u32[]{:S(2)}) async-start(bf16[16,16,256]{2,1,0:T(8,128)(2,1)} %bitcast.1), calls=%async_computation | async-start | bytes 262144 | tf_op jit(solution)/shard_map/all_to_all | solution.py:538
  11.8 0.0 copy-start
  11.8 2.2 %copy-done = f32[16,8,2,32,32]{4,3,2,1,0:T(8,128)S(1)} copy-done((f32[16,8,2,32,32]{4,3,2,1,0:T(8,128)S(1)}, f32[16,8,2,32,32]{4,3,2,1,0:T(8,128)}, u32[]{:S(2)}) %copy-start) | copy-done | bytes 1048600
  14.0 0.7 %prepare.1 = (bf16[4,256,256]{2,1,0:T(8,128)(2,1)S(1)}, bf16[32,128]{1,0:T(8,128)(2,1)S(1)}, bf16[32,128]{1,0:T(8,128)(2,1)S(1)}, bf16[256,256]{1,0:T(8,128)(2,1...) custom-call(f32[16,8,2,32,32]{4,3,2,1,0:T(8,128)S(1)} %copy-done), custom_call_target="tpu_custom_call" | custom-call | flops 4194304 | bytes 524288 | tf_op jit(solution)/shard_map/prepare/pallas_call | solution.py:556
  14.7 3.7 %all-to-all-done = bf16[16,16,256]{2,1,0:T(8,128)(2,1)S(1)} async-done(((bf16[16,16,256]{2,1,0:T(8,128)(2,1)}), bf16[16,16,256]{2,1,0:T(8,128)(2,1)S(1)}, u32[]{:S(2)}, u32[]{:S(2)}) %all-to-all-start) | async-done | bytes 131104 | tf_op jit(solution)/shard_map/all_to_all | solution.py:538
  18.4 0.0 copy-done.1
  18.4 0.0 copy-done.2
  18.4 1.0 %mode.1 = (f32[256,32]{1,0:T(8,128)S(1)}, bf16[256,256]{1,0:T(8,128)(2,1)S(1)}) custom-call(bf16[256,256]{1,0:T(8,128)(2,1)S(1)} %bitcast.23, bf16[256,256]{1,0:T(8,128)(2,1)S(1)} %copy-done.2, bf16[256,256]{1,0:T(8,128)(2,1)S(1)} %copy-done.1, bf16[4,256,256]{2,1,0:T(8,128)(2,1)S(1)} %get-tuple-element.32.weight_ref), custom_call_target="tpu_custom_call" | custom-call | flops 4194304 | bytes 524288 | tf_op jit(solution)/shard_map/mode/pallas_call | solution.py:569
  19.5 10.0 %all_to_all.20 = bf16[16,16,256]{2,1,0:T(8,128)(2,1)S(1)} all-to-all(bf16[16,16,256]{2,1,0:T(8,128)(2,1)S(1)} %bitcast.27), channel_id=1, replica_groups={{0,1,4,5,8,9,12,13,16,17,20,21,24,25,28,29},{2,3,6,7,10,11,14,15,18,19,..., dimensions={0} | all-to-all | bytes 262144 | tf_op jit(solution)/shard_map/all_to_all | solution.py:538
  29.5 0.1 part.2
  29.6 2.5 %collective-permute-start.1 = (bf16[32,256]{1,0:T(8,128)(2,1)S(1)}, bf16[32,256]{1,0:T(8,128)(2,1)S(1)}, u32[]{:S(2)}, u32[]{:S(2)}) collective-permute-start(bf16[32,256]{1,0:T(8,128)(2,1)S(1)} %get-tuple-element.36), channel_id=1, source_target_pairs={{0,2},{1,3},{2,0},{3,1},{4,6},{5,7},{6,4},{7,5},{8,10},{9,11},{10,... | collective-permute-start | bytes 49160 | tf_op jit(solution)/shard_map/ppermute | solution.py:529
  32.1 0.0 copy-done.7
  32.1 0.0 copy-done.9
  32.1 0.1 copy.15.refs_5_
  32.2 0.1 copy.17.refs_9_
  32.3 0.0 copy-done.8
  32.4 0.1 copy.16.refs_7_
  32.5 0.5 collective-permute-done.1.refs_1_
  33.0 0.0 copy-done.4
  33.0 0.0 copy-done.5
  33.0 0.0 copy-done.6
  33.0 1.6 %cell.1 = (f32[8,128]{1,0:T(8,128)}, bf16[32,1024]{1,0:T(8,128)(2,1)S(1)}, bf16[64,256]{1,0:T(8,128)(2,1)S(1)}, f32[32,128]{1,0:T(8,128)S(1)}) custom-call(f32[32,256]{1,0:T(8,128)S(1)} %get-tuple-element.35.refs_0_, bf16[32,256]{1,0:T(8,128)(2,1)S(1)} %collective-permute-done.1.refs_1_, bf16[32,128]{1,0:T(8,128)(2,1)S(1)} %get-tuple-element.37.refs_2_, ...), custom_call_target="tpu_custom_call" | custom-call | flops 4194304 | bytes 524288 | tf_op jit(solution)/shard_map/cell/pallas_call | solution.py:582
  34.6 0.3 collective-permute-start.2
  35.0 0.9 %collective-permute-done.2.refs_1_ = bf16[64,256]{1,0:T(8,128)(2,1)S(1)} collective-permute-done((bf16[64,256]{1,0:T(8,128)(2,1)S(1)}, bf16[64,256]{1,0:T(8,128)(2,1)S(1)}, u32[]{:S(2)}, u32[]{:S(2)}) %collective-permute-start.2) | collective-permute-done | bytes 32800 | tf_op jit(solution)/shard_map/ppermute | solution.py:529
  35.8 0.2 fold.3
  36.0 9.6 %all_to_all.21 = bf16[16,40,128]{2,1,0:T(8,128)(2,1)S(1)} all-to-all(bf16[16,40,128]{2,1,0:T(8,128)(2,1)S(1)} %bitcast.21), channel_id=1, replica_groups={{0,1,4,5,8,9,12,13,16,17,20,21,24,25,28,29},{2,3,6,7,10,11,14,15,18,19,..., dimensions={0} | all-to-all | bytes 327680 | tf_op jit(solution)/shard_map/all_to_all | solution.py:538
  45.6 1.7 %back.1 = (f32[256,32]{1,0:T(8,128)S(1)}, bf16[640,128]{1,0:T(8,128)(2,1)}) custom-call(bf16[640,128]{1,0:T(8,128)(2,1)S(1)} %bitcast.22, bf16[256,256]{1,0:T(8,128)(2,1)S(1)} %copy-done.2, bf16[256,256]{1,0:T(8,128)(2,1)S(1)} %copy-done.1, bf16[4,256,256]{2,1,0:T(8,128)(2,1)S(1)} %get-tuple-element.32.weight_ref), custom_call_target="tpu_custom_call" | custom-call | flops 4194304 | bytes 524288 | tf_op jit(solution)/shard_map/back/pallas_call | solution.py:601
  47.3 4.0 %all-to-all-start.3 = ((bf16[16,40,128]{2,1,0:T(8,128)(2,1)}), bf16[16,40,128]{2,1,0:T(8,128)(2,1)S(1)}, u32[]{:S(2)}, u32[]{:S(2)}) async-start(bf16[16,40,128]{2,1,0:T(8,128)(2,1)} %bitcast.13), calls=%async_computation.3 | async-start | bytes 327680 | tf_op jit(solution)/shard_map/all_to_all | solution.py:538
  51.3 3.6 %outer.1 = (f32[16,8,2,32,32]{4,3,2,1,0:T(8,128)}, f32[8,128]{1,0:T(8,128)S(1)}) custom-call(f32[16,16,32]{2,1,0:T(8,128)S(1)} %bitcast.25, f32[16,16,32]{2,1,0:T(8,128)S(1)} %bitcast.26), custom_call_target="tpu_custom_call" | custom-call | flops 4194304 | bytes 5242880 | tf_op jit(solution)/shard_map/outer/pallas_call | solution.py:606
  54.9 3.2 %all-to-all-done.3 = bf16[16,40,128]{2,1,0:T(8,128)(2,1)S(1)} async-done(((bf16[16,40,128]{2,1,0:T(8,128)(2,1)}), bf16[16,40,128]{2,1,0:T(8,128)(2,1)S(1)}, u32[]{:S(2)}, u32[]{:S(2)}) %all-to-all-start.3) | async-done | bytes 163872 | tf_op jit(solution)/shard_map/all_to_all | solution.py:538
  58.1 0.2 part.3
  58.3 2.5 %collective-permute-start.3 = (bf16[64,256]{1,0:T(8,128)(2,1)S(1)}, bf16[64,256]{1,0:T(8,128)(2,1)S(1)}, u32[]{:S(2)}, u32[]{:S(2)}) collective-permute-start(bf16[64,256]{1,0:T(8,128)(2,1)S(1)} %get-tuple-element.48), channel_id=1, source_target_pairs={{0,2},{1,3},{2,0},{3,1},{4,6},{5,7},{6,4},{7,5},{8,10},{9,11},{10,... | collective-permute-start | bytes 98312 | tf_op jit(solution)/shard_map/ppermute | solution.py:529
  60.7 0.9 %collective-permute-done.3.refs_1_ = bf16[64,256]{1,0:T(8,128)(2,1)S(1)} collective-permute-done((bf16[64,256]{1,0:T(8,128)(2,1)S(1)}, bf16[64,256]{1,0:T(8,128)(2,1)S(1)}, u32[]{:S(2)}, u32[]{:S(2)}) %collective-permute-start.3) | collective-permute-done | bytes 32800 | tf_op jit(solution)/shard_map/ppermute | solution.py:529
  61.6 1.0 %finish.1 = (bf16[256,128]{1,0:T(8,128)(2,1)}, f32[32,32]{1,0:T(8,128)}, f32[32,128]{1,0:T(8,128)}) custom-call(f32[32,256]{1,0:T(8,128)S(1)} %get-tuple-element.47.refs_0_, bf16[64,256]{1,0:T(8,128)(2,1)S(1)} %collective-permute-done.3.refs_1_, bf16[32,128]{1,0:T(8,128)(2,1)S(1)} %get-tuple-element.49.refs_2_, ...), custom_call_target="tpu_custom_call" | custom-call | flops 4194304 | bytes 524288 | tf_op jit(solution)/shard_map/finish/pallas_call | solution.py:629
  (1 shorter events, 0.0 us)
Async XLA Ops:
  0.6 17.8 %copy-start.1 = (bf16[256,256]{1,0:T(8,128)(2,1)S(1)}, bf16[256,256]{1,0:T(8,128)(2,1)}, u32[]{:S(2)}) copy-start(bf16[256,256]{1,0:T(8,128)(2,1)} %constant.5.clone.y_inverse_ref) | copy-start | bytes 393220
  0.6 17.8 %copy-start.2 = (bf16[256,256]{1,0:T(8,128)(2,1)S(1)}, bf16[256,256]{1,0:T(8,128)(2,1)}, u32[]{:S(2)}) copy-start(bf16[256,256]{1,0:T(8,128)(2,1)} %constant.4.clone.y_forward_ref) | copy-start | bytes 393220
  0.7 0.9 %copy-start.3 = (bf16[1,32,8,128]{3,2,1,0:T(8,128)(2,1)S(1)}, bf16[1,32,8,128]{3,2,1,0:T(8,128)(2,1)}, u32[]{:S(2)}) copy-start(bf16[1,32,8,128]{3,2,1,0:T(8,128)(2,1)} %param.10) | copy-start | bytes 196612
  1.5 30.6 %copy-start.7 = (bf16[128]{0:T(256)(128)(2,1)S(1)}, bf16[128]{0:T(256)(128)(2,1)}, u32[]{:S(2)}) copy-start(bf16[128]{0:T(256)(128)(2,1)} %param.16) | copy-start | bytes 772
  1.5 30.6 %copy-start.9 = (f32[32]{0:T(128)S(1)}, f32[32]{0:T(128)}, u32[]{:S(2)}) copy-start(f32[32]{0:T(128)} %param.13) | copy-start | bytes 388
  1.5 30.8 %copy-start.8 = (f32[128]{0:T(128)S(1)}, f32[128]{0:T(128)}, u32[]{:S(2)}) copy-start(f32[128]{0:T(128)} %param.15) | copy-start | bytes 1540
  1.5 31.4 %copy-start.4 = (bf16[32,32]{1,0:T(8,128)(2,1)S(1)}, bf16[32,32]{1,0:T(8,128)(2,1)}, u32[]{:S(2)}) copy-start(bf16[32,32]{1,0:T(8,128)(2,1)} %refs_5_.1) | copy-start | bytes 6148
  1.6 31.4 %copy-start.5 = (bf16[32,128]{1,0:T(8,128)(2,1)S(1)}, bf16[32,128]{1,0:T(8,128)(2,1)}, u32[]{:S(2)}) copy-start(bf16[32,128]{1,0:T(8,128)(2,1)} %refs_6_.1) | copy-start | bytes 24580
  1.6 31.4 %copy-start.6 = (f32[1,8,128]{2,1,0:T(8,128)S(1)}, f32[1,8,128]{2,1,0:T(8,128)}, u32[]{:S(2)}) copy-start(f32[1,8,128]{2,1,0:T(8,128)} %param.17) | copy-start | bytes 12292
  1.9 1.2 %collective-permute-start = (bf16[32,256]{1,0:T(8,128)(2,1)S(1)}, bf16[32,256]{1,0:T(8,128)(2,1)S(1)}, u32[]{:S(2)}, u32[]{:S(2)}) collective-permute-start(bf16[32,256]{1,0:T(8,128)(2,1)S(1)} %get-tuple-element.31.refs_0_), channel_id=1, source_target_pairs={{0,2},{1,3},{2,0},{3,1},{4,6},{5,7},{6,4},{7,5},{8,10},{9,11},{10,... | collective-permute-start | bytes 49160 | tf_op jit(solution)/shard_map/ppermute | solution.py:529
  4.0 14.4 %all-to-all-start = ((bf16[16,16,256]{2,1,0:T(8,128)(2,1)}), bf16[16,16,256]{2,1,0:T(8,128)(2,1)S(1)}, u32[]{:S(2)}, u32[]{:S(2)}) async-start(bf16[16,16,256]{2,1,0:T(8,128)(2,1)} %bitcast.1), calls=%async_computation | async-start | bytes 262144 | tf_op jit(solution)/shard_map/all_to_all | solution.py:538
  11.8 2.2 %copy-start = (f32[16,8,2,32,32]{4,3,2,1,0:T(8,128)S(1)}, f32[16,8,2,32,32]{4,3,2,1,0:T(8,128)}, u32[]{:S(2)}) copy-start(f32[16,8,2,32,32]{4,3,2,1,0:T(8,128)} %weight_ref.1) | copy-start | bytes 3145732
  29.6 3.4 %collective-permute-start.1 = (bf16[32,256]{1,0:T(8,128)(2,1)S(1)}, bf16[32,256]{1,0:T(8,128)(2,1)S(1)}, u32[]{:S(2)}, u32[]{:S(2)}) collective-permute-start(bf16[32,256]{1,0:T(8,128)(2,1)S(1)} %get-tuple-element.36), channel_id=1, source_target_pairs={{0,2},{1,3},{2,0},{3,1},{4,6},{5,7},{6,4},{7,5},{8,10},{9,11},{10,... | collective-permute-start | bytes 49160 | tf_op jit(solution)/shard_map/ppermute | solution.py:529
  34.6 1.2 %collective-permute-start.2 = (bf16[64,256]{1,0:T(8,128)(2,1)S(1)}, bf16[64,256]{1,0:T(8,128)(2,1)S(1)}, u32[]{:S(2)}, u32[]{:S(2)}) collective-permute-start(bf16[64,256]{1,0:T(8,128)(2,1)S(1)} %get-tuple-element.40.refs_0_), channel_id=1, source_target_pairs={{0,2},{1,3},{2,0},{3,1},{4,6},{5,7},{6,4},{7,5},{8,10},{9,11},{10,... | collective-permute-start | bytes 98312 | tf_op jit(solution)/shard_map/ppermute | solution.py:529
  47.3 10.8 %all-to-all-start.3 = ((bf16[16,40,128]{2,1,0:T(8,128)(2,1)}), bf16[16,40,128]{2,1,0:T(8,128)(2,1)S(1)}, u32[]{:S(2)}, u32[]{:S(2)}) async-start(bf16[16,40,128]{2,1,0:T(8,128)(2,1)} %bitcast.13), calls=%async_computation.3 | async-start | bytes 327680 | tf_op jit(solution)/shard_map/all_to_all | solution.py:538
  58.3 3.3 %collective-permute-start.3 = (bf16[64,256]{1,0:T(8,128)(2,1)S(1)}, bf16[64,256]{1,0:T(8,128)(2,1)S(1)}, u32[]{:S(2)}, u32[]{:S(2)}) collective-permute-start(bf16[64,256]{1,0:T(8,128)(2,1)S(1)} %get-tuple-element.48), channel_id=1, source_target_pairs={{0,2},{1,3},{2,0},{3,1},{4,6},{5,7},{6,4},{7,5},{8,10},{9,11},{10,... | collective-permute-start | bytes 98312 | tf_op jit(solution)/shard_map/ppermute | solution.py:529

commit v5 on v4

--- a/solution.py
+++ b/solution.py
@@ -143,9 +143,6 @@
         quarter = self.wide // 4
         small = cosine_of(x * frequency + quarter * ((column & 1) - (row & 1)), self.wide)
         return self.expanded(small).astype(BF16)
-
-    def sum_owner(self, index, inner):
-        return ((index // self.narrow) * 2 + inner) * self.narrow + index % self.narrow
 
 
 def repeat_rows(out_ref, block):
@@ -189,8 +186,7 @@
     lines = jnp.concatenate(
         [turned[:, y * channels : (y + 1) * channels] for y in range(place.rows_y)], axis=0
     )
-    high, low = halves(jnp.concatenate([lines] * copies, axis=1))
-    return dot(y_forward, high) + dot(y_forward, low)
+    return dot(y_forward, jnp.concatenate([lines.astype(BF16)] * copies, axis=1))
 
 
 def spread_lines(place, modes, y_inverse):
@@ -204,14 +200,15 @@
     return jnp.concatenate(blocks, axis=0).astype(BF16)
 
 
-def turn_matrix(place):
+def turn_matrix(place, forward):
     channels, rows_y = place.channels, place.rows_y
-    return selector(
-        place.lanes,
-        place.lanes,
-        lambda row, column: (row % channels == column // rows_y)
-        & (row // channels == column % rows_y),
-    )
+
+    def same(row, column):
+        if forward:
+            row, column = column, row
+        return (row % channels == column // rows_y) & (row // channels == column % rows_y)
+
+    return selector(place.lanes, place.lanes, same)
 
 
 def side_by_side(values, count):
@@ -224,51 +221,51 @@
     return jnp.concatenate([values[:, y * width : (y + 1) * width] for y in range(count)], axis=0)
 
 
-def start_kernel(place, field_ref, field_out_ref, send_ref):
-    turned = dot(turn_matrix(place), field_ref[...]).astype(BF16)
-    field_out_ref[...] = side_by_side(turned, place.rows_y)
-    send_ref[...] = dot_nt(place.z_table(False), turned).astype(BF16)
-
-
-def prepare_kernel(
-    place, weight_ref, packed_ref, z_plain_ref, z_doubled_ref, turn_ref, forward_ref, inverse_ref
-):
+def start_kernel(place, field_ref, twin_ref, send_ref):
+    fields = jnp.concatenate([field_ref[...], twin_ref[...]], axis=0)
+    spectra = dot_nt(place.z_table(False), fields).astype(BF16)
+    values = one_below_other(spectra, 2)
+    values = dot(values, turn_matrix(place, True)).astype(BF16)
+    tables = jnp.concatenate(halves(place.forward_x()), axis=1)
+    send_ref[...] = dot(tables, jnp.concatenate([values, values], axis=0)).astype(BF16)
+
+
+def prepare_kernel(place, weight_ref, field_ref, mix_ref, mix_bias_ref, head_ref, *refs):
+    packed_ref, z_plain_ref, z_doubled_ref, turn_ref, forward_ref, inverse_ref = refs[:6]
+    field_out_ref, pointwise_ref, head_out_ref, held_ref, arrived = refs[6:]
     modes, kz, _, channels, _ = weight_ref.shape
+    copies = []
     for q in range(modes // 4):
-        parts = [weight_ref[4 * q + j // 2, :, j % 2] for j in range(8)]
+        part = pl.ds(4 * q, 4)
+        copies.append(
+            pltpu.make_async_copy(weight_ref.at[part], held_ref.at[part], arrived.at[q])
+        )
+        copies[-1].start()
+    z_plain_ref[...] = place.z_table(False)
+    z_doubled_ref[...] = place.z_table(True)
+    turn_ref[...] = turn_matrix(place, False)
+    forward_ref[...] = jnp.concatenate(halves(place.forward_x()), axis=1)
+    inverse_ref[...] = place.inverse_x()
+    field = side_by_side(dot(turn_ref[...], field_ref[...]).astype(BF16), place.rows_y)
+    field_out_ref[...] = field
+    pointwise_ref[...] = dot_tn(mix_ref[...], field) + mix_bias_ref[...]
+    head_out_ref[...] = jnp.transpose(head_ref[...].astype(F32)).astype(BF16)
+    for q in range(modes // 4):
+        copies[q].wait()
+        parts = [held_ref[4 * q + j // 2, :, j % 2] for j in range(8)]
         packed = jnp.concatenate(parts, axis=-1).reshape(kz * channels, 8 * channels)
         packed_ref[q] = packed.astype(BF16)
-    z_plain_ref[...] = place.z_table(False)
-    z_doubled_ref[...] = place.z_table(True)
-    turn_ref[...] = turn_matrix(place)
-    forward_ref[...] = jnp.concatenate(halves(place.forward_x()), axis=1)
-    inverse_ref[...] = place.inverse_x()
-
-
-def fold_kernel(place, *refs):
-    own_ref, got_ref = refs[:2]
-    height = 2 * MZ
-    values = jnp.concatenate([own_ref[:height], got_ref[:height]], axis=0)
-    if len(refs) > 3:
-        tables, refs = refs[2][...], refs[:2] + refs[3:]
+
+
+def fold_kernel(place, own_ref, got_ref, tables_ref, *refs):
+    values = jnp.concatenate([own_ref[...], got_ref[...]], axis=0)
+    values = jnp.concatenate([values, values], axis=0)
+    partial = dot(tables_ref[...], values).astype(BF16)
+    if place.fold:
+        shares_ref, send_ref = refs
+        write_pieces(place, send_ref, partial, shares_ref[...])
     else:
-        tables = jnp.concatenate(halves(place.forward_x()), axis=1)
-    partial = dot(tables, jnp.concatenate([values, values], axis=0)).astype(BF16)
-    if got_ref.shape[0] == height:
-        refs[2][...] = partial
-        return
-    sums_ref, send_ref = refs[2:]
-    got = got_ref[height:].astype(F32)
-    width = sums_ref.shape[1]
-    high, low = halves(sums_ref[...] + got[:, :width] + got[:, width:])
-    count = place.partners
-    place_of = selector(
-        8 * count,
-        4 * count,
-        lambda row, column: (row % 8 == column // count) & (row // 8 == column % count),
-    )
-    shares = dot(place_of, jnp.concatenate([high, low], axis=0)).astype(BF16)
-    write_pieces(place, send_ref, partial, shares)
+        refs[0][...] = partial
 
 
 def mode_kernel(
@@ -292,34 +289,34 @@
     repeat_rows(send_ref, spread_lines(place, mode, y_inverse_ref[...]))
 
 
-def part_kernel(place, *refs):
-    pieces, shares = read_pieces(place, refs[0])
-    lines = dot(refs[1][...], pieces)
+def part_kernel(place, pieces_ref, table_ref, *refs):
+    pieces, shares = read_pieces(place, pieces_ref)
+    lines = dot(table_ref[...], pieces)
     height = 2 * MZ
-    refs = refs[3:] if place.fold and shares is not None else refs[2:]
-    own_ref, send_ref = refs[:2]
-    own_ref[...] = lines[:height]
     if shares is None:
+        own_ref, send_ref = refs
+        own_ref[...] = lines[:height]
         send_ref[...] = lines[height:].astype(BF16)
         return
-    sums_ref = refs[2]
-    count = place.partners
+    _, own_ref, send_ref, sums_ref = refs
+    own_ref[...] = lines[:height]
+    send_ref[:height] = lines[height:].astype(BF16)
     got = jnp.concatenate(shares, axis=0).astype(BF16)
+    channels = place.channels
 
     def chosen(part):
         return dot(
             selector(
-                2 * count,
-                8 * count,
-                lambda row, column: (row // count + 2 * part == column % 8)
-                & (row % count == column // 8),
+                2 * channels,
+                got.shape[0],
+                lambda row, column: (column // 8 == (row % channels) // 2)
+                & (column % 8 == 4 * part + 2 * (row // channels) + row % 2),
             ),
             got,
         )
 
     high, low = chosen(0), chosen(1)
     sums_ref[...] = high + low
-    send_ref[:height] = lines[height:].astype(BF16)
     send_ref[height:] = jnp.concatenate([high, low], axis=1).astype(BF16)
 
 
@@ -335,27 +332,24 @@
 
 
 def cell_kernel(place, *refs):
-    own_ref, got_ref, z_table_ref, refs = refs[0], refs[1], refs[2], refs[3:]
-    field_ref, mix_ref, mix_bias_ref, head_ref, head_bias_ref = refs[:5]
-    out_row_ref, out_column_ref, cotangent_ref = refs[5:8]
-    prediction_ref, grad_pre_ref, send_ref = refs[8:11]
-    channels, hidden_units = head_ref.shape
+    own_ref, got_ref, z_table_ref, pointwise_ref, head_ref, head_turned_ref = refs[:6]
+    head_bias_ref, out_row_ref, out_column_ref, cotangent_ref = refs[6:10]
+    prediction_ref, grad_pre_ref, send_ref, hidden_ref, head_slope_ref = refs[10:]
     rows_y, z_count = place.rows_y, place.z_count
     z_table = z_table_ref[...]
     lines = (own_ref[...] + got_ref[...].astype(F32)).astype(BF16)
-    branch = side_by_side(dot_tn(lines, z_table), rows_y)
-    field, head = field_ref[...], head_ref[...]
-    head_turned = jnp.transpose(head.astype(F32)).astype(BF16)
-    pre_act = branch + dot_tn(mix_ref[...], field) + mix_bias_ref[...]
+    pre_act = side_by_side(dot_tn(lines, z_table), rows_y) + pointwise_ref[...]
+    head, head_turned = head_ref[...], head_turned_ref[...]
     head_bias, out_row, out_column = head_bias_ref[...], out_row_ref[...], out_column_ref[...]
     width = 2 * z_count
-    hidden, slopes, head_pre = [], [], []
+    slopes, head_pre = [], []
     for first in range(0, rows_y * z_count, width):
         value, slope = normal(pre_act[:, first : first + width])
-        hidden.append(value.astype(BF16))
+        hidden = value.astype(BF16)
+        hidden_ref[:, first : first + width] = hidden
         slopes.append(slope)
-        head_pre.append(dot(head_turned, hidden[-1]))
-    head_slopes, gradients = [], []
+        head_pre.append(dot(head_turned, hidden))
+    gradients = []
     for index, first in enumerate(range(0, rows_y, 2)):
         target = jnp.concatenate(
             [cotangent_ref[y : y + 1] for y in range(first, first + 2)], axis=1
@@ -365,35 +359,32 @@
         prediction_ref[first : first + 1] = predicted[:, :z_count]
         prediction_ref[first + 1 : first + 2] = predicted[:, z_count:]
         head_slope = (target * out_column * slope).astype(BF16)
+        head_slope_ref[:, first * z_count : first * z_count + width] = head_slope
         gradients.append((dot(head, head_slope) * slopes[index]).astype(BF16))
-        head_slopes.append(head_slope)
     gradient = jnp.concatenate(gradients, axis=1)
     grad_pre_ref[...] = gradient
-    height = 2 * MZ
-    send_ref[:height] = dot_nt(z_table, one_below_other(gradient, rows_y)).astype(BF16)
-    grad_mix = dot_nt(field, gradient)
-    grad_head = dot_nt(jnp.concatenate(hidden, axis=1), jnp.concatenate(head_slopes, axis=1))
+    send_ref[...] = dot_nt(z_table, one_below_other(gradient, rows_y)).astype(BF16)
+
+
+def sums_kernel(place, field_ref, gradient_ref, hidden_ref, head_slope_ref, *refs):
+    grad_mix = dot_nt(field_ref[...], gradient_ref[...])
+    grad_head = dot_nt(hidden_ref[...], head_slope_ref[...])
     if not place.fold:
-        refs[-2][...] = grad_mix
-        refs[-1][...] = grad_head
+        refs[0][...] = grad_mix
+        refs[1][...] = grad_head
         return
-    wide_mix = jnp.concatenate(
-        [grad_mix, jnp.zeros((channels, hidden_units - channels), F32)], axis=1
-    )
+    channels, hidden_units = grad_head.shape
+    rest = jnp.zeros((channels, hidden_units - channels), F32)
+    wide_mix = jnp.concatenate([grad_mix, rest], axis=1)
     high, low = halves(jnp.concatenate([grad_head, wide_mix], axis=0))
-    count = place.partners
-    _, inner = place.here()
-
-    def chosen(owner):
-        def condition(row, column):
-            target = place.sum_owner(row % count, owner)
-            return column == (row // count) * channels + target
-
-        picked = selector(2 * count, 2 * channels, condition)
-        return dot(picked, high), dot(picked, low)
-
-    refs[11][...] = sum(chosen(inner))
-    send_ref[height:] = jnp.concatenate(chosen(1 - inner), axis=1).astype(BF16)
+    split = jnp.concatenate([high, low], axis=0)
+    place_of = selector(
+        8 * place.partners,
+        4 * channels,
+        lambda row, column: (column % channels == 2 * (row // 8) + row % 2)
+        & (column // channels == (row % 8) // 2),
+    )
+    refs[0][...] = dot(place_of, split).astype(BF16)
 
 
 def back_kernel(
@@ -427,9 +418,8 @@
         repeat_rows(send_ref, block)
         return
     total = sum(shares[1:], shares[0])
-    high, low = halves(total[0:2] + total[2:4])
-    rest = jnp.zeros((4, total.shape[1]), F32)
-    split = jnp.concatenate([high.astype(F32), low.astype(F32), rest], axis=0)
+    high, low = halves(total[0:4] + total[4:8])
+    split = jnp.concatenate([high.astype(F32), low.astype(F32)], axis=0)
     write_pieces(place, send_ref, block, split.astype(BF16))
 
 
@@ -446,49 +436,44 @@
             out_ref[j, k, 1] = s_real * a_imag - s_imag * a_real
 
 
+def pointwise_kernel(place, mix_ref, gradient_ref, out_ref):
+    z_count = place.z_count
+    product = dot(mix_ref[...], gradient_ref[...])
+    for y in range(place.rows_y):
+        out_ref[:, y, :] = product[:, y * z_count : (y + 1) * z_count]
+
+
 def finish_kernel(place, *refs):
-    own_ref, got_ref, z_table_ref, turn_ref, grad_pre_ref, mix_ref = refs[:6]
+    own_ref, got_ref, z_table_ref, turn_ref, pointwise_ref, prediction_ref = refs[:6]
     refs = refs[6:]
     height = 2 * MZ
-    channels, rows_y = place.channels, place.rows_y
+    channels = place.channels
     lines = (own_ref[...] + got_ref[:height].astype(F32)).astype(BF16)
-    branch = dot_tn(lines, z_table_ref[...])
-    pointwise = one_below_other(dot(mix_ref[...], grad_pre_ref[...]), rows_y)
-    grad_field = dot_tn(turn_ref[...], (branch + pointwise).astype(BF16)).astype(BF16)
+    lines = dot(lines, turn_ref[...]).astype(BF16)
+    pointwise = pointwise_ref[...].reshape(place.lanes, place.z_count)
+    grad_field = (dot_tn(lines, z_table_ref[...]) + pointwise).astype(BF16)
     if not place.fold:
         refs[0][...] = grad_field
+        refs[1][...] = prediction_ref[...]
         return
-    sums_ref, grad_field_ref, grad_mix_ref, grad_head_ref = refs
+    sums_ref, grad_field_ref, out_ref, grad_mix_ref, grad_head_ref = refs
     grad_field_ref[...] = grad_field
-    _, inner = place.here()
-    count = place.partners
+    out_ref[...] = prediction_ref[...]
+    got = got_ref[height:].astype(F32)
     width = sums_ref.shape[1]
-    own_high, own_low = halves(sums_ref[...])
-    got = got_ref[height:]
-
-    def picked(kind):
-        def choose(owner):
-            def condition(row, column):
-                target = place.sum_owner(column % count, owner)
-                return (column // count == kind) & (target == row)
-
-            return selector(channels, 2 * count, condition)
-
-        own, twin = choose(inner), choose(1 - inner)
-        both = dot(twin, got)
-        return dot(own, own_high) + dot(own, own_low) + both[:, :width] + both[:, width:]
-
-    grad_head_ref[...] = picked(0)
-    grad_mix_ref[...] = picked(1)[:, :channels]
-
-
-def call(kernel, outs, name):
+    total = sums_ref[...] + got[:, :width] + got[:, width:]
+    grad_head_ref[...] = total[:channels]
+    grad_mix_ref[...] = total[channels:, :channels]
+
+
+def call(kernel, outs, name, **spec):
     return pl.pallas_call(
         kernel,
         out_shape=[jax.ShapeDtypeStruct(shape, dtype) for shape, dtype in outs],
         compiler_params=pltpu.CompilerParams(vmem_limit_bytes=VMEM_LIMIT),
         cost_estimate=pl.CostEstimate(flops=1 << 22, bytes_accessed=1 << 19, transcendentals=0),
         name=name,
+        **spec,
     )
 
 
@@ -510,7 +495,7 @@
     hidden_units = head_weight.shape[1]
     cells = channels * rows_y
     place = Place(wide, narrow, kz, modes, rows_y, channels, z_count, False)
-    place.fold = devices == channels and hidden_units == 128 and place.lanes == 256 and kz % 8 == 0
+    place.fold = 2 * place.partners == channels and hidden_units == 128 and cells == 256 and kz % 8 == 0
     height = 2 * MZ
     step = 2 * kz
     partners = place.partners
@@ -543,18 +528,19 @@
     plain = ((partners * step, cells), BF16)
     shared = ((partners * (2 * step + 8), cells // 2), BF16) if place.fold else plain
     twin_plain = ((height, cells), BF16)
-    twin_shared = ((2 * height, cells), BF16) if place.fold else twin_plain
-    sums_shape = ((2 * partners, hidden_units), F32)
+    twin_shared = ((height + 2 * channels, cells), BF16) if place.fold else twin_plain
+    sums_shape = ((2 * channels, hidden_units), F32)
     own_lines = ((height, cells), F32)
-
-    field, send = call(
-        functools.partial(start_kernel, place),
-        [((channels, rows_y * z_count), BF16), twin_plain],
-        "start",
-    )(lifted_field.reshape(cells, z_count))
-    some = max(1, modes // 4)
-    weight, z_plain, z_doubled, turn, forward, inverse = call(
-        functools.partial(prepare_kernel, place),
+    across = (channels, rows_y * z_count)
+
+    def run(kernel, outs, name, **spec):
+        return call(functools.partial(kernel, place), outs, name, **spec)
+
+    flat_field = lifted_field.reshape(cells, z_count)
+    (send,) = run(start_kernel, [plain], "start")(flat_field, to_twin(flat_field))
+    vmem = pl.BlockSpec(memory_space=pltpu.VMEM)
+    weight, z_plain, z_doubled, turn, forward, inverse, field, pointwise, head_turned = run(
+        prepare_kernel,
         [
             ((modes // 4, kz * channels, 8 * channels), BF16),
             ((height, z_count), BF16),
@@ -562,47 +548,56 @@
             ((cells, cells), BF16),
             ((wide // 2 * height, 4 * height), BF16),
             ((2 * height, wide // 2 * height), BF16),
+            (across, BF16),
+            (across, F32),
+            ((hidden_units, channels), BF16),
         ],
         "prepare",
-    )(spectral_weight)
-    (send,) = call(functools.partial(fold_kernel, place), [plain], "fold")(send, to_twin(send))
-    spectrum, send = call(
-        functools.partial(mode_kernel, place),
-        [((mode_lines, channels), F32), plain],
-        "mode",
-    )(exchange(send), y_forward, y_inverse, weight)
-    own, send = call(functools.partial(part_kernel, place), [own_lines, twin_plain], "part")(
-        exchange(send), inverse
-    )
-    outs = [((rows_y, z_count), F32), ((channels, rows_y * z_count), BF16), twin_shared]
-    if place.fold:
-        outs += [sums_shape]
-    else:
-        outs += [((channels, channels), F32), ((channels, hidden_units), F32)]
-    prediction, grad_pre, send, *sums = call(functools.partial(cell_kernel, place), outs, "cell")(
+        in_specs=[pl.BlockSpec(memory_space=pltpu.HBM)] + [vmem] * 4,
+        scratch_shapes=[
+            pltpu.VMEM(spectral_weight.shape, F32),
+            pltpu.SemaphoreType.DMA((modes // 4,)),
+        ],
+    )(spectral_weight, flat_field, mix_weight, mix_bias[:, None], head_weight)
+    spectrum, send = run(mode_kernel, [((mode_lines, channels), F32), plain], "mode")(
+        exchange(send), y_forward, y_inverse, weight
+    )
+    own, send = run(part_kernel, [own_lines, twin_plain], "part")(exchange(send), inverse)
+    prediction, grad_pre, send, hidden, head_slope = run(
+        cell_kernel,
+        [
+            ((rows_y, z_count), F32),
+            (across, BF16),
+            twin_plain,
+            (across, BF16),
+            ((hidden_units, rows_y * z_count), BF16),
+        ],
+        "cell",
+    )(
         own,
         to_twin(send),
         z_doubled,
-        field,
-        mix_weight,
-        mix_bias[:, None],
+        pointwise,
         head_weight,
+        head_turned,
         head_bias[:, None],
         out_weight[None],
         out_weight.astype(F32)[:, None],
         cotangent[0],
     )
+    if place.fold:
+        outs = [((8 * partners, hidden_units), BF16)]
+    else:
+        outs = [((channels, channels), F32), ((channels, hidden_units), F32)]
+    sums = run(sums_kernel, outs, "sums")(field, grad_pre, hidden, head_slope)
     if not place.fold:
         totals = lax.psum(tuple(sums), ("wide", "narrow"))
         sums = []
-    (send,) = call(functools.partial(fold_kernel, place), [shared], "fold")(
-        send, to_twin(send), forward, *sums
-    )
-    adjoint, send = call(
-        functools.partial(back_kernel, place),
-        [((mode_lines, channels), F32), shared],
-        "back",
-    )(exchange(send), y_forward, y_inverse, weight)
+    (send,) = run(fold_kernel, [shared], "fold")(send, to_twin(send), forward, *sums)
+    adjoint, send = run(back_kernel, [((mode_lines, channels), F32), shared], "back")(
+        exchange(send), y_forward, y_inverse, weight
+    )
+    some = max(1, modes // 4)
     grad_spectral, done = pl.pallas_call(
         outer_kernel,
         grid=(modes // some,),
@@ -619,15 +614,17 @@
         cost_estimate=pl.CostEstimate(flops=1 << 22, bytes_accessed=5 << 20, transcendentals=0),
         name="outer",
     )(spectrum.reshape(modes, 2 * kz, channels), adjoint.reshape(modes, 2 * kz, channels))
-    pieces = exchange(send)
+    (pointwise,) = run(pointwise_kernel, [((channels, rows_y, z_count), F32)], "pointwise")(
+        mix_weight, grad_pre
+    )
     outs = [own_lines, twin_shared] + ([sums_shape] if place.fold else [])
-    operands = (pieces, inverse, done) if place.fold else (pieces, inverse)
-    own, send, *sums = call(functools.partial(part_kernel, place), outs, "part")(*operands)
-    outs = [((cells, z_count), BF16)]
+    after = (done,) if place.fold else ()
+    own, send, *sums = run(part_kernel, outs, "part")(exchange(send), inverse, *after)
+    outs = [((cells, z_count), BF16), ((rows_y, z_count), F32)]
     if place.fold:
         outs += [((channels, channels), F32), ((channels, hidden_units), F32)]
-    grad_field, *summed = call(functools.partial(finish_kernel, place), outs, "finish")(
-        own, to_twin(send), z_plain, turn, grad_pre, mix_weight, *sums
+    grad_field, prediction, *summed = run(finish_kernel, outs, "finish")(
+        own, to_twin(send), z_plain, turn, pointwise, prediction, *sums
     )
     grad_mix, grad_head = summed if place.fold else totals
     return (

time: 63.3 us -> 65.7 us (1.038)
  waiting for transfers between devices: 10.3 us -> 6.42 us
  local copies, waits for them, and re-layouts: 3.41 us -> 6.25 us
  blocking collectives: 19.6 us -> 22.4 us
    all_to_all x2, waiting for transfers between devices: 6.93 us -> 3.28 us  [exchange(): lax.all_to_all(pieces, ('wide', 'narrow'), 0, 0, axis_index_groups=groups...]
    all_to_all x2, blocking collectives: 19.6 us -> 22.4 us  [exchange(): lax.all_to_all(pieces, ('wide', 'narrow'), 0, 0, axis_index_groups=groups...]
    unnamed x20 -> x24, local copies, waits for them, and re-layouts: 3.09 us -> 5.29 us
    pallas_call x10 -> x11, Pallas kernels: 7.88 us -> 8.48 us  [the longest x1 1.67 us: body(): run(back_kernel, [((mode_lines, channels), F32), shared], 'back')]
  transfers between devices with their start and end apart: 6 -> 6, of which waited for: 6 -> 6; matrix products, arithmetic and copies ran while one was open for 1% -> 1% of each run, Pallas kernels for 7% -> 9%
where the time goes in v5:
time: 65.7 us; the launch traced here: 64.9 us
  blocking collectives  22.4 us (34%)
  starting transfers between devices  17 us (26%)
  Pallas kernels  12 us (18%)
  waiting for transfers between devices  6.42 us (10%)
  local copies, waits for them, and re-layouts  6.25 us (10%)
  between operations  0.73 us (1%)
    all_to_all x2, blocking collectives, exchange(): lax.all_to_all(pieces, ('wide', 'narrow'), 0, 0, axis_index_groups=groups...  22.4 us
    all_to_all x2, starting transfers between devices, exchange(): lax.all_to_all(pieces, ('wide', 'narrow'), 0, 0, axis_index_groups=groups...  11.7 us
    ppermute x4, starting transfers between devices, to_twin(): return lax.ppermute(send, ('wide', 'narrow'), pairs)  5.33 us
    unnamed x24, local copies, waits for them, and re-layouts  5.29 us
    pallas_call x1, Pallas kernels, body(): pl.pallas_call(outer_kernel, grid=(modes // some,), in_specs=[pl.BlockSpe...  3.55 us
    all_to_all x2, waiting for transfers between devices, exchange(): lax.all_to_all(pieces, ('wide', 'narrow'), 0, 0, axis_index_groups=groups...  3.28 us
    ppermute x4, waiting for transfers between devices, to_twin(): return lax.ppermute(send, ('wide', 'narrow'), pairs)  3.15 us
    pallas_call x1, Pallas kernels, body(): run(back_kernel, [((mode_lines, channels), F32), shared], 'back')  1.67 us
  transfers between devices with their start and end apart: 6, of which 6 were waited for; matrix products, arithmetic and copies ran while one was open for 1% of the time, Pallas kernels for 9%

profile of v5, /device:TPU:1, one launch (start us, length us, event | category | flops | bytes accessed | tf_op | source)
XLA Modules:
  0.0 64.9 jit_solution(14004404738334205776)
XLA Ops:
  0.6 0.0 copy-start.1
  0.6 0.0 copy-start.2
  0.7 0.1 collective-permute-start
  0.8 1.4 %collective-permute-done.twin_ref = bf16[256,128]{1,0:T(8,128)(2,1)S(1)} collective-permute-done((bf16[256,128]{1,0:T(8,128)(2,1)}, bf16[256,128]{1,0:T(8,128)(2,1)S(1)}, u32[]{:S(2)}, u32[]{:S(2)}) %collective-permute-start) | collective-permute-done | bytes 65568 | tf_op jit(solution)/shard_map/ppermute | solution.py:514
  2.2 0.0 copy-start.3
  2.2 0.8 %copy-done.3 = bf16[1,32,8,128]{3,2,1,0:T(8,128)(2,1)S(1)} copy-done((bf16[1,32,8,128]{3,2,1,0:T(8,128)(2,1)S(1)}, bf16[1,32,8,128]{3,2,1,0:T(8,128)(2,1)}, u32[]{:S(2)}) %copy-start.3) | copy-done | bytes 65560
  3.0 0.0 copy-start.10
  3.0 0.0 copy-start.11
  3.0 0.0 copy-start.6
  3.0 0.0 copy-start.9
  3.0 1.2 %start.1 = bf16[256,256]{1,0:T(8,128)(2,1)} custom-call(bf16[256,128]{1,0:T(8,128)(2,1)S(1)} %bitcast.26, bf16[256,128]{1,0:T(8,128)(2,1)S(1)} %collective-permute-done.twin_ref), custom_call_target="tpu_custom_call" | custom-call | flops 4194304 | bytes 524288 | tf_op jit(solution)/shard_map/start/pallas_call | solution.py:540
  4.2 7.7 %all-to-all-start = ((bf16[16,16,256]{2,1,0:T(8,128)(2,1)}), bf16[16,16,256]{2,1,0:T(8,128)(2,1)S(1)}, u32[]{:S(2)}, u32[]{:S(2)}) async-start(bf16[16,16,256]{2,1,0:T(8,128)(2,1)} %bitcast.1), calls=%async_computation | async-start | bytes 262144 | tf_op jit(solution)/shard_map/all_to_all | solution.py:523
  12.0 0.7 %copy.15.mix_bias_ref = f32[32,1]{1,0:T(8,128)S(1)} copy(f32[32,1]{0,1:T(1,128)} %bitcast.34) | data formatting | bytes 256 | tf_op jit(solution)/shard_map/broadcast_in_dim | solution.py:561
  12.7 0.0 copy-start
  12.7 2.2 %copy-done = f32[16,8,2,32,32]{4,3,2,1,0:T(8,128)S(1)} copy-done((f32[16,8,2,32,32]{4,3,2,1,0:T(8,128)S(1)}, f32[16,8,2,32,32]{4,3,2,1,0:T(8,128)}, u32[]{:S(2)}) %copy-start) | copy-done | bytes 1048600
  14.9 0.0 copy-start.4
  14.9 0.8 %copy-done.4 = bf16[1,32,8,128]{3,2,1,0:T(8,128)(2,1)S(1)} copy-done((bf16[1,32,8,128]{3,2,1,0:T(8,128)(2,1)S(1)}, bf16[1,32,8,128]{3,2,1,0:T(8,128)(2,1)}, u32[]{:S(2)}) %copy-start.4) | copy-done | bytes 65560
  15.8 0.0 copy-start.5
  15.8 0.7 %copy-done.5 = bf16[32,128]{1,0:T(8,128)(2,1)S(1)} copy-done((bf16[32,128]{1,0:T(8,128)(2,1)S(1)}, bf16[32,128]{1,0:T(8,128)(2,1)}, u32[]{:S(2)}) %copy-start.5) | copy-done | bytes 8216
  16.5 0.0 copy-start.7
  16.5 0.7 %copy-done.7 = bf16[32,32]{1,0:T(8,128)(2,1)S(1)} copy-done((bf16[32,32]{1,0:T(8,128)(2,1)S(1)}, bf16[32,32]{1,0:T(8,128)(2,1)}, u32[]{:S(2)}) %copy-start.7) | copy-done | bytes 2072
  17.2 0.0 copy-start.8
  17.2 1.4 %prepare.1 = (bf16[4,256,256]{2,1,0:T(8,128)(2,1)S(1)}, bf16[32,128]{1,0:T(8,128)(2,1)S(1)}, bf16[32,128]{1,0:T(8,128)(2,1)S(1)}, bf16[256,256]{1,0:T(8,128)(2,1...) custom-call(f32[16,8,2,32,32]{4,3,2,1,0:T(8,128)S(1)} %copy-done, ...), custom_call_target="tpu_custom_call" | custom-call | flops 4194304 | bytes 524288 | tf_op jit(solution)/shard_map/prepare/pallas_call | solution.py:542
  18.6 0.1 all-to-all-done
  18.6 0.0 copy-done.1
  18.6 0.0 copy-done.2
  18.6 0.9 %mode.1 = (f32[256,32]{1,0:T(8,128)S(1)}, bf16[256,256]{1,0:T(8,128)(2,1)S(1)}) custom-call(bf16[256,256]{1,0:T(8,128)(2,1)S(1)} %bitcast.23, bf16[256,256]{1,0:T(8,128)(2,1)S(1)} %copy-done.1, bf16[256,256]{1,0:T(8,128)(2,1)S(1)} %copy-done.2, bf16[4,256,256]{2,1,0:T(8,128)(2,1)S(1)} %get-tuple-element.34.weight_ref), custom_call_target="tpu_custom_call" | custom-call | flops 4194304 | bytes 524288 | tf_op jit(solution)/shard_map/mode/pallas_call | solution.py:562
  19.6 12.8 %all_to_all.20 = bf16[16,16,256]{2,1,0:T(8,128)(2,1)S(1)} all-to-all(bf16[16,16,256]{2,1,0:T(8,128)(2,1)S(1)} %bitcast.30), channel_id=1, replica_groups={{0,1,4,5,8,9,12,13,16,17,20,21,24,25,28,29},{2,3,6,7,10,11,14,15,18,19,..., dimensions={0} | all-to-all | bytes 262144 | tf_op jit(solution)/shard_map/all_to_all | solution.py:523
  32.3 0.1 part.2
  32.5 2.4 %collective-permute-start.1 = (bf16[32,256]{1,0:T(8,128)(2,1)S(1)}, bf16[32,256]{1,0:T(8,128)(2,1)S(1)}, u32[]{:S(2)}, u32[]{:S(2)}) collective-permute-start(bf16[32,256]{1,0:T(8,128)(2,1)S(1)} %get-tuple-element.38), channel_id=1, source_target_pairs={{0,2},{1,3},{2,0},{3,1},{4,6},{5,7},{6,4},{7,5},{8,10},{9,11},{10,... | collective-permute-start | bytes 49160 | tf_op jit(solution)/shard_map/ppermute | solution.py:514
  34.8 0.0 copy-done.10
  34.8 0.0 copy-done.11
  34.8 0.1 copy.16.refs_6_
  34.9 0.1 copy.17.refs_8_
  35.0 0.6 collective-permute-done.1.refs_1_
  35.7 0.0 copy-done.6
  35.7 0.0 copy-done.9
  35.7 1.2 %cell.1 = (f32[8,128]{1,0:T(8,128)S(1)}, bf16[32,1024]{1,0:T(8,128)(2,1)S(1)}, bf16[32,256]{1,0:T(8,128)(2,1)S(1)}, bf16[32,1024]{1,0:T(8,128)(2,1)S(1)}, bf16[128,1024]{1,0:T(8,128)(2,1)S(1)}) custom-call(f32[32,256]{1,0:T(8,128)S(1)} %get-tuple-element.37.refs_0_, bf16[32,256]{1,0:T(8,128)(2,1)S(1)} %collective-permute-done.1.refs_1_, ...), custom_call_target="tpu_custom_call" | custom-call | flops 4194304 | bytes 524288 | tf_op jit(solution)/shard_map/cell/pallas_call | solution.py:566
  36.9 0.4 collective-permute-start.2
  37.3 0.4 sums.1.refs_0_
  37.7 0.5 collective-permute-done.2.got_ref
  38.1 0.2 fold.1
  38.3 9.6 %all_to_all.21 = bf16[16,40,128]{2,1,0:T(8,128)(2,1)S(1)} all-to-all(bf16[16,40,128]{2,1,0:T(8,128)(2,1)S(1)} %bitcast.21), channel_id=1, replica_groups={{0,1,4,5,8,9,12,13,16,17,20,21,24,25,28,29},{2,3,6,7,10,11,14,15,18,19,..., dimensions={0} | all-to-all | bytes 327680 | tf_op jit(solution)/shard_map/all_to_all | solution.py:523
  47.9 1.7 %back.1 = (f32[256,32]{1,0:T(8,128)S(1)}, bf16[640,128]{1,0:T(8,128)(2,1)}) custom-call(bf16[640,128]{1,0:T(8,128)(2,1)S(1)} %bitcast.22, bf16[256,256]{1,0:T(8,128)(2,1)S(1)} %copy-done.1, bf16[256,256]{1,0:T(8,128)(2,1)S(1)} %copy-done.2, bf16[4,256,256]{2,1,0:T(8,128)(2,1)S(1)} %get-tuple-element.34.weight_ref), custom_call_target="tpu_custom_call" | custom-call | flops 4194304 | bytes 524288 | tf_op jit(solution)/shard_map/back/pallas_call | solution.py:597
  49.6 4.0 %all-to-all-start.3 = ((bf16[16,40,128]{2,1,0:T(8,128)(2,1)}), bf16[16,40,128]{2,1,0:T(8,128)(2,1)S(1)}, u32[]{:S(2)}, u32[]{:S(2)}) async-start(bf16[16,40,128]{2,1,0:T(8,128)(2,1)} %bitcast.12), calls=%async_computation.3 | async-start | bytes 327680 | tf_op jit(solution)/shard_map/all_to_all | solution.py:523
  53.6 3.6 %outer.1 = (f32[16,8,2,32,32]{4,3,2,1,0:T(8,128)}, f32[8,128]{1,0:T(8,128)S(1)}) custom-call(f32[16,16,32]{2,1,0:T(8,128)S(1)} %bitcast.28, f32[16,16,32]{2,1,0:T(8,128)S(1)} %bitcast.29), custom_call_target="tpu_custom_call" | custom-call | flops 4194304 | bytes 5242880 | tf_op jit(solution)/shard_map/outer/pallas_call | solution.py:601
  57.1 3.2 %all-to-all-done.3 = bf16[16,40,128]{2,1,0:T(8,128)(2,1)S(1)} async-done(((bf16[16,40,128]{2,1,0:T(8,128)(2,1)}), bf16[16,40,128]{2,1,0:T(8,128)(2,1)S(1)}, u32[]{:S(2)}, u32[]{:S(2)}) %all-to-all-start.3) | async-done | bytes 163872 | tf_op jit(solution)/shard_map/all_to_all | solution.py:523
  60.3 0.2 part.3
  60.5 2.5 %collective-permute-start.3 = (bf16[96,256]{1,0:T(8,128)(2,1)S(1)}, bf16[96,256]{1,0:T(8,128)(2,1)S(1)}, u32[]{:S(2)}, u32[]{:S(2)}) collective-permute-start(bf16[96,256]{1,0:T(8,128)(2,1)S(1)} %get-tuple-element.53), channel_id=1, source_target_pairs={{0,2},{1,3},{2,0},{3,1},{4,6},{5,7},{6,4},{7,5},{8,10},{9,11},{10,... | collective-permute-start | bytes 147464 | tf_op jit(solution)/shard_map/ppermute | solution.py:514
  63.0 0.0 copy-done.8
  63.0 0.2 pointwise.1.refs_4_
  63.2 0.7 %collective-permute-done.3.refs_1_ = bf16[96,256]{1,0:T(8,128)(2,1)S(1)} collective-permute-done((bf16[96,256]{1,0:T(8,128)(2,1)S(1)}, bf16[96,256]{1,0:T(8,128)(2,1)S(1)}, u32[]{:S(2)}, u32[]{:S(2)}) %collective-permute-start.3) | collective-permute-done | bytes 49184 | tf_op jit(solution)/shard_map/ppermute | solution.py:514
  63.9 1.0 %finish.1 = (bf16[256,128]{1,0:T(8,128)(2,1)}, f32[8,128]{1,0:T(8,128)}, f32[32,32]{1,0:T(8,128)}, f32[32,128]{1,0:T(8,128)}) custom-call(f32[32,256]{1,0:T(8,128)S(1)} %get-tuple-element.52.refs_0_, bf16[96,256]{1,0:T(8,128)(2,1)S(1)} %collective-permute-done.3.refs_1_, bf16[32,128]{1,0:T(8,128)(2,1)S(1)} %get-tuple-element.54.refs_2_, ...), custom_call_target="tpu_custom_call" | custom-call | flops 4194304 | bytes 524288 | tf_op jit(solution)/shard_map/finish/pallas_call | solution.py:626
  (1 shorter events, 0.0 us)
Async XLA Ops:
  0.6 18.0 %copy-start.1 = (bf16[256,256]{1,0:T(8,128)(2,1)S(1)}, bf16[256,256]{1,0:T(8,128)(2,1)}, u32[]{:S(2)}) copy-start(bf16[256,256]{1,0:T(8,128)(2,1)} %constant.4.clone.y_forward_ref) | copy-start | bytes 393220
  0.6 18.0 %copy-start.2 = (bf16[256,256]{1,0:T(8,128)(2,1)S(1)}, bf16[256,256]{1,0:T(8,128)(2,1)}, u32[]{:S(2)}) copy-start(bf16[256,256]{1,0:T(8,128)(2,1)} %constant.5.clone.y_inverse_ref) | copy-start | bytes 393220
  0.7 1.5 %collective-permute-start = (bf16[256,128]{1,0:T(8,128)(2,1)}, bf16[256,128]{1,0:T(8,128)(2,1)S(1)}, u32[]{:S(2)}, u32[]{:S(2)}) collective-permute-start(bf16[256,128]{1,0:T(8,128)(2,1)} %bitcast.25), channel_id=1, source_target_pairs={{0,2},{1,3},{2,0},{3,1},{4,6},{5,7},{6,4},{7,5},{8,10},{9,11},{10,... | collective-permute-start | bytes 196616 | tf_op jit(solution)/shard_map/ppermute | solution.py:514
  2.2 0.8 %copy-start.3 = (bf16[1,32,8,128]{3,2,1,0:T(8,128)(2,1)S(1)}, bf16[1,32,8,128]{3,2,1,0:T(8,128)(2,1)}, u32[]{:S(2)}) copy-start(bf16[1,32,8,128]{3,2,1,0:T(8,128)(2,1)} %param.10) | copy-start | bytes 196612
  3.0 31.8 %copy-start.10 = (bf16[128]{0:T(256)(128)(2,1)S(1)}, bf16[128]{0:T(256)(128)(2,1)}, u32[]{:S(2)}) copy-start(bf16[128]{0:T(256)(128)(2,1)} %param.16) | copy-start | bytes 772
  3.0 31.8 %copy-start.11 = (f32[128]{0:T(128)S(1)}, f32[128]{0:T(128)}, u32[]{:S(2)}) copy-start(f32[128]{0:T(128)} %param.15) | copy-start | bytes 1540
  3.0 32.6 %copy-start.6 = (bf16[32,128]{1,0:T(8,128)(2,1)S(1)}, bf16[32,128]{1,0:T(8,128)(2,1)}, u32[]{:S(2)}) copy-start(bf16[32,128]{1,0:T(8,128)(2,1)} %refs_4_.1) | copy-start | bytes 24580
  3.0 32.6 %copy-start.9 = (f32[1,8,128]{2,1,0:T(8,128)S(1)}, f32[1,8,128]{2,1,0:T(8,128)}, u32[]{:S(2)}) copy-start(f32[1,8,128]{2,1,0:T(8,128)} %param.17) | copy-start | bytes 12292
  4.2 14.4 %all-to-all-start = ((bf16[16,16,256]{2,1,0:T(8,128)(2,1)}), bf16[16,16,256]{2,1,0:T(8,128)(2,1)S(1)}, u32[]{:S(2)}, u32[]{:S(2)}) async-start(bf16[16,16,256]{2,1,0:T(8,128)(2,1)} %bitcast.1), calls=%async_computation | async-start | bytes 262144 | tf_op jit(solution)/shard_map/all_to_all | solution.py:523
  12.7 2.2 %copy-start = (f32[16,8,2,32,32]{4,3,2,1,0:T(8,128)S(1)}, f32[16,8,2,32,32]{4,3,2,1,0:T(8,128)}, u32[]{:S(2)}) copy-start(f32[16,8,2,32,32]{4,3,2,1,0:T(8,128)} %weight_ref.1) | copy-start | bytes 3145732
  14.9 0.8 %copy-start.4 = (bf16[1,32,8,128]{3,2,1,0:T(8,128)(2,1)S(1)}, bf16[1,32,8,128]{3,2,1,0:T(8,128)(2,1)}, u32[]{:S(2)}) copy-start(bf16[1,32,8,128]{3,2,1,0:T(8,128)(2,1)} %param.10) | copy-start | bytes 196612
  15.8 0.7 %copy-start.5 = (bf16[32,128]{1,0:T(8,128)(2,1)S(1)}, bf16[32,128]{1,0:T(8,128)(2,1)}, u32[]{:S(2)}) copy-start(bf16[32,128]{1,0:T(8,128)(2,1)} %refs_4_.1) | copy-start | bytes 24580
  16.5 0.7 %copy-start.7 = (bf16[32,32]{1,0:T(8,128)(2,1)S(1)}, bf16[32,32]{1,0:T(8,128)(2,1)}, u32[]{:S(2)}) copy-start(bf16[32,32]{1,0:T(8,128)(2,1)} %mix_ref.3) | copy-start | bytes 6148
  17.2 45.8 %copy-start.8 = (bf16[32,32]{1,0:T(8,128)(2,1)S(1)}, bf16[32,32]{1,0:T(8,128)(2,1)}, u32[]{:S(2)}) copy-start(bf16[32,32]{1,0:T(8,128)(2,1)} %mix_ref.3) | copy-start | bytes 6148
  32.5 3.2 %collective-permute-start.1 = (bf16[32,256]{1,0:T(8,128)(2,1)S(1)}, bf16[32,256]{1,0:T(8,128)(2,1)S(1)}, u32[]{:S(2)}, u32[]{:S(2)}) collective-permute-start(bf16[32,256]{1,0:T(8,128)(2,1)S(1)} %get-tuple-element.38), channel_id=1, source_target_pairs={{0,2},{1,3},{2,0},{3,1},{4,6},{5,7},{6,4},{7,5},{8,10},{9,11},{10,... | collective-permute-start | bytes 49160 | tf_op jit(solution)/shard_map/ppermute | solution.py:514
  36.9 1.2 %collective-permute-start.2 = (bf16[32,256]{1,0:T(8,128)(2,1)S(1)}, bf16[32,256]{1,0:T(8,128)(2,1)S(1)}, u32[]{:S(2)}, u32[]{:S(2)}) collective-permute-start(bf16[32,256]{1,0:T(8,128)(2,1)S(1)} %get-tuple-element.42.own_ref), channel_id=1, source_target_pairs={{0,2},{1,3},{2,0},{3,1},{4,6},{5,7},{6,4},{7,5},{8,10},{9,11},{10,... | collective-permute-start | bytes 49160 | tf_op jit(solution)/shard_map/ppermute | solution.py:514
  49.6 10.7 %all-to-all-start.3 = ((bf16[16,40,128]{2,1,0:T(8,128)(2,1)}), bf16[16,40,128]{2,1,0:T(8,128)(2,1)S(1)}, u32[]{:S(2)}, u32[]{:S(2)}) async-start(bf16[16,40,128]{2,1,0:T(8,128)(2,1)} %bitcast.12), calls=%async_computation.3 | async-start | bytes 327680 | tf_op jit(solution)/shard_map/all_to_all | solution.py:523
  60.5 3.4 %collective-permute-start.3 = (bf16[96,256]{1,0:T(8,128)(2,1)S(1)}, bf16[96,256]{1,0:T(8,128)(2,1)S(1)}, u32[]{:S(2)}, u32[]{:S(2)}) collective-permute-start(bf16[96,256]{1,0:T(8,128)(2,1)S(1)} %get-tuple-element.53), channel_id=1, source_target_pairs={{0,2},{1,3},{2,0},{3,1},{4,6},{5,7},{6,4},{7,5},{8,10},{9,11},{10,... | collective-permute-start | bytes 147464 | tf_op jit(solution)/shard_map/ppermute | solution.py:514

commit v6 on v5

--- a/solution.py
+++ b/solution.py
@@ -221,40 +221,33 @@
     return jnp.concatenate([values[:, y * width : (y + 1) * width] for y in range(count)], axis=0)
 
 
-def start_kernel(place, field_ref, twin_ref, send_ref):
-    fields = jnp.concatenate([field_ref[...], twin_ref[...]], axis=0)
-    spectra = dot_nt(place.z_table(False), fields).astype(BF16)
-    values = one_below_other(spectra, 2)
-    values = dot(values, turn_matrix(place, True)).astype(BF16)
+def own_kernel(place, field_ref, field_out_ref, spectra_ref):
+    turned = dot(turn_matrix(place, False), field_ref[...]).astype(BF16)
+    field_out_ref[...] = side_by_side(turned, place.rows_y)
+    spectra_ref[...] = dot_nt(place.z_table(False), turned).astype(BF16)
+
+
+def start_kernel(place, spectra_ref, twin_ref, send_ref):
+    twin = dot_nt(place.z_table(False), twin_ref[...]).astype(BF16)
+    twin = dot(twin, turn_matrix(place, True)).astype(BF16)
+    values = jnp.concatenate([spectra_ref[...], twin], axis=0)
     tables = jnp.concatenate(halves(place.forward_x()), axis=1)
     send_ref[...] = dot(tables, jnp.concatenate([values, values], axis=0)).astype(BF16)
 
 
-def prepare_kernel(place, weight_ref, field_ref, mix_ref, mix_bias_ref, head_ref, *refs):
-    packed_ref, z_plain_ref, z_doubled_ref, turn_ref, forward_ref, inverse_ref = refs[:6]
-    field_out_ref, pointwise_ref, head_out_ref, held_ref, arrived = refs[6:]
+def pack_kernel(weight_ref, packed_ref):
     modes, kz, _, channels, _ = weight_ref.shape
-    copies = []
     for q in range(modes // 4):
-        part = pl.ds(4 * q, 4)
-        copies.append(
-            pltpu.make_async_copy(weight_ref.at[part], held_ref.at[part], arrived.at[q])
-        )
-        copies[-1].start()
-    z_plain_ref[...] = place.z_table(False)
-    z_doubled_ref[...] = place.z_table(True)
-    turn_ref[...] = turn_matrix(place, False)
-    forward_ref[...] = jnp.concatenate(halves(place.forward_x()), axis=1)
-    inverse_ref[...] = place.inverse_x()
-    field = side_by_side(dot(turn_ref[...], field_ref[...]).astype(BF16), place.rows_y)
-    field_out_ref[...] = field
-    pointwise_ref[...] = dot_tn(mix_ref[...], field) + mix_bias_ref[...]
-    head_out_ref[...] = jnp.transpose(head_ref[...].astype(F32)).astype(BF16)
-    for q in range(modes // 4):
-        copies[q].wait()
-        parts = [held_ref[4 * q + j // 2, :, j % 2] for j in range(8)]
+        parts = [weight_ref[4 * q + j // 2, :, j % 2] for j in range(8)]
         packed = jnp.concatenate(parts, axis=-1).reshape(kz * channels, 8 * channels)
         packed_ref[q] = packed.astype(BF16)
+
+
+def ready_kernel(place, field_ref, mix_ref, mix_bias_ref, head_ref, *refs):
+    pointwise_ref, head_out_ref, z_doubled_ref = refs
+    pointwise_ref[...] = dot_tn(mix_ref[...], field_ref[...]) + mix_bias_ref[...]
+    head_out_ref[...] = jnp.transpose(head_ref[...].astype(F32)).astype(BF16)
+    z_doubled_ref[...] = place.z_table(True)
 
 
 def fold_kernel(place, own_ref, got_ref, tables_ref, *refs):
@@ -289,9 +282,9 @@
     repeat_rows(send_ref, spread_lines(place, mode, y_inverse_ref[...]))
 
 
-def part_kernel(place, pieces_ref, table_ref, *refs):
+def part_kernel(place, pieces_ref, *refs):
     pieces, shares = read_pieces(place, pieces_ref)
-    lines = dot(table_ref[...], pieces)
+    lines = dot(place.inverse_x(), pieces)
     height = 2 * MZ
     if shares is None:
         own_ref, send_ref = refs
@@ -367,6 +360,7 @@
 
 
 def sums_kernel(place, field_ref, gradient_ref, hidden_ref, head_slope_ref, *refs):
+    refs[-1][...] = jnp.concatenate(halves(place.forward_x()), axis=1)
     grad_mix = dot_nt(field_ref[...], gradient_ref[...])
     grad_head = dot_nt(hidden_ref[...], head_slope_ref[...])
     if not place.fold:
@@ -436,7 +430,9 @@
             out_ref[j, k, 1] = s_real * a_imag - s_imag * a_real
 
 
-def pointwise_kernel(place, mix_ref, gradient_ref, out_ref):
+def pointwise_kernel(place, mix_ref, gradient_ref, out_ref, z_plain_ref, turn_ref):
+    z_plain_ref[...] = place.z_table(False)
+    turn_ref[...] = turn_matrix(place, False)
     z_count = place.z_count
     product = dot(mix_ref[...], gradient_ref[...])
     for y in range(place.rows_y):
@@ -537,32 +533,20 @@
         return call(functools.partial(kernel, place), outs, name, **spec)
 
     flat_field = lifted_field.reshape(cells, z_count)
-    (send,) = run(start_kernel, [plain], "start")(flat_field, to_twin(flat_field))
-    vmem = pl.BlockSpec(memory_space=pltpu.VMEM)
-    weight, z_plain, z_doubled, turn, forward, inverse, field, pointwise, head_turned = run(
-        prepare_kernel,
-        [
-            ((modes // 4, kz * channels, 8 * channels), BF16),
-            ((height, z_count), BF16),
-            ((height, z_count), BF16),
-            ((cells, cells), BF16),
-            ((wide // 2 * height, 4 * height), BF16),
-            ((2 * height, wide // 2 * height), BF16),
-            (across, BF16),
-            (across, F32),
-            ((hidden_units, channels), BF16),
-        ],
-        "prepare",
-        in_specs=[pl.BlockSpec(memory_space=pltpu.HBM)] + [vmem] * 4,
-        scratch_shapes=[
-            pltpu.VMEM(spectral_weight.shape, F32),
-            pltpu.SemaphoreType.DMA((modes // 4,)),
-        ],
-    )(spectral_weight, flat_field, mix_weight, mix_bias[:, None], head_weight)
+    twin_field = to_twin(flat_field)
+    field, spectra = run(own_kernel, [(across, BF16), twin_plain], "own")(flat_field)
+    (send,) = run(start_kernel, [plain], "start")(spectra, twin_field)
+    packed_shape = ((modes // 4, kz * channels, 8 * channels), BF16)
+    (weight,) = call(pack_kernel, [packed_shape], "pack")(spectral_weight)
     spectrum, send = run(mode_kernel, [((mode_lines, channels), F32), plain], "mode")(
         exchange(send), y_forward, y_inverse, weight
     )
-    own, send = run(part_kernel, [own_lines, twin_plain], "part")(exchange(send), inverse)
+    own, send = run(part_kernel, [own_lines, twin_plain], "part")(exchange(send))
+    pointwise, head_turned, z_doubled = run(
+        ready_kernel,
+        [(across, F32), ((hidden_units, channels), BF16), ((height, z_count), BF16)],
+        "ready",
+    )(field, mix_weight, mix_bias[:, None], head_weight)
     prediction, grad_pre, send, hidden, head_slope = run(
         cell_kernel,
         [
@@ -589,7 +573,8 @@
         outs = [((8 * partners, hidden_units), BF16)]
     else:
         outs = [((channels, channels), F32), ((channels, hidden_units), F32)]
-    sums = run(sums_kernel, outs, "sums")(field, grad_pre, hidden, head_slope)
+    outs += [((wide // 2 * height, 4 * height), BF16)]
+    *sums, forward = run(sums_kernel, outs, "sums")(field, grad_pre, hidden, head_slope)
     if not place.fold:
         totals = lax.psum(tuple(sums), ("wide", "narrow"))
         sums = []
@@ -614,12 +599,18 @@
         cost_estimate=pl.CostEstimate(flops=1 << 22, bytes_accessed=5 << 20, transcendentals=0),
         name="outer",
     )(spectrum.reshape(modes, 2 * kz, channels), adjoint.reshape(modes, 2 * kz, channels))
-    (pointwise,) = run(pointwise_kernel, [((channels, rows_y, z_count), F32)], "pointwise")(
-        mix_weight, grad_pre
-    )
+    pointwise, z_plain, turn = run(
+        pointwise_kernel,
+        [
+            ((channels, rows_y, z_count), F32),
+            ((height, z_count), BF16),
+            ((cells, cells), BF16),
+        ],
+        "pointwise",
+    )(mix_weight, grad_pre)
     outs = [own_lines, twin_shared] + ([sums_shape] if place.fold else [])
     after = (done,) if place.fold else ()
-    own, send, *sums = run(part_kernel, outs, "part")(exchange(send), inverse, *after)
+    own, send, *sums = run(part_kernel, outs, "part")(exchange(send), *after)
     outs = [((cells, z_count), BF16), ((rows_y, z_count), F32)]
     if place.fold:
         outs += [((channels, channels), F32), ((channels, hidden_units), F32)]

time: 65.7 us -> 62.3 us (0.948)
  local copies, waits for them, and re-layouts: 6.25 us -> 3.37 us
  blocking collectives: 22.4 us -> 19.8 us
  waiting for transfers between devices: 6.42 us -> 8.83 us
    all_to_all x2, waiting for transfers between devices: 3.28 us -> 7.17 us  [exchange(): lax.all_to_all(pieces, ('wide', 'narrow'), 0, 0, axis_index_groups=groups...]
    all_to_all x2, blocking collectives: 22.4 us -> 19.8 us  [exchange(): lax.all_to_all(pieces, ('wide', 'narrow'), 0, 0, axis_index_groups=groups...]
    unnamed x24 -> x20, local copies, waits for them, and re-layouts: 5.29 us -> 3.06 us
    ppermute x4, waiting for transfers between devices: 3.15 us -> 1.66 us  [to_twin(): return lax.ppermute(send, ('wide', 'narrow'), pairs)]
    pallas_call x6 -> x8, Pallas kernels: 3.5 us -> 3.2 us  [the longest x1 1.2 us: body(): send, = run(start_kernel, [plain], 'start')(spectra, twin_field)]
  transfers between devices with their start and end apart: 6 -> 6, of which waited for: 6 -> 6; matrix products, arithmetic and copies ran while one was open for 1% -> 1% of each run, Pallas kernels for 9% -> 8%
where the time goes in v6:
time: 62.3 us; the launch traced here: 61.6 us
  blocking collectives  19.8 us (32%)
  starting transfers between devices  17.1 us (27%)
  Pallas kernels  11.7 us (19%)
  waiting for transfers between devices  8.83 us (14%)
  local copies, waits for them, and re-layouts  3.37 us (5%)
  between operations  0.76 us (1%)
    all_to_all x2, blocking collectives, exchange(): lax.all_to_all(pieces, ('wide', 'narrow'), 0, 0, axis_index_groups=groups...  19.8 us
    all_to_all x2, starting transfers between devices, exchange(): lax.all_to_all(pieces, ('wide', 'narrow'), 0, 0, axis_index_groups=groups...  11.8 us
    all_to_all x2, waiting for transfers between devices, exchange(): lax.all_to_all(pieces, ('wide', 'narrow'), 0, 0, axis_index_groups=groups...  7.17 us
    ppermute x4, starting transfers between devices, to_twin(): return lax.ppermute(send, ('wide', 'narrow'), pairs)  5.29 us
    pallas_call x1, Pallas kernels, body(): pl.pallas_call(outer_kernel, grid=(modes // some,), in_specs=[pl.BlockSpe...  3.55 us
    unnamed x20, local copies, waits for them, and re-layouts  3.06 us
    pallas_call x1, Pallas kernels, body(): run(back_kernel, [((mode_lines, channels), F32), shared], 'back')  1.67 us
    ppermute x4, waiting for transfers between devices, to_twin(): return lax.ppermute(send, ('wide', 'narrow'), pairs)  1.66 us
  transfers between devices with their start and end apart: 6, of which 6 were waited for; matrix products, arithmetic and copies ran while one was open for 1% of the time, Pallas kernels for 8%

profile of v6, /device:TPU:1, one launch (start us, length us, event | category | flops | bytes accessed | tf_op | source)
XLA Modules:
  0.0 61.6 jit_solution(7704709203682232216)
XLA Ops:
  0.6 0.0 copy-start.1
  0.6 0.0 copy-start.2
  0.7 0.1 collective-permute-start
  0.8 0.0 copy-start.3
  0.8 0.8 %copy-done.3 = bf16[1,32,8,128]{3,2,1,0:T(8,128)(2,1)S(1)} copy-done((bf16[1,32,8,128]{3,2,1,0:T(8,128)(2,1)S(1)}, bf16[1,32,8,128]{3,2,1,0:T(8,128)(2,1)}, u32[]{:S(2)}) %copy-start.3) | copy-done | bytes 65560
  1.6 0.0 copy-start.7
  1.6 0.0 copy-start.9
  1.6 0.0 copy-start.8
  1.6 0.0 copy-start.4
  1.6 0.0 copy-start.5
  1.6 0.0 copy-start.6
  1.7 0.3 own.1
  2.0 0.2 collective-permute-done.twin_ref
  2.2 1.2 %start.1 = bf16[256,256]{1,0:T(8,128)(2,1)} custom-call(bf16[32,256]{1,0:T(8,128)(2,1)S(1)} %get-tuple-element.35.spectra_ref, bf16[256,128]{1,0:T(8,128)(2,1)S(1)} %collective-permute-done.twin_ref), custom_call_target="tpu_custom_call" | custom-call | flops 4194304 | bytes 524288 | tf_op jit(solution)/shard_map/start/pallas_call | solution.py:538
  3.4 7.8 %all-to-all-start = ((bf16[16,16,256]{2,1,0:T(8,128)(2,1)}), bf16[16,16,256]{2,1,0:T(8,128)(2,1)S(1)}, u32[]{:S(2)}, u32[]{:S(2)}) async-start(bf16[16,16,256]{2,1,0:T(8,128)(2,1)} %bitcast.1), calls=%async_computation | async-start | bytes 262144 | tf_op jit(solution)/shard_map/all_to_all | solution.py:519
  11.2 0.0 copy-start
  11.2 2.2 %copy-done = f32[16,8,2,32,32]{4,3,2,1,0:T(8,128)S(1)} copy-done((f32[16,8,2,32,32]{4,3,2,1,0:T(8,128)S(1)}, f32[16,8,2,32,32]{4,3,2,1,0:T(8,128)}, u32[]{:S(2)}) %copy-start) | copy-done | bytes 1048600
  13.4 0.5 pack.1.weight_ref
  13.9 3.9 %all-to-all-done = bf16[16,16,256]{2,1,0:T(8,128)(2,1)S(1)} async-done(((bf16[16,16,256]{2,1,0:T(8,128)(2,1)}), bf16[16,16,256]{2,1,0:T(8,128)(2,1)S(1)}, u32[]{:S(2)}, u32[]{:S(2)}) %all-to-all-start) | async-done | bytes 131104 | tf_op jit(solution)/shard_map/all_to_all | solution.py:519
  17.9 0.0 copy-done.1
  17.9 0.0 copy-done.2
  17.9 0.9 %mode.1 = (f32[256,32]{1,0:T(8,128)S(1)}, bf16[256,256]{1,0:T(8,128)(2,1)S(1)}) custom-call(bf16[256,256]{1,0:T(8,128)(2,1)S(1)} %bitcast.23, bf16[256,256]{1,0:T(8,128)(2,1)S(1)} %copy-done.1, bf16[256,256]{1,0:T(8,128)(2,1)S(1)} %copy-done.2, bf16[4,256,256]{2,1,0:T(8,128)(2,1)S(1)} %pack.1.weight_ref), custom_call_target="tpu_custom_call" | custom-call | flops 4194304 | bytes 524288 | tf_op jit(solution)/shard_map/mode/pallas_call | solution.py:541
  18.8 10.2 %all_to_all.20 = bf16[16,16,256]{2,1,0:T(8,128)(2,1)S(1)} all-to-all(bf16[16,16,256]{2,1,0:T(8,128)(2,1)S(1)} %bitcast.27), channel_id=1, replica_groups={{0,1,4,5,8,9,12,13,16,17,20,21,24,25,28,29},{2,3,6,7,10,11,14,15,18,19,..., dimensions={0} | all-to-all | bytes 262144 | tf_op jit(solution)/shard_map/all_to_all | solution.py:519
  29.0 0.2 part.2
  29.2 2.3 %collective-permute-start.1 = (bf16[32,256]{1,0:T(8,128)(2,1)S(1)}, bf16[32,256]{1,0:T(8,128)(2,1)S(1)}, u32[]{:S(2)}, u32[]{:S(2)}) collective-permute-start(bf16[32,256]{1,0:T(8,128)(2,1)S(1)} %get-tuple-element.38), channel_id=1, source_target_pairs={{0,2},{1,3},{2,0},{3,1},{4,6},{5,7},{6,4},{7,5},{8,10},{9,11},{10,... | collective-permute-start | bytes 49160 | tf_op jit(solution)/shard_map/ppermute | solution.py:510
  31.5 0.0 copy-done.7
  31.5 0.0 copy-done.9
  31.5 0.1 copy.15.mix_bias_ref
  31.6 0.0 copy-done.8
  31.6 0.1 copy.16.refs_6_
  31.7 0.1 copy.17.refs_8_
  31.8 0.0 copy-done.4
  31.8 0.0 copy-done.5
  31.8 0.2 ready.1
  32.0 0.3 collective-permute-done.1.refs_1_
  32.3 0.0 copy-done.6
  32.3 1.2 %cell.1 = (f32[8,128]{1,0:T(8,128)S(1)}, bf16[32,1024]{1,0:T(8,128)(2,1)S(1)}, bf16[32,256]{1,0:T(8,128)(2,1)S(1)}, bf16[32,1024]{1,0:T(8,128)(2,1)S(1)}, bf16[128,1024]{1,0:T(8,128)(2,1)S(1)}) custom-call(f32[32,256]{1,0:T(8,128)S(1)} %get-tuple-element.37.refs_0_, bf16[32,256]{1,0:T(8,128)(2,1)S(1)} %collective-permute-done.1.refs_1_, ...), custom_call_target="tpu_custom_call" | custom-call | flops 4194304 | bytes 524288 | tf_op jit(solution)/shard_map/cell/pallas_call | solution.py:550
  33.6 0.4 collective-permute-start.2
  34.0 0.4 sums.1
  34.3 0.5 collective-permute-done.2.got_ref
  34.8 0.2 fold.1
  35.0 9.6 %all_to_all.21 = bf16[16,40,128]{2,1,0:T(8,128)(2,1)S(1)} all-to-all(bf16[16,40,128]{2,1,0:T(8,128)(2,1)S(1)} %bitcast.21), channel_id=1, replica_groups={{0,1,4,5,8,9,12,13,16,17,20,21,24,25,28,29},{2,3,6,7,10,11,14,15,18,19,..., dimensions={0} | all-to-all | bytes 327680 | tf_op jit(solution)/shard_map/all_to_all | solution.py:519
  44.6 1.7 %back.1 = (f32[256,32]{1,0:T(8,128)S(1)}, bf16[640,128]{1,0:T(8,128)(2,1)}) custom-call(bf16[640,128]{1,0:T(8,128)(2,1)S(1)} %bitcast.22, bf16[256,256]{1,0:T(8,128)(2,1)S(1)} %copy-done.1, bf16[256,256]{1,0:T(8,128)(2,1)S(1)} %copy-done.2, bf16[4,256,256]{2,1,0:T(8,128)(2,1)S(1)} %pack.1.weight_ref), custom_call_target="tpu_custom_call" | custom-call | flops 4194304 | bytes 524288 | tf_op jit(solution)/shard_map/back/pallas_call | solution.py:582
  46.3 4.0 %all-to-all-start.3 = ((bf16[16,40,128]{2,1,0:T(8,128)(2,1)}), bf16[16,40,128]{2,1,0:T(8,128)(2,1)S(1)}, u32[]{:S(2)}, u32[]{:S(2)}) async-start(bf16[16,40,128]{2,1,0:T(8,128)(2,1)} %bitcast.12), calls=%async_computation.3 | async-start | bytes 327680 | tf_op jit(solution)/shard_map/all_to_all | solution.py:519
  50.2 3.6 %outer.1 = (f32[16,8,2,32,32]{4,3,2,1,0:T(8,128)}, f32[8,128]{1,0:T(8,128)S(1)}) custom-call(f32[16,16,32]{2,1,0:T(8,128)S(1)} %bitcast.25, f32[16,16,32]{2,1,0:T(8,128)S(1)} %bitcast.26), custom_call_target="tpu_custom_call" | custom-call | flops 4194304 | bytes 5242880 | tf_op jit(solution)/shard_map/outer/pallas_call | solution.py:586
  53.8 3.2 %all-to-all-done.3 = bf16[16,40,128]{2,1,0:T(8,128)(2,1)S(1)} async-done(((bf16[16,40,128]{2,1,0:T(8,128)(2,1)}), bf16[16,40,128]{2,1,0:T(8,128)(2,1)S(1)}, u32[]{:S(2)}, u32[]{:S(2)}) %all-to-all-start.3) | async-done | bytes 163872 | tf_op jit(solution)/shard_map/all_to_all | solution.py:519
  57.0 0.2 part.3
  57.3 2.5 %collective-permute-start.3 = (bf16[96,256]{1,0:T(8,128)(2,1)S(1)}, bf16[96,256]{1,0:T(8,128)(2,1)S(1)}, u32[]{:S(2)}, u32[]{:S(2)}) collective-permute-start(bf16[96,256]{1,0:T(8,128)(2,1)S(1)} %get-tuple-element.54), channel_id=1, source_target_pairs={{0,2},{1,3},{2,0},{3,1},{4,6},{5,7},{6,4},{7,5},{8,10},{9,11},{10,... | collective-permute-start | bytes 147464 | tf_op jit(solution)/shard_map/ppermute | solution.py:510
  59.7 0.2 pointwise.1
  59.9 0.7 %collective-permute-done.3.refs_1_ = bf16[96,256]{1,0:T(8,128)(2,1)S(1)} collective-permute-done((bf16[96,256]{1,0:T(8,128)(2,1)S(1)}, bf16[96,256]{1,0:T(8,128)(2,1)S(1)}, u32[]{:S(2)}, u32[]{:S(2)}) %collective-permute-start.3) | collective-permute-done | bytes 49184 | tf_op jit(solution)/shard_map/ppermute | solution.py:510
  60.6 1.0 %finish.1 = (bf16[256,128]{1,0:T(8,128)(2,1)}, f32[8,128]{1,0:T(8,128)}, f32[32,32]{1,0:T(8,128)}, f32[32,128]{1,0:T(8,128)}) custom-call(f32[32,256]{1,0:T(8,128)S(1)} %get-tuple-element.53.refs_0_, bf16[96,256]{1,0:T(8,128)(2,1)S(1)} %collective-permute-done.3.refs_1_, bf16[32,128]{1,0:T(8,128)(2,1)S(1)} %get-tuple-element.55.refs_2_, ...), custom_call_target="tpu_custom_call" | custom-call | flops 4194304 | bytes 524288 | tf_op jit(solution)/shard_map/finish/pallas_call | solution.py:617
  (1 shorter events, 0.0 us)
Async XLA Ops:
  0.6 17.2 %copy-start.1 = (bf16[256,256]{1,0:T(8,128)(2,1)S(1)}, bf16[256,256]{1,0:T(8,128)(2,1)}, u32[]{:S(2)}) copy-start(bf16[256,256]{1,0:T(8,128)(2,1)} %constant.4.clone.y_forward_ref) | copy-start | bytes 393220
  0.6 17.2 %copy-start.2 = (bf16[256,256]{1,0:T(8,128)(2,1)S(1)}, bf16[256,256]{1,0:T(8,128)(2,1)}, u32[]{:S(2)}) copy-start(bf16[256,256]{1,0:T(8,128)(2,1)} %constant.5.clone.y_inverse_ref) | copy-start | bytes 393220
  0.7 1.5 %collective-permute-start = (bf16[256,128]{1,0:T(8,128)(2,1)}, bf16[256,128]{1,0:T(8,128)(2,1)S(1)}, u32[]{:S(2)}, u32[]{:S(2)}) collective-permute-start(bf16[256,128]{1,0:T(8,128)(2,1)} %bitcast.28), channel_id=1, source_target_pairs={{0,2},{1,3},{2,0},{3,1},{4,6},{5,7},{6,4},{7,5},{8,10},{9,11},{10,... | collective-permute-start | bytes 196616 | tf_op jit(solution)/shard_map/ppermute | solution.py:510
  0.8 0.8 %copy-start.3 = (bf16[1,32,8,128]{3,2,1,0:T(8,128)(2,1)S(1)}, bf16[1,32,8,128]{3,2,1,0:T(8,128)(2,1)}, u32[]{:S(2)}) copy-start(bf16[1,32,8,128]{3,2,1,0:T(8,128)(2,1)} %param.10) | copy-start | bytes 196612
  1.6 29.9 %copy-start.7 = (bf16[128]{0:T(256)(128)(2,1)S(1)}, bf16[128]{0:T(256)(128)(2,1)}, u32[]{:S(2)}) copy-start(bf16[128]{0:T(256)(128)(2,1)} %param.16) | copy-start | bytes 772
  1.6 29.9 %copy-start.9 = (f32[32]{0:T(128)S(1)}, f32[32]{0:T(128)}, u32[]{:S(2)}) copy-start(f32[32]{0:T(128)} %param.13) | copy-start | bytes 388
  1.6 30.0 %copy-start.8 = (f32[128]{0:T(128)S(1)}, f32[128]{0:T(128)}, u32[]{:S(2)}) copy-start(f32[128]{0:T(128)} %param.15) | copy-start | bytes 1540
  1.6 30.2 %copy-start.4 = (bf16[32,128]{1,0:T(8,128)(2,1)S(1)}, bf16[32,128]{1,0:T(8,128)(2,1)}, u32[]{:S(2)}) copy-start(bf16[32,128]{1,0:T(8,128)(2,1)} %refs_4_.1) | copy-start | bytes 24580
  1.6 30.2 %copy-start.5 = (bf16[32,32]{1,0:T(8,128)(2,1)S(1)}, bf16[32,32]{1,0:T(8,128)(2,1)}, u32[]{:S(2)}) copy-start(bf16[32,32]{1,0:T(8,128)(2,1)} %mix_ref.3) | copy-start | bytes 6148
  1.6 30.7 %copy-start.6 = (f32[1,8,128]{2,1,0:T(8,128)S(1)}, f32[1,8,128]{2,1,0:T(8,128)}, u32[]{:S(2)}) copy-start(f32[1,8,128]{2,1,0:T(8,128)} %param.17) | copy-start | bytes 12292
  3.4 14.5 %all-to-all-start = ((bf16[16,16,256]{2,1,0:T(8,128)(2,1)}), bf16[16,16,256]{2,1,0:T(8,128)(2,1)S(1)}, u32[]{:S(2)}, u32[]{:S(2)}) async-start(bf16[16,16,256]{2,1,0:T(8,128)(2,1)} %bitcast.1), calls=%async_computation | async-start | bytes 262144 | tf_op jit(solution)/shard_map/all_to_all | solution.py:519
  11.2 2.2 %copy-start = (f32[16,8,2,32,32]{4,3,2,1,0:T(8,128)S(1)}, f32[16,8,2,32,32]{4,3,2,1,0:T(8,128)}, u32[]{:S(2)}) copy-start(f32[16,8,2,32,32]{4,3,2,1,0:T(8,128)} %weight_ref.1) | copy-start | bytes 3145732
  29.2 3.1 %collective-permute-start.1 = (bf16[32,256]{1,0:T(8,128)(2,1)S(1)}, bf16[32,256]{1,0:T(8,128)(2,1)S(1)}, u32[]{:S(2)}, u32[]{:S(2)}) collective-permute-start(bf16[32,256]{1,0:T(8,128)(2,1)S(1)} %get-tuple-element.38), channel_id=1, source_target_pairs={{0,2},{1,3},{2,0},{3,1},{4,6},{5,7},{6,4},{7,5},{8,10},{9,11},{10,... | collective-permute-start | bytes 49160 | tf_op jit(solution)/shard_map/ppermute | solution.py:510
  33.6 1.2 %collective-permute-start.2 = (bf16[32,256]{1,0:T(8,128)(2,1)S(1)}, bf16[32,256]{1,0:T(8,128)(2,1)S(1)}, u32[]{:S(2)}, u32[]{:S(2)}) collective-permute-start(bf16[32,256]{1,0:T(8,128)(2,1)S(1)} %get-tuple-element.43.own_ref), channel_id=1, source_target_pairs={{0,2},{1,3},{2,0},{3,1},{4,6},{5,7},{6,4},{7,5},{8,10},{9,11},{10,... | collective-permute-start | bytes 49160 | tf_op jit(solution)/shard_map/ppermute | solution.py:510
  46.3 10.7 %all-to-all-start.3 = ((bf16[16,40,128]{2,1,0:T(8,128)(2,1)}), bf16[16,40,128]{2,1,0:T(8,128)(2,1)S(1)}, u32[]{:S(2)}, u32[]{:S(2)}) async-start(bf16[16,40,128]{2,1,0:T(8,128)(2,1)} %bitcast.12), calls=%async_computation.3 | async-start | bytes 327680 | tf_op jit(solution)/shard_map/all_to_all | solution.py:519
  57.3 3.4 %collective-permute-start.3 = (bf16[96,256]{1,0:T(8,128)(2,1)S(1)}, bf16[96,256]{1,0:T(8,128)(2,1)S(1)}, u32[]{:S(2)}, u32[]{:S(2)}) collective-permute-start(bf16[96,256]{1,0:T(8,128)(2,1)S(1)} %get-tuple-element.54), channel_id=1, source_target_pairs={{0,2},{1,3},{2,0},{3,1},{4,6},{5,7},{6,4},{7,5},{8,10},{9,11},{10,... | collective-permute-start | bytes 147464 | tf_op jit(solution)/shard_map/ppermute | solution.py:510

commit v7 on v5

--- a/solution.py
+++ b/solution.py
@@ -15,6 +15,7 @@
 F32 = jnp.float32
 BF16 = jnp.bfloat16
 VMEM_LIMIT = 32 * 1024 * 1024
+FETCH_LIMIT = 52 * 1024 * 1024
 
 TAIL_SLOPE = 0.275
 TAIL = (
@@ -221,18 +222,9 @@
     return jnp.concatenate([values[:, y * width : (y + 1) * width] for y in range(count)], axis=0)
 
 
-def start_kernel(place, field_ref, twin_ref, send_ref):
-    fields = jnp.concatenate([field_ref[...], twin_ref[...]], axis=0)
-    spectra = dot_nt(place.z_table(False), fields).astype(BF16)
-    values = one_below_other(spectra, 2)
-    values = dot(values, turn_matrix(place, True)).astype(BF16)
-    tables = jnp.concatenate(halves(place.forward_x()), axis=1)
-    send_ref[...] = dot(tables, jnp.concatenate([values, values], axis=0)).astype(BF16)
-
-
-def prepare_kernel(place, weight_ref, field_ref, mix_ref, mix_bias_ref, head_ref, *refs):
-    packed_ref, z_plain_ref, z_doubled_ref, turn_ref, forward_ref, inverse_ref = refs[:6]
-    field_out_ref, pointwise_ref, head_out_ref, held_ref, arrived = refs[6:]
+def fetch_kernel(place, weight_ref, *refs):
+    packed_ref, z_plain_ref, z_doubled_ref, turn_in_ref, turn_out_ref = refs[:5]
+    forward_ref, inverse_ref, held_ref, arrived = refs[5:]
     modes, kz, _, channels, _ = weight_ref.shape
     copies = []
     for q in range(modes // 4):
@@ -243,18 +235,34 @@
         copies[-1].start()
     z_plain_ref[...] = place.z_table(False)
     z_doubled_ref[...] = place.z_table(True)
-    turn_ref[...] = turn_matrix(place, False)
+    turn_in_ref[...] = turn_matrix(place, True)
+    turn_out_ref[...] = turn_matrix(place, False)
     forward_ref[...] = jnp.concatenate(halves(place.forward_x()), axis=1)
     inverse_ref[...] = place.inverse_x()
-    field = side_by_side(dot(turn_ref[...], field_ref[...]).astype(BF16), place.rows_y)
-    field_out_ref[...] = field
-    pointwise_ref[...] = dot_tn(mix_ref[...], field) + mix_bias_ref[...]
-    head_out_ref[...] = jnp.transpose(head_ref[...].astype(F32)).astype(BF16)
     for q in range(modes // 4):
         copies[q].wait()
         parts = [held_ref[4 * q + j // 2, :, j % 2] for j in range(8)]
         packed = jnp.concatenate(parts, axis=-1).reshape(kz * channels, 8 * channels)
         packed_ref[q] = packed.astype(BF16)
+
+
+def own_kernel(place, field_ref, z_table_ref, turn_ref, field_out_ref, spectra_ref):
+    turned = dot(turn_ref[...], field_ref[...]).astype(BF16)
+    field_out_ref[...] = side_by_side(turned, place.rows_y)
+    spectra_ref[...] = dot_nt(z_table_ref[...], turned).astype(BF16)
+
+
+def start_kernel(place, spectra_ref, twin_ref, z_table_ref, turn_ref, tables_ref, send_ref):
+    twin = dot_nt(z_table_ref[...], twin_ref[...]).astype(BF16)
+    twin = dot(twin, turn_ref[...]).astype(BF16)
+    values = jnp.concatenate([spectra_ref[...], twin], axis=0)
+    send_ref[...] = dot(tables_ref[...], jnp.concatenate([values, values], axis=0)).astype(BF16)
+
+
+def ready_kernel(place, field_ref, mix_ref, mix_bias_ref, head_ref, *refs):
+    pointwise_ref, head_out_ref = refs
+    pointwise_ref[...] = dot_tn(mix_ref[...], field_ref[...]) + mix_bias_ref[...]
+    head_out_ref[...] = jnp.transpose(head_ref[...].astype(F32)).astype(BF16)
 
 
 def fold_kernel(place, own_ref, got_ref, tables_ref, *refs):
@@ -466,11 +474,11 @@
     grad_mix_ref[...] = total[channels:, :channels]
 
 
-def call(kernel, outs, name, **spec):
+def call(kernel, outs, name, limit=VMEM_LIMIT, **spec):
     return pl.pallas_call(
         kernel,
         out_shape=[jax.ShapeDtypeStruct(shape, dtype) for shape, dtype in outs],
-        compiler_params=pltpu.CompilerParams(vmem_limit_bytes=VMEM_LIMIT),
+        compiler_params=pltpu.CompilerParams(vmem_limit_bytes=limit),
         cost_estimate=pl.CostEstimate(flops=1 << 22, bytes_accessed=1 << 19, transcendentals=0),
         name=name,
         **spec,
@@ -537,32 +545,37 @@
         return call(functools.partial(kernel, place), outs, name, **spec)
 
     flat_field = lifted_field.reshape(cells, z_count)
-    (send,) = run(start_kernel, [plain], "start")(flat_field, to_twin(flat_field))
-    vmem = pl.BlockSpec(memory_space=pltpu.VMEM)
-    weight, z_plain, z_doubled, turn, forward, inverse, field, pointwise, head_turned = run(
-        prepare_kernel,
+    twin_field = to_twin(flat_field)
+    weight, z_plain, z_doubled, turn_in, turn, forward, inverse = run(
+        fetch_kernel,
         [
             ((modes // 4, kz * channels, 8 * channels), BF16),
             ((height, z_count), BF16),
             ((height, z_count), BF16),
             ((cells, cells), BF16),
+            ((cells, cells), BF16),
             ((wide // 2 * height, 4 * height), BF16),
             ((2 * height, wide // 2 * height), BF16),
-            (across, BF16),
-            (across, F32),
-            ((hidden_units, channels), BF16),
         ],
-        "prepare",
-        in_specs=[pl.BlockSpec(memory_space=pltpu.HBM)] + [vmem] * 4,
+        "fetch",
+        limit=FETCH_LIMIT,
+        in_specs=[pl.BlockSpec(memory_space=pl.ANY)],
         scratch_shapes=[
             pltpu.VMEM(spectral_weight.shape, F32),
             pltpu.SemaphoreType.DMA((modes // 4,)),
         ],
-    )(spectral_weight, flat_field, mix_weight, mix_bias[:, None], head_weight)
+    )(spectral_weight)
+    field, spectra = run(own_kernel, [(across, BF16), twin_plain], "own")(
+        flat_field, z_plain, turn
+    )
+    (send,) = run(start_kernel, [plain], "start")(spectra, twin_field, z_plain, turn_in, forward)
     spectrum, send = run(mode_kernel, [((mode_lines, channels), F32), plain], "mode")(
         exchange(send), y_forward, y_inverse, weight
     )
     own, send = run(part_kernel, [own_lines, twin_plain], "part")(exchange(send), inverse)
+    pointwise, head_turned = run(
+        ready_kernel, [(across, F32), ((hidden_units, channels), BF16)], "ready"
+    )(field, mix_weight, mix_bias[:, None], head_weight)
     prediction, grad_pre, send, hidden, head_slope = run(
         cell_kernel,
         [

time: 65.7 us -> 62.9 us (0.957)
  blocking collectives: 22.4 us -> 34.3 us
  starting transfers between devices: 17 us -> 9.21 us
  local copies, waits for them, and re-layouts: 6.25 us -> 0.35 us
  waiting for transfers between devices: 6.42 us -> 4.67 us
  Pallas kernels: 12 us -> 12.9 us
    all_to_all x2 -> x3, blocking collectives: 22.4 us -> 34.3 us  [exchange(): lax.all_to_all(pieces, ('wide', 'narrow'), 0, 0, axis_index_groups=groups...]
    all_to_all x2 -> x1, starting transfers between devices: 11.7 us -> 3.96 us  [exchange(): lax.all_to_all(pieces, ('wide', 'narrow'), 0, 0, axis_index_groups=groups...]
    unnamed x24 -> x18, local copies, waits for them, and re-layouts: 5.29 us -> 0.04 us
    ppermute x4, waiting for transfers between devices: 3.15 us -> 1.45 us  [to_twin(): return lax.ppermute(send, ('wide', 'narrow'), pairs)]
    pallas_call x2 -> x4, Pallas kernels: 2.63 us -> 3.51 us  [the longest x1 2.55 us: body(): run(fetch_kernel, [((modes // 4, kz * channels, 8 * channels), BF16), ((h...]
    all_to_all x2 -> x1, waiting for transfers between devices: 3.28 us -> 3.22 us  [exchange(): lax.all_to_all(pieces, ('wide', 'narrow'), 0, 0, axis_index_groups=groups...]
  transfers between devices with their start and end apart: 6 -> 5, of which waited for: 6 -> 4; matrix products, arithmetic and copies ran while one was open for 1% -> 1% of each run, Pallas kernels for 9% -> 12%
where the time goes in v7:
time: 62.9 us; the launch traced here: 62.3 us
  blocking collectives  34.3 us (55%)
  Pallas kernels  12.9 us (21%)
  starting transfers between devices  9.21 us (15%)
  waiting for transfers between devices  4.67 us (7%)
  between operations  0.8 us (1%)
    all_to_all x3, blocking collectives, exchange(): lax.all_to_all(pieces, ('wide', 'narrow'), 0, 0, axis_index_groups=groups...  34.3 us
    ppermute x4, starting transfers between devices, to_twin(): return lax.ppermute(send, ('wide', 'narrow'), pairs)  5.25 us
    all_to_all x1, starting transfers between devices, exchange(): lax.all_to_all(pieces, ('wide', 'narrow'), 0, 0, axis_index_groups=groups...  3.96 us
    pallas_call x1, Pallas kernels, body(): pl.pallas_call(outer_kernel, grid=(modes // some,), in_specs=[pl.BlockSpe...  3.55 us
    all_to_all x1, waiting for transfers between devices, exchange(): lax.all_to_all(pieces, ('wide', 'narrow'), 0, 0, axis_index_groups=groups...  3.22 us
    pallas_call x1, Pallas kernels, body(): run(fetch_kernel, [((modes // 4, kz * channels, 8 * channels), BF16), ((h...  2.55 us
    pallas_call x1, Pallas kernels, body(): run(back_kernel, [((mode_lines, channels), F32), shared], 'back')  1.67 us
    ppermute x4, waiting for transfers between devices, to_twin(): return lax.ppermute(send, ('wide', 'narrow'), pairs)  1.45 us
  transfers between devices with their start and end apart: 5, of which 4 were waited for; matrix products, arithmetic and copies ran while one was open for 1% of the time, Pallas kernels for 12%

profile of v7, /device:TPU:1, one launch (start us, length us, event | category | flops | bytes accessed | tf_op | source)
XLA Modules:
  0.0 62.3 jit_solution(5877660982272554396)
XLA Ops:
  0.6 0.0 copy-start
  0.6 0.0 copy-start.1
  0.7 0.0 copy-start.2
  0.7 0.0 copy-start.6
  0.7 0.0 copy-start.8
  0.7 0.0 copy-start.7
  0.7 0.0 copy-start.4
  0.7 0.0 copy-start.3
  0.7 0.0 copy-start.5
  0.7 0.1 collective-permute-start
  0.9 2.5 %fetch.1 = (bf16[4,256,256]{2,1,0:T(8,128)(2,1)S(1)}, bf16[32,128]{1,0:T(8,128)(2,1)S(1)}, bf16[32,128]{1,0:T(8,128)(2,1)S(1)}, bf16[256,256]{1,0:T(8,128)(2,1)S...) custom-call(f32[16,8,2,32,32]{4,3,2,1,0:T(8,128)} %weight_ref.1), custom_call_target="tpu_custom_call" | custom-call | flops 4194304 | bytes 524288 | tf_op jit(solution)/shard_map/fetch/pallas_call | solution.py:549
  3.4 0.0 copy-done.2
  3.4 0.3 own.1
  3.7 0.0 collective-permute-done.twin_ref
  3.7 0.5 start.1
  4.2 14.5 %all_to_all.20 = bf16[16,16,256]{2,1,0:T(8,128)(2,1)S(1)} all-to-all(bf16[16,16,256]{2,1,0:T(8,128)(2,1)S(1)} %bitcast.23), channel_id=1, replica_groups={{0,1,4,5,8,9,12,13,16,17,20,21,24,25,28,29},{2,3,6,7,10,11,14,15,18,19,..., dimensions={0} | all-to-all | bytes 262144 | tf_op jit(solution)/shard_map/all_to_all | solution.py:531
  18.7 0.0 copy-done
  18.7 0.0 copy-done.1
  18.7 0.9 %mode.1 = (f32[256,32]{1,0:T(8,128)S(1)}, bf16[256,256]{1,0:T(8,128)(2,1)S(1)}) custom-call(bf16[256,256]{1,0:T(8,128)(2,1)S(1)} %bitcast.24, bf16[256,256]{1,0:T(8,128)(2,1)S(1)} %copy-done, bf16[256,256]{1,0:T(8,128)(2,1)S(1)} %copy-done.1, bf16[4,256,256]{2,1,0:T(8,128)(2,1)S(1)} %get-tuple-element.41.weight_ref), custom_call_target="tpu_custom_call" | custom-call | flops 4194304 | bytes 524288 | tf_op jit(solution)/shard_map/mode/pallas_call | solution.py:572
  19.6 10.2 %all_to_all.21 = bf16[16,16,256]{2,1,0:T(8,128)(2,1)S(1)} all-to-all(bf16[16,16,256]{2,1,0:T(8,128)(2,1)S(1)} %bitcast.28), channel_id=1, replica_groups={{0,1,4,5,8,9,12,13,16,17,20,21,24,25,28,29},{2,3,6,7,10,11,14,15,18,19,..., dimensions={0} | all-to-all | bytes 262144 | tf_op jit(solution)/shard_map/all_to_all | solution.py:531
  29.8 0.1 part.2
  30.0 2.3 %collective-permute-start.1 = (bf16[32,256]{1,0:T(8,128)(2,1)S(1)}, bf16[32,256]{1,0:T(8,128)(2,1)S(1)}, u32[]{:S(2)}, u32[]{:S(2)}) collective-permute-start(bf16[32,256]{1,0:T(8,128)(2,1)S(1)} %get-tuple-element.45), channel_id=1, source_target_pairs={{0,2},{1,3},{2,0},{3,1},{4,6},{5,7},{6,4},{7,5},{8,10},{9,11},{10,... | collective-permute-start | bytes 49160 | tf_op jit(solution)/shard_map/ppermute | solution.py:522
  32.3 0.0 copy-done.6
  32.3 0.0 copy-done.8
  32.3 0.1 copy.15.mix_bias_ref
  32.3 0.0 copy-done.7
  32.3 0.1 copy.16.refs_6_
  32.5 0.1 copy.17.refs_8_
  32.6 0.0 copy-done.4
  32.6 0.0 copy-done.3
  32.6 0.2 ready.1
  32.8 0.3 collective-permute-done.1.refs_1_
  33.1 0.0 copy-done.5
  33.1 1.2 %cell.1 = (f32[8,128]{1,0:T(8,128)S(1)}, bf16[32,1024]{1,0:T(8,128)(2,1)S(1)}, bf16[32,256]{1,0:T(8,128)(2,1)S(1)}, bf16[32,1024]{1,0:T(8,128)(2,1)S(1)}, bf16[128,1024]{1,0:T(8,128)(2,1)S(1)}) custom-call(f32[32,256]{1,0:T(8,128)S(1)} %get-tuple-element.44.refs_0_, bf16[32,256]{1,0:T(8,128)(2,1)S(1)} %collective-permute-done.1.refs_1_, ...), custom_call_target="tpu_custom_call" | custom-call | flops 4194304 | bytes 524288 | tf_op jit(solution)/shard_map/cell/pallas_call | solution.py:579
  34.3 0.4 collective-permute-start.2
  34.7 0.4 sums.1.refs_0_
  35.1 0.5 collective-permute-done.2.got_ref
  35.5 0.2 fold.1
  35.7 9.6 %all_to_all.22 = bf16[16,40,128]{2,1,0:T(8,128)(2,1)S(1)} all-to-all(bf16[16,40,128]{2,1,0:T(8,128)(2,1)S(1)} %bitcast.21), channel_id=1, replica_groups={{0,1,4,5,8,9,12,13,16,17,20,21,24,25,28,29},{2,3,6,7,10,11,14,15,18,19,..., dimensions={0} | all-to-all | bytes 327680 | tf_op jit(solution)/shard_map/all_to_all | solution.py:531
  45.4 1.7 %back.1 = (f32[256,32]{1,0:T(8,128)S(1)}, bf16[640,128]{1,0:T(8,128)(2,1)}) custom-call(bf16[640,128]{1,0:T(8,128)(2,1)S(1)} %bitcast.22, bf16[256,256]{1,0:T(8,128)(2,1)S(1)} %copy-done, bf16[256,256]{1,0:T(8,128)(2,1)S(1)} %copy-done.1, bf16[4,256,256]{2,1,0:T(8,128)(2,1)S(1)} %get-tuple-element.41.weight_ref), custom_call_target="tpu_custom_call" | custom-call | flops 4194304 | bytes 524288 | tf_op jit(solution)/shard_map/back/pallas_call | solution.py:610
  47.0 4.0 %all-to-all-start.3 = ((bf16[16,40,128]{2,1,0:T(8,128)(2,1)}), bf16[16,40,128]{2,1,0:T(8,128)(2,1)S(1)}, u32[]{:S(2)}, u32[]{:S(2)}) async-start(bf16[16,40,128]{2,1,0:T(8,128)(2,1)} %bitcast.12), calls=%async_computation.3 | async-start | bytes 327680 | tf_op jit(solution)/shard_map/all_to_all | solution.py:531
  51.0 3.6 %outer.1 = (f32[16,8,2,32,32]{4,3,2,1,0:T(8,128)}, f32[8,128]{1,0:T(8,128)S(1)}) custom-call(f32[16,16,32]{2,1,0:T(8,128)S(1)} %bitcast.26, f32[16,16,32]{2,1,0:T(8,128)S(1)} %bitcast.27), custom_call_target="tpu_custom_call" | custom-call | flops 4194304 | bytes 5242880 | tf_op jit(solution)/shard_map/outer/pallas_call | solution.py:614
  54.6 3.2 %all-to-all-done.3 = bf16[16,40,128]{2,1,0:T(8,128)(2,1)S(1)} async-done(((bf16[16,40,128]{2,1,0:T(8,128)(2,1)}), bf16[16,40,128]{2,1,0:T(8,128)(2,1)S(1)}, u32[]{:S(2)}, u32[]{:S(2)}) %all-to-all-start.3) | async-done | bytes 163872 | tf_op jit(solution)/shard_map/all_to_all | solution.py:531
  57.8 0.2 part.3
  57.9 2.5 %collective-permute-start.3 = (bf16[96,256]{1,0:T(8,128)(2,1)S(1)}, bf16[96,256]{1,0:T(8,128)(2,1)S(1)}, u32[]{:S(2)}, u32[]{:S(2)}) collective-permute-start(bf16[96,256]{1,0:T(8,128)(2,1)S(1)} %get-tuple-element.59), channel_id=1, source_target_pairs={{0,2},{1,3},{2,0},{3,1},{4,6},{5,7},{6,4},{7,5},{8,10},{9,11},{10,... | collective-permute-start | bytes 147464 | tf_op jit(solution)/shard_map/ppermute | solution.py:522
  60.4 0.2 pointwise.1.refs_4_
  60.6 0.7 %collective-permute-done.3.refs_1_ = bf16[96,256]{1,0:T(8,128)(2,1)S(1)} collective-permute-done((bf16[96,256]{1,0:T(8,128)(2,1)S(1)}, bf16[96,256]{1,0:T(8,128)(2,1)S(1)}, u32[]{:S(2)}, u32[]{:S(2)}) %collective-permute-start.3) | collective-permute-done | bytes 49184 | tf_op jit(solution)/shard_map/ppermute | solution.py:522
  61.3 1.0 %finish.1 = (bf16[256,128]{1,0:T(8,128)(2,1)}, f32[8,128]{1,0:T(8,128)}, f32[32,32]{1,0:T(8,128)}, f32[32,128]{1,0:T(8,128)}) custom-call(f32[32,256]{1,0:T(8,128)S(1)} %get-tuple-element.58.refs_0_, bf16[96,256]{1,0:T(8,128)(2,1)S(1)} %collective-permute-done.3.refs_1_, bf16[32,128]{1,0:T(8,128)(2,1)S(1)} %get-tuple-element.36.z_table_ref.refs_2_, ...), custom_call_target="tpu_custom_call" | custom-call | flops 4194304 | bytes 524288 | tf_op jit(solution)/shard_map/finish/pallas_call | solution.py:639
  (1 shorter events, 0.0 us)
Async XLA Ops:
  0.6 18.0 %copy-start = (bf16[256,256]{1,0:T(8,128)(2,1)S(1)}, bf16[256,256]{1,0:T(8,128)(2,1)}, u32[]{:S(2)}) copy-start(bf16[256,256]{1,0:T(8,128)(2,1)} %constant.4.clone.y_forward_ref) | copy-start | bytes 393220
  0.6 18.0 %copy-start.1 = (bf16[256,256]{1,0:T(8,128)(2,1)S(1)}, bf16[256,256]{1,0:T(8,128)(2,1)}, u32[]{:S(2)}) copy-start(bf16[256,256]{1,0:T(8,128)(2,1)} %constant.5.clone.y_inverse_ref) | copy-start | bytes 393220
  0.7 2.8 %copy-start.2 = (bf16[1,32,8,128]{3,2,1,0:T(8,128)(2,1)S(1)}, bf16[1,32,8,128]{3,2,1,0:T(8,128)(2,1)}, u32[]{:S(2)}) copy-start(bf16[1,32,8,128]{3,2,1,0:T(8,128)(2,1)} %param.10) | copy-start | bytes 196612
  0.7 31.6 %copy-start.6 = (bf16[128]{0:T(256)(128)(2,1)S(1)}, bf16[128]{0:T(256)(128)(2,1)}, u32[]{:S(2)}) copy-start(bf16[128]{0:T(256)(128)(2,1)} %param.16) | copy-start | bytes 772
  0.7 31.6 %copy-start.8 = (f32[32]{0:T(128)S(1)}, f32[32]{0:T(128)}, u32[]{:S(2)}) copy-start(f32[32]{0:T(128)} %param.13) | copy-start | bytes 388
  0.7 31.7 %copy-start.7 = (f32[128]{0:T(128)S(1)}, f32[128]{0:T(128)}, u32[]{:S(2)}) copy-start(f32[128]{0:T(128)} %param.15) | copy-start | bytes 1540
  0.7 31.9 %copy-start.4 = (bf16[32,32]{1,0:T(8,128)(2,1)S(1)}, bf16[32,32]{1,0:T(8,128)(2,1)}, u32[]{:S(2)}) copy-start(bf16[32,32]{1,0:T(8,128)(2,1)} %mix_ref.3) | copy-start | bytes 6148
  0.7 31.9 %copy-start.3 = (bf16[32,128]{1,0:T(8,128)(2,1)S(1)}, bf16[32,128]{1,0:T(8,128)(2,1)}, u32[]{:S(2)}) copy-start(bf16[32,128]{1,0:T(8,128)(2,1)} %refs_4_.1) | copy-start | bytes 24580
  0.7 32.4 %copy-start.5 = (f32[1,8,128]{2,1,0:T(8,128)S(1)}, f32[1,8,128]{2,1,0:T(8,128)}, u32[]{:S(2)}) copy-start(f32[1,8,128]{2,1,0:T(8,128)} %param.17) | copy-start | bytes 12292
  0.7 3.0 %collective-permute-start = (bf16[256,128]{1,0:T(8,128)(2,1)}, bf16[256,128]{1,0:T(8,128)(2,1)S(1)}, u32[]{:S(2)}, u32[]{:S(2)}) collective-permute-start(bf16[256,128]{1,0:T(8,128)(2,1)} %bitcast.29), channel_id=1, source_target_pairs={{0,2},{1,3},{2,0},{3,1},{4,6},{5,7},{6,4},{7,5},{8,10},{9,11},{10,... | collective-permute-start | bytes 196616 | tf_op jit(solution)/shard_map/ppermute | solution.py:522
  30.0 3.1 %collective-permute-start.1 = (bf16[32,256]{1,0:T(8,128)(2,1)S(1)}, bf16[32,256]{1,0:T(8,128)(2,1)S(1)}, u32[]{:S(2)}, u32[]{:S(2)}) collective-permute-start(bf16[32,256]{1,0:T(8,128)(2,1)S(1)} %get-tuple-element.45), channel_id=1, source_target_pairs={{0,2},{1,3},{2,0},{3,1},{4,6},{5,7},{6,4},{7,5},{8,10},{9,11},{10,... | collective-permute-start | bytes 49160 | tf_op jit(solution)/shard_map/ppermute | solution.py:522
  34.3 1.2 %collective-permute-start.2 = (bf16[32,256]{1,0:T(8,128)(2,1)S(1)}, bf16[32,256]{1,0:T(8,128)(2,1)S(1)}, u32[]{:S(2)}, u32[]{:S(2)}) collective-permute-start(bf16[32,256]{1,0:T(8,128)(2,1)S(1)} %get-tuple-element.50.own_ref), channel_id=1, source_target_pairs={{0,2},{1,3},{2,0},{3,1},{4,6},{5,7},{6,4},{7,5},{8,10},{9,11},{10,... | collective-permute-start | bytes 49160 | tf_op jit(solution)/shard_map/ppermute | solution.py:522
  47.0 10.7 %all-to-all-start.3 = ((bf16[16,40,128]{2,1,0:T(8,128)(2,1)}), bf16[16,40,128]{2,1,0:T(8,128)(2,1)S(1)}, u32[]{:S(2)}, u32[]{:S(2)}) async-start(bf16[16,40,128]{2,1,0:T(8,128)(2,1)} %bitcast.12), calls=%async_computation.3 | async-start | bytes 327680 | tf_op jit(solution)/shard_map/all_to_all | solution.py:531
  57.9 3.4 %collective-permute-start.3 = (bf16[96,256]{1,0:T(8,128)(2,1)S(1)}, bf16[96,256]{1,0:T(8,128)(2,1)S(1)}, u32[]{:S(2)}, u32[]{:S(2)}) collective-permute-start(bf16[96,256]{1,0:T(8,128)(2,1)S(1)} %get-tuple-element.59), channel_id=1, source_target_pairs={{0,2},{1,3},{2,0},{3,1},{4,6},{5,7},{6,4},{7,5},{8,10},{9,11},{10,... | collective-permute-start | bytes 147464 | tf_op jit(solution)/shard_map/ppermute | solution.py:522

commit v8 on v6

--- a/solution.py
+++ b/solution.py
@@ -15,6 +15,7 @@
 F32 = jnp.float32
 BF16 = jnp.bfloat16
 VMEM_LIMIT = 32 * 1024 * 1024
+FIRST = 2
 
 TAIL_SLOPE = 0.275
 TAIL = (
@@ -130,7 +131,7 @@
         outer, inner = self.here()
         row, column = grid_of(2 * self.outer, 4 * MZ)
         x = 2 * outer + (inner ^ (column // (2 * MZ)))
-        frequency = self.frequency(2 * (row >> 1) + inner)
+        frequency = self.frequency(2 * ((row >> 1) ^ FIRST) + inner)
         quarter = self.wide // 4
         small = cosine_of(x * frequency + quarter * ((row & 1) - (column & 1)), self.wide)
         return self.expanded(small)
@@ -139,7 +140,7 @@
         outer, inner = self.here()
         row, column = grid_of(4, self.outer * 2 * MZ)
         x = 2 * outer + (inner ^ (row >> 1))
-        frequency = self.frequency(2 * (column // (2 * MZ)) + inner)
+        frequency = self.frequency(2 * ((column // (2 * MZ)) ^ FIRST) + inner)
         quarter = self.wide // 4
         small = cosine_of(x * frequency + quarter * ((column & 1) - (row & 1)), self.wide)
         return self.expanded(small).astype(BF16)
@@ -510,7 +511,11 @@
         return lax.ppermute(send, ("wide", "narrow"), pairs)
 
     groups = [
-        [(2 * outer + inner) * narrow + n for outer in range(wide // 2) for n in range(narrow)]
+        [
+            (2 * (outer ^ FIRST) + inner) * narrow + n
+            for outer in range(wide // 2)
+            for n in range(narrow)
+        ]
         for inner in range(2)
     ]
 

time: 62.3 us -> 60 us (0.963)
  blocking collectives: 19.8 us -> 17.7 us
  waiting for transfers between devices: 8.83 us -> 7.54 us
  starting transfers between devices: 17.1 us -> 18.1 us
    all_to_all x2, blocking collectives: 19.8 us -> 17.7 us  [exchange(): lax.all_to_all(pieces, ('wide', 'narrow'), 0, 0, axis_index_groups=groups...]
    ppermute x4, starting transfers between devices: 5.29 us -> 6.62 us  [to_twin(): return lax.ppermute(send, ('wide', 'narrow'), pairs)]
    all_to_all x2, waiting for transfers between devices: 7.17 us -> 5.87 us  [exchange(): lax.all_to_all(pieces, ('wide', 'narrow'), 0, 0, axis_index_groups=groups...]
  transfers between devices with their start and end apart: 6 -> 6, of which waited for: 6 -> 6; matrix products, arithmetic and copies ran while one was open for 1% -> 1% of each run, Pallas kernels for 8% -> 9%
where the time goes in v8:
time: 60 us; the launch traced here: 59.3 us
  starting transfers between devices  18.1 us (30%)
  blocking collectives  17.7 us (30%)
  Pallas kernels  11.7 us (20%)
  waiting for transfers between devices  7.54 us (13%)
  local copies, waits for them, and re-layouts  3.37 us (6%)
  between operations  0.74 us (1%)
    all_to_all x2, blocking collectives, exchange(): lax.all_to_all(pieces, ('wide', 'narrow'), 0, 0, axis_index_groups=groups...  17.7 us
    all_to_all x2, starting transfers between devices, exchange(): lax.all_to_all(pieces, ('wide', 'narrow'), 0, 0, axis_index_groups=groups...  11.5 us
    ppermute x4, starting transfers between devices, to_twin(): return lax.ppermute(send, ('wide', 'narrow'), pairs)  6.62 us
    all_to_all x2, waiting for transfers between devices, exchange(): lax.all_to_all(pieces, ('wide', 'narrow'), 0, 0, axis_index_groups=groups...  5.87 us
    pallas_call x1, Pallas kernels, body(): pl.pallas_call(outer_kernel, grid=(modes // some,), in_specs=[pl.BlockSpe...  3.55 us
    unnamed x20, local copies, waits for them, and re-layouts  3.06 us
    pallas_call x1, Pallas kernels, body(): run(back_kernel, [((mode_lines, channels), F32), shared], 'back')  1.67 us
    ppermute x4, waiting for transfers between devices, to_twin(): return lax.ppermute(send, ('wide', 'narrow'), pairs)  1.66 us
  transfers between devices with their start and end apart: 6, of which 6 were waited for; matrix products, arithmetic and copies ran while one was open for 1% of the time, Pallas kernels for 9%

profile of v8, /device:TPU:1, one launch (start us, length us, event | category | flops | bytes accessed | tf_op | source)
XLA Modules:
  0.0 59.3 jit_solution(346096171466744754)
XLA Ops:
  0.6 0.0 copy-start.1
  0.6 0.0 copy-start.2
  0.7 0.1 collective-permute-start
  0.8 0.0 copy-start.3
  0.8 0.8 %copy-done.3 = bf16[1,32,8,128]{3,2,1,0:T(8,128)(2,1)S(1)} copy-done((bf16[1,32,8,128]{3,2,1,0:T(8,128)(2,1)S(1)}, bf16[1,32,8,128]{3,2,1,0:T(8,128)(2,1)}, u32[]{:S(2)}) %copy-start.3) | copy-done | bytes 65560
  1.6 0.0 copy-start.7
  1.6 0.0 copy-start.9
  1.6 0.0 copy-start.8
  1.6 0.0 copy-start.4
  1.6 0.0 copy-start.5
  1.6 0.0 copy-start.6
  1.7 0.3 own.1
  2.0 0.2 collective-permute-done.twin_ref
  2.2 1.2 %start.1 = bf16[256,256]{1,0:T(8,128)(2,1)} custom-call(bf16[32,256]{1,0:T(8,128)(2,1)S(1)} %get-tuple-element.35.spectra_ref, bf16[256,128]{1,0:T(8,128)(2,1)S(1)} %collective-permute-done.twin_ref), custom_call_target="tpu_custom_call" | custom-call | flops 4194304 | bytes 524288 | tf_op jit(solution)/shard_map/start/pallas_call | solution.py:543
  3.4 8.0 %all-to-all-start = ((bf16[16,16,256]{2,1,0:T(8,128)(2,1)}), bf16[16,16,256]{2,1,0:T(8,128)(2,1)S(1)}, u32[]{:S(2)}, u32[]{:S(2)}) async-start(bf16[16,16,256]{2,1,0:T(8,128)(2,1)} %bitcast.1), calls=%async_computation | async-start | bytes 262144 | tf_op jit(solution)/shard_map/all_to_all | solution.py:524
  11.4 0.0 copy-start
  11.4 2.2 %copy-done = f32[16,8,2,32,32]{4,3,2,1,0:T(8,128)S(1)} copy-done((f32[16,8,2,32,32]{4,3,2,1,0:T(8,128)S(1)}, f32[16,8,2,32,32]{4,3,2,1,0:T(8,128)}, u32[]{:S(2)}) %copy-start) | copy-done | bytes 1048600
  13.6 0.5 pack.1.weight_ref
  14.1 3.2 %all-to-all-done = bf16[16,16,256]{2,1,0:T(8,128)(2,1)S(1)} async-done(((bf16[16,16,256]{2,1,0:T(8,128)(2,1)}), bf16[16,16,256]{2,1,0:T(8,128)(2,1)S(1)}, u32[]{:S(2)}, u32[]{:S(2)}) %all-to-all-start) | async-done | bytes 131104 | tf_op jit(solution)/shard_map/all_to_all | solution.py:524
  17.3 0.0 copy-done.1
  17.3 0.0 copy-done.2
  17.3 0.9 %mode.1 = (f32[256,32]{1,0:T(8,128)S(1)}, bf16[256,256]{1,0:T(8,128)(2,1)S(1)}) custom-call(bf16[256,256]{1,0:T(8,128)(2,1)S(1)} %bitcast.23, bf16[256,256]{1,0:T(8,128)(2,1)S(1)} %copy-done.1, bf16[256,256]{1,0:T(8,128)(2,1)S(1)} %copy-done.2, bf16[4,256,256]{2,1,0:T(8,128)(2,1)S(1)} %pack.1.weight_ref), custom_call_target="tpu_custom_call" | custom-call | flops 4194304 | bytes 524288 | tf_op jit(solution)/shard_map/mode/pallas_call | solution.py:546
  18.2 8.9 %all_to_all.20 = bf16[16,16,256]{2,1,0:T(8,128)(2,1)S(1)} all-to-all(bf16[16,16,256]{2,1,0:T(8,128)(2,1)S(1)} %bitcast.27), channel_id=1, replica_groups={{8,9,12,13,0,1,4,5,24,25,28,29,16,17,20,21},{10,11,14,15,2,3,6,7,26,27,..., dimensions={0} | all-to-all | bytes 262144 | tf_op jit(solution)/shard_map/all_to_all | solution.py:524
  27.1 0.2 part.2
  27.3 3.0 %collective-permute-start.1 = (bf16[32,256]{1,0:T(8,128)(2,1)S(1)}, bf16[32,256]{1,0:T(8,128)(2,1)S(1)}, u32[]{:S(2)}, u32[]{:S(2)}) collective-permute-start(bf16[32,256]{1,0:T(8,128)(2,1)S(1)} %get-tuple-element.38), channel_id=1, source_target_pairs={{0,2},{1,3},{2,0},{3,1},{4,6},{5,7},{6,4},{7,5},{8,10},{9,11},{10,... | collective-permute-start | bytes 49160 | tf_op jit(solution)/shard_map/ppermute | solution.py:511
  30.4 0.0 copy-done.7
  30.4 0.0 copy-done.9
  30.4 0.1 copy.15.mix_bias_ref
  30.4 0.0 copy-done.8
  30.5 0.1 copy.16.refs_6_
  30.6 0.1 copy.17.refs_8_
  30.7 0.0 copy-done.4
  30.7 0.0 copy-done.5
  30.7 0.2 ready.1
  30.9 0.3 collective-permute-done.1.refs_1_
  31.2 0.0 copy-done.6
  31.2 1.2 %cell.1 = (f32[8,128]{1,0:T(8,128)S(1)}, bf16[32,1024]{1,0:T(8,128)(2,1)S(1)}, bf16[32,256]{1,0:T(8,128)(2,1)S(1)}, bf16[32,1024]{1,0:T(8,128)(2,1)S(1)}, bf16[128,1024]{1,0:T(8,128)(2,1)S(1)}) custom-call(f32[32,256]{1,0:T(8,128)S(1)} %get-tuple-element.37.refs_0_, bf16[32,256]{1,0:T(8,128)(2,1)S(1)} %collective-permute-done.1.refs_1_, ...), custom_call_target="tpu_custom_call" | custom-call | flops 4194304 | bytes 524288 | tf_op jit(solution)/shard_map/cell/pallas_call | solution.py:555
  32.4 0.4 collective-permute-start.2
  32.8 0.4 sums.1
  33.2 0.5 collective-permute-done.2.got_ref
  33.6 0.2 fold.1
  33.8 8.9 %all_to_all.21 = bf16[16,40,128]{2,1,0:T(8,128)(2,1)S(1)} all-to-all(bf16[16,40,128]{2,1,0:T(8,128)(2,1)S(1)} %bitcast.21), channel_id=1, replica_groups={{8,9,12,13,0,1,4,5,24,25,28,29,16,17,20,21},{10,11,14,15,2,3,6,7,26,27,..., dimensions={0} | all-to-all | bytes 327680 | tf_op jit(solution)/shard_map/all_to_all | solution.py:524
  42.7 1.7 %back.1 = (f32[256,32]{1,0:T(8,128)S(1)}, bf16[640,128]{1,0:T(8,128)(2,1)}) custom-call(bf16[640,128]{1,0:T(8,128)(2,1)S(1)} %bitcast.22, bf16[256,256]{1,0:T(8,128)(2,1)S(1)} %copy-done.1, bf16[256,256]{1,0:T(8,128)(2,1)S(1)} %copy-done.2, bf16[4,256,256]{2,1,0:T(8,128)(2,1)S(1)} %pack.1.weight_ref), custom_call_target="tpu_custom_call" | custom-call | flops 4194304 | bytes 524288 | tf_op jit(solution)/shard_map/back/pallas_call | solution.py:587
  44.4 3.5 %all-to-all-start.3 = ((bf16[16,40,128]{2,1,0:T(8,128)(2,1)}), bf16[16,40,128]{2,1,0:T(8,128)(2,1)S(1)}, u32[]{:S(2)}, u32[]{:S(2)}) async-start(bf16[16,40,128]{2,1,0:T(8,128)(2,1)} %bitcast.12), calls=%async_computation.3 | async-start | bytes 327680 | tf_op jit(solution)/shard_map/all_to_all | solution.py:524
  47.8 3.5 %outer.1 = (f32[16,8,2,32,32]{4,3,2,1,0:T(8,128)}, f32[8,128]{1,0:T(8,128)S(1)}) custom-call(f32[16,16,32]{2,1,0:T(8,128)S(1)} %bitcast.25, f32[16,16,32]{2,1,0:T(8,128)S(1)} %bitcast.26), custom_call_target="tpu_custom_call" | custom-call | flops 4194304 | bytes 5242880 | tf_op jit(solution)/shard_map/outer/pallas_call | solution.py:591
  51.4 2.7 %all-to-all-done.3 = bf16[16,40,128]{2,1,0:T(8,128)(2,1)S(1)} async-done(((bf16[16,40,128]{2,1,0:T(8,128)(2,1)}), bf16[16,40,128]{2,1,0:T(8,128)(2,1)S(1)}, u32[]{:S(2)}, u32[]{:S(2)}) %all-to-all-start.3) | async-done | bytes 163872 | tf_op jit(solution)/shard_map/all_to_all | solution.py:524
  54.1 0.2 part.3
  54.3 3.1 %collective-permute-start.3 = (bf16[96,256]{1,0:T(8,128)(2,1)S(1)}, bf16[96,256]{1,0:T(8,128)(2,1)S(1)}, u32[]{:S(2)}, u32[]{:S(2)}) collective-permute-start(bf16[96,256]{1,0:T(8,128)(2,1)S(1)} %get-tuple-element.54), channel_id=1, source_target_pairs={{0,2},{1,3},{2,0},{3,1},{4,6},{5,7},{6,4},{7,5},{8,10},{9,11},{10,... | collective-permute-start | bytes 147464 | tf_op jit(solution)/shard_map/ppermute | solution.py:511
  57.4 0.2 pointwise.1
  57.6 0.7 %collective-permute-done.3.refs_1_ = bf16[96,256]{1,0:T(8,128)(2,1)S(1)} collective-permute-done((bf16[96,256]{1,0:T(8,128)(2,1)S(1)}, bf16[96,256]{1,0:T(8,128)(2,1)S(1)}, u32[]{:S(2)}, u32[]{:S(2)}) %collective-permute-start.3) | collective-permute-done | bytes 49184 | tf_op jit(solution)/shard_map/ppermute | solution.py:511
  58.3 1.0 %finish.1 = (bf16[256,128]{1,0:T(8,128)(2,1)}, f32[8,128]{1,0:T(8,128)}, f32[32,32]{1,0:T(8,128)}, f32[32,128]{1,0:T(8,128)}) custom-call(f32[32,256]{1,0:T(8,128)S(1)} %get-tuple-element.53.refs_0_, bf16[96,256]{1,0:T(8,128)(2,1)S(1)} %collective-permute-done.3.refs_1_, bf16[32,128]{1,0:T(8,128)(2,1)S(1)} %get-tuple-element.55.refs_2_, ...), custom_call_target="tpu_custom_call" | custom-call | flops 4194304 | bytes 524288 | tf_op jit(solution)/shard_map/finish/pallas_call | solution.py:622
  (1 shorter events, 0.0 us)
Async XLA Ops:
  0.6 16.7 %copy-start.1 = (bf16[256,256]{1,0:T(8,128)(2,1)S(1)}, bf16[256,256]{1,0:T(8,128)(2,1)}, u32[]{:S(2)}) copy-start(bf16[256,256]{1,0:T(8,128)(2,1)} %constant.4.clone.y_forward_ref) | copy-start | bytes 393220
  0.6 16.7 %copy-start.2 = (bf16[256,256]{1,0:T(8,128)(2,1)S(1)}, bf16[256,256]{1,0:T(8,128)(2,1)}, u32[]{:S(2)}) copy-start(bf16[256,256]{1,0:T(8,128)(2,1)} %constant.5.clone.y_inverse_ref) | copy-start | bytes 393220
  0.7 1.5 %collective-permute-start = (bf16[256,128]{1,0:T(8,128)(2,1)}, bf16[256,128]{1,0:T(8,128)(2,1)S(1)}, u32[]{:S(2)}, u32[]{:S(2)}) collective-permute-start(bf16[256,128]{1,0:T(8,128)(2,1)} %bitcast.28), channel_id=1, source_target_pairs={{0,2},{1,3},{2,0},{3,1},{4,6},{5,7},{6,4},{7,5},{8,10},{9,11},{10,... | collective-permute-start | bytes 196616 | tf_op jit(solution)/shard_map/ppermute | solution.py:511
  0.8 0.8 %copy-start.3 = (bf16[1,32,8,128]{3,2,1,0:T(8,128)(2,1)S(1)}, bf16[1,32,8,128]{3,2,1,0:T(8,128)(2,1)}, u32[]{:S(2)}) copy-start(bf16[1,32,8,128]{3,2,1,0:T(8,128)(2,1)} %param.10) | copy-start | bytes 196612
  1.6 28.7 %copy-start.7 = (bf16[128]{0:T(256)(128)(2,1)S(1)}, bf16[128]{0:T(256)(128)(2,1)}, u32[]{:S(2)}) copy-start(bf16[128]{0:T(256)(128)(2,1)} %param.16) | copy-start | bytes 772
  1.6 28.7 %copy-start.9 = (f32[32]{0:T(128)S(1)}, f32[32]{0:T(128)}, u32[]{:S(2)}) copy-start(f32[32]{0:T(128)} %param.13) | copy-start | bytes 388
  1.6 28.8 %copy-start.8 = (f32[128]{0:T(128)S(1)}, f32[128]{0:T(128)}, u32[]{:S(2)}) copy-start(f32[128]{0:T(128)} %param.15) | copy-start | bytes 1540
  1.6 29.1 %copy-start.4 = (bf16[32,128]{1,0:T(8,128)(2,1)S(1)}, bf16[32,128]{1,0:T(8,128)(2,1)}, u32[]{:S(2)}) copy-start(bf16[32,128]{1,0:T(8,128)(2,1)} %refs_4_.1) | copy-start | bytes 24580
  1.6 29.1 %copy-start.5 = (bf16[32,32]{1,0:T(8,128)(2,1)S(1)}, bf16[32,32]{1,0:T(8,128)(2,1)}, u32[]{:S(2)}) copy-start(bf16[32,32]{1,0:T(8,128)(2,1)} %mix_ref.3) | copy-start | bytes 6148
  1.6 29.6 %copy-start.6 = (f32[1,8,128]{2,1,0:T(8,128)S(1)}, f32[1,8,128]{2,1,0:T(8,128)}, u32[]{:S(2)}) copy-start(f32[1,8,128]{2,1,0:T(8,128)} %param.17) | copy-start | bytes 12292
  3.4 13.9 %all-to-all-start = ((bf16[16,16,256]{2,1,0:T(8,128)(2,1)}), bf16[16,16,256]{2,1,0:T(8,128)(2,1)S(1)}, u32[]{:S(2)}, u32[]{:S(2)}) async-start(bf16[16,16,256]{2,1,0:T(8,128)(2,1)} %bitcast.1), calls=%async_computation | async-start | bytes 262144 | tf_op jit(solution)/shard_map/all_to_all | solution.py:524
  11.4 2.2 %copy-start = (f32[16,8,2,32,32]{4,3,2,1,0:T(8,128)S(1)}, f32[16,8,2,32,32]{4,3,2,1,0:T(8,128)}, u32[]{:S(2)}) copy-start(f32[16,8,2,32,32]{4,3,2,1,0:T(8,128)} %weight_ref.1) | copy-start | bytes 3145732
  27.3 3.9 %collective-permute-start.1 = (bf16[32,256]{1,0:T(8,128)(2,1)S(1)}, bf16[32,256]{1,0:T(8,128)(2,1)S(1)}, u32[]{:S(2)}, u32[]{:S(2)}) collective-permute-start(bf16[32,256]{1,0:T(8,128)(2,1)S(1)} %get-tuple-element.38), channel_id=1, source_target_pairs={{0,2},{1,3},{2,0},{3,1},{4,6},{5,7},{6,4},{7,5},{8,10},{9,11},{10,... | collective-permute-start | bytes 49160 | tf_op jit(solution)/shard_map/ppermute | solution.py:511
  32.4 1.2 %collective-permute-start.2 = (bf16[32,256]{1,0:T(8,128)(2,1)S(1)}, bf16[32,256]{1,0:T(8,128)(2,1)S(1)}, u32[]{:S(2)}, u32[]{:S(2)}) collective-permute-start(bf16[32,256]{1,0:T(8,128)(2,1)S(1)} %get-tuple-element.43.own_ref), channel_id=1, source_target_pairs={{0,2},{1,3},{2,0},{3,1},{4,6},{5,7},{6,4},{7,5},{8,10},{9,11},{10,... | collective-permute-start | bytes 49160 | tf_op jit(solution)/shard_map/ppermute | solution.py:511
  44.4 9.7 %all-to-all-start.3 = ((bf16[16,40,128]{2,1,0:T(8,128)(2,1)}), bf16[16,40,128]{2,1,0:T(8,128)(2,1)S(1)}, u32[]{:S(2)}, u32[]{:S(2)}) async-start(bf16[16,40,128]{2,1,0:T(8,128)(2,1)} %bitcast.12), calls=%async_computation.3 | async-start | bytes 327680 | tf_op jit(solution)/shard_map/all_to_all | solution.py:524
  54.3 4.0 %collective-permute-start.3 = (bf16[96,256]{1,0:T(8,128)(2,1)S(1)}, bf16[96,256]{1,0:T(8,128)(2,1)S(1)}, u32[]{:S(2)}, u32[]{:S(2)}) collective-permute-start(bf16[96,256]{1,0:T(8,128)(2,1)S(1)} %get-tuple-element.54), channel_id=1, source_target_pairs={{0,2},{1,3},{2,0},{3,1},{4,6},{5,7},{6,4},{7,5},{8,10},{9,11},{10,... | collective-permute-start | bytes 147464 | tf_op jit(solution)/shard_map/ppermute | solution.py:511

commit v9 on v8

--- a/solution.py
+++ b/solution.py
@@ -106,6 +106,10 @@
         wide = lax.axis_index("wide")
         return wide // 2, wide % 2
 
+    def partner(self, outer, inner, other):
+        half = self.outer // 2
+        return 2 * other + (inner ^ (outer // half) ^ (other // half))
+
     def frequency(self, wide):
         index = (wide * self.modes) // MY
         return jnp.where(index < MX // 2, index, index - MX)
@@ -131,7 +135,7 @@
         outer, inner = self.here()
         row, column = grid_of(2 * self.outer, 4 * MZ)
         x = 2 * outer + (inner ^ (column // (2 * MZ)))
-        frequency = self.frequency(2 * ((row >> 1) ^ FIRST) + inner)
+        frequency = self.frequency(self.partner(outer, inner, (row >> 1) ^ FIRST))
         quarter = self.wide // 4
         small = cosine_of(x * frequency + quarter * ((row & 1) - (column & 1)), self.wide)
         return self.expanded(small)
@@ -140,7 +144,7 @@
         outer, inner = self.here()
         row, column = grid_of(4, self.outer * 2 * MZ)
         x = 2 * outer + (inner ^ (row >> 1))
-        frequency = self.frequency(2 * ((column // (2 * MZ)) ^ FIRST) + inner)
+        frequency = self.frequency(self.partner(outer, inner, (column // (2 * MZ)) ^ FIRST))
         quarter = self.wide // 4
         small = cosine_of(x * frequency + quarter * ((column & 1) - (row & 1)), self.wide)
         return self.expanded(small).astype(BF16)
@@ -512,7 +516,7 @@
 
     groups = [
         [
-            (2 * (outer ^ FIRST) + inner) * narrow + n
+            place.partner(0, inner, outer ^ FIRST) * narrow + n
             for outer in range(wide // 2)
             for n in range(narrow)
         ]

time: 60 us -> 60.9 us (1.015)
  starting transfers between devices: 18.1 us -> 12.9 us
  blocking collectives: 17.7 us -> 21.1 us
  waiting for transfers between devices: 7.54 us -> 10.3 us
    ppermute x4, starting transfers between devices: 6.62 us -> 1.35 us  [to_twin(): return lax.ppermute(send, ('wide', 'narrow'), pairs)]
    all_to_all x2, blocking collectives: 17.7 us -> 21.1 us  [exchange(): lax.all_to_all(pieces, ('wide', 'narrow'), 0, 0, axis_index_groups=groups...]
    all_to_all x2, waiting for transfers between devices: 5.87 us -> 8.66 us  [exchange(): lax.all_to_all(pieces, ('wide', 'narrow'), 0, 0, axis_index_groups=groups...]
where the time goes in v9:
time: 60.9 us; the launch traced here: 60.2 us
  blocking collectives  21.1 us (35%)
  starting transfers between devices  12.9 us (21%)
  Pallas kernels  11.8 us (19%)
  waiting for transfers between devices  10.3 us (17%)
  local copies, waits for them, and re-layouts  3.37 us (6%)
  between operations  0.75 us (1%)
    all_to_all x2, blocking collectives, exchange(): lax.all_to_all(pieces, ('wide', 'narrow'), 0, 0, axis_index_groups=groups...  21.1 us
    all_to_all x2, starting transfers between devices, exchange(): lax.all_to_all(pieces, ('wide', 'narrow'), 0, 0, axis_index_groups=groups...  11.6 us
    all_to_all x2, waiting for transfers between devices, exchange(): lax.all_to_all(pieces, ('wide', 'narrow'), 0, 0, axis_index_groups=groups...  8.66 us
    pallas_call x1, Pallas kernels, body(): pl.pallas_call(outer_kernel, grid=(modes // some,), in_specs=[pl.BlockSpe...  3.55 us
    unnamed x20, local copies, waits for them, and re-layouts  3.06 us
    pallas_call x1, Pallas kernels, body(): run(back_kernel, [((mode_lines, channels), F32), shared], 'back')  1.67 us
    ppermute x4, waiting for transfers between devices, to_twin(): return lax.ppermute(send, ('wide', 'narrow'), pairs)  1.66 us
    ppermute x4, starting transfers between devices, to_twin(): return lax.ppermute(send, ('wide', 'narrow'), pairs)  1.35 us
  transfers between devices with their start and end apart: 6, of which 6 were waited for; matrix products, arithmetic and copies ran while one was open for 1% of the time, Pallas kernels for 9%

profile of v9, /device:TPU:1, one launch (start us, length us, event | category | flops | bytes accessed | tf_op | source)
XLA Modules:
  0.0 60.2 jit_solution(4198234266959077274)
XLA Ops:
  0.6 0.0 copy-start.1
  0.6 0.0 copy-start.2
  0.7 0.1 collective-permute-start
  0.8 0.0 copy-start.3
  0.8 0.8 %copy-done.3 = bf16[1,32,8,128]{3,2,1,0:T(8,128)(2,1)S(1)} copy-done((bf16[1,32,8,128]{3,2,1,0:T(8,128)(2,1)S(1)}, bf16[1,32,8,128]{3,2,1,0:T(8,128)(2,1)}, u32[]{:S(2)}) %copy-start.3) | copy-done | bytes 65560
  1.6 0.0 copy-start.7
  1.6 0.0 copy-start.9
  1.6 0.0 copy-start.8
  1.6 0.0 copy-start.4
  1.6 0.0 copy-start.5
  1.6 0.0 copy-start.6
  1.7 0.3 own.1
  2.0 0.2 collective-permute-done.twin_ref
  2.2 1.2 %start.1 = bf16[256,256]{1,0:T(8,128)(2,1)} custom-call(bf16[32,256]{1,0:T(8,128)(2,1)S(1)} %get-tuple-element.35.spectra_ref, bf16[256,128]{1,0:T(8,128)(2,1)S(1)} %collective-permute-done.twin_ref), custom_call_target="tpu_custom_call" | custom-call | flops 4194304 | bytes 524288 | tf_op jit(solution)/shard_map/start/pallas_call | solution.py:547
  3.4 8.2 %all-to-all-start = ((bf16[16,16,256]{2,1,0:T(8,128)(2,1)}), bf16[16,16,256]{2,1,0:T(8,128)(2,1)S(1)}, u32[]{:S(2)}, u32[]{:S(2)}) async-start(bf16[16,16,256]{2,1,0:T(8,128)(2,1)} %bitcast.1), calls=%async_computation | async-start | bytes 262144 | tf_op jit(solution)/shard_map/all_to_all | solution.py:528
  11.6 0.0 copy-start
  11.6 2.2 %copy-done = f32[16,8,2,32,32]{4,3,2,1,0:T(8,128)S(1)} copy-done((f32[16,8,2,32,32]{4,3,2,1,0:T(8,128)S(1)}, f32[16,8,2,32,32]{4,3,2,1,0:T(8,128)}, u32[]{:S(2)}) %copy-start) | copy-done | bytes 1048600
  13.8 0.5 pack.1.weight_ref
  14.3 4.4 %all-to-all-done = bf16[16,16,256]{2,1,0:T(8,128)(2,1)S(1)} async-done(((bf16[16,16,256]{2,1,0:T(8,128)(2,1)}), bf16[16,16,256]{2,1,0:T(8,128)(2,1)S(1)}, u32[]{:S(2)}, u32[]{:S(2)}) %all-to-all-start) | async-done | bytes 131104 | tf_op jit(solution)/shard_map/all_to_all | solution.py:528
  18.7 0.0 copy-done.1
  18.7 0.0 copy-done.2
  18.7 0.9 %mode.1 = (f32[256,32]{1,0:T(8,128)S(1)}, bf16[256,256]{1,0:T(8,128)(2,1)S(1)}) custom-call(bf16[256,256]{1,0:T(8,128)(2,1)S(1)} %bitcast.23, bf16[256,256]{1,0:T(8,128)(2,1)S(1)} %copy-done.1, bf16[256,256]{1,0:T(8,128)(2,1)S(1)} %copy-done.2, bf16[4,256,256]{2,1,0:T(8,128)(2,1)S(1)} %pack.1.weight_ref), custom_call_target="tpu_custom_call" | custom-call | flops 4194304 | bytes 524288 | tf_op jit(solution)/shard_map/mode/pallas_call | solution.py:550
  19.6 10.2 %all_to_all.20 = bf16[16,16,256]{2,1,0:T(8,128)(2,1)S(1)} all-to-all(bf16[16,16,256]{2,1,0:T(8,128)(2,1)S(1)} %bitcast.27), channel_id=1, replica_groups={{8,9,12,13,0,1,4,5,26,27,30,31,18,19,22,23},{10,11,14,15,2,3,6,7,24,25,..., dimensions={0} | all-to-all | bytes 262144 | tf_op jit(solution)/shard_map/all_to_all | solution.py:528
  29.8 0.2 part.2
  30.0 0.4 collective-permute-start.1
  30.4 0.0 copy-done.7
  30.4 0.0 copy-done.9
  30.4 0.1 copy.15.mix_bias_ref
  30.5 0.0 copy-done.8
  30.5 0.1 copy.16.refs_6_
  30.6 0.1 copy.17.refs_8_
  30.7 0.0 copy-done.4
  30.7 0.0 copy-done.5
  30.7 0.2 ready.1
  30.9 0.3 collective-permute-done.1.refs_1_
  31.2 0.0 copy-done.6
  31.2 1.2 %cell.1 = (f32[8,128]{1,0:T(8,128)S(1)}, bf16[32,1024]{1,0:T(8,128)(2,1)S(1)}, bf16[32,256]{1,0:T(8,128)(2,1)S(1)}, bf16[32,1024]{1,0:T(8,128)(2,1)S(1)}, bf16[128,1024]{1,0:T(8,128)(2,1)S(1)}) custom-call(f32[32,256]{1,0:T(8,128)S(1)} %get-tuple-element.37.refs_0_, bf16[32,256]{1,0:T(8,128)(2,1)S(1)} %collective-permute-done.1.refs_1_, ...), custom_call_target="tpu_custom_call" | custom-call | flops 4194304 | bytes 524288 | tf_op jit(solution)/shard_map/cell/pallas_call | solution.py:559
  32.5 0.4 collective-permute-start.2
  32.9 0.4 sums.1
  33.2 0.5 collective-permute-done.2.got_ref
  33.7 0.2 fold.1
  33.9 10.9 %all_to_all.21 = bf16[16,40,128]{2,1,0:T(8,128)(2,1)S(1)} all-to-all(bf16[16,40,128]{2,1,0:T(8,128)(2,1)S(1)} %bitcast.21), channel_id=1, replica_groups={{8,9,12,13,0,1,4,5,26,27,30,31,18,19,22,23},{10,11,14,15,2,3,6,7,24,25,..., dimensions={0} | all-to-all | bytes 327680 | tf_op jit(solution)/shard_map/all_to_all | solution.py:528
  44.7 1.7 %back.1 = (f32[256,32]{1,0:T(8,128)S(1)}, bf16[640,128]{1,0:T(8,128)(2,1)}) custom-call(bf16[640,128]{1,0:T(8,128)(2,1)S(1)} %bitcast.22, bf16[256,256]{1,0:T(8,128)(2,1)S(1)} %copy-done.1, bf16[256,256]{1,0:T(8,128)(2,1)S(1)} %copy-done.2, bf16[4,256,256]{2,1,0:T(8,128)(2,1)S(1)} %pack.1.weight_ref), custom_call_target="tpu_custom_call" | custom-call | flops 4194304 | bytes 524288 | tf_op jit(solution)/shard_map/back/pallas_call | solution.py:591
  46.4 3.4 %all-to-all-start.3 = ((bf16[16,40,128]{2,1,0:T(8,128)(2,1)}), bf16[16,40,128]{2,1,0:T(8,128)(2,1)S(1)}, u32[]{:S(2)}, u32[]{:S(2)}) async-start(bf16[16,40,128]{2,1,0:T(8,128)(2,1)} %bitcast.12), calls=%async_computation.3 | async-start | bytes 327680 | tf_op jit(solution)/shard_map/all_to_all | solution.py:528
  49.8 3.6 %outer.1 = (f32[16,8,2,32,32]{4,3,2,1,0:T(8,128)}, f32[8,128]{1,0:T(8,128)S(1)}) custom-call(f32[16,16,32]{2,1,0:T(8,128)S(1)} %bitcast.25, f32[16,16,32]{2,1,0:T(8,128)S(1)} %bitcast.26), custom_call_target="tpu_custom_call" | custom-call | flops 4194304 | bytes 5242880 | tf_op jit(solution)/shard_map/outer/pallas_call | solution.py:595
  53.4 4.3 %all-to-all-done.3 = bf16[16,40,128]{2,1,0:T(8,128)(2,1)S(1)} async-done(((bf16[16,40,128]{2,1,0:T(8,128)(2,1)}), bf16[16,40,128]{2,1,0:T(8,128)(2,1)S(1)}, u32[]{:S(2)}, u32[]{:S(2)}) %all-to-all-start.3) | async-done | bytes 163872 | tf_op jit(solution)/shard_map/all_to_all | solution.py:528
  57.6 0.2 part.3
  57.9 0.5 collective-permute-start.3
  58.3 0.2 pointwise.1
  58.6 0.7 %collective-permute-done.3.refs_1_ = bf16[96,256]{1,0:T(8,128)(2,1)S(1)} collective-permute-done((bf16[96,256]{1,0:T(8,128)(2,1)S(1)}, bf16[96,256]{1,0:T(8,128)(2,1)S(1)}, u32[]{:S(2)}, u32[]{:S(2)}) %collective-permute-start.3) | collective-permute-done | bytes 49184 | tf_op jit(solution)/shard_map/ppermute | solution.py:515
  59.2 1.0 %finish.1 = (bf16[256,128]{1,0:T(8,128)(2,1)}, f32[8,128]{1,0:T(8,128)}, f32[32,32]{1,0:T(8,128)}, f32[32,128]{1,0:T(8,128)}) custom-call(f32[32,256]{1,0:T(8,128)S(1)} %get-tuple-element.53.refs_0_, bf16[96,256]{1,0:T(8,128)(2,1)S(1)} %collective-permute-done.3.refs_1_, bf16[32,128]{1,0:T(8,128)(2,1)S(1)} %get-tuple-element.55.refs_2_, ...), custom_call_target="tpu_custom_call" | custom-call | flops 4194304 | bytes 524288 | tf_op jit(solution)/shard_map/finish/pallas_call | solution.py:626
  (1 shorter events, 0.0 us)
Async XLA Ops:
  0.6 18.0 %copy-start.1 = (bf16[256,256]{1,0:T(8,128)(2,1)S(1)}, bf16[256,256]{1,0:T(8,128)(2,1)}, u32[]{:S(2)}) copy-start(bf16[256,256]{1,0:T(8,128)(2,1)} %constant.4.clone.y_forward_ref) | copy-start | bytes 393220
  0.6 18.0 %copy-start.2 = (bf16[256,256]{1,0:T(8,128)(2,1)S(1)}, bf16[256,256]{1,0:T(8,128)(2,1)}, u32[]{:S(2)}) copy-start(bf16[256,256]{1,0:T(8,128)(2,1)} %constant.5.clone.y_inverse_ref) | copy-start | bytes 393220
  0.7 1.5 %collective-permute-start = (bf16[256,128]{1,0:T(8,128)(2,1)}, bf16[256,128]{1,0:T(8,128)(2,1)S(1)}, u32[]{:S(2)}, u32[]{:S(2)}) collective-permute-start(bf16[256,128]{1,0:T(8,128)(2,1)} %bitcast.28), channel_id=1, source_target_pairs={{0,2},{1,3},{2,0},{3,1},{4,6},{5,7},{6,4},{7,5},{8,10},{9,11},{10,... | collective-permute-start | bytes 196616 | tf_op jit(solution)/shard_map/ppermute | solution.py:515
  0.8 0.8 %copy-start.3 = (bf16[1,32,8,128]{3,2,1,0:T(8,128)(2,1)S(1)}, bf16[1,32,8,128]{3,2,1,0:T(8,128)(2,1)}, u32[]{:S(2)}) copy-start(bf16[1,32,8,128]{3,2,1,0:T(8,128)(2,1)} %param.10) | copy-start | bytes 196612
  1.6 28.8 %copy-start.7 = (bf16[128]{0:T(256)(128)(2,1)S(1)}, bf16[128]{0:T(256)(128)(2,1)}, u32[]{:S(2)}) copy-start(bf16[128]{0:T(256)(128)(2,1)} %param.16) | copy-start | bytes 772
  1.6 28.8 %copy-start.9 = (f32[32]{0:T(128)S(1)}, f32[32]{0:T(128)}, u32[]{:S(2)}) copy-start(f32[32]{0:T(128)} %param.13) | copy-start | bytes 388
  1.6 28.9 %copy-start.8 = (f32[128]{0:T(128)S(1)}, f32[128]{0:T(128)}, u32[]{:S(2)}) copy-start(f32[128]{0:T(128)} %param.15) | copy-start | bytes 1540
  1.6 29.1 %copy-start.4 = (bf16[32,128]{1,0:T(8,128)(2,1)S(1)}, bf16[32,128]{1,0:T(8,128)(2,1)}, u32[]{:S(2)}) copy-start(bf16[32,128]{1,0:T(8,128)(2,1)} %refs_4_.1) | copy-start | bytes 24580
  1.6 29.1 %copy-start.5 = (bf16[32,32]{1,0:T(8,128)(2,1)S(1)}, bf16[32,32]{1,0:T(8,128)(2,1)}, u32[]{:S(2)}) copy-start(bf16[32,32]{1,0:T(8,128)(2,1)} %mix_ref.3) | copy-start | bytes 6148
  1.6 29.6 %copy-start.6 = (f32[1,8,128]{2,1,0:T(8,128)S(1)}, f32[1,8,128]{2,1,0:T(8,128)}, u32[]{:S(2)}) copy-start(f32[1,8,128]{2,1,0:T(8,128)} %param.17) | copy-start | bytes 12292
  3.4 15.3 %all-to-all-start = ((bf16[16,16,256]{2,1,0:T(8,128)(2,1)}), bf16[16,16,256]{2,1,0:T(8,128)(2,1)S(1)}, u32[]{:S(2)}, u32[]{:S(2)}) async-start(bf16[16,16,256]{2,1,0:T(8,128)(2,1)} %bitcast.1), calls=%async_computation | async-start | bytes 262144 | tf_op jit(solution)/shard_map/all_to_all | solution.py:528
  11.6 2.2 %copy-start = (f32[16,8,2,32,32]{4,3,2,1,0:T(8,128)S(1)}, f32[16,8,2,32,32]{4,3,2,1,0:T(8,128)}, u32[]{:S(2)}) copy-start(f32[16,8,2,32,32]{4,3,2,1,0:T(8,128)} %weight_ref.1) | copy-start | bytes 3145732
  30.0 1.2 %collective-permute-start.1 = (bf16[32,256]{1,0:T(8,128)(2,1)S(1)}, bf16[32,256]{1,0:T(8,128)(2,1)S(1)}, u32[]{:S(2)}, u32[]{:S(2)}) collective-permute-start(bf16[32,256]{1,0:T(8,128)(2,1)S(1)} %get-tuple-element.38), channel_id=1, source_target_pairs={{0,2},{1,3},{2,0},{3,1},{4,6},{5,7},{6,4},{7,5},{8,10},{9,11},{10,... | collective-permute-start | bytes 49160 | tf_op jit(solution)/shard_map/ppermute | solution.py:515
  32.5 1.2 %collective-permute-start.2 = (bf16[32,256]{1,0:T(8,128)(2,1)S(1)}, bf16[32,256]{1,0:T(8,128)(2,1)S(1)}, u32[]{:S(2)}, u32[]{:S(2)}) collective-permute-start(bf16[32,256]{1,0:T(8,128)(2,1)S(1)} %get-tuple-element.43.own_ref), channel_id=1, source_target_pairs={{0,2},{1,3},{2,0},{3,1},{4,6},{5,7},{6,4},{7,5},{8,10},{9,11},{10,... | collective-permute-start | bytes 49160 | tf_op jit(solution)/shard_map/ppermute | solution.py:515
  46.4 11.2 %all-to-all-start.3 = ((bf16[16,40,128]{2,1,0:T(8,128)(2,1)}), bf16[16,40,128]{2,1,0:T(8,128)(2,1)S(1)}, u32[]{:S(2)}, u32[]{:S(2)}) async-start(bf16[16,40,128]{2,1,0:T(8,128)(2,1)} %bitcast.12), calls=%async_computation.3 | async-start | bytes 327680 | tf_op jit(solution)/shard_map/all_to_all | solution.py:528
  57.9 1.3 %collective-permute-start.3 = (bf16[96,256]{1,0:T(8,128)(2,1)S(1)}, bf16[96,256]{1,0:T(8,128)(2,1)S(1)}, u32[]{:S(2)}, u32[]{:S(2)}) collective-permute-start(bf16[96,256]{1,0:T(8,128)(2,1)S(1)} %get-tuple-element.54), channel_id=1, source_target_pairs={{0,2},{1,3},{2,0},{3,1},{4,6},{5,7},{6,4},{7,5},{8,10},{9,11},{10,... | collective-permute-start | bytes 147464 | tf_op jit(solution)/shard_map/ppermute | solution.py:515

commit v10 on v8

--- a/solution.py
+++ b/solution.py
@@ -15,7 +15,7 @@
 F32 = jnp.float32
 BF16 = jnp.bfloat16
 VMEM_LIMIT = 32 * 1024 * 1024
-FIRST = 2
+FIRST = 4
 
 TAIL_SLOPE = 0.275
 TAIL = (

time: 60 us -> 58.6 us (0.977)
  waiting for transfers between devices: 7.54 us -> 4.93 us
  starting transfers between devices: 18.1 us -> 19.6 us
    all_to_all x2, waiting for transfers between devices: 5.87 us -> 3.27 us  [exchange(): lax.all_to_all(pieces, ('wide', 'narrow'), 0, 0, axis_index_groups=groups...]
    all_to_all x2, starting transfers between devices: 11.5 us -> 12.8 us  [exchange(): lax.all_to_all(pieces, ('wide', 'narrow'), 0, 0, axis_index_groups=groups...]
where the time goes in v10:
time: 58.6 us; the launch traced here: 57.9 us
  starting transfers between devices  19.6 us (33%)
  blocking collectives  17.5 us (30%)
  Pallas kernels  11.7 us (20%)
  waiting for transfers between devices  4.93 us (8%)
  local copies, waits for them, and re-layouts  3.37 us (6%)
  between operations  0.74 us (1%)
    all_to_all x2, blocking collectives, exchange(): lax.all_to_all(pieces, ('wide', 'narrow'), 0, 0, axis_index_groups=groups...  17.5 us
    all_to_all x2, starting transfers between devices, exchange(): lax.all_to_all(pieces, ('wide', 'narrow'), 0, 0, axis_index_groups=groups...  12.8 us
    ppermute x4, starting transfers between devices, to_twin(): return lax.ppermute(send, ('wide', 'narrow'), pairs)  6.85 us
    pallas_call x1, Pallas kernels, body(): pl.pallas_call(outer_kernel, grid=(modes // some,), in_specs=[pl.BlockSpe...  3.55 us
    all_to_all x2, waiting for transfers between devices, exchange(): lax.all_to_all(pieces, ('wide', 'narrow'), 0, 0, axis_index_groups=groups...  3.27 us
    unnamed x20, local copies, waits for them, and re-layouts  3.06 us
    pallas_call x1, Pallas kernels, body(): run(back_kernel, [((mode_lines, channels), F32), shared], 'back')  1.67 us
    ppermute x4, waiting for transfers between devices, to_twin(): return lax.ppermute(send, ('wide', 'narrow'), pairs)  1.66 us
  transfers between devices with their start and end apart: 6, of which 6 were waited for; matrix products, arithmetic and copies ran while one was open for 1% of the time, Pallas kernels for 9%

profile of v10, /device:TPU:1, one launch (start us, length us, event | category | flops | bytes accessed | tf_op | source)
XLA Modules:
  0.0 57.9 jit_solution(8207769167388809907)
XLA Ops:
  0.6 0.0 copy-start.1
  0.6 0.0 copy-start.2
  0.7 0.1 collective-permute-start
  0.8 0.0 copy-start.3
  0.8 0.8 %copy-done.3 = bf16[1,32,8,128]{3,2,1,0:T(8,128)(2,1)S(1)} copy-done((bf16[1,32,8,128]{3,2,1,0:T(8,128)(2,1)S(1)}, bf16[1,32,8,128]{3,2,1,0:T(8,128)(2,1)}, u32[]{:S(2)}) %copy-start.3) | copy-done | bytes 65560
  1.6 0.0 copy-start.7
  1.6 0.0 copy-start.9
  1.6 0.0 copy-start.8
  1.6 0.0 copy-start.4
  1.6 0.0 copy-start.5
  1.6 0.0 copy-start.6
  1.7 0.3 own.1
  2.0 0.2 collective-permute-done.twin_ref
  2.2 1.2 %start.1 = bf16[256,256]{1,0:T(8,128)(2,1)} custom-call(bf16[32,256]{1,0:T(8,128)(2,1)S(1)} %get-tuple-element.35.spectra_ref, bf16[256,128]{1,0:T(8,128)(2,1)S(1)} %collective-permute-done.twin_ref), custom_call_target="tpu_custom_call" | custom-call | flops 4194304 | bytes 524288 | tf_op jit(solution)/shard_map/start/pallas_call | solution.py:543
  3.4 8.0 %all-to-all-start = ((bf16[16,16,256]{2,1,0:T(8,128)(2,1)}), bf16[16,16,256]{2,1,0:T(8,128)(2,1)S(1)}, u32[]{:S(2)}, u32[]{:S(2)}) async-start(bf16[16,16,256]{2,1,0:T(8,128)(2,1)} %bitcast.1), calls=%async_computation | async-start | bytes 262144 | tf_op jit(solution)/shard_map/all_to_all | solution.py:524
  11.4 0.0 copy-start
  11.4 2.2 %copy-done = f32[16,8,2,32,32]{4,3,2,1,0:T(8,128)S(1)} copy-done((f32[16,8,2,32,32]{4,3,2,1,0:T(8,128)S(1)}, f32[16,8,2,32,32]{4,3,2,1,0:T(8,128)}, u32[]{:S(2)}) %copy-start) | copy-done | bytes 1048600
  13.6 0.5 pack.1.weight_ref
  14.1 2.0 %all-to-all-done = bf16[16,16,256]{2,1,0:T(8,128)(2,1)S(1)} async-done(((bf16[16,16,256]{2,1,0:T(8,128)(2,1)}), bf16[16,16,256]{2,1,0:T(8,128)(2,1)S(1)}, u32[]{:S(2)}, u32[]{:S(2)}) %all-to-all-start) | async-done | bytes 131104 | tf_op jit(solution)/shard_map/all_to_all | solution.py:524
  16.1 0.0 copy-done.1
  16.1 0.0 copy-done.2
  16.1 0.9 %mode.1 = (f32[256,32]{1,0:T(8,128)S(1)}, bf16[256,256]{1,0:T(8,128)(2,1)S(1)}) custom-call(bf16[256,256]{1,0:T(8,128)(2,1)S(1)} %bitcast.23, bf16[256,256]{1,0:T(8,128)(2,1)S(1)} %copy-done.1, bf16[256,256]{1,0:T(8,128)(2,1)S(1)} %copy-done.2, bf16[4,256,256]{2,1,0:T(8,128)(2,1)S(1)} %pack.1.weight_ref), custom_call_target="tpu_custom_call" | custom-call | flops 4194304 | bytes 524288 | tf_op jit(solution)/shard_map/mode/pallas_call | solution.py:546
  17.0 8.7 %all_to_all.20 = bf16[16,16,256]{2,1,0:T(8,128)(2,1)S(1)} all-to-all(bf16[16,16,256]{2,1,0:T(8,128)(2,1)S(1)} %bitcast.27), channel_id=1, replica_groups={{16,17,20,21,24,25,28,29,0,1,4,5,8,9,12,13},{18,19,22,23,26,27,30,31,2,..., dimensions={0} | all-to-all | bytes 262144 | tf_op jit(solution)/shard_map/all_to_all | solution.py:524
  25.7 0.2 part.2
  25.9 3.2 %collective-permute-start.1 = (bf16[32,256]{1,0:T(8,128)(2,1)S(1)}, bf16[32,256]{1,0:T(8,128)(2,1)S(1)}, u32[]{:S(2)}, u32[]{:S(2)}) collective-permute-start(bf16[32,256]{1,0:T(8,128)(2,1)S(1)} %get-tuple-element.38), channel_id=1, source_target_pairs={{0,2},{1,3},{2,0},{3,1},{4,6},{5,7},{6,4},{7,5},{8,10},{9,11},{10,... | collective-permute-start | bytes 49160 | tf_op jit(solution)/shard_map/ppermute | solution.py:511
  29.1 0.0 copy-done.7
  29.1 0.0 copy-done.9
  29.1 0.1 copy.15.mix_bias_ref
  29.2 0.0 copy-done.8
  29.2 0.1 copy.16.refs_6_
  29.3 0.1 copy.17.refs_8_
  29.4 0.0 copy-done.4
  29.4 0.0 copy-done.5
  29.4 0.2 ready.1
  29.6 0.3 collective-permute-done.1.refs_1_
  29.9 0.0 copy-done.6
  29.9 1.2 %cell.1 = (f32[8,128]{1,0:T(8,128)S(1)}, bf16[32,1024]{1,0:T(8,128)(2,1)S(1)}, bf16[32,256]{1,0:T(8,128)(2,1)S(1)}, bf16[32,1024]{1,0:T(8,128)(2,1)S(1)}, bf16[128,1024]{1,0:T(8,128)(2,1)S(1)}) custom-call(f32[32,256]{1,0:T(8,128)S(1)} %get-tuple-element.37.refs_0_, bf16[32,256]{1,0:T(8,128)(2,1)S(1)} %collective-permute-done.1.refs_1_, ...), custom_call_target="tpu_custom_call" | custom-call | flops 4194304 | bytes 524288 | tf_op jit(solution)/shard_map/cell/pallas_call | solution.py:555
  31.2 0.4 collective-permute-start.2
  31.6 0.4 sums.1
  31.9 0.5 collective-permute-done.2.got_ref
  32.4 0.2 fold.1
  32.6 8.8 %all_to_all.21 = bf16[16,40,128]{2,1,0:T(8,128)(2,1)S(1)} all-to-all(bf16[16,40,128]{2,1,0:T(8,128)(2,1)S(1)} %bitcast.21), channel_id=1, replica_groups={{16,17,20,21,24,25,28,29,0,1,4,5,8,9,12,13},{18,19,22,23,26,27,30,31,2,..., dimensions={0} | all-to-all | bytes 327680 | tf_op jit(solution)/shard_map/all_to_all | solution.py:524
  41.4 1.7 %back.1 = (f32[256,32]{1,0:T(8,128)S(1)}, bf16[640,128]{1,0:T(8,128)(2,1)}) custom-call(bf16[640,128]{1,0:T(8,128)(2,1)S(1)} %bitcast.22, bf16[256,256]{1,0:T(8,128)(2,1)S(1)} %copy-done.1, bf16[256,256]{1,0:T(8,128)(2,1)S(1)} %copy-done.2, bf16[4,256,256]{2,1,0:T(8,128)(2,1)S(1)} %pack.1.weight_ref), custom_call_target="tpu_custom_call" | custom-call | flops 4194304 | bytes 524288 | tf_op jit(solution)/shard_map/back/pallas_call | solution.py:587
  43.1 4.8 %all-to-all-start.3 = ((bf16[16,40,128]{2,1,0:T(8,128)(2,1)}), bf16[16,40,128]{2,1,0:T(8,128)(2,1)S(1)}, u32[]{:S(2)}, u32[]{:S(2)}) async-start(bf16[16,40,128]{2,1,0:T(8,128)(2,1)} %bitcast.12), calls=%async_computation.3 | async-start | bytes 327680 | tf_op jit(solution)/shard_map/all_to_all | solution.py:524
  47.8 3.5 %outer.1 = (f32[16,8,2,32,32]{4,3,2,1,0:T(8,128)}, f32[8,128]{1,0:T(8,128)S(1)}) custom-call(f32[16,16,32]{2,1,0:T(8,128)S(1)} %bitcast.25, f32[16,16,32]{2,1,0:T(8,128)S(1)} %bitcast.26), custom_call_target="tpu_custom_call" | custom-call | flops 4194304 | bytes 5242880 | tf_op jit(solution)/shard_map/outer/pallas_call | solution.py:591
  51.4 1.3 %all-to-all-done.3 = bf16[16,40,128]{2,1,0:T(8,128)(2,1)S(1)} async-done(((bf16[16,40,128]{2,1,0:T(8,128)(2,1)}), bf16[16,40,128]{2,1,0:T(8,128)(2,1)S(1)}, u32[]{:S(2)}, u32[]{:S(2)}) %all-to-all-start.3) | async-done | bytes 163872 | tf_op jit(solution)/shard_map/all_to_all | solution.py:524
  52.7 0.2 part.3
  52.9 3.1 %collective-permute-start.3 = (bf16[96,256]{1,0:T(8,128)(2,1)S(1)}, bf16[96,256]{1,0:T(8,128)(2,1)S(1)}, u32[]{:S(2)}, u32[]{:S(2)}) collective-permute-start(bf16[96,256]{1,0:T(8,128)(2,1)S(1)} %get-tuple-element.54), channel_id=1, source_target_pairs={{0,2},{1,3},{2,0},{3,1},{4,6},{5,7},{6,4},{7,5},{8,10},{9,11},{10,... | collective-permute-start | bytes 147464 | tf_op jit(solution)/shard_map/ppermute | solution.py:511
  56.0 0.2 pointwise.1
  56.2 0.7 %collective-permute-done.3.refs_1_ = bf16[96,256]{1,0:T(8,128)(2,1)S(1)} collective-permute-done((bf16[96,256]{1,0:T(8,128)(2,1)S(1)}, bf16[96,256]{1,0:T(8,128)(2,1)S(1)}, u32[]{:S(2)}, u32[]{:S(2)}) %collective-permute-start.3) | collective-permute-done | bytes 49184 | tf_op jit(solution)/shard_map/ppermute | solution.py:511
  56.9 1.0 %finish.1 = (bf16[256,128]{1,0:T(8,128)(2,1)}, f32[8,128]{1,0:T(8,128)}, f32[32,32]{1,0:T(8,128)}, f32[32,128]{1,0:T(8,128)}) custom-call(f32[32,256]{1,0:T(8,128)S(1)} %get-tuple-element.53.refs_0_, bf16[96,256]{1,0:T(8,128)(2,1)S(1)} %collective-permute-done.3.refs_1_, bf16[32,128]{1,0:T(8,128)(2,1)S(1)} %get-tuple-element.55.refs_2_, ...), custom_call_target="tpu_custom_call" | custom-call | flops 4194304 | bytes 524288 | tf_op jit(solution)/shard_map/finish/pallas_call | solution.py:622
  (1 shorter events, 0.0 us)
Async XLA Ops:
  0.6 15.5 %copy-start.1 = (bf16[256,256]{1,0:T(8,128)(2,1)S(1)}, bf16[256,256]{1,0:T(8,128)(2,1)}, u32[]{:S(2)}) copy-start(bf16[256,256]{1,0:T(8,128)(2,1)} %constant.4.clone.y_forward_ref) | copy-start | bytes 393220
  0.6 15.4 %copy-start.2 = (bf16[256,256]{1,0:T(8,128)(2,1)S(1)}, bf16[256,256]{1,0:T(8,128)(2,1)}, u32[]{:S(2)}) copy-start(bf16[256,256]{1,0:T(8,128)(2,1)} %constant.5.clone.y_inverse_ref) | copy-start | bytes 393220
  0.7 1.5 %collective-permute-start = (bf16[256,128]{1,0:T(8,128)(2,1)}, bf16[256,128]{1,0:T(8,128)(2,1)S(1)}, u32[]{:S(2)}, u32[]{:S(2)}) collective-permute-start(bf16[256,128]{1,0:T(8,128)(2,1)} %bitcast.28), channel_id=1, source_target_pairs={{0,2},{1,3},{2,0},{3,1},{4,6},{5,7},{6,4},{7,5},{8,10},{9,11},{10,... | collective-permute-start | bytes 196616 | tf_op jit(solution)/shard_map/ppermute | solution.py:511
  0.8 0.8 %copy-start.3 = (bf16[1,32,8,128]{3,2,1,0:T(8,128)(2,1)S(1)}, bf16[1,32,8,128]{3,2,1,0:T(8,128)(2,1)}, u32[]{:S(2)}) copy-start(bf16[1,32,8,128]{3,2,1,0:T(8,128)(2,1)} %param.10) | copy-start | bytes 196612
  1.6 27.5 %copy-start.7 = (bf16[128]{0:T(256)(128)(2,1)S(1)}, bf16[128]{0:T(256)(128)(2,1)}, u32[]{:S(2)}) copy-start(bf16[128]{0:T(256)(128)(2,1)} %param.16) | copy-start | bytes 772
  1.6 27.5 %copy-start.9 = (f32[32]{0:T(128)S(1)}, f32[32]{0:T(128)}, u32[]{:S(2)}) copy-start(f32[32]{0:T(128)} %param.13) | copy-start | bytes 388
  1.6 27.6 %copy-start.8 = (f32[128]{0:T(128)S(1)}, f32[128]{0:T(128)}, u32[]{:S(2)}) copy-start(f32[128]{0:T(128)} %param.15) | copy-start | bytes 1540
  1.6 27.8 %copy-start.4 = (bf16[32,128]{1,0:T(8,128)(2,1)S(1)}, bf16[32,128]{1,0:T(8,128)(2,1)}, u32[]{:S(2)}) copy-start(bf16[32,128]{1,0:T(8,128)(2,1)} %refs_4_.1) | copy-start | bytes 24580
  1.6 27.8 %copy-start.5 = (bf16[32,32]{1,0:T(8,128)(2,1)S(1)}, bf16[32,32]{1,0:T(8,128)(2,1)}, u32[]{:S(2)}) copy-start(bf16[32,32]{1,0:T(8,128)(2,1)} %mix_ref.3) | copy-start | bytes 6148
  1.6 28.3 %copy-start.6 = (f32[1,8,128]{2,1,0:T(8,128)S(1)}, f32[1,8,128]{2,1,0:T(8,128)}, u32[]{:S(2)}) copy-start(f32[1,8,128]{2,1,0:T(8,128)} %param.17) | copy-start | bytes 12292
  3.4 12.7 %all-to-all-start = ((bf16[16,16,256]{2,1,0:T(8,128)(2,1)}), bf16[16,16,256]{2,1,0:T(8,128)(2,1)S(1)}, u32[]{:S(2)}, u32[]{:S(2)}) async-start(bf16[16,16,256]{2,1,0:T(8,128)(2,1)} %bitcast.1), calls=%async_computation | async-start | bytes 262144 | tf_op jit(solution)/shard_map/all_to_all | solution.py:524
  11.4 2.2 %copy-start = (f32[16,8,2,32,32]{4,3,2,1,0:T(8,128)S(1)}, f32[16,8,2,32,32]{4,3,2,1,0:T(8,128)}, u32[]{:S(2)}) copy-start(f32[16,8,2,32,32]{4,3,2,1,0:T(8,128)} %weight_ref.1) | copy-start | bytes 3145732
  25.9 4.1 %collective-permute-start.1 = (bf16[32,256]{1,0:T(8,128)(2,1)S(1)}, bf16[32,256]{1,0:T(8,128)(2,1)S(1)}, u32[]{:S(2)}, u32[]{:S(2)}) collective-permute-start(bf16[32,256]{1,0:T(8,128)(2,1)S(1)} %get-tuple-element.38), channel_id=1, source_target_pairs={{0,2},{1,3},{2,0},{3,1},{4,6},{5,7},{6,4},{7,5},{8,10},{9,11},{10,... | collective-permute-start | bytes 49160 | tf_op jit(solution)/shard_map/ppermute | solution.py:511
  31.2 1.2 %collective-permute-start.2 = (bf16[32,256]{1,0:T(8,128)(2,1)S(1)}, bf16[32,256]{1,0:T(8,128)(2,1)S(1)}, u32[]{:S(2)}, u32[]{:S(2)}) collective-permute-start(bf16[32,256]{1,0:T(8,128)(2,1)S(1)} %get-tuple-element.43.own_ref), channel_id=1, source_target_pairs={{0,2},{1,3},{2,0},{3,1},{4,6},{5,7},{6,4},{7,5},{8,10},{9,11},{10,... | collective-permute-start | bytes 49160 | tf_op jit(solution)/shard_map/ppermute | solution.py:511
  43.1 9.6 %all-to-all-start.3 = ((bf16[16,40,128]{2,1,0:T(8,128)(2,1)}), bf16[16,40,128]{2,1,0:T(8,128)(2,1)S(1)}, u32[]{:S(2)}, u32[]{:S(2)}) async-start(bf16[16,40,128]{2,1,0:T(8,128)(2,1)} %bitcast.12), calls=%async_computation.3 | async-start | bytes 327680 | tf_op jit(solution)/shard_map/all_to_all | solution.py:524
  52.9 4.0 %collective-permute-start.3 = (bf16[96,256]{1,0:T(8,128)(2,1)S(1)}, bf16[96,256]{1,0:T(8,128)(2,1)S(1)}, u32[]{:S(2)}, u32[]{:S(2)}) collective-permute-start(bf16[96,256]{1,0:T(8,128)(2,1)S(1)} %get-tuple-element.54), channel_id=1, source_target_pairs={{0,2},{1,3},{2,0},{3,1},{4,6},{5,7},{6,4},{7,5},{8,10},{9,11},{10,... | collective-permute-start | bytes 147464 | tf_op jit(solution)/shard_map/ppermute | solution.py:511

commit v11 on v10

--- a/solution.py
+++ b/solution.py
@@ -15,7 +15,6 @@
 F32 = jnp.float32
 BF16 = jnp.bfloat16
 VMEM_LIMIT = 32 * 1024 * 1024
-FIRST = 4
 
 TAIL_SLOPE = 0.275
 TAIL = (
@@ -106,6 +105,10 @@
         wide = lax.axis_index("wide")
         return wide // 2, wide % 2
 
+    def listed(self, position):
+        lines = self.outer // 2
+        return ((lines // 2 - position // 2) & (lines - 1)) * 2 + position % 2
+
     def frequency(self, wide):
         index = (wide * self.modes) // MY
         return jnp.where(index < MX // 2, index, index - MX)
@@ -131,7 +134,7 @@
         outer, inner = self.here()
         row, column = grid_of(2 * self.outer, 4 * MZ)
         x = 2 * outer + (inner ^ (column // (2 * MZ)))
-        frequency = self.frequency(2 * ((row >> 1) ^ FIRST) + inner)
+        frequency = self.frequency(2 * self.listed(row >> 1) + inner)
         quarter = self.wide // 4
         small = cosine_of(x * frequency + quarter * ((row & 1) - (column & 1)), self.wide)
         return self.expanded(small)
@@ -140,7 +143,7 @@
         outer, inner = self.here()
         row, column = grid_of(4, self.outer * 2 * MZ)
         x = 2 * outer + (inner ^ (row >> 1))
-        frequency = self.frequency(2 * ((column // (2 * MZ)) ^ FIRST) + inner)
+        frequency = self.frequency(2 * self.listed(column // (2 * MZ)) + inner)
         quarter = self.wide // 4
         small = cosine_of(x * frequency + quarter * ((column & 1) - (row & 1)), self.wide)
         return self.expanded(small).astype(BF16)
@@ -512,8 +515,8 @@
 
     groups = [
         [
-            (2 * (outer ^ FIRST) + inner) * narrow + n
-            for outer in range(wide // 2)
+            (2 * place.listed(outer) + inner) * narrow + n
+            for outer in range(place.outer)
             for n in range(narrow)
         ]
         for inner in range(2)

time: 58.6 us -> 59.3 us (1.012)
  waiting for transfers between devices: 4.93 us -> 5.76 us
    all_to_all x2, waiting for transfers between devices: 3.27 us -> 4.09 us  [exchange(): lax.all_to_all(pieces, ('wide', 'narrow'), 0, 0, axis_index_groups=groups...]
where the time goes in v11:
time: 59.3 us; the launch traced here: 58.6 us
  starting transfers between devices  19.4 us (33%)
  blocking collectives  17.6 us (30%)
  Pallas kernels  11.7 us (20%)
  waiting for transfers between devices  5.76 us (10%)
  local copies, waits for them, and re-layouts  3.37 us (6%)
  between operations  0.74 us (1%)
    all_to_all x2, blocking collectives, exchange(): lax.all_to_all(pieces, ('wide', 'narrow'), 0, 0, axis_index_groups=groups...  17.6 us
    all_to_all x2, starting transfers between devices, exchange(): lax.all_to_all(pieces, ('wide', 'narrow'), 0, 0, axis_index_groups=groups...  12.4 us
    ppermute x4, starting transfers between devices, to_twin(): return lax.ppermute(send, ('wide', 'narrow'), pairs)  6.98 us
    all_to_all x2, waiting for transfers between devices, exchange(): lax.all_to_all(pieces, ('wide', 'narrow'), 0, 0, axis_index_groups=groups...  4.09 us
    pallas_call x1, Pallas kernels, body(): pl.pallas_call(outer_kernel, grid=(modes // some,), in_specs=[pl.BlockSpe...  3.55 us
    unnamed x20, local copies, waits for them, and re-layouts  3.06 us
    pallas_call x1, Pallas kernels, body(): run(back_kernel, [((mode_lines, channels), F32), shared], 'back')  1.67 us
    ppermute x4, waiting for transfers between devices, to_twin(): return lax.ppermute(send, ('wide', 'narrow'), pairs)  1.66 us
  transfers between devices with their start and end apart: 6, of which 6 were waited for; matrix products, arithmetic and copies ran while one was open for 1% of the time, Pallas kernels for 9%

profile of v11, /device:TPU:1, one launch (start us, length us, event | category | flops | bytes accessed | tf_op | source)
XLA Modules:
  0.0 58.6 jit_solution(13712952588745012180)
XLA Ops:
  0.6 0.0 copy-start.1
  0.6 0.0 copy-start.2
  0.7 0.1 collective-permute-start
  0.8 0.0 copy-start.3
  0.8 0.8 %copy-done.3 = bf16[1,32,8,128]{3,2,1,0:T(8,128)(2,1)S(1)} copy-done((bf16[1,32,8,128]{3,2,1,0:T(8,128)(2,1)S(1)}, bf16[1,32,8,128]{3,2,1,0:T(8,128)(2,1)}, u32[]{:S(2)}) %copy-start.3) | copy-done | bytes 65560
  1.6 0.0 copy-start.7
  1.6 0.0 copy-start.9
  1.6 0.0 copy-start.8
  1.6 0.0 copy-start.4
  1.6 0.0 copy-start.5
  1.6 0.0 copy-start.6
  1.7 0.3 own.1
  2.0 0.2 collective-permute-done.twin_ref
  2.2 1.2 %start.1 = bf16[256,256]{1,0:T(8,128)(2,1)} custom-call(bf16[32,256]{1,0:T(8,128)(2,1)S(1)} %get-tuple-element.35.spectra_ref, bf16[256,128]{1,0:T(8,128)(2,1)S(1)} %collective-permute-done.twin_ref), custom_call_target="tpu_custom_call" | custom-call | flops 4194304 | bytes 524288 | tf_op jit(solution)/shard_map/start/pallas_call | solution.py:546
  3.4 8.0 %all-to-all-start = ((bf16[16,16,256]{2,1,0:T(8,128)(2,1)}), bf16[16,16,256]{2,1,0:T(8,128)(2,1)S(1)}, u32[]{:S(2)}, u32[]{:S(2)}) async-start(bf16[16,16,256]{2,1,0:T(8,128)(2,1)} %bitcast.1), calls=%async_computation | async-start | bytes 262144 | tf_op jit(solution)/shard_map/all_to_all | solution.py:527
  11.4 0.0 copy-start
  11.4 2.2 %copy-done = f32[16,8,2,32,32]{4,3,2,1,0:T(8,128)S(1)} copy-done((f32[16,8,2,32,32]{4,3,2,1,0:T(8,128)S(1)}, f32[16,8,2,32,32]{4,3,2,1,0:T(8,128)}, u32[]{:S(2)}) %copy-start) | copy-done | bytes 1048600
  13.6 0.5 pack.1.weight_ref
  14.1 2.3 %all-to-all-done = bf16[16,16,256]{2,1,0:T(8,128)(2,1)S(1)} async-done(((bf16[16,16,256]{2,1,0:T(8,128)(2,1)}), bf16[16,16,256]{2,1,0:T(8,128)(2,1)S(1)}, u32[]{:S(2)}, u32[]{:S(2)}) %all-to-all-start) | async-done | bytes 131104 | tf_op jit(solution)/shard_map/all_to_all | solution.py:527
  16.4 0.0 copy-done.1
  16.4 0.0 copy-done.2
  16.4 0.9 %mode.1 = (f32[256,32]{1,0:T(8,128)S(1)}, bf16[256,256]{1,0:T(8,128)(2,1)S(1)}) custom-call(bf16[256,256]{1,0:T(8,128)(2,1)S(1)} %bitcast.23, bf16[256,256]{1,0:T(8,128)(2,1)S(1)} %copy-done.1, bf16[256,256]{1,0:T(8,128)(2,1)S(1)} %copy-done.2, bf16[4,256,256]{2,1,0:T(8,128)(2,1)S(1)} %pack.1.weight_ref), custom_call_target="tpu_custom_call" | custom-call | flops 4194304 | bytes 524288 | tf_op jit(solution)/shard_map/mode/pallas_call | solution.py:549
  17.3 8.7 %all_to_all.20 = bf16[16,16,256]{2,1,0:T(8,128)(2,1)S(1)} all-to-all(bf16[16,16,256]{2,1,0:T(8,128)(2,1)S(1)} %bitcast.27), channel_id=1, replica_groups={{16,17,20,21,8,9,12,13,0,1,4,5,24,25,28,29},{18,19,22,23,10,11,14,15,2,..., dimensions={0} | all-to-all | bytes 262144 | tf_op jit(solution)/shard_map/all_to_all | solution.py:527
  26.1 0.2 part.2
  26.3 3.2 %collective-permute-start.1 = (bf16[32,256]{1,0:T(8,128)(2,1)S(1)}, bf16[32,256]{1,0:T(8,128)(2,1)S(1)}, u32[]{:S(2)}, u32[]{:S(2)}) collective-permute-start(bf16[32,256]{1,0:T(8,128)(2,1)S(1)} %get-tuple-element.38), channel_id=1, source_target_pairs={{0,2},{1,3},{2,0},{3,1},{4,6},{5,7},{6,4},{7,5},{8,10},{9,11},{10,... | collective-permute-start | bytes 49160 | tf_op jit(solution)/shard_map/ppermute | solution.py:514
  29.5 0.0 copy-done.7
  29.5 0.0 copy-done.9
  29.5 0.1 copy.15.mix_bias_ref
  29.6 0.0 copy-done.8
  29.6 0.1 copy.16.refs_6_
  29.7 0.1 copy.17.refs_8_
  29.8 0.0 copy-done.4
  29.8 0.0 copy-done.5
  29.8 0.2 ready.1
  30.0 0.3 collective-permute-done.1.refs_1_
  30.3 0.0 copy-done.6
  30.3 1.2 %cell.1 = (f32[8,128]{1,0:T(8,128)S(1)}, bf16[32,1024]{1,0:T(8,128)(2,1)S(1)}, bf16[32,256]{1,0:T(8,128)(2,1)S(1)}, bf16[32,1024]{1,0:T(8,128)(2,1)S(1)}, bf16[128,1024]{1,0:T(8,128)(2,1)S(1)}) custom-call(f32[32,256]{1,0:T(8,128)S(1)} %get-tuple-element.37.refs_0_, bf16[32,256]{1,0:T(8,128)(2,1)S(1)} %collective-permute-done.1.refs_1_, ...), custom_call_target="tpu_custom_call" | custom-call | flops 4194304 | bytes 524288 | tf_op jit(solution)/shard_map/cell/pallas_call | solution.py:558
  31.6 0.4 collective-permute-start.2
  31.9 0.4 sums.1
  32.3 0.5 collective-permute-done.2.got_ref
  32.8 0.2 fold.1
  32.9 8.9 %all_to_all.21 = bf16[16,40,128]{2,1,0:T(8,128)(2,1)S(1)} all-to-all(bf16[16,40,128]{2,1,0:T(8,128)(2,1)S(1)} %bitcast.21), channel_id=1, replica_groups={{16,17,20,21,8,9,12,13,0,1,4,5,24,25,28,29},{18,19,22,23,10,11,14,15,2,..., dimensions={0} | all-to-all | bytes 327680 | tf_op jit(solution)/shard_map/all_to_all | solution.py:527
  41.8 1.7 %back.1 = (f32[256,32]{1,0:T(8,128)S(1)}, bf16[640,128]{1,0:T(8,128)(2,1)}) custom-call(bf16[640,128]{1,0:T(8,128)(2,1)S(1)} %bitcast.22, bf16[256,256]{1,0:T(8,128)(2,1)S(1)} %copy-done.1, bf16[256,256]{1,0:T(8,128)(2,1)S(1)} %copy-done.2, bf16[4,256,256]{2,1,0:T(8,128)(2,1)S(1)} %pack.1.weight_ref), custom_call_target="tpu_custom_call" | custom-call | flops 4194304 | bytes 524288 | tf_op jit(solution)/shard_map/back/pallas_call | solution.py:590
  43.5 4.4 %all-to-all-start.3 = ((bf16[16,40,128]{2,1,0:T(8,128)(2,1)}), bf16[16,40,128]{2,1,0:T(8,128)(2,1)S(1)}, u32[]{:S(2)}, u32[]{:S(2)}) async-start(bf16[16,40,128]{2,1,0:T(8,128)(2,1)} %bitcast.12), calls=%async_computation.3 | async-start | bytes 327680 | tf_op jit(solution)/shard_map/all_to_all | solution.py:527
  47.9 3.5 %outer.1 = (f32[16,8,2,32,32]{4,3,2,1,0:T(8,128)}, f32[8,128]{1,0:T(8,128)S(1)}) custom-call(f32[16,16,32]{2,1,0:T(8,128)S(1)} %bitcast.25, f32[16,16,32]{2,1,0:T(8,128)S(1)} %bitcast.26), custom_call_target="tpu_custom_call" | custom-call | flops 4194304 | bytes 5242880 | tf_op jit(solution)/shard_map/outer/pallas_call | solution.py:594
  51.4 1.8 %all-to-all-done.3 = bf16[16,40,128]{2,1,0:T(8,128)(2,1)S(1)} async-done(((bf16[16,40,128]{2,1,0:T(8,128)(2,1)}), bf16[16,40,128]{2,1,0:T(8,128)(2,1)S(1)}, u32[]{:S(2)}, u32[]{:S(2)}) %all-to-all-start.3) | async-done | bytes 163872 | tf_op jit(solution)/shard_map/all_to_all | solution.py:527
  53.2 0.2 part.3
  53.4 3.3 %collective-permute-start.3 = (bf16[96,256]{1,0:T(8,128)(2,1)S(1)}, bf16[96,256]{1,0:T(8,128)(2,1)S(1)}, u32[]{:S(2)}, u32[]{:S(2)}) collective-permute-start(bf16[96,256]{1,0:T(8,128)(2,1)S(1)} %get-tuple-element.54), channel_id=1, source_target_pairs={{0,2},{1,3},{2,0},{3,1},{4,6},{5,7},{6,4},{7,5},{8,10},{9,11},{10,... | collective-permute-start | bytes 147464 | tf_op jit(solution)/shard_map/ppermute | solution.py:514
  56.7 0.2 pointwise.1
  56.9 0.7 %collective-permute-done.3.refs_1_ = bf16[96,256]{1,0:T(8,128)(2,1)S(1)} collective-permute-done((bf16[96,256]{1,0:T(8,128)(2,1)S(1)}, bf16[96,256]{1,0:T(8,128)(2,1)S(1)}, u32[]{:S(2)}, u32[]{:S(2)}) %collective-permute-start.3) | collective-permute-done | bytes 49184 | tf_op jit(solution)/shard_map/ppermute | solution.py:514
  57.6 1.0 %finish.1 = (bf16[256,128]{1,0:T(8,128)(2,1)}, f32[8,128]{1,0:T(8,128)}, f32[32,32]{1,0:T(8,128)}, f32[32,128]{1,0:T(8,128)}) custom-call(f32[32,256]{1,0:T(8,128)S(1)} %get-tuple-element.53.refs_0_, bf16[96,256]{1,0:T(8,128)(2,1)S(1)} %collective-permute-done.3.refs_1_, bf16[32,128]{1,0:T(8,128)(2,1)S(1)} %get-tuple-element.55.refs_2_, ...), custom_call_target="tpu_custom_call" | custom-call | flops 4194304 | bytes 524288 | tf_op jit(solution)/shard_map/finish/pallas_call | solution.py:625
  (1 shorter events, 0.0 us)
Async XLA Ops:
  0.6 15.8 %copy-start.1 = (bf16[256,256]{1,0:T(8,128)(2,1)S(1)}, bf16[256,256]{1,0:T(8,128)(2,1)}, u32[]{:S(2)}) copy-start(bf16[256,256]{1,0:T(8,128)(2,1)} %constant.4.clone.y_forward_ref) | copy-start | bytes 393220
  0.6 15.8 %copy-start.2 = (bf16[256,256]{1,0:T(8,128)(2,1)S(1)}, bf16[256,256]{1,0:T(8,128)(2,1)}, u32[]{:S(2)}) copy-start(bf16[256,256]{1,0:T(8,128)(2,1)} %constant.5.clone.y_inverse_ref) | copy-start | bytes 393220
  0.7 1.5 %collective-permute-start = (bf16[256,128]{1,0:T(8,128)(2,1)}, bf16[256,128]{1,0:T(8,128)(2,1)S(1)}, u32[]{:S(2)}, u32[]{:S(2)}) collective-permute-start(bf16[256,128]{1,0:T(8,128)(2,1)} %bitcast.28), channel_id=1, source_target_pairs={{0,2},{1,3},{2,0},{3,1},{4,6},{5,7},{6,4},{7,5},{8,10},{9,11},{10,... | collective-permute-start | bytes 196616 | tf_op jit(solution)/shard_map/ppermute | solution.py:514
  0.8 0.8 %copy-start.3 = (bf16[1,32,8,128]{3,2,1,0:T(8,128)(2,1)S(1)}, bf16[1,32,8,128]{3,2,1,0:T(8,128)(2,1)}, u32[]{:S(2)}) copy-start(bf16[1,32,8,128]{3,2,1,0:T(8,128)(2,1)} %param.10) | copy-start | bytes 196612
  1.6 27.8 %copy-start.7 = (bf16[128]{0:T(256)(128)(2,1)S(1)}, bf16[128]{0:T(256)(128)(2,1)}, u32[]{:S(2)}) copy-start(bf16[128]{0:T(256)(128)(2,1)} %param.16) | copy-start | bytes 772
  1.6 27.8 %copy-start.9 = (f32[32]{0:T(128)S(1)}, f32[32]{0:T(128)}, u32[]{:S(2)}) copy-start(f32[32]{0:T(128)} %param.13) | copy-start | bytes 388
  1.6 27.9 %copy-start.8 = (f32[128]{0:T(128)S(1)}, f32[128]{0:T(128)}, u32[]{:S(2)}) copy-start(f32[128]{0:T(128)} %param.15) | copy-start | bytes 1540
  1.6 28.2 %copy-start.4 = (bf16[32,128]{1,0:T(8,128)(2,1)S(1)}, bf16[32,128]{1,0:T(8,128)(2,1)}, u32[]{:S(2)}) copy-start(bf16[32,128]{1,0:T(8,128)(2,1)} %refs_4_.1) | copy-start | bytes 24580
  1.6 28.2 %copy-start.5 = (bf16[32,32]{1,0:T(8,128)(2,1)S(1)}, bf16[32,32]{1,0:T(8,128)(2,1)}, u32[]{:S(2)}) copy-start(bf16[32,32]{1,0:T(8,128)(2,1)} %mix_ref.3) | copy-start | bytes 6148
  1.6 28.7 %copy-start.6 = (f32[1,8,128]{2,1,0:T(8,128)S(1)}, f32[1,8,128]{2,1,0:T(8,128)}, u32[]{:S(2)}) copy-start(f32[1,8,128]{2,1,0:T(8,128)} %param.17) | copy-start | bytes 12292
  3.4 13.0 %all-to-all-start = ((bf16[16,16,256]{2,1,0:T(8,128)(2,1)}), bf16[16,16,256]{2,1,0:T(8,128)(2,1)S(1)}, u32[]{:S(2)}, u32[]{:S(2)}) async-start(bf16[16,16,256]{2,1,0:T(8,128)(2,1)} %bitcast.1), calls=%async_computation | async-start | bytes 262144 | tf_op jit(solution)/shard_map/all_to_all | solution.py:527
  11.4 2.2 %copy-start = (f32[16,8,2,32,32]{4,3,2,1,0:T(8,128)S(1)}, f32[16,8,2,32,32]{4,3,2,1,0:T(8,128)}, u32[]{:S(2)}) copy-start(f32[16,8,2,32,32]{4,3,2,1,0:T(8,128)} %weight_ref.1) | copy-start | bytes 3145732
  26.3 4.0 %collective-permute-start.1 = (bf16[32,256]{1,0:T(8,128)(2,1)S(1)}, bf16[32,256]{1,0:T(8,128)(2,1)S(1)}, u32[]{:S(2)}, u32[]{:S(2)}) collective-permute-start(bf16[32,256]{1,0:T(8,128)(2,1)S(1)} %get-tuple-element.38), channel_id=1, source_target_pairs={{0,2},{1,3},{2,0},{3,1},{4,6},{5,7},{6,4},{7,5},{8,10},{9,11},{10,... | collective-permute-start | bytes 49160 | tf_op jit(solution)/shard_map/ppermute | solution.py:514
  31.6 1.2 %collective-permute-start.2 = (bf16[32,256]{1,0:T(8,128)(2,1)S(1)}, bf16[32,256]{1,0:T(8,128)(2,1)S(1)}, u32[]{:S(2)}, u32[]{:S(2)}) collective-permute-start(bf16[32,256]{1,0:T(8,128)(2,1)S(1)} %get-tuple-element.43.own_ref), channel_id=1, source_target_pairs={{0,2},{1,3},{2,0},{3,1},{4,6},{5,7},{6,4},{7,5},{8,10},{9,11},{10,... | collective-permute-start | bytes 49160 | tf_op jit(solution)/shard_map/ppermute | solution.py:514
  43.5 9.7 %all-to-all-start.3 = ((bf16[16,40,128]{2,1,0:T(8,128)(2,1)}), bf16[16,40,128]{2,1,0:T(8,128)(2,1)S(1)}, u32[]{:S(2)}, u32[]{:S(2)}) async-start(bf16[16,40,128]{2,1,0:T(8,128)(2,1)} %bitcast.12), calls=%async_computation.3 | async-start | bytes 327680 | tf_op jit(solution)/shard_map/all_to_all | solution.py:527
  53.4 4.2 %collective-permute-start.3 = (bf16[96,256]{1,0:T(8,128)(2,1)S(1)}, bf16[96,256]{1,0:T(8,128)(2,1)S(1)}, u32[]{:S(2)}, u32[]{:S(2)}) collective-permute-start(bf16[96,256]{1,0:T(8,128)(2,1)S(1)} %get-tuple-element.54), channel_id=1, source_target_pairs={{0,2},{1,3},{2,0},{3,1},{4,6},{5,7},{6,4},{7,5},{8,10},{9,11},{10,... | collective-permute-start | bytes 147464 | tf_op jit(solution)/shard_map/ppermute | solution.py:514

commit v12 on v6

--- a/solution.py
+++ b/solution.py
@@ -100,10 +100,16 @@
         self.outer = wide // 2
         self.partners = self.outer * narrow
         self.lanes = rows_y * channels
+        middle, last = self.outer // 4, self.outer // 2 - 1
+        self.firsts = (last, middle, middle, last)
 
     def here(self):
         wide = lax.axis_index("wide")
         return wide // 2, wide % 2
+
+    def listed(self, position, first):
+        lines = self.outer // 2
+        return ((first + position // 2) & (lines - 1)) * 2 + position % 2
 
     def frequency(self, wide):
         index = (wide * self.modes) // MY
@@ -126,20 +132,20 @@
             blocks.append(jnp.where(same, value, 0.0))
         return jnp.concatenate(blocks, axis=0)
 
-    def forward_x(self):
+    def forward_x(self, first):
         outer, inner = self.here()
         row, column = grid_of(2 * self.outer, 4 * MZ)
         x = 2 * outer + (inner ^ (column // (2 * MZ)))
-        frequency = self.frequency(2 * (row >> 1) + inner)
+        frequency = self.frequency(2 * self.listed(row >> 1, first) + inner)
         quarter = self.wide // 4
         small = cosine_of(x * frequency + quarter * ((row & 1) - (column & 1)), self.wide)
         return self.expanded(small)
 
-    def inverse_x(self):
+    def inverse_x(self, first):
         outer, inner = self.here()
         row, column = grid_of(4, self.outer * 2 * MZ)
         x = 2 * outer + (inner ^ (row >> 1))
-        frequency = self.frequency(2 * (column // (2 * MZ)) + inner)
+        frequency = self.frequency(2 * self.listed(column // (2 * MZ), first) + inner)
         quarter = self.wide // 4
         small = cosine_of(x * frequency + quarter * ((column & 1) - (row & 1)), self.wide)
         return self.expanded(small).astype(BF16)
@@ -231,7 +237,7 @@
     twin = dot_nt(place.z_table(False), twin_ref[...]).astype(BF16)
     twin = dot(twin, turn_matrix(place, True)).astype(BF16)
     values = jnp.concatenate([spectra_ref[...], twin], axis=0)
-    tables = jnp.concatenate(halves(place.forward_x()), axis=1)
+    tables = jnp.concatenate(halves(place.forward_x(place.firsts[0])), axis=1)
     send_ref[...] = dot(tables, jnp.concatenate([values, values], axis=0)).astype(BF16)
 
 
@@ -282,9 +288,9 @@
     repeat_rows(send_ref, spread_lines(place, mode, y_inverse_ref[...]))
 
 
-def part_kernel(place, pieces_ref, *refs):
+def part_kernel(place, first, pieces_ref, *refs):
     pieces, shares = read_pieces(place, pieces_ref)
-    lines = dot(place.inverse_x(), pieces)
+    lines = dot(place.inverse_x(first), pieces)
     height = 2 * MZ
     if shares is None:
         own_ref, send_ref = refs
@@ -295,18 +301,18 @@
     own_ref[...] = lines[:height]
     send_ref[:height] = lines[height:].astype(BF16)
     got = jnp.concatenate(shares, axis=0).astype(BF16)
-    channels = place.channels
+    channels, narrow = place.channels, place.narrow
 
     def chosen(part):
-        return dot(
-            selector(
-                2 * channels,
-                got.shape[0],
-                lambda row, column: (column // 8 == (row % channels) // 2)
-                & (column % 8 == 4 * part + 2 * (row // channels) + row % 2),
-            ),
-            got,
-        )
+        def condition(row, column):
+            owner, source = (row % channels) // 2, column // 8
+            return (
+                (place.listed(owner // narrow, place.firsts[2]) == place.listed(source // narrow, first))
+                & (owner % narrow == source % narrow)
+                & (column % 8 == 4 * part + 2 * (row // channels) + row % 2)
+            )
+
+        return dot(selector(2 * channels, got.shape[0], condition), got)
 
     high, low = chosen(0), chosen(1)
     sums_ref[...] = high + low
@@ -360,7 +366,7 @@
 
 
 def sums_kernel(place, field_ref, gradient_ref, hidden_ref, head_slope_ref, *refs):
-    refs[-1][...] = jnp.concatenate(halves(place.forward_x()), axis=1)
+    refs[-1][...] = jnp.concatenate(halves(place.forward_x(place.firsts[2])), axis=1)
     grad_mix = dot_nt(field_ref[...], gradient_ref[...])
     grad_head = dot_nt(hidden_ref[...], head_slope_ref[...])
     if not place.fold:
@@ -509,12 +515,16 @@
         pairs = [(p, p ^ narrow) for p in range(devices)]
         return lax.ppermute(send, ("wide", "narrow"), pairs)
 
-    groups = [
-        [(2 * outer + inner) * narrow + n for outer in range(wide // 2) for n in range(narrow)]
-        for inner in range(2)
-    ]
-
-    def exchange(send):
+    def exchange(send, transform):
+        first = place.firsts[transform]
+        groups = [
+            [
+                (2 * place.listed(outer, first) + inner) * narrow + n
+                for outer in range(place.outer)
+                for n in range(narrow)
+            ]
+            for inner in range(2)
+        ]
         pieces = send.reshape(partners, -1, send.shape[1])
         got = lax.all_to_all(
             pieces, ("wide", "narrow"), 0, 0, axis_index_groups=groups, tiled=True
@@ -539,9 +549,10 @@
     packed_shape = ((modes // 4, kz * channels, 8 * channels), BF16)
     (weight,) = call(pack_kernel, [packed_shape], "pack")(spectral_weight)
     spectrum, send = run(mode_kernel, [((mode_lines, channels), F32), plain], "mode")(
-        exchange(send), y_forward, y_inverse, weight
-    )
-    own, send = run(part_kernel, [own_lines, twin_plain], "part")(exchange(send))
+        exchange(send, 0), y_forward, y_inverse, weight
+    )
+    part = functools.partial(part_kernel, place, place.firsts[1])
+    own, send = call(part, [own_lines, twin_plain], "part")(exchange(send, 1))
     pointwise, head_turned, z_doubled = run(
         ready_kernel,
         [(across, F32), ((hidden_units, channels), BF16), ((height, z_count), BF16)],
@@ -580,7 +591,7 @@
         sums = []
     (send,) = run(fold_kernel, [shared], "fold")(send, to_twin(send), forward, *sums)
     adjoint, send = run(back_kernel, [((mode_lines, channels), F32), shared], "back")(
-        exchange(send), y_forward, y_inverse, weight
+        exchange(send, 2), y_forward, y_inverse, weight
     )
     some = max(1, modes // 4)
     grad_spectral, done = pl.pallas_call(
@@ -610,7 +621,8 @@
     )(mix_weight, grad_pre)
     outs = [own_lines, twin_shared] + ([sums_shape] if place.fold else [])
     after = (done,) if place.fold else ()
-    own, send, *sums = run(part_kernel, outs, "part")(exchange(send), *after)
+    part = functools.partial(part_kernel, place, place.firsts[3])
+    own, send, *sums = call(part, outs, "part")(exchange(send, 3), *after)
     outs = [((cells, z_count), BF16), ((rows_y, z_count), F32)]
     if place.fold:
         outs += [((channels, channels), F32), ((channels, hidden_units), F32)]

time: 62.3 us -> 59.6 us (0.957)
  waiting for transfers between devices: 8.83 us -> 5.08 us
  starting transfers between devices: 17.1 us -> 20.3 us
  blocking collectives: 19.8 us -> 17.5 us
    all_to_all x2, waiting for transfers between devices: 7.17 us -> 3.42 us  [exchange(): lax.all_to_all(pieces, ('wide', 'narrow'), 0, 0, axis_index_groups=groups...]
    all_to_all x2, blocking collectives: 19.8 us -> 17.5 us  [exchange(): lax.all_to_all(pieces, ('wide', 'narrow'), 0, 0, axis_index_groups=groups...]
    all_to_all x2, starting transfers between devices: 11.8 us -> 13.8 us  [exchange(): lax.all_to_all(pieces, ('wide', 'narrow'), 0, 0, axis_index_groups=groups...]
    ppermute x4, starting transfers between devices: 5.29 us -> 6.54 us  [to_twin(): return lax.ppermute(send, ('wide', 'narrow'), pairs)]
  transfers between devices with their start and end apart: 6 -> 6, of which waited for: 6 -> 6; matrix products, arithmetic and copies ran while one was open for 1% -> 1% of each run, Pallas kernels for 8% -> 9%
where the time goes in v12:
time: 59.6 us; the launch traced here: 58.9 us
  starting transfers between devices  20.3 us (34%)
  blocking collectives  17.5 us (29%)
  Pallas kernels  11.8 us (20%)
  waiting for transfers between devices  5.08 us (9%)
  local copies, waits for them, and re-layouts  3.37 us (6%)
  between operations  0.74 us (1%)
    all_to_all x2, blocking collectives, exchange(): lax.all_to_all(pieces, ('wide', 'narrow'), 0, 0, axis_index_groups=groups...  17.5 us
    all_to_all x2, starting transfers between devices, exchange(): lax.all_to_all(pieces, ('wide', 'narrow'), 0, 0, axis_index_groups=groups...  13.8 us
    ppermute x4, starting transfers between devices, to_twin(): return lax.ppermute(send, ('wide', 'narrow'), pairs)  6.54 us
    pallas_call x1, Pallas kernels, body(): pl.pallas_call(outer_kernel, grid=(modes // some,), in_specs=[pl.BlockSpe...  3.55 us
    all_to_all x2, waiting for transfers between devices, exchange(): lax.all_to_all(pieces, ('wide', 'narrow'), 0, 0, axis_index_groups=groups...  3.42 us
    unnamed x20, local copies, waits for them, and re-layouts  3.06 us
    pallas_call x1, Pallas kernels, body(): run(back_kernel, [((mode_lines, channels), F32), shared], 'back')  1.67 us
    ppermute x4, waiting for transfers between devices, to_twin(): return lax.ppermute(send, ('wide', 'narrow'), pairs)  1.66 us
  transfers between devices with their start and end apart: 6, of which 6 were waited for; matrix products, arithmetic and copies ran while one was open for 1% of the time, Pallas kernels for 9%

profile of v12, /device:TPU:1, one launch (start us, length us, event | category | flops | bytes accessed | tf_op | source)
XLA Modules:
  0.0 58.9 jit_solution(15447941128144571463)
XLA Ops:
  0.6 0.0 copy-start.1
  0.6 0.0 copy-start.2
  0.7 0.1 collective-permute-start
  0.8 0.0 copy-start.3
  0.8 0.8 %copy-done.3 = bf16[1,32,8,128]{3,2,1,0:T(8,128)(2,1)S(1)} copy-done((bf16[1,32,8,128]{3,2,1,0:T(8,128)(2,1)S(1)}, bf16[1,32,8,128]{3,2,1,0:T(8,128)(2,1)}, u32[]{:S(2)}) %copy-start.3) | copy-done | bytes 65560
  1.6 0.0 copy-start.7
  1.6 0.0 copy-start.9
  1.6 0.0 copy-start.8
  1.6 0.0 copy-start.4
  1.6 0.0 copy-start.5
  1.6 0.0 copy-start.6
  1.7 0.3 own.1
  2.0 0.2 collective-permute-done.twin_ref
  2.2 1.2 %start.1 = bf16[256,256]{1,0:T(8,128)(2,1)} custom-call(bf16[32,256]{1,0:T(8,128)(2,1)S(1)} %get-tuple-element.35.spectra_ref, bf16[256,128]{1,0:T(8,128)(2,1)S(1)} %collective-permute-done.twin_ref), custom_call_target="tpu_custom_call" | custom-call | flops 4194304 | bytes 524288 | tf_op jit(solution)/shard_map/start/pallas_call | solution.py:548
  3.4 8.0 %all-to-all-start = ((bf16[16,16,256]{2,1,0:T(8,128)(2,1)}), bf16[16,16,256]{2,1,0:T(8,128)(2,1)S(1)}, u32[]{:S(2)}, u32[]{:S(2)}) async-start(bf16[16,16,256]{2,1,0:T(8,128)(2,1)} %bitcast.1), calls=%async_computation | async-start | bytes 262144 | tf_op jit(solution)/shard_map/all_to_all | solution.py:529
  11.4 0.0 copy-start
  11.4 2.2 %copy-done = f32[16,8,2,32,32]{4,3,2,1,0:T(8,128)S(1)} copy-done((f32[16,8,2,32,32]{4,3,2,1,0:T(8,128)S(1)}, f32[16,8,2,32,32]{4,3,2,1,0:T(8,128)}, u32[]{:S(2)}) %copy-start) | copy-done | bytes 1048600
  13.6 0.5 pack.1.weight_ref
  14.1 2.3 %all-to-all-done = bf16[16,16,256]{2,1,0:T(8,128)(2,1)S(1)} async-done(((bf16[16,16,256]{2,1,0:T(8,128)(2,1)}), bf16[16,16,256]{2,1,0:T(8,128)(2,1)S(1)}, u32[]{:S(2)}, u32[]{:S(2)}) %all-to-all-start) | async-done | bytes 131104 | tf_op jit(solution)/shard_map/all_to_all | solution.py:529
  16.4 0.0 copy-done.1
  16.4 0.0 copy-done.2
  16.4 0.9 %mode.1 = (f32[256,32]{1,0:T(8,128)S(1)}, bf16[256,256]{1,0:T(8,128)(2,1)S(1)}) custom-call(bf16[256,256]{1,0:T(8,128)(2,1)S(1)} %bitcast.23, bf16[256,256]{1,0:T(8,128)(2,1)S(1)} %copy-done.1, bf16[256,256]{1,0:T(8,128)(2,1)S(1)} %copy-done.2, bf16[4,256,256]{2,1,0:T(8,128)(2,1)S(1)} %pack.1.weight_ref), custom_call_target="tpu_custom_call" | custom-call | flops 4194304 | bytes 524288 | tf_op jit(solution)/shard_map/mode/pallas_call | solution.py:551
  17.4 8.7 %all_to_all.20 = bf16[16,16,256]{2,1,0:T(8,128)(2,1)S(1)} all-to-all(bf16[16,16,256]{2,1,0:T(8,128)(2,1)S(1)} %bitcast.27), channel_id=1, replica_groups={{16,17,20,21,24,25,28,29,0,1,4,5,8,9,12,13},{18,19,22,23,26,27,30,31,2,..., dimensions={0} | all-to-all | bytes 262144 | tf_op jit(solution)/shard_map/all_to_all | solution.py:529
  26.1 0.2 part.2
  26.3 2.8 %collective-permute-start.1 = (bf16[32,256]{1,0:T(8,128)(2,1)S(1)}, bf16[32,256]{1,0:T(8,128)(2,1)S(1)}, u32[]{:S(2)}, u32[]{:S(2)}) collective-permute-start(bf16[32,256]{1,0:T(8,128)(2,1)S(1)} %get-tuple-element.38), channel_id=1, source_target_pairs={{0,2},{1,3},{2,0},{3,1},{4,6},{5,7},{6,4},{7,5},{8,10},{9,11},{10,... | collective-permute-start | bytes 49160 | tf_op jit(solution)/shard_map/ppermute | solution.py:516
  29.1 0.0 copy-done.7
  29.1 0.0 copy-done.9
  29.1 0.1 copy.15.mix_bias_ref
  29.2 0.0 copy-done.8
  29.2 0.1 copy.16.refs_6_
  29.3 0.1 copy.17.refs_8_
  29.4 0.0 copy-done.4
  29.4 0.0 copy-done.5
  29.4 0.2 ready.1
  29.6 0.3 collective-permute-done.1.refs_1_
  29.9 0.0 copy-done.6
  30.0 1.2 %cell.1 = (f32[8,128]{1,0:T(8,128)S(1)}, bf16[32,1024]{1,0:T(8,128)(2,1)S(1)}, bf16[32,256]{1,0:T(8,128)(2,1)S(1)}, bf16[32,1024]{1,0:T(8,128)(2,1)S(1)}, bf16[128,1024]{1,0:T(8,128)(2,1)S(1)}) custom-call(f32[32,256]{1,0:T(8,128)S(1)} %get-tuple-element.37.refs_0_, bf16[32,256]{1,0:T(8,128)(2,1)S(1)} %collective-permute-done.1.refs_1_, ...), custom_call_target="tpu_custom_call" | custom-call | flops 4194304 | bytes 524288 | tf_op jit(solution)/shard_map/cell/pallas_call | solution.py:561
  31.2 0.4 collective-permute-start.2
  31.6 0.4 sums.1
  31.9 0.5 collective-permute-done.2.got_ref
  32.4 0.2 fold.1
  32.6 8.8 %all_to_all.21 = bf16[16,40,128]{2,1,0:T(8,128)(2,1)S(1)} all-to-all(bf16[16,40,128]{2,1,0:T(8,128)(2,1)S(1)} %bitcast.21), channel_id=1, replica_groups={{16,17,20,21,24,25,28,29,0,1,4,5,8,9,12,13},{18,19,22,23,26,27,30,31,2,..., dimensions={0} | all-to-all | bytes 327680 | tf_op jit(solution)/shard_map/all_to_all | solution.py:529
  41.4 1.7 %back.1 = (f32[256,32]{1,0:T(8,128)S(1)}, bf16[640,128]{1,0:T(8,128)(2,1)}) custom-call(bf16[640,128]{1,0:T(8,128)(2,1)S(1)} %bitcast.22, bf16[256,256]{1,0:T(8,128)(2,1)S(1)} %copy-done.1, bf16[256,256]{1,0:T(8,128)(2,1)S(1)} %copy-done.2, bf16[4,256,256]{2,1,0:T(8,128)(2,1)S(1)} %pack.1.weight_ref), custom_call_target="tpu_custom_call" | custom-call | flops 4194304 | bytes 524288 | tf_op jit(solution)/shard_map/back/pallas_call | solution.py:593
  43.1 5.8 %all-to-all-start.3 = ((bf16[16,40,128]{2,1,0:T(8,128)(2,1)}), bf16[16,40,128]{2,1,0:T(8,128)(2,1)S(1)}, u32[]{:S(2)}, u32[]{:S(2)}) async-start(bf16[16,40,128]{2,1,0:T(8,128)(2,1)} %bitcast.12), calls=%async_computation.3 | async-start | bytes 327680 | tf_op jit(solution)/shard_map/all_to_all | solution.py:529
  48.9 3.5 %outer.1 = (f32[16,8,2,32,32]{4,3,2,1,0:T(8,128)}, f32[8,128]{1,0:T(8,128)S(1)}) custom-call(f32[16,16,32]{2,1,0:T(8,128)S(1)} %bitcast.25, f32[16,16,32]{2,1,0:T(8,128)S(1)} %bitcast.26), custom_call_target="tpu_custom_call" | custom-call | flops 4194304 | bytes 5242880 | tf_op jit(solution)/shard_map/outer/pallas_call | solution.py:597
  52.4 1.1 %all-to-all-done.3 = bf16[16,40,128]{2,1,0:T(8,128)(2,1)S(1)} async-done(((bf16[16,40,128]{2,1,0:T(8,128)(2,1)}), bf16[16,40,128]{2,1,0:T(8,128)(2,1)S(1)}, u32[]{:S(2)}, u32[]{:S(2)}) %all-to-all-start.3) | async-done | bytes 163872 | tf_op jit(solution)/shard_map/all_to_all | solution.py:529
  53.5 0.3 part.3
  53.8 3.2 %collective-permute-start.3 = (bf16[96,256]{1,0:T(8,128)(2,1)S(1)}, bf16[96,256]{1,0:T(8,128)(2,1)S(1)}, u32[]{:S(2)}, u32[]{:S(2)}) collective-permute-start(bf16[96,256]{1,0:T(8,128)(2,1)S(1)} %get-tuple-element.54), channel_id=1, source_target_pairs={{0,2},{1,3},{2,0},{3,1},{4,6},{5,7},{6,4},{7,5},{8,10},{9,11},{10,... | collective-permute-start | bytes 147464 | tf_op jit(solution)/shard_map/ppermute | solution.py:516
  57.0 0.2 pointwise.1
  57.2 0.7 %collective-permute-done.3.refs_1_ = bf16[96,256]{1,0:T(8,128)(2,1)S(1)} collective-permute-done((bf16[96,256]{1,0:T(8,128)(2,1)S(1)}, bf16[96,256]{1,0:T(8,128)(2,1)S(1)}, u32[]{:S(2)}, u32[]{:S(2)}) %collective-permute-start.3) | collective-permute-done | bytes 49184 | tf_op jit(solution)/shard_map/ppermute | solution.py:516
  57.9 1.0 %finish.1 = (bf16[256,128]{1,0:T(8,128)(2,1)}, f32[8,128]{1,0:T(8,128)}, f32[32,32]{1,0:T(8,128)}, f32[32,128]{1,0:T(8,128)}) custom-call(f32[32,256]{1,0:T(8,128)S(1)} %get-tuple-element.53.refs_0_, bf16[96,256]{1,0:T(8,128)(2,1)S(1)} %collective-permute-done.3.refs_1_, bf16[32,128]{1,0:T(8,128)(2,1)S(1)} %get-tuple-element.55.refs_2_, ...), custom_call_target="tpu_custom_call" | custom-call | flops 4194304 | bytes 524288 | tf_op jit(solution)/shard_map/finish/pallas_call | solution.py:629
  (1 shorter events, 0.0 us)
Async XLA Ops:
  0.6 15.8 %copy-start.1 = (bf16[256,256]{1,0:T(8,128)(2,1)S(1)}, bf16[256,256]{1,0:T(8,128)(2,1)}, u32[]{:S(2)}) copy-start(bf16[256,256]{1,0:T(8,128)(2,1)} %constant.4.clone.y_forward_ref) | copy-start | bytes 393220
  0.6 15.8 %copy-start.2 = (bf16[256,256]{1,0:T(8,128)(2,1)S(1)}, bf16[256,256]{1,0:T(8,128)(2,1)}, u32[]{:S(2)}) copy-start(bf16[256,256]{1,0:T(8,128)(2,1)} %constant.5.clone.y_inverse_ref) | copy-start | bytes 393220
  0.7 1.5 %collective-permute-start = (bf16[256,128]{1,0:T(8,128)(2,1)}, bf16[256,128]{1,0:T(8,128)(2,1)S(1)}, u32[]{:S(2)}, u32[]{:S(2)}) collective-permute-start(bf16[256,128]{1,0:T(8,128)(2,1)} %bitcast.28), channel_id=1, source_target_pairs={{0,2},{1,3},{2,0},{3,1},{4,6},{5,7},{6,4},{7,5},{8,10},{9,11},{10,... | collective-permute-start | bytes 196616 | tf_op jit(solution)/shard_map/ppermute | solution.py:516
  0.8 0.8 %copy-start.3 = (bf16[1,32,8,128]{3,2,1,0:T(8,128)(2,1)S(1)}, bf16[1,32,8,128]{3,2,1,0:T(8,128)(2,1)}, u32[]{:S(2)}) copy-start(bf16[1,32,8,128]{3,2,1,0:T(8,128)(2,1)} %param.10) | copy-start | bytes 196612
  1.6 27.5 %copy-start.7 = (bf16[128]{0:T(256)(128)(2,1)S(1)}, bf16[128]{0:T(256)(128)(2,1)}, u32[]{:S(2)}) copy-start(bf16[128]{0:T(256)(128)(2,1)} %param.16) | copy-start | bytes 772
  1.6 27.5 %copy-start.9 = (f32[32]{0:T(128)S(1)}, f32[32]{0:T(128)}, u32[]{:S(2)}) copy-start(f32[32]{0:T(128)} %param.13) | copy-start | bytes 388
  1.6 27.6 %copy-start.8 = (f32[128]{0:T(128)S(1)}, f32[128]{0:T(128)}, u32[]{:S(2)}) copy-start(f32[128]{0:T(128)} %param.15) | copy-start | bytes 1540
  1.6 27.8 %copy-start.4 = (bf16[32,128]{1,0:T(8,128)(2,1)S(1)}, bf16[32,128]{1,0:T(8,128)(2,1)}, u32[]{:S(2)}) copy-start(bf16[32,128]{1,0:T(8,128)(2,1)} %refs_4_.1) | copy-start | bytes 24580
  1.6 27.8 %copy-start.5 = (bf16[32,32]{1,0:T(8,128)(2,1)S(1)}, bf16[32,32]{1,0:T(8,128)(2,1)}, u32[]{:S(2)}) copy-start(bf16[32,32]{1,0:T(8,128)(2,1)} %mix_ref.3) | copy-start | bytes 6148
  1.6 28.3 %copy-start.6 = (f32[1,8,128]{2,1,0:T(8,128)S(1)}, f32[1,8,128]{2,1,0:T(8,128)}, u32[]{:S(2)}) copy-start(f32[1,8,128]{2,1,0:T(8,128)} %param.17) | copy-start | bytes 12292
  3.4 13.0 %all-to-all-start = ((bf16[16,16,256]{2,1,0:T(8,128)(2,1)}), bf16[16,16,256]{2,1,0:T(8,128)(2,1)S(1)}, u32[]{:S(2)}, u32[]{:S(2)}) async-start(bf16[16,16,256]{2,1,0:T(8,128)(2,1)} %bitcast.1), calls=%async_computation | async-start | bytes 262144 | tf_op jit(solution)/shard_map/all_to_all | solution.py:529
  11.4 2.2 %copy-start = (f32[16,8,2,32,32]{4,3,2,1,0:T(8,128)S(1)}, f32[16,8,2,32,32]{4,3,2,1,0:T(8,128)}, u32[]{:S(2)}) copy-start(f32[16,8,2,32,32]{4,3,2,1,0:T(8,128)} %weight_ref.1) | copy-start | bytes 3145732
  26.3 3.7 %collective-permute-start.1 = (bf16[32,256]{1,0:T(8,128)(2,1)S(1)}, bf16[32,256]{1,0:T(8,128)(2,1)S(1)}, u32[]{:S(2)}, u32[]{:S(2)}) collective-permute-start(bf16[32,256]{1,0:T(8,128)(2,1)S(1)} %get-tuple-element.38), channel_id=1, source_target_pairs={{0,2},{1,3},{2,0},{3,1},{4,6},{5,7},{6,4},{7,5},{8,10},{9,11},{10,... | collective-permute-start | bytes 49160 | tf_op jit(solution)/shard_map/ppermute | solution.py:516
  31.2 1.2 %collective-permute-start.2 = (bf16[32,256]{1,0:T(8,128)(2,1)S(1)}, bf16[32,256]{1,0:T(8,128)(2,1)S(1)}, u32[]{:S(2)}, u32[]{:S(2)}) collective-permute-start(bf16[32,256]{1,0:T(8,128)(2,1)S(1)} %get-tuple-element.43.own_ref), channel_id=1, source_target_pairs={{0,2},{1,3},{2,0},{3,1},{4,6},{5,7},{6,4},{7,5},{8,10},{9,11},{10,... | collective-permute-start | bytes 49160 | tf_op jit(solution)/shard_map/ppermute | solution.py:516
  43.1 10.4 %all-to-all-start.3 = ((bf16[16,40,128]{2,1,0:T(8,128)(2,1)}), bf16[16,40,128]{2,1,0:T(8,128)(2,1)S(1)}, u32[]{:S(2)}, u32[]{:S(2)}) async-start(bf16[16,40,128]{2,1,0:T(8,128)(2,1)} %bitcast.12), calls=%async_computation.3 | async-start | bytes 327680 | tf_op jit(solution)/shard_map/all_to_all | solution.py:529
  53.8 4.1 %collective-permute-start.3 = (bf16[96,256]{1,0:T(8,128)(2,1)S(1)}, bf16[96,256]{1,0:T(8,128)(2,1)S(1)}, u32[]{:S(2)}, u32[]{:S(2)}) collective-permute-start(bf16[96,256]{1,0:T(8,128)(2,1)S(1)} %get-tuple-element.54), channel_id=1, source_target_pairs={{0,2},{1,3},{2,0},{3,1},{4,6},{5,7},{6,4},{7,5},{8,10},{9,11},{10,... | collective-permute-start | bytes 147464 | tf_op jit(solution)/shard_map/ppermute | solution.py:516

commit v13 on v12

--- a/solution.py
+++ b/solution.py
@@ -101,7 +101,7 @@
         self.partners = self.outer * narrow
         self.lanes = rows_y * channels
         middle, last = self.outer // 4, self.outer // 2 - 1
-        self.firsts = (last, middle, middle, last)
+        self.firsts = (last, middle, middle, middle)
 
     def here(self):
         wide = lax.axis_index("wide")

time: 59.6 us -> 58.7 us (0.985)
  starting transfers between devices: 20.3 us -> 19.2 us
    all_to_all x2, starting transfers between devices: 13.8 us -> 12.8 us  [exchange(): lax.all_to_all(pieces, ('wide', 'narrow'), 0, 0, axis_index_groups=groups...]
where the time goes in v13:
time: 58.7 us; the launch traced here: 58 us
  starting transfers between devices  19.2 us (33%)
  blocking collectives  17.5 us (30%)
  Pallas kernels  11.8 us (20%)
  waiting for transfers between devices  5.26 us (9%)
  local copies, waits for them, and re-layouts  3.37 us (6%)
  between operations  0.74 us (1%)
    all_to_all x2, blocking collectives, exchange(): lax.all_to_all(pieces, ('wide', 'narrow'), 0, 0, axis_index_groups=groups...  17.5 us
    all_to_all x2, starting transfers between devices, exchange(): lax.all_to_all(pieces, ('wide', 'narrow'), 0, 0, axis_index_groups=groups...  12.8 us
    ppermute x4, starting transfers between devices, to_twin(): return lax.ppermute(send, ('wide', 'narrow'), pairs)  6.45 us
    all_to_all x2, waiting for transfers between devices, exchange(): lax.all_to_all(pieces, ('wide', 'narrow'), 0, 0, axis_index_groups=groups...  3.6 us
    pallas_call x1, Pallas kernels, body(): pl.pallas_call(outer_kernel, grid=(modes // some,), in_specs=[pl.BlockSpe...  3.55 us
    unnamed x20, local copies, waits for them, and re-layouts  3.06 us
    pallas_call x1, Pallas kernels, body(): run(back_kernel, [((mode_lines, channels), F32), shared], 'back')  1.67 us
    ppermute x4, waiting for transfers between devices, to_twin(): return lax.ppermute(send, ('wide', 'narrow'), pairs)  1.66 us
  transfers between devices with their start and end apart: 6, of which 6 were waited for; matrix products, arithmetic and copies ran while one was open for 1% of the time, Pallas kernels for 9%

profile of v13, /device:TPU:1, one launch (start us, length us, event | category | flops | bytes accessed | tf_op | source)
XLA Modules:
  0.0 58.0 jit_solution(10380624461742791529)
XLA Ops:
  0.6 0.0 copy-start.1
  0.6 0.0 copy-start.2
  0.7 0.1 collective-permute-start
  0.8 0.0 copy-start.3
  0.8 0.8 %copy-done.3 = bf16[1,32,8,128]{3,2,1,0:T(8,128)(2,1)S(1)} copy-done((bf16[1,32,8,128]{3,2,1,0:T(8,128)(2,1)S(1)}, bf16[1,32,8,128]{3,2,1,0:T(8,128)(2,1)}, u32[]{:S(2)}) %copy-start.3) | copy-done | bytes 65560
  1.6 0.0 copy-start.7
  1.6 0.0 copy-start.9
  1.6 0.0 copy-start.8
  1.6 0.0 copy-start.4
  1.6 0.0 copy-start.5
  1.6 0.0 copy-start.6
  1.7 0.3 own.1
  2.0 0.2 collective-permute-done.twin_ref
  2.2 1.2 %start.1 = bf16[256,256]{1,0:T(8,128)(2,1)} custom-call(bf16[32,256]{1,0:T(8,128)(2,1)S(1)} %get-tuple-element.35.spectra_ref, bf16[256,128]{1,0:T(8,128)(2,1)S(1)} %collective-permute-done.twin_ref), custom_call_target="tpu_custom_call" | custom-call | flops 4194304 | bytes 524288 | tf_op jit(solution)/shard_map/start/pallas_call | solution.py:548
  3.4 8.0 %all-to-all-start = ((bf16[16,16,256]{2,1,0:T(8,128)(2,1)}), bf16[16,16,256]{2,1,0:T(8,128)(2,1)S(1)}, u32[]{:S(2)}, u32[]{:S(2)}) async-start(bf16[16,16,256]{2,1,0:T(8,128)(2,1)} %bitcast.1), calls=%async_computation | async-start | bytes 262144 | tf_op jit(solution)/shard_map/all_to_all | solution.py:529
  11.4 0.0 copy-start
  11.4 2.2 %copy-done = f32[16,8,2,32,32]{4,3,2,1,0:T(8,128)S(1)} copy-done((f32[16,8,2,32,32]{4,3,2,1,0:T(8,128)S(1)}, f32[16,8,2,32,32]{4,3,2,1,0:T(8,128)}, u32[]{:S(2)}) %copy-start) | copy-done | bytes 1048600
  13.6 0.5 pack.1.weight_ref
  14.1 2.3 %all-to-all-done = bf16[16,16,256]{2,1,0:T(8,128)(2,1)S(1)} async-done(((bf16[16,16,256]{2,1,0:T(8,128)(2,1)}), bf16[16,16,256]{2,1,0:T(8,128)(2,1)S(1)}, u32[]{:S(2)}, u32[]{:S(2)}) %all-to-all-start) | async-done | bytes 131104 | tf_op jit(solution)/shard_map/all_to_all | solution.py:529
  16.4 0.0 copy-done.1
  16.4 0.0 copy-done.2
  16.4 0.9 %mode.1 = (f32[256,32]{1,0:T(8,128)S(1)}, bf16[256,256]{1,0:T(8,128)(2,1)S(1)}) custom-call(bf16[256,256]{1,0:T(8,128)(2,1)S(1)} %bitcast.23, bf16[256,256]{1,0:T(8,128)(2,1)S(1)} %copy-done.1, bf16[256,256]{1,0:T(8,128)(2,1)S(1)} %copy-done.2, bf16[4,256,256]{2,1,0:T(8,128)(2,1)S(1)} %pack.1.weight_ref), custom_call_target="tpu_custom_call" | custom-call | flops 4194304 | bytes 524288 | tf_op jit(solution)/shard_map/mode/pallas_call | solution.py:551
  17.4 8.7 %all_to_all.20 = bf16[16,16,256]{2,1,0:T(8,128)(2,1)S(1)} all-to-all(bf16[16,16,256]{2,1,0:T(8,128)(2,1)S(1)} %bitcast.27), channel_id=1, replica_groups={{16,17,20,21,24,25,28,29,0,1,4,5,8,9,12,13},{18,19,22,23,26,27,30,31,2,..., dimensions={0} | all-to-all | bytes 262144 | tf_op jit(solution)/shard_map/all_to_all | solution.py:529
  26.1 0.2 part.2
  26.3 2.8 %collective-permute-start.1 = (bf16[32,256]{1,0:T(8,128)(2,1)S(1)}, bf16[32,256]{1,0:T(8,128)(2,1)S(1)}, u32[]{:S(2)}, u32[]{:S(2)}) collective-permute-start(bf16[32,256]{1,0:T(8,128)(2,1)S(1)} %get-tuple-element.38), channel_id=1, source_target_pairs={{0,2},{1,3},{2,0},{3,1},{4,6},{5,7},{6,4},{7,5},{8,10},{9,11},{10,... | collective-permute-start | bytes 49160 | tf_op jit(solution)/shard_map/ppermute | solution.py:516
  29.1 0.0 copy-done.7
  29.1 0.0 copy-done.9
  29.1 0.1 copy.15.mix_bias_ref
  29.2 0.0 copy-done.8
  29.2 0.1 copy.16.refs_6_
  29.3 0.1 copy.17.refs_8_
  29.4 0.0 copy-done.4
  29.4 0.0 copy-done.5
  29.4 0.2 ready.1
  29.6 0.3 collective-permute-done.1.refs_1_
  29.9 0.0 copy-done.6
  30.0 1.2 %cell.1 = (f32[8,128]{1,0:T(8,128)S(1)}, bf16[32,1024]{1,0:T(8,128)(2,1)S(1)}, bf16[32,256]{1,0:T(8,128)(2,1)S(1)}, bf16[32,1024]{1,0:T(8,128)(2,1)S(1)}, bf16[128,1024]{1,0:T(8,128)(2,1)S(1)}) custom-call(f32[32,256]{1,0:T(8,128)S(1)} %get-tuple-element.37.refs_0_, bf16[32,256]{1,0:T(8,128)(2,1)S(1)} %collective-permute-done.1.refs_1_, ...), custom_call_target="tpu_custom_call" | custom-call | flops 4194304 | bytes 524288 | tf_op jit(solution)/shard_map/cell/pallas_call | solution.py:561
  31.2 0.4 collective-permute-start.2
  31.6 0.4 sums.1
  31.9 0.5 collective-permute-done.2.got_ref
  32.4 0.2 fold.1
  32.6 8.8 %all_to_all.21 = bf16[16,40,128]{2,1,0:T(8,128)(2,1)S(1)} all-to-all(bf16[16,40,128]{2,1,0:T(8,128)(2,1)S(1)} %bitcast.21), channel_id=1, replica_groups={{16,17,20,21,24,25,28,29,0,1,4,5,8,9,12,13},{18,19,22,23,26,27,30,31,2,..., dimensions={0} | all-to-all | bytes 327680 | tf_op jit(solution)/shard_map/all_to_all | solution.py:529
  41.4 1.7 %back.1 = (f32[256,32]{1,0:T(8,128)S(1)}, bf16[640,128]{1,0:T(8,128)(2,1)}) custom-call(bf16[640,128]{1,0:T(8,128)(2,1)S(1)} %bitcast.22, bf16[256,256]{1,0:T(8,128)(2,1)S(1)} %copy-done.1, bf16[256,256]{1,0:T(8,128)(2,1)S(1)} %copy-done.2, bf16[4,256,256]{2,1,0:T(8,128)(2,1)S(1)} %pack.1.weight_ref), custom_call_target="tpu_custom_call" | custom-call | flops 4194304 | bytes 524288 | tf_op jit(solution)/shard_map/back/pallas_call | solution.py:593
  43.1 4.8 %all-to-all-start.3 = ((bf16[16,40,128]{2,1,0:T(8,128)(2,1)}), bf16[16,40,128]{2,1,0:T(8,128)(2,1)S(1)}, u32[]{:S(2)}, u32[]{:S(2)}) async-start(bf16[16,40,128]{2,1,0:T(8,128)(2,1)} %bitcast.12), calls=%async_computation.3 | async-start | bytes 327680 | tf_op jit(solution)/shard_map/all_to_all | solution.py:529
  47.8 3.5 %outer.1 = (f32[16,8,2,32,32]{4,3,2,1,0:T(8,128)}, f32[8,128]{1,0:T(8,128)S(1)}) custom-call(f32[16,16,32]{2,1,0:T(8,128)S(1)} %bitcast.25, f32[16,16,32]{2,1,0:T(8,128)S(1)} %bitcast.26), custom_call_target="tpu_custom_call" | custom-call | flops 4194304 | bytes 5242880 | tf_op jit(solution)/shard_map/outer/pallas_call | solution.py:597
  51.4 1.3 %all-to-all-done.3 = bf16[16,40,128]{2,1,0:T(8,128)(2,1)S(1)} async-done(((bf16[16,40,128]{2,1,0:T(8,128)(2,1)}), bf16[16,40,128]{2,1,0:T(8,128)(2,1)S(1)}, u32[]{:S(2)}, u32[]{:S(2)}) %all-to-all-start.3) | async-done | bytes 163872 | tf_op jit(solution)/shard_map/all_to_all | solution.py:529
  52.7 0.3 part.3
  52.9 3.1 %collective-permute-start.3 = (bf16[96,256]{1,0:T(8,128)(2,1)S(1)}, bf16[96,256]{1,0:T(8,128)(2,1)S(1)}, u32[]{:S(2)}, u32[]{:S(2)}) collective-permute-start(bf16[96,256]{1,0:T(8,128)(2,1)S(1)} %get-tuple-element.54), channel_id=1, source_target_pairs={{0,2},{1,3},{2,0},{3,1},{4,6},{5,7},{6,4},{7,5},{8,10},{9,11},{10,... | collective-permute-start | bytes 147464 | tf_op jit(solution)/shard_map/ppermute | solution.py:516
  56.1 0.2 pointwise.1
  56.3 0.7 %collective-permute-done.3.refs_1_ = bf16[96,256]{1,0:T(8,128)(2,1)S(1)} collective-permute-done((bf16[96,256]{1,0:T(8,128)(2,1)S(1)}, bf16[96,256]{1,0:T(8,128)(2,1)S(1)}, u32[]{:S(2)}, u32[]{:S(2)}) %collective-permute-start.3) | collective-permute-done | bytes 49184 | tf_op jit(solution)/shard_map/ppermute | solution.py:516
  57.0 1.0 %finish.1 = (bf16[256,128]{1,0:T(8,128)(2,1)}, f32[8,128]{1,0:T(8,128)}, f32[32,32]{1,0:T(8,128)}, f32[32,128]{1,0:T(8,128)}) custom-call(f32[32,256]{1,0:T(8,128)S(1)} %get-tuple-element.53.refs_0_, bf16[96,256]{1,0:T(8,128)(2,1)S(1)} %collective-permute-done.3.refs_1_, bf16[32,128]{1,0:T(8,128)(2,1)S(1)} %get-tuple-element.55.refs_2_, ...), custom_call_target="tpu_custom_call" | custom-call | flops 4194304 | bytes 524288 | tf_op jit(solution)/shard_map/finish/pallas_call | solution.py:629
  (1 shorter events, 0.0 us)
Async XLA Ops:
  0.6 15.8 %copy-start.1 = (bf16[256,256]{1,0:T(8,128)(2,1)S(1)}, bf16[256,256]{1,0:T(8,128)(2,1)}, u32[]{:S(2)}) copy-start(bf16[256,256]{1,0:T(8,128)(2,1)} %constant.4.clone.y_forward_ref) | copy-start | bytes 393220
  0.6 15.8 %copy-start.2 = (bf16[256,256]{1,0:T(8,128)(2,1)S(1)}, bf16[256,256]{1,0:T(8,128)(2,1)}, u32[]{:S(2)}) copy-start(bf16[256,256]{1,0:T(8,128)(2,1)} %constant.5.clone.y_inverse_ref) | copy-start | bytes 393220
  0.7 1.5 %collective-permute-start = (bf16[256,128]{1,0:T(8,128)(2,1)}, bf16[256,128]{1,0:T(8,128)(2,1)S(1)}, u32[]{:S(2)}, u32[]{:S(2)}) collective-permute-start(bf16[256,128]{1,0:T(8,128)(2,1)} %bitcast.28), channel_id=1, source_target_pairs={{0,2},{1,3},{2,0},{3,1},{4,6},{5,7},{6,4},{7,5},{8,10},{9,11},{10,... | collective-permute-start | bytes 196616 | tf_op jit(solution)/shard_map/ppermute | solution.py:516
  0.8 0.8 %copy-start.3 = (bf16[1,32,8,128]{3,2,1,0:T(8,128)(2,1)S(1)}, bf16[1,32,8,128]{3,2,1,0:T(8,128)(2,1)}, u32[]{:S(2)}) copy-start(bf16[1,32,8,128]{3,2,1,0:T(8,128)(2,1)} %param.10) | copy-start | bytes 196612
  1.6 27.5 %copy-start.7 = (bf16[128]{0:T(256)(128)(2,1)S(1)}, bf16[128]{0:T(256)(128)(2,1)}, u32[]{:S(2)}) copy-start(bf16[128]{0:T(256)(128)(2,1)} %param.16) | copy-start | bytes 772
  1.6 27.5 %copy-start.9 = (f32[32]{0:T(128)S(1)}, f32[32]{0:T(128)}, u32[]{:S(2)}) copy-start(f32[32]{0:T(128)} %param.13) | copy-start | bytes 388
  1.6 27.6 %copy-start.8 = (f32[128]{0:T(128)S(1)}, f32[128]{0:T(128)}, u32[]{:S(2)}) copy-start(f32[128]{0:T(128)} %param.15) | copy-start | bytes 1540
  1.6 27.8 %copy-start.4 = (bf16[32,128]{1,0:T(8,128)(2,1)S(1)}, bf16[32,128]{1,0:T(8,128)(2,1)}, u32[]{:S(2)}) copy-start(bf16[32,128]{1,0:T(8,128)(2,1)} %refs_4_.1) | copy-start | bytes 24580
  1.6 27.8 %copy-start.5 = (bf16[32,32]{1,0:T(8,128)(2,1)S(1)}, bf16[32,32]{1,0:T(8,128)(2,1)}, u32[]{:S(2)}) copy-start(bf16[32,32]{1,0:T(8,128)(2,1)} %mix_ref.3) | copy-start | bytes 6148
  1.6 28.3 %copy-start.6 = (f32[1,8,128]{2,1,0:T(8,128)S(1)}, f32[1,8,128]{2,1,0:T(8,128)}, u32[]{:S(2)}) copy-start(f32[1,8,128]{2,1,0:T(8,128)} %param.17) | copy-start | bytes 12292
  3.4 13.0 %all-to-all-start = ((bf16[16,16,256]{2,1,0:T(8,128)(2,1)}), bf16[16,16,256]{2,1,0:T(8,128)(2,1)S(1)}, u32[]{:S(2)}, u32[]{:S(2)}) async-start(bf16[16,16,256]{2,1,0:T(8,128)(2,1)} %bitcast.1), calls=%async_computation | async-start | bytes 262144 | tf_op jit(solution)/shard_map/all_to_all | solution.py:529
  11.4 2.2 %copy-start = (f32[16,8,2,32,32]{4,3,2,1,0:T(8,128)S(1)}, f32[16,8,2,32,32]{4,3,2,1,0:T(8,128)}, u32[]{:S(2)}) copy-start(f32[16,8,2,32,32]{4,3,2,1,0:T(8,128)} %weight_ref.1) | copy-start | bytes 3145732
  26.3 3.7 %collective-permute-start.1 = (bf16[32,256]{1,0:T(8,128)(2,1)S(1)}, bf16[32,256]{1,0:T(8,128)(2,1)S(1)}, u32[]{:S(2)}, u32[]{:S(2)}) collective-permute-start(bf16[32,256]{1,0:T(8,128)(2,1)S(1)} %get-tuple-element.38), channel_id=1, source_target_pairs={{0,2},{1,3},{2,0},{3,1},{4,6},{5,7},{6,4},{7,5},{8,10},{9,11},{10,... | collective-permute-start | bytes 49160 | tf_op jit(solution)/shard_map/ppermute | solution.py:516
  31.2 1.2 %collective-permute-start.2 = (bf16[32,256]{1,0:T(8,128)(2,1)S(1)}, bf16[32,256]{1,0:T(8,128)(2,1)S(1)}, u32[]{:S(2)}, u32[]{:S(2)}) collective-permute-start(bf16[32,256]{1,0:T(8,128)(2,1)S(1)} %get-tuple-element.43.own_ref), channel_id=1, source_target_pairs={{0,2},{1,3},{2,0},{3,1},{4,6},{5,7},{6,4},{7,5},{8,10},{9,11},{10,... | collective-permute-start | bytes 49160 | tf_op jit(solution)/shard_map/ppermute | solution.py:516
  43.1 9.6 %all-to-all-start.3 = ((bf16[16,40,128]{2,1,0:T(8,128)(2,1)}), bf16[16,40,128]{2,1,0:T(8,128)(2,1)S(1)}, u32[]{:S(2)}, u32[]{:S(2)}) async-start(bf16[16,40,128]{2,1,0:T(8,128)(2,1)} %bitcast.12), calls=%async_computation.3 | async-start | bytes 327680 | tf_op jit(solution)/shard_map/all_to_all | solution.py:529
  52.9 4.0 %collective-permute-start.3 = (bf16[96,256]{1,0:T(8,128)(2,1)S(1)}, bf16[96,256]{1,0:T(8,128)(2,1)S(1)}, u32[]{:S(2)}, u32[]{:S(2)}) collective-permute-start(bf16[96,256]{1,0:T(8,128)(2,1)S(1)} %get-tuple-element.54), channel_id=1, source_target_pairs={{0,2},{1,3},{2,0},{3,1},{4,6},{5,7},{6,4},{7,5},{8,10},{9,11},{10,... | collective-permute-start | bytes 147464 | tf_op jit(solution)/shard_map/ppermute | solution.py:516

commit v14 on v13

--- a/solution.py
+++ b/solution.py
@@ -101,15 +101,22 @@
         self.partners = self.outer * narrow
         self.lanes = rows_y * channels
         middle, last = self.outer // 4, self.outer // 2 - 1
-        self.firsts = (last, middle, middle, middle)
+        self.lists = ((last, 1), (middle, 0), (middle, 0), (middle, 1))
 
     def here(self):
         wide = lax.axis_index("wide")
         return wide // 2, wide % 2
 
-    def listed(self, position, first):
+    def listed(self, position, transform):
         lines = self.outer // 2
-        return ((first + position // 2) & (lines - 1)) * 2 + position % 2
+        first, far = self.lists[transform]
+        return ((first + position // 2) & (lines - 1)) * 2 + (position % 2 ^ far)
+
+    def turned_narrow(self, transform):
+        return self.lists[transform][1] * (self.narrow - 1)
+
+    def in_list_order(self, blocks, transform):
+        return blocks[::-1] if self.lists[transform][1] else blocks
 
     def frequency(self, wide):
         index = (wide * self.modes) // MY
@@ -123,32 +130,33 @@
             value = jnp.where(frequency > 0, 2.0 * value, value)
         return value.astype(BF16)
 
-    def expanded(self, small):
+    def expanded(self, small, transform):
         row, column = grid_of(2 * MZ, small.shape[1])
-        same = (row >> 1) == ((column >> 1) & (MZ - 1))
+        turned = self.turned_narrow(transform) * self.kz
+        same = ((row >> 1) ^ turned) == ((column >> 1) & (MZ - 1))
         blocks = []
         for g in range(small.shape[0] // 2):
             value = jnp.where((row & 1) == 0, small[2 * g : 2 * g + 1], small[2 * g + 1 : 2 * g + 2])
             blocks.append(jnp.where(same, value, 0.0))
         return jnp.concatenate(blocks, axis=0)
 
-    def forward_x(self, first):
+    def forward_x(self, transform):
         outer, inner = self.here()
         row, column = grid_of(2 * self.outer, 4 * MZ)
         x = 2 * outer + (inner ^ (column // (2 * MZ)))
-        frequency = self.frequency(2 * self.listed(row >> 1, first) + inner)
+        frequency = self.frequency(2 * self.listed(row >> 1, transform) + inner)
         quarter = self.wide // 4
         small = cosine_of(x * frequency + quarter * ((row & 1) - (column & 1)), self.wide)
-        return self.expanded(small)
-
-    def inverse_x(self, first):
+        return self.expanded(small, transform)
+
+    def inverse_x(self, transform):
         outer, inner = self.here()
         row, column = grid_of(4, self.outer * 2 * MZ)
         x = 2 * outer + (inner ^ (row >> 1))
-        frequency = self.frequency(2 * self.listed(column // (2 * MZ), first) + inner)
+        frequency = self.frequency(2 * self.listed(column // (2 * MZ), transform) + inner)
         quarter = self.wide // 4
         small = cosine_of(x * frequency + quarter * ((column & 1) - (row & 1)), self.wide)
-        return self.expanded(small).astype(BF16)
+        return self.expanded(small, transform).astype(BF16)
 
 
 def repeat_rows(out_ref, block):
@@ -183,11 +191,18 @@
     return jnp.concatenate(blocks, axis=0), shares
 
 
-def analysed(place, pieces, y_forward, copies):
+def analysed(place, pieces, y_forward, copies, transform):
     height = 2 * MZ
     turned = sum(
         pieces[first : first + height].astype(F32) for first in range(0, pieces.shape[0], height)
     )
+    step = 2 * place.kz
+    turned = jnp.concatenate(
+        place.in_list_order(
+            [turned[first : first + step] for first in range(0, height, step)], transform
+        ),
+        axis=0,
+    )
     channels = place.channels
     lines = jnp.concatenate(
         [turned[:, y * channels : (y + 1) * channels] for y in range(place.rows_y)], axis=0
@@ -195,7 +210,7 @@
     return dot(y_forward, jnp.concatenate([lines.astype(BF16)] * copies, axis=1))
 
 
-def spread_lines(place, modes, y_inverse):
+def spread_lines(place, modes, y_inverse, transform):
     lines = dot(y_inverse, modes)
     step = 2 * place.kz
     blocks = []
@@ -203,7 +218,7 @@
         first = n * place.rows_y
         parts = [lines[(first + y) * step : (first + y + 1) * step] for y in range(place.rows_y)]
         blocks.append(jnp.concatenate(parts, axis=1))
-    return jnp.concatenate(blocks, axis=0).astype(BF16)
+    return jnp.concatenate(place.in_list_order(blocks, transform), axis=0).astype(BF16)
 
 
 def turn_matrix(place, forward):
@@ -237,7 +252,7 @@
     twin = dot_nt(place.z_table(False), twin_ref[...]).astype(BF16)
     twin = dot(twin, turn_matrix(place, True)).astype(BF16)
     values = jnp.concatenate([spectra_ref[...], twin], axis=0)
-    tables = jnp.concatenate(halves(place.forward_x(place.firsts[0])), axis=1)
+    tables = jnp.concatenate(halves(place.forward_x(0)), axis=1)
     send_ref[...] = dot(tables, jnp.concatenate([values, values], axis=0)).astype(BF16)
 
 
@@ -271,7 +286,7 @@
     place, pieces_ref, y_forward_ref, y_inverse_ref, weight_ref, spectrum_ref, send_ref
 ):
     kz, channels = place.kz, place.channels
-    spectrum = analysed(place, pieces_ref[...], y_forward_ref[...], kz)
+    spectrum = analysed(place, pieces_ref[...], y_forward_ref[...], kz, 0)
     spectrum_ref[...] = spectrum[:, :channels]
     row, lane = grid_of(*spectrum.shape)
     blocked = jnp.where(row % kz == lane // channels, spectrum, 0.0)
@@ -285,12 +300,12 @@
             mixed.append(real[:kz] - imag[kz:])
             mixed.append(imag[:kz] + real[kz:])
     mode = jnp.concatenate(mixed, axis=0).astype(BF16)
-    repeat_rows(send_ref, spread_lines(place, mode, y_inverse_ref[...]))
-
-
-def part_kernel(place, first, pieces_ref, *refs):
+    repeat_rows(send_ref, spread_lines(place, mode, y_inverse_ref[...], 1))
+
+
+def part_kernel(place, transform, pieces_ref, *refs):
     pieces, shares = read_pieces(place, pieces_ref)
-    lines = dot(place.inverse_x(first), pieces)
+    lines = dot(place.inverse_x(transform), pieces)
     height = 2 * MZ
     if shares is None:
         own_ref, send_ref = refs
@@ -306,9 +321,10 @@
     def chosen(part):
         def condition(row, column):
             owner, source = (row % channels) // 2, column // 8
+            turned = place.turned_narrow(2) ^ place.turned_narrow(transform)
             return (
-                (place.listed(owner // narrow, place.firsts[2]) == place.listed(source // narrow, first))
-                & (owner % narrow == source % narrow)
+                (place.listed(owner // narrow, 2) == place.listed(source // narrow, transform))
+                & (owner % narrow == (source % narrow) ^ turned)
                 & (column % 8 == 4 * part + 2 * (row // channels) + row % 2)
             )
 
@@ -366,7 +382,7 @@
 
 
 def sums_kernel(place, field_ref, gradient_ref, hidden_ref, head_slope_ref, *refs):
-    refs[-1][...] = jnp.concatenate(halves(place.forward_x(place.firsts[2])), axis=1)
+    refs[-1][...] = jnp.concatenate(halves(place.forward_x(2)), axis=1)
     grad_mix = dot_nt(field_ref[...], gradient_ref[...])
     grad_head = dot_nt(hidden_ref[...], head_slope_ref[...])
     if not place.fold:
@@ -392,7 +408,7 @@
 ):
     kz, channels = place.kz, place.channels
     pieces, shares = read_pieces(place, pieces_ref)
-    adjoint = analysed(place, pieces, y_forward_ref[...], 1)
+    adjoint = analysed(place, pieces, y_forward_ref[...], 1, 2)
     adjoint_ref[...] = adjoint
     turned = []
     for first in range(0, adjoint.shape[0], 2 * kz):
@@ -413,7 +429,7 @@
         kz * channels, channels, lambda row, column: row % channels == column
     )
     modes_back = dot(pulled, gather).astype(BF16)
-    block = spread_lines(place, modes_back, y_inverse_ref[...])
+    block = spread_lines(place, modes_back, y_inverse_ref[...], 3)
     if shares is None:
         repeat_rows(send_ref, block)
         return
@@ -516,10 +532,10 @@
         return lax.ppermute(send, ("wide", "narrow"), pairs)
 
     def exchange(send, transform):
-        first = place.firsts[transform]
+        turned = place.turned_narrow(transform)
         groups = [
             [
-                (2 * place.listed(outer, first) + inner) * narrow + n
+                (2 * place.listed(outer, transform) + inner) * narrow + (n ^ turned)
                 for outer in range(place.outer)
                 for n in range(narrow)
             ]
@@ -551,7 +567,7 @@
     spectrum, send = run(mode_kernel, [((mode_lines, channels), F32), plain], "mode")(
         exchange(send, 0), y_forward, y_inverse, weight
     )
-    part = functools.partial(part_kernel, place, place.firsts[1])
+    part = functools.partial(part_kernel, place, 1)
     own, send = call(part, [own_lines, twin_plain], "part")(exchange(send, 1))
     pointwise, head_turned, z_doubled = run(
         ready_kernel,
@@ -621,7 +637,7 @@
     )(mix_weight, grad_pre)
     outs = [own_lines, twin_shared] + ([sums_shape] if place.fold else [])
     after = (done,) if place.fold else ()
-    part = functools.partial(part_kernel, place, place.firsts[3])
+    part = functools.partial(part_kernel, place, 3)
     own, send, *sums = call(part, outs, "part")(exchange(send, 3), *after)
     outs = [((cells, z_count), BF16), ((rows_y, z_count), F32)]
     if place.fold:

time: 58.7 us -> 60 us (1.022)
  starting transfers between devices: 19.2 us -> 22.2 us
  waiting for transfers between devices: 5.26 us -> 2.94 us
  blocking collectives: 17.5 us -> 18.2 us
    all_to_all x2, starting transfers between devices: 12.8 us -> 15.6 us  [exchange(): lax.all_to_all(pieces, ('wide', 'narrow'), 0, 0, axis_index_groups=groups...]
    all_to_all x2, waiting for transfers between devices: 3.6 us -> 1.28 us  [exchange(): lax.all_to_all(pieces, ('wide', 'narrow'), 0, 0, axis_index_groups=groups...]
    all_to_all x2, blocking collectives: 17.5 us -> 18.2 us  [exchange(): lax.all_to_all(pieces, ('wide', 'narrow'), 0, 0, axis_index_groups=groups...]
  transfers between devices with their start and end apart: 6 -> 6, of which waited for: 6 -> 5; matrix products, arithmetic and copies ran while one was open for 1% -> 1% of each run, Pallas kernels for 9% -> 9%
where the time goes in v14:
time: 60 us; the launch traced here: 59.3 us
  starting transfers between devices  22.2 us (37%)
  blocking collectives  18.2 us (30%)
  Pallas kernels  11.8 us (20%)
  local copies, waits for them, and re-layouts  3.37 us (6%)
  waiting for transfers between devices  2.94 us (5%)
  between operations  0.74 us (1%)
    all_to_all x2, blocking collectives, exchange(): lax.all_to_all(pieces, ('wide', 'narrow'), 0, 0, axis_index_groups=groups...  18.2 us
    all_to_all x2, starting transfers between devices, exchange(): lax.all_to_all(pieces, ('wide', 'narrow'), 0, 0, axis_index_groups=groups...  15.6 us
    ppermute x4, starting transfers between devices, to_twin(): return lax.ppermute(send, ('wide', 'narrow'), pairs)  6.55 us
    pallas_call x1, Pallas kernels, body(): pl.pallas_call(outer_kernel, grid=(modes // some,), in_specs=[pl.BlockSpe...  3.55 us
    unnamed x20, local copies, waits for them, and re-layouts  3.06 us
    pallas_call x1, Pallas kernels, body(): run(back_kernel, [((mode_lines, channels), F32), shared], 'back')  1.67 us
    ppermute x4, waiting for transfers between devices, to_twin(): return lax.ppermute(send, ('wide', 'narrow'), pairs)  1.66 us
    all_to_all x2, waiting for transfers between devices, exchange(): lax.all_to_all(pieces, ('wide', 'narrow'), 0, 0, axis_index_groups=groups...  1.28 us
  transfers between devices with their start and end apart: 6, of which 5 were waited for; matrix products, arithmetic and copies ran while one was open for 1% of the time, Pallas kernels for 9%

profile of v14, /device:TPU:1, one launch (start us, length us, event | category | flops | bytes accessed | tf_op | source)
XLA Modules:
  0.0 59.3 jit_solution(12882154377238953776)
XLA Ops:
  0.6 0.0 copy-start.1
  0.6 0.0 copy-start.2
  0.7 0.1 collective-permute-start
  0.8 0.0 copy-start.3
  0.8 0.8 %copy-done.3 = bf16[1,32,8,128]{3,2,1,0:T(8,128)(2,1)S(1)} copy-done((bf16[1,32,8,128]{3,2,1,0:T(8,128)(2,1)S(1)}, bf16[1,32,8,128]{3,2,1,0:T(8,128)(2,1)}, u32[]{:S(2)}) %copy-start.3) | copy-done | bytes 65560
  1.6 0.0 copy-start.7
  1.6 0.0 copy-start.9
  1.6 0.0 copy-start.8
  1.6 0.0 copy-start.4
  1.6 0.0 copy-start.5
  1.6 0.0 copy-start.6
  1.7 0.3 own.1
  2.0 0.2 collective-permute-done.twin_ref
  2.2 1.2 %start.1 = bf16[256,256]{1,0:T(8,128)(2,1)} custom-call(bf16[32,256]{1,0:T(8,128)(2,1)S(1)} %get-tuple-element.35.spectra_ref, bf16[256,128]{1,0:T(8,128)(2,1)S(1)} %collective-permute-done.twin_ref), custom_call_target="tpu_custom_call" | custom-call | flops 4194304 | bytes 524288 | tf_op jit(solution)/shard_map/start/pallas_call | solution.py:564
  3.4 9.8 %all-to-all-start = ((bf16[16,16,256]{2,1,0:T(8,128)(2,1)}), bf16[16,16,256]{2,1,0:T(8,128)(2,1)S(1)}, u32[]{:S(2)}, u32[]{:S(2)}) async-start(bf16[16,16,256]{2,1,0:T(8,128)(2,1)} %bitcast.1), calls=%async_computation | async-start | bytes 262144 | tf_op jit(solution)/shard_map/all_to_all | solution.py:545
  13.2 0.0 copy-start
  13.2 2.2 %copy-done = f32[16,8,2,32,32]{4,3,2,1,0:T(8,128)S(1)} copy-done((f32[16,8,2,32,32]{4,3,2,1,0:T(8,128)S(1)}, f32[16,8,2,32,32]{4,3,2,1,0:T(8,128)}, u32[]{:S(2)}) %copy-start) | copy-done | bytes 1048600
  15.4 0.5 pack.1.weight_ref
  15.9 1.3 %all-to-all-done = bf16[16,16,256]{2,1,0:T(8,128)(2,1)S(1)} async-done(((bf16[16,16,256]{2,1,0:T(8,128)(2,1)}), bf16[16,16,256]{2,1,0:T(8,128)(2,1)S(1)}, u32[]{:S(2)}, u32[]{:S(2)}) %all-to-all-start) | async-done | bytes 131104 | tf_op jit(solution)/shard_map/all_to_all | solution.py:545
  17.2 0.0 copy-done.1
  17.2 0.0 copy-done.2
  17.2 0.9 %mode.1 = (f32[256,32]{1,0:T(8,128)S(1)}, bf16[256,256]{1,0:T(8,128)(2,1)S(1)}) custom-call(bf16[256,256]{1,0:T(8,128)(2,1)S(1)} %bitcast.23, bf16[256,256]{1,0:T(8,128)(2,1)S(1)} %copy-done.1, bf16[256,256]{1,0:T(8,128)(2,1)S(1)} %copy-done.2, bf16[4,256,256]{2,1,0:T(8,128)(2,1)S(1)} %pack.1.weight_ref), custom_call_target="tpu_custom_call" | custom-call | flops 4194304 | bytes 524288 | tf_op jit(solution)/shard_map/mode/pallas_call | solution.py:567
  18.1 9.4 %all_to_all.20 = bf16[16,16,256]{2,1,0:T(8,128)(2,1)S(1)} all-to-all(bf16[16,16,256]{2,1,0:T(8,128)(2,1)S(1)} %bitcast.27), channel_id=1, replica_groups={{16,17,20,21,24,25,28,29,0,1,4,5,8,9,12,13},{18,19,22,23,26,27,30,31,2,..., dimensions={0} | all-to-all | bytes 262144 | tf_op jit(solution)/shard_map/all_to_all | solution.py:545
  27.5 0.2 part.2
  27.7 2.9 %collective-permute-start.1 = (bf16[32,256]{1,0:T(8,128)(2,1)S(1)}, bf16[32,256]{1,0:T(8,128)(2,1)S(1)}, u32[]{:S(2)}, u32[]{:S(2)}) collective-permute-start(bf16[32,256]{1,0:T(8,128)(2,1)S(1)} %get-tuple-element.38), channel_id=1, source_target_pairs={{0,2},{1,3},{2,0},{3,1},{4,6},{5,7},{6,4},{7,5},{8,10},{9,11},{10,... | collective-permute-start | bytes 49160 | tf_op jit(solution)/shard_map/ppermute | solution.py:532
  30.6 0.0 copy-done.7
  30.6 0.0 copy-done.9
  30.6 0.1 copy.15.mix_bias_ref
  30.7 0.0 copy-done.8
  30.7 0.1 copy.16.refs_6_
  30.8 0.1 copy.17.refs_8_
  30.9 0.0 copy-done.4
  30.9 0.0 copy-done.5
  30.9 0.2 ready.1
  31.1 0.3 collective-permute-done.1.refs_1_
  31.4 0.0 copy-done.6
  31.4 1.2 %cell.1 = (f32[8,128]{1,0:T(8,128)S(1)}, bf16[32,1024]{1,0:T(8,128)(2,1)S(1)}, bf16[32,256]{1,0:T(8,128)(2,1)S(1)}, bf16[32,1024]{1,0:T(8,128)(2,1)S(1)}, bf16[128,1024]{1,0:T(8,128)(2,1)S(1)}) custom-call(f32[32,256]{1,0:T(8,128)S(1)} %get-tuple-element.37.refs_0_, bf16[32,256]{1,0:T(8,128)(2,1)S(1)} %collective-permute-done.1.refs_1_, ...), custom_call_target="tpu_custom_call" | custom-call | flops 4194304 | bytes 524288 | tf_op jit(solution)/shard_map/cell/pallas_call | solution.py:577
  32.7 0.4 collective-permute-start.2
  33.1 0.4 sums.1
  33.4 0.5 collective-permute-done.2.got_ref
  33.9 0.2 fold.1
  34.1 8.8 %all_to_all.21 = bf16[16,40,128]{2,1,0:T(8,128)(2,1)S(1)} all-to-all(bf16[16,40,128]{2,1,0:T(8,128)(2,1)S(1)} %bitcast.21), channel_id=1, replica_groups={{16,17,20,21,24,25,28,29,0,1,4,5,8,9,12,13},{18,19,22,23,26,27,30,31,2,..., dimensions={0} | all-to-all | bytes 327680 | tf_op jit(solution)/shard_map/all_to_all | solution.py:545
  42.9 1.7 %back.1 = (f32[256,32]{1,0:T(8,128)S(1)}, bf16[640,128]{1,0:T(8,128)(2,1)}) custom-call(bf16[640,128]{1,0:T(8,128)(2,1)S(1)} %bitcast.22, bf16[256,256]{1,0:T(8,128)(2,1)S(1)} %copy-done.1, bf16[256,256]{1,0:T(8,128)(2,1)S(1)} %copy-done.2, bf16[4,256,256]{2,1,0:T(8,128)(2,1)S(1)} %pack.1.weight_ref), custom_call_target="tpu_custom_call" | custom-call | flops 4194304 | bytes 524288 | tf_op jit(solution)/shard_map/back/pallas_call | solution.py:609
  44.6 5.8 %all-to-all-start.3 = ((bf16[16,40,128]{2,1,0:T(8,128)(2,1)}), bf16[16,40,128]{2,1,0:T(8,128)(2,1)S(1)}, u32[]{:S(2)}, u32[]{:S(2)}) async-start(bf16[16,40,128]{2,1,0:T(8,128)(2,1)} %bitcast.12), calls=%async_computation.3 | async-start | bytes 327680 | tf_op jit(solution)/shard_map/all_to_all | solution.py:545
  50.4 3.5 %outer.1 = (f32[16,8,2,32,32]{4,3,2,1,0:T(8,128)}, f32[8,128]{1,0:T(8,128)S(1)}) custom-call(f32[16,16,32]{2,1,0:T(8,128)S(1)} %bitcast.25, f32[16,16,32]{2,1,0:T(8,128)S(1)} %bitcast.26), custom_call_target="tpu_custom_call" | custom-call | flops 4194304 | bytes 5242880 | tf_op jit(solution)/shard_map/outer/pallas_call | solution.py:613
  54.0 0.0 all-to-all-done.3
  54.0 0.3 part.3
  54.2 3.2 %collective-permute-start.3 = (bf16[96,256]{1,0:T(8,128)(2,1)S(1)}, bf16[96,256]{1,0:T(8,128)(2,1)S(1)}, u32[]{:S(2)}, u32[]{:S(2)}) collective-permute-start(bf16[96,256]{1,0:T(8,128)(2,1)S(1)} %get-tuple-element.54), channel_id=1, source_target_pairs={{0,2},{1,3},{2,0},{3,1},{4,6},{5,7},{6,4},{7,5},{8,10},{9,11},{10,... | collective-permute-start | bytes 147464 | tf_op jit(solution)/shard_map/ppermute | solution.py:532
  57.4 0.2 pointwise.1
  57.6 0.7 %collective-permute-done.3.refs_1_ = bf16[96,256]{1,0:T(8,128)(2,1)S(1)} collective-permute-done((bf16[96,256]{1,0:T(8,128)(2,1)S(1)}, bf16[96,256]{1,0:T(8,128)(2,1)S(1)}, u32[]{:S(2)}, u32[]{:S(2)}) %collective-permute-start.3) | collective-permute-done | bytes 49184 | tf_op jit(solution)/shard_map/ppermute | solution.py:532
  58.3 1.0 %finish.1 = (bf16[256,128]{1,0:T(8,128)(2,1)}, f32[8,128]{1,0:T(8,128)}, f32[32,32]{1,0:T(8,128)}, f32[32,128]{1,0:T(8,128)}) custom-call(f32[32,256]{1,0:T(8,128)S(1)} %get-tuple-element.53.refs_0_, bf16[96,256]{1,0:T(8,128)(2,1)S(1)} %collective-permute-done.3.refs_1_, bf16[32,128]{1,0:T(8,128)(2,1)S(1)} %get-tuple-element.55.refs_2_, ...), custom_call_target="tpu_custom_call" | custom-call | flops 4194304 | bytes 524288 | tf_op jit(solution)/shard_map/finish/pallas_call | solution.py:645
  (1 shorter events, 0.0 us)
Async XLA Ops:
  0.6 16.5 %copy-start.1 = (bf16[256,256]{1,0:T(8,128)(2,1)S(1)}, bf16[256,256]{1,0:T(8,128)(2,1)}, u32[]{:S(2)}) copy-start(bf16[256,256]{1,0:T(8,128)(2,1)} %constant.4.clone.y_forward_ref) | copy-start | bytes 393220
  0.6 16.5 %copy-start.2 = (bf16[256,256]{1,0:T(8,128)(2,1)S(1)}, bf16[256,256]{1,0:T(8,128)(2,1)}, u32[]{:S(2)}) copy-start(bf16[256,256]{1,0:T(8,128)(2,1)} %constant.5.clone.y_inverse_ref) | copy-start | bytes 393220
  0.7 1.5 %collective-permute-start = (bf16[256,128]{1,0:T(8,128)(2,1)}, bf16[256,128]{1,0:T(8,128)(2,1)S(1)}, u32[]{:S(2)}, u32[]{:S(2)}) collective-permute-start(bf16[256,128]{1,0:T(8,128)(2,1)} %bitcast.28), channel_id=1, source_target_pairs={{0,2},{1,3},{2,0},{3,1},{4,6},{5,7},{6,4},{7,5},{8,10},{9,11},{10,... | collective-permute-start | bytes 196616 | tf_op jit(solution)/shard_map/ppermute | solution.py:532
  0.8 0.8 %copy-start.3 = (bf16[1,32,8,128]{3,2,1,0:T(8,128)(2,1)S(1)}, bf16[1,32,8,128]{3,2,1,0:T(8,128)(2,1)}, u32[]{:S(2)}) copy-start(bf16[1,32,8,128]{3,2,1,0:T(8,128)(2,1)} %param.10) | copy-start | bytes 196612
  1.6 29.0 %copy-start.7 = (bf16[128]{0:T(256)(128)(2,1)S(1)}, bf16[128]{0:T(256)(128)(2,1)}, u32[]{:S(2)}) copy-start(bf16[128]{0:T(256)(128)(2,1)} %param.16) | copy-start | bytes 772
  1.6 29.0 %copy-start.9 = (f32[32]{0:T(128)S(1)}, f32[32]{0:T(128)}, u32[]{:S(2)}) copy-start(f32[32]{0:T(128)} %param.13) | copy-start | bytes 388
  1.6 29.1 %copy-start.8 = (f32[128]{0:T(128)S(1)}, f32[128]{0:T(128)}, u32[]{:S(2)}) copy-start(f32[128]{0:T(128)} %param.15) | copy-start | bytes 1540
  1.6 29.3 %copy-start.4 = (bf16[32,128]{1,0:T(8,128)(2,1)S(1)}, bf16[32,128]{1,0:T(8,128)(2,1)}, u32[]{:S(2)}) copy-start(bf16[32,128]{1,0:T(8,128)(2,1)} %refs_4_.1) | copy-start | bytes 24580
  1.6 29.3 %copy-start.5 = (bf16[32,32]{1,0:T(8,128)(2,1)S(1)}, bf16[32,32]{1,0:T(8,128)(2,1)}, u32[]{:S(2)}) copy-start(bf16[32,32]{1,0:T(8,128)(2,1)} %mix_ref.3) | copy-start | bytes 6148
  1.6 29.8 %copy-start.6 = (f32[1,8,128]{2,1,0:T(8,128)S(1)}, f32[1,8,128]{2,1,0:T(8,128)}, u32[]{:S(2)}) copy-start(f32[1,8,128]{2,1,0:T(8,128)} %param.17) | copy-start | bytes 12292
  3.4 13.8 %all-to-all-start = ((bf16[16,16,256]{2,1,0:T(8,128)(2,1)}), bf16[16,16,256]{2,1,0:T(8,128)(2,1)S(1)}, u32[]{:S(2)}, u32[]{:S(2)}) async-start(bf16[16,16,256]{2,1,0:T(8,128)(2,1)} %bitcast.1), calls=%async_computation | async-start | bytes 262144 | tf_op jit(solution)/shard_map/all_to_all | solution.py:545
  13.2 2.2 %copy-start = (f32[16,8,2,32,32]{4,3,2,1,0:T(8,128)S(1)}, f32[16,8,2,32,32]{4,3,2,1,0:T(8,128)}, u32[]{:S(2)}) copy-start(f32[16,8,2,32,32]{4,3,2,1,0:T(8,128)} %weight_ref.1) | copy-start | bytes 3145732
  27.7 3.7 %collective-permute-start.1 = (bf16[32,256]{1,0:T(8,128)(2,1)S(1)}, bf16[32,256]{1,0:T(8,128)(2,1)S(1)}, u32[]{:S(2)}, u32[]{:S(2)}) collective-permute-start(bf16[32,256]{1,0:T(8,128)(2,1)S(1)} %get-tuple-element.38), channel_id=1, source_target_pairs={{0,2},{1,3},{2,0},{3,1},{4,6},{5,7},{6,4},{7,5},{8,10},{9,11},{10,... | collective-permute-start | bytes 49160 | tf_op jit(solution)/shard_map/ppermute | solution.py:532
  32.7 1.2 %collective-permute-start.2 = (bf16[32,256]{1,0:T(8,128)(2,1)S(1)}, bf16[32,256]{1,0:T(8,128)(2,1)S(1)}, u32[]{:S(2)}, u32[]{:S(2)}) collective-permute-start(bf16[32,256]{1,0:T(8,128)(2,1)S(1)} %get-tuple-element.43.own_ref), channel_id=1, source_target_pairs={{0,2},{1,3},{2,0},{3,1},{4,6},{5,7},{6,4},{7,5},{8,10},{9,11},{10,... | collective-permute-start | bytes 49160 | tf_op jit(solution)/shard_map/ppermute | solution.py:532
  44.6 9.4 %all-to-all-start.3 = ((bf16[16,40,128]{2,1,0:T(8,128)(2,1)}), bf16[16,40,128]{2,1,0:T(8,128)(2,1)S(1)}, u32[]{:S(2)}, u32[]{:S(2)}) async-start(bf16[16,40,128]{2,1,0:T(8,128)(2,1)} %bitcast.12), calls=%async_computation.3 | async-start | bytes 327680 | tf_op jit(solution)/shard_map/all_to_all | solution.py:545
  54.2 4.0 %collective-permute-start.3 = (bf16[96,256]{1,0:T(8,128)(2,1)S(1)}, bf16[96,256]{1,0:T(8,128)(2,1)S(1)}, u32[]{:S(2)}, u32[]{:S(2)}) collective-permute-start(bf16[96,256]{1,0:T(8,128)(2,1)S(1)} %get-tuple-element.54), channel_id=1, source_target_pairs={{0,2},{1,3},{2,0},{3,1},{4,6},{5,7},{6,4},{7,5},{8,10},{9,11},{10,... | collective-permute-start | bytes 147464 | tf_op jit(solution)/shard_map/ppermute | solution.py:532

commit v15 on v13

--- a/solution.py
+++ b/solution.py
@@ -100,6 +100,7 @@
         self.outer = wide // 2
         self.partners = self.outer * narrow
         self.lanes = rows_y * channels
+        self.along = kz % 8 == 0
         middle, last = self.outer // 4, self.outer // 2 - 1
         self.firsts = (last, middle, middle, middle)
 
@@ -109,7 +110,11 @@
 
     def listed(self, position, first):
         lines = self.outer // 2
-        return ((first + position // 2) & (lines - 1)) * 2 + position % 2
+        if self.along:
+            line, rest = position % lines, position // lines
+            return ((first + line) & (lines - 1)) * 2 + rest // self.narrow, rest % self.narrow
+        line, rest = position // (2 * self.narrow), position % (2 * self.narrow)
+        return ((first + line) & (lines - 1)) * 2 + rest // self.narrow, rest % self.narrow
 
     def frequency(self, wide):
         index = (wide * self.modes) // MY
@@ -123,49 +128,60 @@
             value = jnp.where(frequency > 0, 2.0 * value, value)
         return value.astype(BF16)
 
-    def expanded(self, small):
-        row, column = grid_of(2 * MZ, small.shape[1])
-        same = (row >> 1) == ((column >> 1) & (MZ - 1))
+    def forward_x(self, first):
+        outer, inner = self.here()
+        step, quarter = 2 * self.kz, self.wide // 4
+        row, column = grid_of(2 * self.partners, 4 * MZ)
+        x = 2 * outer + (inner ^ (column // (2 * MZ)))
+        frequency = self.frequency(2 * self.listed(row >> 1, first)[0] + inner)
+        small = cosine_of(x * frequency + quarter * ((row & 1) - (column & 1)), self.wide)
+        row, column = grid_of(step, 4 * MZ)
         blocks = []
-        for g in range(small.shape[0] // 2):
+        for p in range(self.partners):
+            _, narrow = self.listed(p, first)
+            same = narrow * self.kz + (row >> 1) == ((column >> 1) & (MZ - 1))
+            value = jnp.where((row & 1) == 0, small[2 * p : 2 * p + 1], small[2 * p + 1 : 2 * p + 2])
+            blocks.append(jnp.where(same, value, 0.0))
+        return jnp.concatenate(blocks, axis=0)
+
+    def inverse_x(self, first):
+        outer, inner = self.here()
+        step, quarter = 2 * self.kz, self.wide // 4
+        row, column = grid_of(4, self.partners * step)
+        x = 2 * outer + (inner ^ (row >> 1))
+        frequency = self.frequency(2 * self.listed(column // step, first)[0] + inner)
+        small = cosine_of(x * frequency + quarter * ((column & 1) - (row & 1)), self.wide)
+        row, column = grid_of(2 * MZ, self.partners * step)
+        narrow = self.listed(column // step, first)[1]
+        same = (row >> 1) == narrow * self.kz + (column >> 1) % self.kz
+        blocks = []
+        for g in range(2):
             value = jnp.where((row & 1) == 0, small[2 * g : 2 * g + 1], small[2 * g + 1 : 2 * g + 2])
             blocks.append(jnp.where(same, value, 0.0))
-        return jnp.concatenate(blocks, axis=0)
-
-    def forward_x(self, first):
-        outer, inner = self.here()
-        row, column = grid_of(2 * self.outer, 4 * MZ)
-        x = 2 * outer + (inner ^ (column // (2 * MZ)))
-        frequency = self.frequency(2 * self.listed(row >> 1, first) + inner)
-        quarter = self.wide // 4
-        small = cosine_of(x * frequency + quarter * ((row & 1) - (column & 1)), self.wide)
-        return self.expanded(small)
-
-    def inverse_x(self, first):
-        outer, inner = self.here()
-        row, column = grid_of(4, self.outer * 2 * MZ)
-        x = 2 * outer + (inner ^ (row >> 1))
-        frequency = self.frequency(2 * self.listed(column // (2 * MZ), first) + inner)
-        quarter = self.wide // 4
-        small = cosine_of(x * frequency + quarter * ((column & 1) - (row & 1)), self.wide)
-        return self.expanded(small).astype(BF16)
-
-
-def repeat_rows(out_ref, block):
-    height = block.shape[0]
-    for first in range(0, out_ref.shape[0], height):
-        out_ref[first : first + height] = block
-
-
-def write_pieces(place, send_ref, block, shares):
+        return jnp.concatenate(blocks, axis=0).astype(BF16)
+
+
+def repeat_rows(place, out_ref, block, first):
+    step, height = 2 * place.kz, block.shape[0]
+    if not place.along:
+        for start in range(0, out_ref.shape[0], height):
+            out_ref[start : start + height] = block
+        return
+    for p in range(place.partners):
+        _, narrow = place.listed(p, first)
+        out_ref[p * step : (p + 1) * step] = block[narrow * step : (narrow + 1) * step]
+
+
+def write_pieces(place, send_ref, block, shares, first=None):
     step, half = 2 * place.kz, place.lanes // 2
     height = send_ref.shape[0] // place.partners
     for p in range(place.partners):
-        own = block[p * step % block.shape[0] :][:step]
-        first = p * height
-        send_ref[first : first + step] = own[:, :half]
-        send_ref[first + step : first + 2 * step] = own[:, half:]
-        send_ref[first + 2 * step : first + height] = shares[p * 8 % shares.shape[0] :][:8]
+        index = p if first is None else place.listed(p, first)[1]
+        own = block[index * step : (index + 1) * step]
+        start = p * height
+        send_ref[start : start + step] = own[:, :half]
+        send_ref[start + step : start + 2 * step] = own[:, half:]
+        send_ref[start + 2 * step : start + height] = shares[p * 8 % shares.shape[0] :][:8]
 
 
 def read_pieces(place, pieces_ref):
@@ -183,11 +199,19 @@
     return jnp.concatenate(blocks, axis=0), shares
 
 
-def analysed(place, pieces, y_forward, copies):
-    height = 2 * MZ
-    turned = sum(
-        pieces[first : first + height].astype(F32) for first in range(0, pieces.shape[0], height)
-    )
+def analysed(place, pieces, y_forward, copies, first):
+    if place.along:
+        step = 2 * place.kz
+        halves_of = [[] for _ in range(place.narrow)]
+        for p in range(place.partners):
+            part = pieces[p * step : (p + 1) * step].astype(F32)
+            halves_of[place.listed(p, first)[1]].append(part)
+        turned = jnp.concatenate([sum(parts[1:], parts[0]) for parts in halves_of], axis=0)
+    else:
+        height = 2 * MZ
+        turned = sum(
+            pieces[start : start + height].astype(F32) for start in range(0, pieces.shape[0], height)
+        )
     channels = place.channels
     lines = jnp.concatenate(
         [turned[:, y * channels : (y + 1) * channels] for y in range(place.rows_y)], axis=0
@@ -271,7 +295,7 @@
     place, pieces_ref, y_forward_ref, y_inverse_ref, weight_ref, spectrum_ref, send_ref
 ):
     kz, channels = place.kz, place.channels
-    spectrum = analysed(place, pieces_ref[...], y_forward_ref[...], kz)
+    spectrum = analysed(place, pieces_ref[...], y_forward_ref[...], kz, place.firsts[0])
     spectrum_ref[...] = spectrum[:, :channels]
     row, lane = grid_of(*spectrum.shape)
     blocked = jnp.where(row % kz == lane // channels, spectrum, 0.0)
@@ -285,7 +309,7 @@
             mixed.append(real[:kz] - imag[kz:])
             mixed.append(imag[:kz] + real[kz:])
     mode = jnp.concatenate(mixed, axis=0).astype(BF16)
-    repeat_rows(send_ref, spread_lines(place, mode, y_inverse_ref[...]))
+    repeat_rows(place, send_ref, spread_lines(place, mode, y_inverse_ref[...]), place.firsts[1])
 
 
 def part_kernel(place, first, pieces_ref, *refs):
@@ -301,14 +325,15 @@
     own_ref[...] = lines[:height]
     send_ref[:height] = lines[height:].astype(BF16)
     got = jnp.concatenate(shares, axis=0).astype(BF16)
-    channels, narrow = place.channels, place.narrow
+    channels = place.channels
 
     def chosen(part):
         def condition(row, column):
-            owner, source = (row % channels) // 2, column // 8
+            owner = place.listed((row % channels) // 2, place.firsts[2])
+            source = place.listed(column // 8, first)
             return (
-                (place.listed(owner // narrow, place.firsts[2]) == place.listed(source // narrow, first))
-                & (owner % narrow == source % narrow)
+                (owner[0] == source[0])
+                & (owner[1] == source[1])
                 & (column % 8 == 4 * part + 2 * (row // channels) + row % 2)
             )
 
@@ -392,7 +417,7 @@
 ):
     kz, channels = place.kz, place.channels
     pieces, shares = read_pieces(place, pieces_ref)
-    adjoint = analysed(place, pieces, y_forward_ref[...], 1)
+    adjoint = analysed(place, pieces, y_forward_ref[...], 1, place.firsts[2])
     adjoint_ref[...] = adjoint
     turned = []
     for first in range(0, adjoint.shape[0], 2 * kz):
@@ -415,12 +440,12 @@
     modes_back = dot(pulled, gather).astype(BF16)
     block = spread_lines(place, modes_back, y_inverse_ref[...])
     if shares is None:
-        repeat_rows(send_ref, block)
+        repeat_rows(place, send_ref, block, place.firsts[3])
         return
     total = sum(shares[1:], shares[0])
     high, low = halves(total[0:4] + total[4:8])
     split = jnp.concatenate([high.astype(F32), low.astype(F32)], axis=0)
-    write_pieces(place, send_ref, block, split.astype(BF16))
+    write_pieces(place, send_ref, block, split.astype(BF16), place.firsts[3])
 
 
 def outer_kernel(spectrum_ref, adjoint_ref, out_ref, done_ref):
@@ -517,14 +542,8 @@
 
     def exchange(send, transform):
         first = place.firsts[transform]
-        groups = [
-            [
-                (2 * place.listed(outer, first) + inner) * narrow + n
-                for outer in range(place.outer)
-                for n in range(narrow)
-            ]
-            for inner in range(2)
-        ]
+        listed = [place.listed(p, first) for p in range(partners)]
+        groups = [[(2 * outer + inner) * narrow + n for outer, n in listed] for inner in range(2)]
         pieces = send.reshape(partners, -1, send.shape[1])
         got = lax.all_to_all(
             pieces, ("wide", "narrow"), 0, 0, axis_index_groups=groups, tiled=True

time: 58.7 us -> 59.2 us (level)
  waiting for transfers between devices: 5.26 us -> 6 us
    all_to_all x2, starting transfers between devices: 12.8 us -> 13.7 us  [exchange(): lax.all_to_all(pieces, ('wide', 'narrow'), 0, 0, axis_index_groups=groups...]
    all_to_all x2, waiting for transfers between devices: 3.6 us -> 4.36 us  [exchange(): lax.all_to_all(pieces, ('wide', 'narrow'), 0, 0, axis_index_groups=groups...]
    ppermute x4, starting transfers between devices: 6.45 us -> 5.7 us  [to_twin(): return lax.ppermute(send, ('wide', 'narrow'), pairs)]
where the time goes in v15:
time: 59.2 us; the launch traced here: 58.5 us
  starting transfers between devices  19.4 us (33%)
  blocking collectives  17.1 us (29%)
  Pallas kernels  11.8 us (20%)
  waiting for transfers between devices  6 us (10%)
  local copies, waits for them, and re-layouts  3.37 us (6%)
  between operations  0.74 us (1%)
    all_to_all x2, blocking collectives, exchange(): lax.all_to_all(pieces, ('wide', 'narrow'), 0, 0, axis_index_groups=groups...  17.1 us
    all_to_all x2, starting transfers between devices, exchange(): lax.all_to_all(pieces, ('wide', 'narrow'), 0, 0, axis_index_groups=groups...  13.7 us
    ppermute x4, starting transfers between devices, to_twin(): return lax.ppermute(send, ('wide', 'narrow'), pairs)  5.7 us
    all_to_all x2, waiting for transfers between devices, exchange(): lax.all_to_all(pieces, ('wide', 'narrow'), 0, 0, axis_index_groups=groups...  4.36 us
    pallas_call x1, Pallas kernels, body(): pl.pallas_call(outer_kernel, grid=(modes // some,), in_specs=[pl.BlockSpe...  3.55 us
    unnamed x20, local copies, waits for them, and re-layouts  3.06 us
    pallas_call x1, Pallas kernels, body(): run(back_kernel, [((mode_lines, channels), F32), shared], 'back')  1.67 us
    ppermute x4, waiting for transfers between devices, to_twin(): return lax.ppermute(send, ('wide', 'narrow'), pairs)  1.64 us
  transfers between devices with their start and end apart: 6, of which 6 were waited for; matrix products, arithmetic and copies ran while one was open for 1% of the time, Pallas kernels for 9%

profile of v15, /device:TPU:1, one launch (start us, length us, event | category | flops | bytes accessed | tf_op | source)
XLA Modules:
  0.0 58.5 jit_solution(6324186749403492306)
XLA Ops:
  0.6 0.0 copy-start.1
  0.6 0.0 copy-start.2
  0.7 0.1 collective-permute-start
  0.8 0.0 copy-start.3
  0.8 0.8 %copy-done.3 = bf16[1,32,8,128]{3,2,1,0:T(8,128)(2,1)S(1)} copy-done((bf16[1,32,8,128]{3,2,1,0:T(8,128)(2,1)S(1)}, bf16[1,32,8,128]{3,2,1,0:T(8,128)(2,1)}, u32[]{:S(2)}) %copy-start.3) | copy-done | bytes 65560
  1.6 0.0 copy-start.7
  1.6 0.0 copy-start.9
  1.6 0.0 copy-start.8
  1.6 0.0 copy-start.4
  1.6 0.0 copy-start.5
  1.6 0.0 copy-start.6
  1.7 0.3 own.1
  2.0 0.2 collective-permute-done.twin_ref
  2.2 1.2 %start.1 = bf16[256,256]{1,0:T(8,128)(2,1)} custom-call(bf16[32,256]{1,0:T(8,128)(2,1)S(1)} %get-tuple-element.35.spectra_ref, bf16[256,128]{1,0:T(8,128)(2,1)S(1)} %collective-permute-done.twin_ref), custom_call_target="tpu_custom_call" | custom-call | flops 4194304 | bytes 524288 | tf_op jit(solution)/shard_map/start/pallas_call | solution.py:567
  3.4 8.0 %all-to-all-start = ((bf16[16,16,256]{2,1,0:T(8,128)(2,1)}), bf16[16,16,256]{2,1,0:T(8,128)(2,1)S(1)}, u32[]{:S(2)}, u32[]{:S(2)}) async-start(bf16[16,16,256]{2,1,0:T(8,128)(2,1)} %bitcast.1), calls=%async_computation | async-start | bytes 262144 | tf_op jit(solution)/shard_map/all_to_all | solution.py:548
  11.4 0.0 copy-start
  11.4 2.2 %copy-done = f32[16,8,2,32,32]{4,3,2,1,0:T(8,128)S(1)} copy-done((f32[16,8,2,32,32]{4,3,2,1,0:T(8,128)S(1)}, f32[16,8,2,32,32]{4,3,2,1,0:T(8,128)}, u32[]{:S(2)}) %copy-start) | copy-done | bytes 1048600
  13.6 0.5 pack.1.weight_ref
  14.1 3.0 %all-to-all-done = bf16[16,16,256]{2,1,0:T(8,128)(2,1)S(1)} async-done(((bf16[16,16,256]{2,1,0:T(8,128)(2,1)}), bf16[16,16,256]{2,1,0:T(8,128)(2,1)S(1)}, u32[]{:S(2)}, u32[]{:S(2)}) %all-to-all-start) | async-done | bytes 131104 | tf_op jit(solution)/shard_map/all_to_all | solution.py:548
  17.1 0.0 copy-done.1
  17.1 0.0 copy-done.2
  17.1 0.9 %mode.1 = (f32[256,32]{1,0:T(8,128)S(1)}, bf16[256,256]{1,0:T(8,128)(2,1)S(1)}) custom-call(bf16[256,256]{1,0:T(8,128)(2,1)S(1)} %bitcast.23, bf16[256,256]{1,0:T(8,128)(2,1)S(1)} %copy-done.1, bf16[256,256]{1,0:T(8,128)(2,1)S(1)} %copy-done.2, bf16[4,256,256]{2,1,0:T(8,128)(2,1)S(1)} %pack.1.weight_ref), custom_call_target="tpu_custom_call" | custom-call | flops 4194304 | bytes 524288 | tf_op jit(solution)/shard_map/mode/pallas_call | solution.py:570
  18.0 8.1 %all_to_all.20 = bf16[16,16,256]{2,1,0:T(8,128)(2,1)S(1)} all-to-all(bf16[16,16,256]{2,1,0:T(8,128)(2,1)S(1)} %bitcast.27), channel_id=1, replica_groups={{16,24,0,8,17,25,1,9,20,28,4,12,21,29,5,13},{18,26,2,10,19,27,3,11,22,3..., dimensions={0} | all-to-all | bytes 262144 | tf_op jit(solution)/shard_map/all_to_all | solution.py:548
  26.1 0.2 part.2
  26.4 2.6 %collective-permute-start.1 = (bf16[32,256]{1,0:T(8,128)(2,1)S(1)}, bf16[32,256]{1,0:T(8,128)(2,1)S(1)}, u32[]{:S(2)}, u32[]{:S(2)}) collective-permute-start(bf16[32,256]{1,0:T(8,128)(2,1)S(1)} %get-tuple-element.38), channel_id=1, source_target_pairs={{0,2},{1,3},{2,0},{3,1},{4,6},{5,7},{6,4},{7,5},{8,10},{9,11},{10,... | collective-permute-start | bytes 49160 | tf_op jit(solution)/shard_map/ppermute | solution.py:541
  28.9 0.0 copy-done.7
  28.9 0.0 copy-done.9
  28.9 0.1 copy.15.mix_bias_ref
  29.0 0.0 copy-done.8
  29.0 0.1 copy.16.refs_6_
  29.1 0.1 copy.17.refs_8_
  29.3 0.0 copy-done.4
  29.3 0.0 copy-done.5
  29.3 0.2 ready.1
  29.5 0.3 collective-permute-done.1.refs_1_
  29.8 0.0 copy-done.6
  29.8 1.2 %cell.1 = (f32[8,128]{1,0:T(8,128)S(1)}, bf16[32,1024]{1,0:T(8,128)(2,1)S(1)}, bf16[32,256]{1,0:T(8,128)(2,1)S(1)}, bf16[32,1024]{1,0:T(8,128)(2,1)S(1)}, bf16[128,1024]{1,0:T(8,128)(2,1)S(1)}) custom-call(f32[32,256]{1,0:T(8,128)S(1)} %get-tuple-element.37.refs_0_, bf16[32,256]{1,0:T(8,128)(2,1)S(1)} %collective-permute-done.1.refs_1_, ...), custom_call_target="tpu_custom_call" | custom-call | flops 4194304 | bytes 524288 | tf_op jit(solution)/shard_map/cell/pallas_call | solution.py:580
  31.0 0.4 collective-permute-start.2
  31.4 0.4 sums.1
  31.8 0.4 collective-permute-done.2.got_ref
  32.2 0.2 fold.1
  32.4 9.0 %all_to_all.21 = bf16[16,40,128]{2,1,0:T(8,128)(2,1)S(1)} all-to-all(bf16[16,40,128]{2,1,0:T(8,128)(2,1)S(1)} %bitcast.21), channel_id=1, replica_groups={{16,24,0,8,17,25,1,9,20,28,4,12,21,29,5,13},{18,26,2,10,19,27,3,11,22,3..., dimensions={0} | all-to-all | bytes 327680 | tf_op jit(solution)/shard_map/all_to_all | solution.py:548
  41.4 1.7 %back.1 = (f32[256,32]{1,0:T(8,128)S(1)}, bf16[640,128]{1,0:T(8,128)(2,1)}) custom-call(bf16[640,128]{1,0:T(8,128)(2,1)S(1)} %bitcast.22, bf16[256,256]{1,0:T(8,128)(2,1)S(1)} %copy-done.1, bf16[256,256]{1,0:T(8,128)(2,1)S(1)} %copy-done.2, bf16[4,256,256]{2,1,0:T(8,128)(2,1)S(1)} %pack.1.weight_ref), custom_call_target="tpu_custom_call" | custom-call | flops 4194304 | bytes 524288 | tf_op jit(solution)/shard_map/back/pallas_call | solution.py:612
  43.1 5.7 %all-to-all-start.3 = ((bf16[16,40,128]{2,1,0:T(8,128)(2,1)}), bf16[16,40,128]{2,1,0:T(8,128)(2,1)S(1)}, u32[]{:S(2)}, u32[]{:S(2)}) async-start(bf16[16,40,128]{2,1,0:T(8,128)(2,1)} %bitcast.12), calls=%async_computation.3 | async-start | bytes 327680 | tf_op jit(solution)/shard_map/all_to_all | solution.py:548
  48.8 3.5 %outer.1 = (f32[16,8,2,32,32]{4,3,2,1,0:T(8,128)}, f32[8,128]{1,0:T(8,128)S(1)}) custom-call(f32[16,16,32]{2,1,0:T(8,128)S(1)} %bitcast.25, f32[16,16,32]{2,1,0:T(8,128)S(1)} %bitcast.26), custom_call_target="tpu_custom_call" | custom-call | flops 4194304 | bytes 5242880 | tf_op jit(solution)/shard_map/outer/pallas_call | solution.py:616
  52.3 1.4 %all-to-all-done.3 = bf16[16,40,128]{2,1,0:T(8,128)(2,1)S(1)} async-done(((bf16[16,40,128]{2,1,0:T(8,128)(2,1)}), bf16[16,40,128]{2,1,0:T(8,128)(2,1)S(1)}, u32[]{:S(2)}, u32[]{:S(2)}) %all-to-all-start.3) | async-done | bytes 163872 | tf_op jit(solution)/shard_map/all_to_all | solution.py:548
  53.7 0.3 part.3
  53.9 2.6 %collective-permute-start.3 = (bf16[96,256]{1,0:T(8,128)(2,1)S(1)}, bf16[96,256]{1,0:T(8,128)(2,1)S(1)}, u32[]{:S(2)}, u32[]{:S(2)}) collective-permute-start(bf16[96,256]{1,0:T(8,128)(2,1)S(1)} %get-tuple-element.54), channel_id=1, source_target_pairs={{0,2},{1,3},{2,0},{3,1},{4,6},{5,7},{6,4},{7,5},{8,10},{9,11},{10,... | collective-permute-start | bytes 147464 | tf_op jit(solution)/shard_map/ppermute | solution.py:541
  56.6 0.2 pointwise.1
  56.8 0.7 %collective-permute-done.3.refs_1_ = bf16[96,256]{1,0:T(8,128)(2,1)S(1)} collective-permute-done((bf16[96,256]{1,0:T(8,128)(2,1)S(1)}, bf16[96,256]{1,0:T(8,128)(2,1)S(1)}, u32[]{:S(2)}, u32[]{:S(2)}) %collective-permute-start.3) | collective-permute-done | bytes 49184 | tf_op jit(solution)/shard_map/ppermute | solution.py:541
  57.5 1.0 %finish.1 = (bf16[256,128]{1,0:T(8,128)(2,1)}, f32[8,128]{1,0:T(8,128)}, f32[32,32]{1,0:T(8,128)}, f32[32,128]{1,0:T(8,128)}) custom-call(f32[32,256]{1,0:T(8,128)S(1)} %get-tuple-element.53.refs_0_, bf16[96,256]{1,0:T(8,128)(2,1)S(1)} %collective-permute-done.3.refs_1_, bf16[32,128]{1,0:T(8,128)(2,1)S(1)} %get-tuple-element.55.refs_2_, ...), custom_call_target="tpu_custom_call" | custom-call | flops 4194304 | bytes 524288 | tf_op jit(solution)/shard_map/finish/pallas_call | solution.py:648
  (1 shorter events, 0.0 us)
Async XLA Ops:
  0.6 16.5 %copy-start.1 = (bf16[256,256]{1,0:T(8,128)(2,1)S(1)}, bf16[256,256]{1,0:T(8,128)(2,1)}, u32[]{:S(2)}) copy-start(bf16[256,256]{1,0:T(8,128)(2,1)} %constant.4.clone.y_forward_ref) | copy-start | bytes 393220
  0.6 16.5 %copy-start.2 = (bf16[256,256]{1,0:T(8,128)(2,1)S(1)}, bf16[256,256]{1,0:T(8,128)(2,1)}, u32[]{:S(2)}) copy-start(bf16[256,256]{1,0:T(8,128)(2,1)} %constant.5.clone.y_inverse_ref) | copy-start | bytes 393220
  0.7 1.5 %collective-permute-start = (bf16[256,128]{1,0:T(8,128)(2,1)}, bf16[256,128]{1,0:T(8,128)(2,1)S(1)}, u32[]{:S(2)}, u32[]{:S(2)}) collective-permute-start(bf16[256,128]{1,0:T(8,128)(2,1)} %bitcast.28), channel_id=1, source_target_pairs={{0,2},{1,3},{2,0},{3,1},{4,6},{5,7},{6,4},{7,5},{8,10},{9,11},{10,... | collective-permute-start | bytes 196616 | tf_op jit(solution)/shard_map/ppermute | solution.py:541
  0.8 0.8 %copy-start.3 = (bf16[1,32,8,128]{3,2,1,0:T(8,128)(2,1)S(1)}, bf16[1,32,8,128]{3,2,1,0:T(8,128)(2,1)}, u32[]{:S(2)}) copy-start(bf16[1,32,8,128]{3,2,1,0:T(8,128)(2,1)} %param.10) | copy-start | bytes 196612
  1.6 27.3 %copy-start.7 = (bf16[128]{0:T(256)(128)(2,1)S(1)}, bf16[128]{0:T(256)(128)(2,1)}, u32[]{:S(2)}) copy-start(bf16[128]{0:T(256)(128)(2,1)} %param.16) | copy-start | bytes 772
  1.6 27.3 %copy-start.9 = (f32[32]{0:T(128)S(1)}, f32[32]{0:T(128)}, u32[]{:S(2)}) copy-start(f32[32]{0:T(128)} %param.13) | copy-start | bytes 388
  1.6 27.4 %copy-start.8 = (f32[128]{0:T(128)S(1)}, f32[128]{0:T(128)}, u32[]{:S(2)}) copy-start(f32[128]{0:T(128)} %param.15) | copy-start | bytes 1540
  1.6 27.6 %copy-start.4 = (bf16[32,128]{1,0:T(8,128)(2,1)S(1)}, bf16[32,128]{1,0:T(8,128)(2,1)}, u32[]{:S(2)}) copy-start(bf16[32,128]{1,0:T(8,128)(2,1)} %refs_4_.1) | copy-start | bytes 24580
  1.6 27.6 %copy-start.5 = (bf16[32,32]{1,0:T(8,128)(2,1)S(1)}, bf16[32,32]{1,0:T(8,128)(2,1)}, u32[]{:S(2)}) copy-start(bf16[32,32]{1,0:T(8,128)(2,1)} %mix_ref.3) | copy-start | bytes 6148
  1.6 28.1 %copy-start.6 = (f32[1,8,128]{2,1,0:T(8,128)S(1)}, f32[1,8,128]{2,1,0:T(8,128)}, u32[]{:S(2)}) copy-start(f32[1,8,128]{2,1,0:T(8,128)} %param.17) | copy-start | bytes 12292
  3.4 13.7 %all-to-all-start = ((bf16[16,16,256]{2,1,0:T(8,128)(2,1)}), bf16[16,16,256]{2,1,0:T(8,128)(2,1)S(1)}, u32[]{:S(2)}, u32[]{:S(2)}) async-start(bf16[16,16,256]{2,1,0:T(8,128)(2,1)} %bitcast.1), calls=%async_computation | async-start | bytes 262144 | tf_op jit(solution)/shard_map/all_to_all | solution.py:548
  11.4 2.2 %copy-start = (f32[16,8,2,32,32]{4,3,2,1,0:T(8,128)S(1)}, f32[16,8,2,32,32]{4,3,2,1,0:T(8,128)}, u32[]{:S(2)}) copy-start(f32[16,8,2,32,32]{4,3,2,1,0:T(8,128)} %weight_ref.1) | copy-start | bytes 3145732
  26.4 3.4 %collective-permute-start.1 = (bf16[32,256]{1,0:T(8,128)(2,1)S(1)}, bf16[32,256]{1,0:T(8,128)(2,1)S(1)}, u32[]{:S(2)}, u32[]{:S(2)}) collective-permute-start(bf16[32,256]{1,0:T(8,128)(2,1)S(1)} %get-tuple-element.38), channel_id=1, source_target_pairs={{0,2},{1,3},{2,0},{3,1},{4,6},{5,7},{6,4},{7,5},{8,10},{9,11},{10,... | collective-permute-start | bytes 49160 | tf_op jit(solution)/shard_map/ppermute | solution.py:541
  31.0 1.2 %collective-permute-start.2 = (bf16[32,256]{1,0:T(8,128)(2,1)S(1)}, bf16[32,256]{1,0:T(8,128)(2,1)S(1)}, u32[]{:S(2)}, u32[]{:S(2)}) collective-permute-start(bf16[32,256]{1,0:T(8,128)(2,1)S(1)} %get-tuple-element.43.own_ref), channel_id=1, source_target_pairs={{0,2},{1,3},{2,0},{3,1},{4,6},{5,7},{6,4},{7,5},{8,10},{9,11},{10,... | collective-permute-start | bytes 49160 | tf_op jit(solution)/shard_map/ppermute | solution.py:541
  43.1 10.6 %all-to-all-start.3 = ((bf16[16,40,128]{2,1,0:T(8,128)(2,1)}), bf16[16,40,128]{2,1,0:T(8,128)(2,1)S(1)}, u32[]{:S(2)}, u32[]{:S(2)}) async-start(bf16[16,40,128]{2,1,0:T(8,128)(2,1)} %bitcast.12), calls=%async_computation.3 | async-start | bytes 327680 | tf_op jit(solution)/shard_map/all_to_all | solution.py:548
  53.9 3.5 %collective-permute-start.3 = (bf16[96,256]{1,0:T(8,128)(2,1)S(1)}, bf16[96,256]{1,0:T(8,128)(2,1)S(1)}, u32[]{:S(2)}, u32[]{:S(2)}) collective-permute-start(bf16[96,256]{1,0:T(8,128)(2,1)S(1)} %get-tuple-element.54), channel_id=1, source_target_pairs={{0,2},{1,3},{2,0},{3,1},{4,6},{5,7},{6,4},{7,5},{8,10},{9,11},{10,... | collective-permute-start | bytes 147464 | tf_op jit(solution)/shard_map/ppermute | solution.py:541

commit v16 on v13

--- a/solution.py
+++ b/solution.py
@@ -183,6 +183,20 @@
     return jnp.concatenate(blocks, axis=0), shares
 
 
+def lane_sum(values, width):
+    while values.shape[1] > 128:
+        half = values.shape[1] // 2
+        values = values[:, :half] + values[:, half:]
+    if values.shape[1] < 128:
+        blocks = range(0, values.shape[1], width)
+        return sum(values[:, first : first + width] for first in blocks)
+    shift = 64
+    while shift >= width:
+        values = values + pltpu.roll(values, shift, 1)
+        shift //= 2
+    return values[:, :width]
+
+
 def analysed(place, pieces, y_forward, copies):
     height = 2 * MZ
     turned = sum(
@@ -241,7 +255,8 @@
     send_ref[...] = dot(tables, jnp.concatenate([values, values], axis=0)).astype(BF16)
 
 
-def pack_kernel(weight_ref, packed_ref):
+def pack_kernel(place, weight_ref, packed_ref, inverse_ref):
+    inverse_ref[...] = place.inverse_x(place.firsts[1])
     modes, kz, _, channels, _ = weight_ref.shape
     for q in range(modes // 4):
         parts = [weight_ref[4 * q + j // 2, :, j % 2] for j in range(8)]
@@ -288,9 +303,9 @@
     repeat_rows(send_ref, spread_lines(place, mode, y_inverse_ref[...]))
 
 
-def part_kernel(place, first, pieces_ref, *refs):
+def part_kernel(place, pieces_ref, table_ref, *refs):
     pieces, shares = read_pieces(place, pieces_ref)
-    lines = dot(place.inverse_x(first), pieces)
+    lines = dot(table_ref[...], pieces)
     height = 2 * MZ
     if shares is None:
         own_ref, send_ref = refs
@@ -301,14 +316,13 @@
     own_ref[...] = lines[:height]
     send_ref[:height] = lines[height:].astype(BF16)
     got = jnp.concatenate(shares, axis=0).astype(BF16)
-    channels, narrow = place.channels, place.narrow
+    channels = place.channels
 
     def chosen(part):
         def condition(row, column):
             owner, source = (row % channels) // 2, column // 8
             return (
-                (place.listed(owner // narrow, place.firsts[2]) == place.listed(source // narrow, first))
-                & (owner % narrow == source % narrow)
+                (owner == source)
                 & (column % 8 == 4 * part + 2 * (row // channels) + row % 2)
             )
 
@@ -320,8 +334,8 @@
 
 
 def normal(values):
-    scaled = 1.0 / (1.0 + TAIL_SLOPE * jnp.abs(values))
-    decay = jnp.exp(-0.5 * values * values)
+    scaled = pl.reciprocal(1.0 + jnp.abs(TAIL_SLOPE * values), approx=True)
+    decay = jnp.exp2(values * values * (-0.5 / math.log(2.0)))
     tail = TAIL[-1]
     for factor in TAIL[-2::-1]:
         tail = tail * scaled + factor
@@ -408,11 +422,8 @@
     ]
     pulled = jnp.concatenate(pulled, axis=0)
     row, lane = grid_of(*pulled.shape)
-    pulled = jnp.where(row % kz == lane // channels, pulled, 0.0).astype(BF16)
-    gather = selector(
-        kz * channels, channels, lambda row, column: row % channels == column
-    )
-    modes_back = dot(pulled, gather).astype(BF16)
+    pulled = jnp.where(row % kz == lane // channels, pulled, 0.0)
+    modes_back = lane_sum(pulled, channels).astype(BF16)
     block = spread_lines(place, modes_back, y_inverse_ref[...])
     if shares is None:
         repeat_rows(send_ref, block)
@@ -547,12 +558,12 @@
     field, spectra = run(own_kernel, [(across, BF16), twin_plain], "own")(flat_field)
     (send,) = run(start_kernel, [plain], "start")(spectra, twin_field)
     packed_shape = ((modes // 4, kz * channels, 8 * channels), BF16)
-    (weight,) = call(pack_kernel, [packed_shape], "pack")(spectral_weight)
+    inverse_shape = ((2 * height, wide // 2 * height), BF16)
+    weight, inverse = run(pack_kernel, [packed_shape, inverse_shape], "pack")(spectral_weight)
     spectrum, send = run(mode_kernel, [((mode_lines, channels), F32), plain], "mode")(
         exchange(send, 0), y_forward, y_inverse, weight
     )
-    part = functools.partial(part_kernel, place, place.firsts[1])
-    own, send = call(part, [own_lines, twin_plain], "part")(exchange(send, 1))
+    own, send = run(part_kernel, [own_lines, twin_plain], "part")(exchange(send, 1), inverse)
     pointwise, head_turned, z_doubled = run(
         ready_kernel,
         [(across, F32), ((hidden_units, channels), BF16), ((height, z_count), BF16)],
@@ -621,8 +632,7 @@
     )(mix_weight, grad_pre)
     outs = [own_lines, twin_shared] + ([sums_shape] if place.fold else [])
     after = (done,) if place.fold else ()
-    part = functools.partial(part_kernel, place, place.firsts[3])
-    own, send, *sums = call(part, outs, "part")(exchange(send, 3), *after)
+    own, send, *sums = run(part_kernel, outs, "part")(exchange(send, 3), inverse, *after)
     outs = [((cells, z_count), BF16), ((rows_y, z_count), F32)]
     if place.fold:
         outs += [((channels, channels), F32), ((channels, hidden_units), F32)]

time: 58.7 us -> 58.5 us (level)
  no operation moved by 1% of the time
where the time goes in v16:
time: 58.5 us; the launch traced here: 57.8 us
  starting transfers between devices  19.3 us (33%)
  blocking collectives  17.5 us (30%)
  Pallas kernels  11.6 us (20%)
  waiting for transfers between devices  5.25 us (9%)
  local copies, waits for them, and re-layouts  3.37 us (6%)
  between operations  0.74 us (1%)
    all_to_all x2, blocking collectives, exchange(): lax.all_to_all(pieces, ('wide', 'narrow'), 0, 0, axis_index_groups=groups...  17.5 us
    all_to_all x2, starting transfers between devices, exchange(): lax.all_to_all(pieces, ('wide', 'narrow'), 0, 0, axis_index_groups=groups...  12.8 us
    ppermute x4, starting transfers between devices, to_twin(): return lax.ppermute(send, ('wide', 'narrow'), pairs)  6.46 us
    all_to_all x2, waiting for transfers between devices, exchange(): lax.all_to_all(pieces, ('wide', 'narrow'), 0, 0, axis_index_groups=groups...  3.59 us
    pallas_call x1, Pallas kernels, body(): pl.pallas_call(outer_kernel, grid=(modes // some,), in_specs=[pl.BlockSpe...  3.55 us
    unnamed x20, local copies, waits for them, and re-layouts  3.06 us
    ppermute x4, waiting for transfers between devices, to_twin(): return lax.ppermute(send, ('wide', 'narrow'), pairs)  1.66 us
    pallas_call x1, Pallas kernels, body(): run(back_kernel, [((mode_lines, channels), F32), shared], 'back')  1.65 us
  transfers between devices with their start and end apart: 6, of which 6 were waited for; matrix products, arithmetic and copies ran while one was open for 1% of the time, Pallas kernels for 9%

profile of v16, /device:TPU:1, one launch (start us, length us, event | category | flops | bytes accessed | tf_op | source)
XLA Modules:
  0.0 57.8 jit_solution(8994680392772218082)
XLA Ops:
  0.6 0.0 copy-start.1
  0.6 0.0 copy-start.2
  0.7 0.1 collective-permute-start
  0.8 0.0 copy-start.3
  0.8 0.8 %copy-done.3 = bf16[1,32,8,128]{3,2,1,0:T(8,128)(2,1)S(1)} copy-done((bf16[1,32,8,128]{3,2,1,0:T(8,128)(2,1)S(1)}, bf16[1,32,8,128]{3,2,1,0:T(8,128)(2,1)}, u32[]{:S(2)}) %copy-start.3) | copy-done | bytes 65560
  1.6 0.0 copy-start.7
  1.6 0.0 copy-start.9
  1.6 0.0 copy-start.8
  1.6 0.0 copy-start.4
  1.6 0.0 copy-start.5
  1.6 0.0 copy-start.6
  1.7 0.3 own.1
  2.0 0.2 collective-permute-done.twin_ref
  2.2 1.2 %start.1 = bf16[256,256]{1,0:T(8,128)(2,1)} custom-call(bf16[32,256]{1,0:T(8,128)(2,1)S(1)} %get-tuple-element.37.spectra_ref, bf16[256,128]{1,0:T(8,128)(2,1)S(1)} %collective-permute-done.twin_ref), custom_call_target="tpu_custom_call" | custom-call | flops 4194304 | bytes 524288 | tf_op jit(solution)/shard_map/start/pallas_call | solution.py:559
  3.4 8.0 %all-to-all-start = ((bf16[16,16,256]{2,1,0:T(8,128)(2,1)}), bf16[16,16,256]{2,1,0:T(8,128)(2,1)S(1)}, u32[]{:S(2)}, u32[]{:S(2)}) async-start(bf16[16,16,256]{2,1,0:T(8,128)(2,1)} %bitcast.1), calls=%async_computation | async-start | bytes 262144 | tf_op jit(solution)/shard_map/all_to_all | solution.py:540
  11.4 0.0 copy-start
  11.4 2.2 %copy-done = f32[16,8,2,32,32]{4,3,2,1,0:T(8,128)S(1)} copy-done((f32[16,8,2,32,32]{4,3,2,1,0:T(8,128)S(1)}, f32[16,8,2,32,32]{4,3,2,1,0:T(8,128)}, u32[]{:S(2)}) %copy-start) | copy-done | bytes 1048600
  13.6 0.5 pack.1
  14.1 2.3 %all-to-all-done = bf16[16,16,256]{2,1,0:T(8,128)(2,1)S(1)} async-done(((bf16[16,16,256]{2,1,0:T(8,128)(2,1)}), bf16[16,16,256]{2,1,0:T(8,128)(2,1)S(1)}, u32[]{:S(2)}, u32[]{:S(2)}) %all-to-all-start) | async-done | bytes 131104 | tf_op jit(solution)/shard_map/all_to_all | solution.py:540
  16.4 0.0 copy-done.1
  16.4 0.0 copy-done.2
  16.4 0.9 %mode.1 = (f32[256,32]{1,0:T(8,128)S(1)}, bf16[256,256]{1,0:T(8,128)(2,1)S(1)}) custom-call(bf16[256,256]{1,0:T(8,128)(2,1)S(1)} %bitcast.23, bf16[256,256]{1,0:T(8,128)(2,1)S(1)} %copy-done.1, bf16[256,256]{1,0:T(8,128)(2,1)S(1)} %copy-done.2, bf16[4,256,256]{2,1,0:T(8,128)(2,1)S(1)} %get-tuple-element.38.weight_ref), custom_call_target="tpu_custom_call" | custom-call | flops 4194304 | bytes 524288 | tf_op jit(solution)/shard_map/mode/pallas_call | solution.py:563
  17.4 8.7 %all_to_all.20 = bf16[16,16,256]{2,1,0:T(8,128)(2,1)S(1)} all-to-all(bf16[16,16,256]{2,1,0:T(8,128)(2,1)S(1)} %bitcast.27), channel_id=1, replica_groups={{16,17,20,21,24,25,28,29,0,1,4,5,8,9,12,13},{18,19,22,23,26,27,30,31,2,..., dimensions={0} | all-to-all | bytes 262144 | tf_op jit(solution)/shard_map/all_to_all | solution.py:540
  26.1 0.1 part.2
  26.2 2.8 %collective-permute-start.1 = (bf16[32,256]{1,0:T(8,128)(2,1)S(1)}, bf16[32,256]{1,0:T(8,128)(2,1)S(1)}, u32[]{:S(2)}, u32[]{:S(2)}) collective-permute-start(bf16[32,256]{1,0:T(8,128)(2,1)S(1)} %get-tuple-element.42), channel_id=1, source_target_pairs={{0,2},{1,3},{2,0},{3,1},{4,6},{5,7},{6,4},{7,5},{8,10},{9,11},{10,... | collective-permute-start | bytes 49160 | tf_op jit(solution)/shard_map/ppermute | solution.py:527
  29.1 0.0 copy-done.7
  29.1 0.0 copy-done.9
  29.1 0.1 copy.15.mix_bias_ref
  29.2 0.0 copy-done.8
  29.2 0.1 copy.16.refs_6_
  29.3 0.1 copy.17.refs_8_
  29.4 0.0 copy-done.4
  29.4 0.0 copy-done.5
  29.4 0.2 ready.1
  29.6 0.3 collective-permute-done.1.refs_1_
  29.9 0.0 copy-done.6
  29.9 1.2 %cell.1 = (f32[8,128]{1,0:T(8,128)S(1)}, bf16[32,1024]{1,0:T(8,128)(2,1)S(1)}, bf16[32,256]{1,0:T(8,128)(2,1)S(1)}, bf16[32,1024]{1,0:T(8,128)(2,1)S(1)}, bf16[128,1024]{1,0:T(8,128)(2,1)S(1)}) custom-call(f32[32,256]{1,0:T(8,128)S(1)} %get-tuple-element.41.refs_0_, bf16[32,256]{1,0:T(8,128)(2,1)S(1)} %collective-permute-done.1.refs_1_, ...), custom_call_target="tpu_custom_call" | custom-call | flops 4194304 | bytes 524288 | tf_op jit(solution)/shard_map/cell/pallas_call | solution.py:572
  31.1 0.4 collective-permute-start.2
  31.5 0.4 sums.1
  31.9 0.5 collective-permute-done.2.got_ref
  32.3 0.2 fold.1
  32.5 8.8 %all_to_all.21 = bf16[16,40,128]{2,1,0:T(8,128)(2,1)S(1)} all-to-all(bf16[16,40,128]{2,1,0:T(8,128)(2,1)S(1)} %bitcast.21), channel_id=1, replica_groups={{16,17,20,21,24,25,28,29,0,1,4,5,8,9,12,13},{18,19,22,23,26,27,30,31,2,..., dimensions={0} | all-to-all | bytes 327680 | tf_op jit(solution)/shard_map/all_to_all | solution.py:540
  41.3 1.6 %back.1 = (f32[256,32]{1,0:T(8,128)S(1)}, bf16[640,128]{1,0:T(8,128)(2,1)}) custom-call(bf16[640,128]{1,0:T(8,128)(2,1)S(1)} %bitcast.22, bf16[256,256]{1,0:T(8,128)(2,1)S(1)} %copy-done.1, bf16[256,256]{1,0:T(8,128)(2,1)S(1)} %copy-done.2, bf16[4,256,256]{2,1,0:T(8,128)(2,1)S(1)} %get-tuple-element.38.weight_ref), custom_call_target="tpu_custom_call" | custom-call | flops 4194304 | bytes 524288 | tf_op jit(solution)/shard_map/back/pallas_call | solution.py:604
  43.0 4.8 %all-to-all-start.3 = ((bf16[16,40,128]{2,1,0:T(8,128)(2,1)}), bf16[16,40,128]{2,1,0:T(8,128)(2,1)S(1)}, u32[]{:S(2)}, u32[]{:S(2)}) async-start(bf16[16,40,128]{2,1,0:T(8,128)(2,1)} %bitcast.12), calls=%async_computation.3 | async-start | bytes 327680 | tf_op jit(solution)/shard_map/all_to_all | solution.py:540
  47.8 3.5 %outer.1 = (f32[16,8,2,32,32]{4,3,2,1,0:T(8,128)}, f32[8,128]{1,0:T(8,128)S(1)}) custom-call(f32[16,16,32]{2,1,0:T(8,128)S(1)} %bitcast.25, f32[16,16,32]{2,1,0:T(8,128)S(1)} %bitcast.26), custom_call_target="tpu_custom_call" | custom-call | flops 4194304 | bytes 5242880 | tf_op jit(solution)/shard_map/outer/pallas_call | solution.py:608
  51.3 1.3 %all-to-all-done.3 = bf16[16,40,128]{2,1,0:T(8,128)(2,1)S(1)} async-done(((bf16[16,40,128]{2,1,0:T(8,128)(2,1)}), bf16[16,40,128]{2,1,0:T(8,128)(2,1)S(1)}, u32[]{:S(2)}, u32[]{:S(2)}) %all-to-all-start.3) | async-done | bytes 163872 | tf_op jit(solution)/shard_map/all_to_all | solution.py:540
  52.6 0.2 part.3
  52.8 3.1 %collective-permute-start.3 = (bf16[96,256]{1,0:T(8,128)(2,1)S(1)}, bf16[96,256]{1,0:T(8,128)(2,1)S(1)}, u32[]{:S(2)}, u32[]{:S(2)}) collective-permute-start(bf16[96,256]{1,0:T(8,128)(2,1)S(1)} %get-tuple-element.58), channel_id=1, source_target_pairs={{0,2},{1,3},{2,0},{3,1},{4,6},{5,7},{6,4},{7,5},{8,10},{9,11},{10,... | collective-permute-start | bytes 147464 | tf_op jit(solution)/shard_map/ppermute | solution.py:527
  55.9 0.2 pointwise.1
  56.1 0.7 %collective-permute-done.3.refs_1_ = bf16[96,256]{1,0:T(8,128)(2,1)S(1)} collective-permute-done((bf16[96,256]{1,0:T(8,128)(2,1)S(1)}, bf16[96,256]{1,0:T(8,128)(2,1)S(1)}, u32[]{:S(2)}, u32[]{:S(2)}) %collective-permute-start.3) | collective-permute-done | bytes 49184 | tf_op jit(solution)/shard_map/ppermute | solution.py:527
  56.8 1.0 %finish.1 = (bf16[256,128]{1,0:T(8,128)(2,1)}, f32[8,128]{1,0:T(8,128)}, f32[32,32]{1,0:T(8,128)}, f32[32,128]{1,0:T(8,128)}) custom-call(f32[32,256]{1,0:T(8,128)S(1)} %get-tuple-element.57.refs_0_, bf16[96,256]{1,0:T(8,128)(2,1)S(1)} %collective-permute-done.3.refs_1_, bf16[32,128]{1,0:T(8,128)(2,1)S(1)} %get-tuple-element.59.refs_2_, ...), custom_call_target="tpu_custom_call" | custom-call | flops 4194304 | bytes 524288 | tf_op jit(solution)/shard_map/finish/pallas_call | solution.py:639
  (1 shorter events, 0.0 us)
Async XLA Ops:
  0.6 15.8 %copy-start.1 = (bf16[256,256]{1,0:T(8,128)(2,1)S(1)}, bf16[256,256]{1,0:T(8,128)(2,1)}, u32[]{:S(2)}) copy-start(bf16[256,256]{1,0:T(8,128)(2,1)} %constant.4.clone.y_forward_ref) | copy-start | bytes 393220
  0.6 15.8 %copy-start.2 = (bf16[256,256]{1,0:T(8,128)(2,1)S(1)}, bf16[256,256]{1,0:T(8,128)(2,1)}, u32[]{:S(2)}) copy-start(bf16[256,256]{1,0:T(8,128)(2,1)} %constant.5.clone.y_inverse_ref) | copy-start | bytes 393220
  0.7 1.5 %collective-permute-start = (bf16[256,128]{1,0:T(8,128)(2,1)}, bf16[256,128]{1,0:T(8,128)(2,1)S(1)}, u32[]{:S(2)}, u32[]{:S(2)}) collective-permute-start(bf16[256,128]{1,0:T(8,128)(2,1)} %bitcast.28), channel_id=1, source_target_pairs={{0,2},{1,3},{2,0},{3,1},{4,6},{5,7},{6,4},{7,5},{8,10},{9,11},{10,... | collective-permute-start | bytes 196616 | tf_op jit(solution)/shard_map/ppermute | solution.py:527
  0.8 0.8 %copy-start.3 = (bf16[1,32,8,128]{3,2,1,0:T(8,128)(2,1)S(1)}, bf16[1,32,8,128]{3,2,1,0:T(8,128)(2,1)}, u32[]{:S(2)}) copy-start(bf16[1,32,8,128]{3,2,1,0:T(8,128)(2,1)} %param.10) | copy-start | bytes 196612
  1.6 27.4 %copy-start.7 = (bf16[128]{0:T(256)(128)(2,1)S(1)}, bf16[128]{0:T(256)(128)(2,1)}, u32[]{:S(2)}) copy-start(bf16[128]{0:T(256)(128)(2,1)} %param.16) | copy-start | bytes 772
  1.6 27.4 %copy-start.9 = (f32[32]{0:T(128)S(1)}, f32[32]{0:T(128)}, u32[]{:S(2)}) copy-start(f32[32]{0:T(128)} %param.13) | copy-start | bytes 388
  1.6 27.5 %copy-start.8 = (f32[128]{0:T(128)S(1)}, f32[128]{0:T(128)}, u32[]{:S(2)}) copy-start(f32[128]{0:T(128)} %param.15) | copy-start | bytes 1540
  1.6 27.8 %copy-start.4 = (bf16[32,128]{1,0:T(8,128)(2,1)S(1)}, bf16[32,128]{1,0:T(8,128)(2,1)}, u32[]{:S(2)}) copy-start(bf16[32,128]{1,0:T(8,128)(2,1)} %refs_4_.1) | copy-start | bytes 24580
  1.6 27.8 %copy-start.5 = (bf16[32,32]{1,0:T(8,128)(2,1)S(1)}, bf16[32,32]{1,0:T(8,128)(2,1)}, u32[]{:S(2)}) copy-start(bf16[32,32]{1,0:T(8,128)(2,1)} %mix_ref.3) | copy-start | bytes 6148
  1.6 28.3 %copy-start.6 = (f32[1,8,128]{2,1,0:T(8,128)S(1)}, f32[1,8,128]{2,1,0:T(8,128)}, u32[]{:S(2)}) copy-start(f32[1,8,128]{2,1,0:T(8,128)} %param.17) | copy-start | bytes 12292
  3.4 13.0 %all-to-all-start = ((bf16[16,16,256]{2,1,0:T(8,128)(2,1)}), bf16[16,16,256]{2,1,0:T(8,128)(2,1)S(1)}, u32[]{:S(2)}, u32[]{:S(2)}) async-start(bf16[16,16,256]{2,1,0:T(8,128)(2,1)} %bitcast.1), calls=%async_computation | async-start | bytes 262144 | tf_op jit(solution)/shard_map/all_to_all | solution.py:540
  11.4 2.2 %copy-start = (f32[16,8,2,32,32]{4,3,2,1,0:T(8,128)S(1)}, f32[16,8,2,32,32]{4,3,2,1,0:T(8,128)}, u32[]{:S(2)}) copy-start(f32[16,8,2,32,32]{4,3,2,1,0:T(8,128)} %weight_ref.1) | copy-start | bytes 3145732
  26.2 3.7 %collective-permute-start.1 = (bf16[32,256]{1,0:T(8,128)(2,1)S(1)}, bf16[32,256]{1,0:T(8,128)(2,1)S(1)}, u32[]{:S(2)}, u32[]{:S(2)}) collective-permute-start(bf16[32,256]{1,0:T(8,128)(2,1)S(1)} %get-tuple-element.42), channel_id=1, source_target_pairs={{0,2},{1,3},{2,0},{3,1},{4,6},{5,7},{6,4},{7,5},{8,10},{9,11},{10,... | collective-permute-start | bytes 49160 | tf_op jit(solution)/shard_map/ppermute | solution.py:527
  31.1 1.2 %collective-permute-start.2 = (bf16[32,256]{1,0:T(8,128)(2,1)S(1)}, bf16[32,256]{1,0:T(8,128)(2,1)S(1)}, u32[]{:S(2)}, u32[]{:S(2)}) collective-permute-start(bf16[32,256]{1,0:T(8,128)(2,1)S(1)} %get-tuple-element.47.own_ref), channel_id=1, source_target_pairs={{0,2},{1,3},{2,0},{3,1},{4,6},{5,7},{6,4},{7,5},{8,10},{9,11},{10,... | collective-permute-start | bytes 49160 | tf_op jit(solution)/shard_map/ppermute | solution.py:527
  43.0 9.6 %all-to-all-start.3 = ((bf16[16,40,128]{2,1,0:T(8,128)(2,1)}), bf16[16,40,128]{2,1,0:T(8,128)(2,1)S(1)}, u32[]{:S(2)}, u32[]{:S(2)}) async-start(bf16[16,40,128]{2,1,0:T(8,128)(2,1)} %bitcast.12), calls=%async_computation.3 | async-start | bytes 327680 | tf_op jit(solution)/shard_map/all_to_all | solution.py:540
  52.8 4.0 %collective-permute-start.3 = (bf16[96,256]{1,0:T(8,128)(2,1)S(1)}, bf16[96,256]{1,0:T(8,128)(2,1)S(1)}, u32[]{:S(2)}, u32[]{:S(2)}) collective-permute-start(bf16[96,256]{1,0:T(8,128)(2,1)S(1)} %get-tuple-element.58), channel_id=1, source_target_pairs={{0,2},{1,3},{2,0},{3,1},{4,6},{5,7},{6,4},{7,5},{8,10},{9,11},{10,... | collective-permute-start | bytes 147464 | tf_op jit(solution)/shard_map/ppermute | solution.py:527

commit v17 on v16

--- a/solution.py
+++ b/solution.py
@@ -101,14 +101,15 @@
         self.partners = self.outer * narrow
         self.lanes = rows_y * channels
         middle, last = self.outer // 4, self.outer // 2 - 1
-        self.firsts = (last, middle, middle, middle)
+        self.firsts = ((last, last), (middle, 0), (middle, 0), (middle, 0))
 
     def here(self):
         wide = lax.axis_index("wide")
         return wide // 2, wide % 2
 
-    def listed(self, position, first):
+    def listed(self, position, firsts, inner):
         lines = self.outer // 2
+        first = firsts[0] + (firsts[1] - firsts[0]) * inner
         return ((first + position // 2) & (lines - 1)) * 2 + position % 2
 
     def frequency(self, wide):
@@ -132,20 +133,20 @@
             blocks.append(jnp.where(same, value, 0.0))
         return jnp.concatenate(blocks, axis=0)
 
-    def forward_x(self, first):
+    def forward_x(self, firsts):
         outer, inner = self.here()
         row, column = grid_of(2 * self.outer, 4 * MZ)
         x = 2 * outer + (inner ^ (column // (2 * MZ)))
-        frequency = self.frequency(2 * self.listed(row >> 1, first) + inner)
+        frequency = self.frequency(2 * self.listed(row >> 1, firsts, inner) + inner)
         quarter = self.wide // 4
         small = cosine_of(x * frequency + quarter * ((row & 1) - (column & 1)), self.wide)
         return self.expanded(small)
 
-    def inverse_x(self, first):
+    def inverse_x(self, firsts):
         outer, inner = self.here()
         row, column = grid_of(4, self.outer * 2 * MZ)
         x = 2 * outer + (inner ^ (row >> 1))
-        frequency = self.frequency(2 * self.listed(column // (2 * MZ), first) + inner)
+        frequency = self.frequency(2 * self.listed(column // (2 * MZ), firsts, inner) + inner)
         quarter = self.wide // 4
         small = cosine_of(x * frequency + quarter * ((column & 1) - (row & 1)), self.wide)
         return self.expanded(small).astype(BF16)
@@ -527,10 +528,10 @@
         return lax.ppermute(send, ("wide", "narrow"), pairs)
 
     def exchange(send, transform):
-        first = place.firsts[transform]
+        firsts = place.firsts[transform]
         groups = [
             [
-                (2 * place.listed(outer, first) + inner) * narrow + n
+                (2 * place.listed(outer, firsts, inner) + inner) * narrow + n
                 for outer in range(place.outer)
                 for n in range(narrow)
             ]

time: 58.5 us -> 60.4 us (1.032)
  starting transfers between devices: 19.3 us -> 14.3 us
  blocking collectives: 17.5 us -> 21.1 us
  waiting for transfers between devices: 5.25 us -> 8.5 us
    ppermute x4, starting transfers between devices: 6.46 us -> 2.67 us  [to_twin(): return lax.ppermute(send, ('wide', 'narrow'), pairs)]
    all_to_all x2, blocking collectives: 17.5 us -> 21.1 us  [exchange(): lax.all_to_all(pieces, ('wide', 'narrow'), 0, 0, axis_index_groups=groups...]
    all_to_all x2, waiting for transfers between devices: 3.59 us -> 6.84 us  [exchange(): lax.all_to_all(pieces, ('wide', 'narrow'), 0, 0, axis_index_groups=groups...]
    all_to_all x2, starting transfers between devices: 12.8 us -> 11.7 us  [exchange(): lax.all_to_all(pieces, ('wide', 'narrow'), 0, 0, axis_index_groups=groups...]
where the time goes in v17:
time: 60.4 us; the launch traced here: 59.7 us
  blocking collectives  21.1 us (35%)
  starting transfers between devices  14.3 us (24%)
  Pallas kernels  11.6 us (19%)
  waiting for transfers between devices  8.5 us (14%)
  local copies, waits for them, and re-layouts  3.37 us (6%)
  between operations  0.75 us (1%)
    all_to_all x2, blocking collectives, exchange(): lax.all_to_all(pieces, ('wide', 'narrow'), 0, 0, axis_index_groups=groups...  21.1 us
    all_to_all x2, starting transfers between devices, exchange(): lax.all_to_all(pieces, ('wide', 'narrow'), 0, 0, axis_index_groups=groups...  11.7 us
    all_to_all x2, waiting for transfers between devices, exchange(): lax.all_to_all(pieces, ('wide', 'narrow'), 0, 0, axis_index_groups=groups...  6.84 us
    pallas_call x1, Pallas kernels, body(): pl.pallas_call(outer_kernel, grid=(modes // some,), in_specs=[pl.BlockSpe...  3.55 us
    unnamed x20, local copies, waits for them, and re-layouts  3.06 us
    ppermute x4, starting transfers between devices, to_twin(): return lax.ppermute(send, ('wide', 'narrow'), pairs)  2.67 us
    ppermute x4, waiting for transfers between devices, to_twin(): return lax.ppermute(send, ('wide', 'narrow'), pairs)  1.66 us
    pallas_call x1, Pallas kernels, body(): run(back_kernel, [((mode_lines, channels), F32), shared], 'back')  1.65 us
  transfers between devices with their start and end apart: 6, of which 6 were waited for; matrix products, arithmetic and copies ran while one was open for 1% of the time, Pallas kernels for 9%

profile of v17, /device:TPU:1, one launch (start us, length us, event | category | flops | bytes accessed | tf_op | source)
XLA Modules:
  0.0 59.7 jit_solution(7972927790083615629)
XLA Ops:
  0.6 0.0 copy-start.1
  0.6 0.0 copy-start.2
  0.7 0.1 collective-permute-start
  0.8 0.0 copy-start.3
  0.8 0.8 %copy-done.3 = bf16[1,32,8,128]{3,2,1,0:T(8,128)(2,1)S(1)} copy-done((bf16[1,32,8,128]{3,2,1,0:T(8,128)(2,1)S(1)}, bf16[1,32,8,128]{3,2,1,0:T(8,128)(2,1)}, u32[]{:S(2)}) %copy-start.3) | copy-done | bytes 65560
  1.6 0.0 copy-start.7
  1.6 0.0 copy-start.9
  1.6 0.0 copy-start.8
  1.6 0.0 copy-start.4
  1.6 0.0 copy-start.5
  1.6 0.0 copy-start.6
  1.7 0.3 own.1
  2.0 0.2 collective-permute-done.twin_ref
  2.2 1.2 %start.1 = bf16[256,256]{1,0:T(8,128)(2,1)} custom-call(bf16[32,256]{1,0:T(8,128)(2,1)S(1)} %get-tuple-element.37.spectra_ref, bf16[256,128]{1,0:T(8,128)(2,1)S(1)} %collective-permute-done.twin_ref), custom_call_target="tpu_custom_call" | custom-call | flops 4194304 | bytes 524288 | tf_op jit(solution)/shard_map/start/pallas_call | solution.py:560
  3.4 8.0 %all-to-all-start = ((bf16[16,16,256]{2,1,0:T(8,128)(2,1)}), bf16[16,16,256]{2,1,0:T(8,128)(2,1)S(1)}, u32[]{:S(2)}, u32[]{:S(2)}) async-start(bf16[16,16,256]{2,1,0:T(8,128)(2,1)} %bitcast.1), calls=%async_computation | async-start | bytes 262144 | tf_op jit(solution)/shard_map/all_to_all | solution.py:541
  11.4 0.0 copy-start
  11.4 2.2 %copy-done = f32[16,8,2,32,32]{4,3,2,1,0:T(8,128)S(1)} copy-done((f32[16,8,2,32,32]{4,3,2,1,0:T(8,128)S(1)}, f32[16,8,2,32,32]{4,3,2,1,0:T(8,128)}, u32[]{:S(2)}) %copy-start) | copy-done | bytes 1048600
  13.6 0.5 pack.1
  14.1 2.3 %all-to-all-done = bf16[16,16,256]{2,1,0:T(8,128)(2,1)S(1)} async-done(((bf16[16,16,256]{2,1,0:T(8,128)(2,1)}), bf16[16,16,256]{2,1,0:T(8,128)(2,1)S(1)}, u32[]{:S(2)}, u32[]{:S(2)}) %all-to-all-start) | async-done | bytes 131104 | tf_op jit(solution)/shard_map/all_to_all | solution.py:541
  16.4 0.0 copy-done.1
  16.4 0.0 copy-done.2
  16.4 0.9 %mode.1 = (f32[256,32]{1,0:T(8,128)S(1)}, bf16[256,256]{1,0:T(8,128)(2,1)S(1)}) custom-call(bf16[256,256]{1,0:T(8,128)(2,1)S(1)} %bitcast.23, bf16[256,256]{1,0:T(8,128)(2,1)S(1)} %copy-done.1, bf16[256,256]{1,0:T(8,128)(2,1)S(1)} %copy-done.2, bf16[4,256,256]{2,1,0:T(8,128)(2,1)S(1)} %get-tuple-element.38.weight_ref), custom_call_target="tpu_custom_call" | custom-call | flops 4194304 | bytes 524288 | tf_op jit(solution)/shard_map/mode/pallas_call | solution.py:564
  17.4 10.2 %all_to_all.20 = bf16[16,16,256]{2,1,0:T(8,128)(2,1)S(1)} all-to-all(bf16[16,16,256]{2,1,0:T(8,128)(2,1)S(1)} %bitcast.27), channel_id=1, replica_groups={{16,17,20,21,24,25,28,29,0,1,4,5,8,9,12,13},{2,3,6,7,10,11,14,15,18,19,..., dimensions={0} | all-to-all | bytes 262144 | tf_op jit(solution)/shard_map/all_to_all | solution.py:541
  27.5 0.1 part.2
  27.6 1.7 %collective-permute-start.1 = (bf16[32,256]{1,0:T(8,128)(2,1)S(1)}, bf16[32,256]{1,0:T(8,128)(2,1)S(1)}, u32[]{:S(2)}, u32[]{:S(2)}) collective-permute-start(bf16[32,256]{1,0:T(8,128)(2,1)S(1)} %get-tuple-element.42), channel_id=1, source_target_pairs={{0,2},{1,3},{2,0},{3,1},{4,6},{5,7},{6,4},{7,5},{8,10},{9,11},{10,... | collective-permute-start | bytes 49160 | tf_op jit(solution)/shard_map/ppermute | solution.py:528
  29.4 0.0 copy-done.7
  29.4 0.0 copy-done.9
  29.4 0.1 copy.15.mix_bias_ref
  29.5 0.0 copy-done.8
  29.5 0.1 copy.16.refs_6_
  29.6 0.1 copy.17.refs_8_
  29.7 0.0 copy-done.4
  29.7 0.0 copy-done.5
  29.7 0.2 ready.1
  29.9 0.3 collective-permute-done.1.refs_1_
  30.2 0.0 copy-done.6
  30.2 1.2 %cell.1 = (f32[8,128]{1,0:T(8,128)S(1)}, bf16[32,1024]{1,0:T(8,128)(2,1)S(1)}, bf16[32,256]{1,0:T(8,128)(2,1)S(1)}, bf16[32,1024]{1,0:T(8,128)(2,1)S(1)}, bf16[128,1024]{1,0:T(8,128)(2,1)S(1)}) custom-call(f32[32,256]{1,0:T(8,128)S(1)} %get-tuple-element.41.refs_0_, bf16[32,256]{1,0:T(8,128)(2,1)S(1)} %collective-permute-done.1.refs_1_, ...), custom_call_target="tpu_custom_call" | custom-call | flops 4194304 | bytes 524288 | tf_op jit(solution)/shard_map/cell/pallas_call | solution.py:573
  31.5 0.4 collective-permute-start.2
  31.8 0.4 sums.1
  32.2 0.5 collective-permute-done.2.got_ref
  32.7 0.2 fold.1
  32.8 11.0 %all_to_all.21 = bf16[16,40,128]{2,1,0:T(8,128)(2,1)S(1)} all-to-all(bf16[16,40,128]{2,1,0:T(8,128)(2,1)S(1)} %bitcast.21), channel_id=1, replica_groups={{16,17,20,21,24,25,28,29,0,1,4,5,8,9,12,13},{2,3,6,7,10,11,14,15,18,19,..., dimensions={0} | all-to-all | bytes 327680 | tf_op jit(solution)/shard_map/all_to_all | solution.py:541
  43.8 1.6 %back.1 = (f32[256,32]{1,0:T(8,128)S(1)}, bf16[640,128]{1,0:T(8,128)(2,1)}) custom-call(bf16[640,128]{1,0:T(8,128)(2,1)S(1)} %bitcast.22, bf16[256,256]{1,0:T(8,128)(2,1)S(1)} %copy-done.1, bf16[256,256]{1,0:T(8,128)(2,1)S(1)} %copy-done.2, bf16[4,256,256]{2,1,0:T(8,128)(2,1)S(1)} %get-tuple-element.38.weight_ref), custom_call_target="tpu_custom_call" | custom-call | flops 4194304 | bytes 524288 | tf_op jit(solution)/shard_map/back/pallas_call | solution.py:605
  45.5 3.6 %all-to-all-start.3 = ((bf16[16,40,128]{2,1,0:T(8,128)(2,1)}), bf16[16,40,128]{2,1,0:T(8,128)(2,1)S(1)}, u32[]{:S(2)}, u32[]{:S(2)}) async-start(bf16[16,40,128]{2,1,0:T(8,128)(2,1)} %bitcast.12), calls=%async_computation.3 | async-start | bytes 327680 | tf_op jit(solution)/shard_map/all_to_all | solution.py:541
  49.1 3.6 %outer.1 = (f32[16,8,2,32,32]{4,3,2,1,0:T(8,128)}, f32[8,128]{1,0:T(8,128)S(1)}) custom-call(f32[16,16,32]{2,1,0:T(8,128)S(1)} %bitcast.25, f32[16,16,32]{2,1,0:T(8,128)S(1)} %bitcast.26), custom_call_target="tpu_custom_call" | custom-call | flops 4194304 | bytes 5242880 | tf_op jit(solution)/shard_map/outer/pallas_call | solution.py:609
  52.7 4.5 %all-to-all-done.3 = bf16[16,40,128]{2,1,0:T(8,128)(2,1)S(1)} async-done(((bf16[16,40,128]{2,1,0:T(8,128)(2,1)}), bf16[16,40,128]{2,1,0:T(8,128)(2,1)S(1)}, u32[]{:S(2)}, u32[]{:S(2)}) %all-to-all-start.3) | async-done | bytes 163872 | tf_op jit(solution)/shard_map/all_to_all | solution.py:541
  57.2 0.2 part.3
  57.4 0.5 collective-permute-start.3
  57.8 0.2 pointwise.1
  58.0 0.7 %collective-permute-done.3.refs_1_ = bf16[96,256]{1,0:T(8,128)(2,1)S(1)} collective-permute-done((bf16[96,256]{1,0:T(8,128)(2,1)S(1)}, bf16[96,256]{1,0:T(8,128)(2,1)S(1)}, u32[]{:S(2)}, u32[]{:S(2)}) %collective-permute-start.3) | collective-permute-done | bytes 49184 | tf_op jit(solution)/shard_map/ppermute | solution.py:528
  58.7 1.0 %finish.1 = (bf16[256,128]{1,0:T(8,128)(2,1)}, f32[8,128]{1,0:T(8,128)}, f32[32,32]{1,0:T(8,128)}, f32[32,128]{1,0:T(8,128)}) custom-call(f32[32,256]{1,0:T(8,128)S(1)} %get-tuple-element.57.refs_0_, bf16[96,256]{1,0:T(8,128)(2,1)S(1)} %collective-permute-done.3.refs_1_, bf16[32,128]{1,0:T(8,128)(2,1)S(1)} %get-tuple-element.59.refs_2_, ...), custom_call_target="tpu_custom_call" | custom-call | flops 4194304 | bytes 524288 | tf_op jit(solution)/shard_map/finish/pallas_call | solution.py:640
  (1 shorter events, 0.0 us)
Async XLA Ops:
  0.6 15.8 %copy-start.1 = (bf16[256,256]{1,0:T(8,128)(2,1)S(1)}, bf16[256,256]{1,0:T(8,128)(2,1)}, u32[]{:S(2)}) copy-start(bf16[256,256]{1,0:T(8,128)(2,1)} %constant.4.clone.y_forward_ref) | copy-start | bytes 393220
  0.6 15.8 %copy-start.2 = (bf16[256,256]{1,0:T(8,128)(2,1)S(1)}, bf16[256,256]{1,0:T(8,128)(2,1)}, u32[]{:S(2)}) copy-start(bf16[256,256]{1,0:T(8,128)(2,1)} %constant.5.clone.y_inverse_ref) | copy-start | bytes 393220
  0.7 1.5 %collective-permute-start = (bf16[256,128]{1,0:T(8,128)(2,1)}, bf16[256,128]{1,0:T(8,128)(2,1)S(1)}, u32[]{:S(2)}, u32[]{:S(2)}) collective-permute-start(bf16[256,128]{1,0:T(8,128)(2,1)} %bitcast.28), channel_id=1, source_target_pairs={{0,2},{1,3},{2,0},{3,1},{4,6},{5,7},{6,4},{7,5},{8,10},{9,11},{10,... | collective-permute-start | bytes 196616 | tf_op jit(solution)/shard_map/ppermute | solution.py:528
  0.8 0.8 %copy-start.3 = (bf16[1,32,8,128]{3,2,1,0:T(8,128)(2,1)S(1)}, bf16[1,32,8,128]{3,2,1,0:T(8,128)(2,1)}, u32[]{:S(2)}) copy-start(bf16[1,32,8,128]{3,2,1,0:T(8,128)(2,1)} %param.10) | copy-start | bytes 196612
  1.6 27.8 %copy-start.7 = (bf16[128]{0:T(256)(128)(2,1)S(1)}, bf16[128]{0:T(256)(128)(2,1)}, u32[]{:S(2)}) copy-start(bf16[128]{0:T(256)(128)(2,1)} %param.16) | copy-start | bytes 772
  1.6 27.8 %copy-start.9 = (f32[32]{0:T(128)S(1)}, f32[32]{0:T(128)}, u32[]{:S(2)}) copy-start(f32[32]{0:T(128)} %param.13) | copy-start | bytes 388
  1.6 27.8 %copy-start.8 = (f32[128]{0:T(128)S(1)}, f32[128]{0:T(128)}, u32[]{:S(2)}) copy-start(f32[128]{0:T(128)} %param.15) | copy-start | bytes 1540
  1.6 28.1 %copy-start.4 = (bf16[32,128]{1,0:T(8,128)(2,1)S(1)}, bf16[32,128]{1,0:T(8,128)(2,1)}, u32[]{:S(2)}) copy-start(bf16[32,128]{1,0:T(8,128)(2,1)} %refs_4_.1) | copy-start | bytes 24580
  1.6 28.1 %copy-start.5 = (bf16[32,32]{1,0:T(8,128)(2,1)S(1)}, bf16[32,32]{1,0:T(8,128)(2,1)}, u32[]{:S(2)}) copy-start(bf16[32,32]{1,0:T(8,128)(2,1)} %mix_ref.3) | copy-start | bytes 6148
  1.6 28.6 %copy-start.6 = (f32[1,8,128]{2,1,0:T(8,128)S(1)}, f32[1,8,128]{2,1,0:T(8,128)}, u32[]{:S(2)}) copy-start(f32[1,8,128]{2,1,0:T(8,128)} %param.17) | copy-start | bytes 12292
  3.4 13.0 %all-to-all-start = ((bf16[16,16,256]{2,1,0:T(8,128)(2,1)}), bf16[16,16,256]{2,1,0:T(8,128)(2,1)S(1)}, u32[]{:S(2)}, u32[]{:S(2)}) async-start(bf16[16,16,256]{2,1,0:T(8,128)(2,1)} %bitcast.1), calls=%async_computation | async-start | bytes 262144 | tf_op jit(solution)/shard_map/all_to_all | solution.py:541
  11.4 2.2 %copy-start = (f32[16,8,2,32,32]{4,3,2,1,0:T(8,128)S(1)}, f32[16,8,2,32,32]{4,3,2,1,0:T(8,128)}, u32[]{:S(2)}) copy-start(f32[16,8,2,32,32]{4,3,2,1,0:T(8,128)} %weight_ref.1) | copy-start | bytes 3145732
  27.6 2.6 %collective-permute-start.1 = (bf16[32,256]{1,0:T(8,128)(2,1)S(1)}, bf16[32,256]{1,0:T(8,128)(2,1)S(1)}, u32[]{:S(2)}, u32[]{:S(2)}) collective-permute-start(bf16[32,256]{1,0:T(8,128)(2,1)S(1)} %get-tuple-element.42), channel_id=1, source_target_pairs={{0,2},{1,3},{2,0},{3,1},{4,6},{5,7},{6,4},{7,5},{8,10},{9,11},{10,... | collective-permute-start | bytes 49160 | tf_op jit(solution)/shard_map/ppermute | solution.py:528
  31.5 1.2 %collective-permute-start.2 = (bf16[32,256]{1,0:T(8,128)(2,1)S(1)}, bf16[32,256]{1,0:T(8,128)(2,1)S(1)}, u32[]{:S(2)}, u32[]{:S(2)}) collective-permute-start(bf16[32,256]{1,0:T(8,128)(2,1)S(1)} %get-tuple-element.47.own_ref), channel_id=1, source_target_pairs={{0,2},{1,3},{2,0},{3,1},{4,6},{5,7},{6,4},{7,5},{8,10},{9,11},{10,... | collective-permute-start | bytes 49160 | tf_op jit(solution)/shard_map/ppermute | solution.py:528
  45.5 11.7 %all-to-all-start.3 = ((bf16[16,40,128]{2,1,0:T(8,128)(2,1)}), bf16[16,40,128]{2,1,0:T(8,128)(2,1)S(1)}, u32[]{:S(2)}, u32[]{:S(2)}) async-start(bf16[16,40,128]{2,1,0:T(8,128)(2,1)} %bitcast.12), calls=%async_computation.3 | async-start | bytes 327680 | tf_op jit(solution)/shard_map/all_to_all | solution.py:541
  57.4 1.3 %collective-permute-start.3 = (bf16[96,256]{1,0:T(8,128)(2,1)S(1)}, bf16[96,256]{1,0:T(8,128)(2,1)S(1)}, u32[]{:S(2)}, u32[]{:S(2)}) collective-permute-start(bf16[96,256]{1,0:T(8,128)(2,1)S(1)} %get-tuple-element.58), channel_id=1, source_target_pairs={{0,2},{1,3},{2,0},{3,1},{4,6},{5,7},{6,4},{7,5},{8,10},{9,11},{10,... | collective-permute-start | bytes 147464 | tf_op jit(solution)/shard_map/ppermute | solution.py:528

commit v18 on v17

--- a/solution.py
+++ b/solution.py
@@ -101,7 +101,7 @@
         self.partners = self.outer * narrow
         self.lanes = rows_y * channels
         middle, last = self.outer // 4, self.outer // 2 - 1
-        self.firsts = ((last, last), (middle, 0), (middle, 0), (middle, 0))
+        self.firsts = ((last, last), (middle, middle - 1), (middle, middle - 1), (middle, middle - 1))
 
     def here(self):
         wide = lax.axis_index("wide")

time: 60.4 us -> 59.4 us (0.983)
  starting transfers between devices: 14.3 us -> 16.8 us
  waiting for transfers between devices: 8.5 us -> 6.2 us
  blocking collectives: 21.1 us -> 20 us
    all_to_all x2, waiting for transfers between devices: 6.84 us -> 4.54 us  [exchange(): lax.all_to_all(pieces, ('wide', 'narrow'), 0, 0, axis_index_groups=groups...]
    ppermute x4, starting transfers between devices: 2.67 us -> 4.8 us  [to_twin(): return lax.ppermute(send, ('wide', 'narrow'), pairs)]
    all_to_all x2, blocking collectives: 21.1 us -> 20 us  [exchange(): lax.all_to_all(pieces, ('wide', 'narrow'), 0, 0, axis_index_groups=groups...]
where the time goes in v18:
time: 59.4 us; the launch traced here: 58.7 us
  blocking collectives  20 us (34%)
  starting transfers between devices  16.8 us (28%)
  Pallas kernels  11.6 us (20%)
  waiting for transfers between devices  6.2 us (10%)
  local copies, waits for them, and re-layouts  3.37 us (6%)
  between operations  0.74 us (1%)
    all_to_all x2, blocking collectives, exchange(): lax.all_to_all(pieces, ('wide', 'narrow'), 0, 0, axis_index_groups=groups...  20 us
    all_to_all x2, starting transfers between devices, exchange(): lax.all_to_all(pieces, ('wide', 'narrow'), 0, 0, axis_index_groups=groups...  12 us
    ppermute x4, starting transfers between devices, to_twin(): return lax.ppermute(send, ('wide', 'narrow'), pairs)  4.8 us
    all_to_all x2, waiting for transfers between devices, exchange(): lax.all_to_all(pieces, ('wide', 'narrow'), 0, 0, axis_index_groups=groups...  4.54 us
    pallas_call x1, Pallas kernels, body(): pl.pallas_call(outer_kernel, grid=(modes // some,), in_specs=[pl.BlockSpe...  3.55 us
    unnamed x20, local copies, waits for them, and re-layouts  3.06 us
    ppermute x4, waiting for transfers between devices, to_twin(): return lax.ppermute(send, ('wide', 'narrow'), pairs)  1.66 us
    pallas_call x1, Pallas kernels, body(): run(back_kernel, [((mode_lines, channels), F32), shared], 'back')  1.65 us
  transfers between devices with their start and end apart: 6, of which 6 were waited for; matrix products, arithmetic and copies ran while one was open for 1% of the time, Pallas kernels for 9%

profile of v18, /device:TPU:1, one launch (start us, length us, event | category | flops | bytes accessed | tf_op | source)
XLA Modules:
  0.0 58.7 jit_solution(2390662181278285371)
XLA Ops:
  0.6 0.0 copy-start.1
  0.6 0.0 copy-start.2
  0.7 0.1 collective-permute-start
  0.8 0.0 copy-start.3
  0.8 0.8 %copy-done.3 = bf16[1,32,8,128]{3,2,1,0:T(8,128)(2,1)S(1)} copy-done((bf16[1,32,8,128]{3,2,1,0:T(8,128)(2,1)S(1)}, bf16[1,32,8,128]{3,2,1,0:T(8,128)(2,1)}, u32[]{:S(2)}) %copy-start.3) | copy-done | bytes 65560
  1.6 0.0 copy-start.7
  1.6 0.0 copy-start.9
  1.6 0.0 copy-start.8
  1.6 0.0 copy-start.4
  1.6 0.0 copy-start.5
  1.6 0.0 copy-start.6
  1.7 0.3 own.1
  2.0 0.2 collective-permute-done.twin_ref
  2.2 1.2 %start.1 = bf16[256,256]{1,0:T(8,128)(2,1)} custom-call(bf16[32,256]{1,0:T(8,128)(2,1)S(1)} %get-tuple-element.37.spectra_ref, bf16[256,128]{1,0:T(8,128)(2,1)S(1)} %collective-permute-done.twin_ref), custom_call_target="tpu_custom_call" | custom-call | flops 4194304 | bytes 524288 | tf_op jit(solution)/shard_map/start/pallas_call | solution.py:560
  3.4 8.0 %all-to-all-start = ((bf16[16,16,256]{2,1,0:T(8,128)(2,1)}), bf16[16,16,256]{2,1,0:T(8,128)(2,1)S(1)}, u32[]{:S(2)}, u32[]{:S(2)}) async-start(bf16[16,16,256]{2,1,0:T(8,128)(2,1)} %bitcast.1), calls=%async_computation | async-start | bytes 262144 | tf_op jit(solution)/shard_map/all_to_all | solution.py:541
  11.4 0.0 copy-start
  11.4 2.2 %copy-done = f32[16,8,2,32,32]{4,3,2,1,0:T(8,128)S(1)} copy-done((f32[16,8,2,32,32]{4,3,2,1,0:T(8,128)S(1)}, f32[16,8,2,32,32]{4,3,2,1,0:T(8,128)}, u32[]{:S(2)}) %copy-start) | copy-done | bytes 1048600
  13.6 0.5 pack.1
  14.1 2.3 %all-to-all-done = bf16[16,16,256]{2,1,0:T(8,128)(2,1)S(1)} async-done(((bf16[16,16,256]{2,1,0:T(8,128)(2,1)}), bf16[16,16,256]{2,1,0:T(8,128)(2,1)S(1)}, u32[]{:S(2)}, u32[]{:S(2)}) %all-to-all-start) | async-done | bytes 131104 | tf_op jit(solution)/shard_map/all_to_all | solution.py:541
  16.4 0.0 copy-done.1
  16.4 0.0 copy-done.2
  16.4 0.9 %mode.1 = (f32[256,32]{1,0:T(8,128)S(1)}, bf16[256,256]{1,0:T(8,128)(2,1)S(1)}) custom-call(bf16[256,256]{1,0:T(8,128)(2,1)S(1)} %bitcast.23, bf16[256,256]{1,0:T(8,128)(2,1)S(1)} %copy-done.1, bf16[256,256]{1,0:T(8,128)(2,1)S(1)} %copy-done.2, bf16[4,256,256]{2,1,0:T(8,128)(2,1)S(1)} %get-tuple-element.38.weight_ref), custom_call_target="tpu_custom_call" | custom-call | flops 4194304 | bytes 524288 | tf_op jit(solution)/shard_map/mode/pallas_call | solution.py:564
  17.4 9.2 %all_to_all.20 = bf16[16,16,256]{2,1,0:T(8,128)(2,1)S(1)} all-to-all(bf16[16,16,256]{2,1,0:T(8,128)(2,1)S(1)} %bitcast.27), channel_id=1, replica_groups={{16,17,20,21,24,25,28,29,0,1,4,5,8,9,12,13},{10,11,14,15,18,19,22,23,26..., dimensions={0} | all-to-all | bytes 262144 | tf_op jit(solution)/shard_map/all_to_all | solution.py:541
  26.6 0.1 part.2
  26.7 2.3 %collective-permute-start.1 = (bf16[32,256]{1,0:T(8,128)(2,1)S(1)}, bf16[32,256]{1,0:T(8,128)(2,1)S(1)}, u32[]{:S(2)}, u32[]{:S(2)}) collective-permute-start(bf16[32,256]{1,0:T(8,128)(2,1)S(1)} %get-tuple-element.42), channel_id=1, source_target_pairs={{0,2},{1,3},{2,0},{3,1},{4,6},{5,7},{6,4},{7,5},{8,10},{9,11},{10,... | collective-permute-start | bytes 49160 | tf_op jit(solution)/shard_map/ppermute | solution.py:528
  29.1 0.0 copy-done.7
  29.1 0.0 copy-done.9
  29.1 0.1 copy.15.mix_bias_ref
  29.2 0.0 copy-done.8
  29.2 0.1 copy.16.refs_6_
  29.3 0.1 copy.17.refs_8_
  29.4 0.0 copy-done.4
  29.4 0.0 copy-done.5
  29.4 0.2 ready.1
  29.6 0.3 collective-permute-done.1.refs_1_
  29.9 0.0 copy-done.6
  29.9 1.2 %cell.1 = (f32[8,128]{1,0:T(8,128)S(1)}, bf16[32,1024]{1,0:T(8,128)(2,1)S(1)}, bf16[32,256]{1,0:T(8,128)(2,1)S(1)}, bf16[32,1024]{1,0:T(8,128)(2,1)S(1)}, bf16[128,1024]{1,0:T(8,128)(2,1)S(1)}) custom-call(f32[32,256]{1,0:T(8,128)S(1)} %get-tuple-element.41.refs_0_, bf16[32,256]{1,0:T(8,128)(2,1)S(1)} %collective-permute-done.1.refs_1_, ...), custom_call_target="tpu_custom_call" | custom-call | flops 4194304 | bytes 524288 | tf_op jit(solution)/shard_map/cell/pallas_call | solution.py:573
  31.1 0.4 collective-permute-start.2
  31.5 0.4 sums.1
  31.9 0.5 collective-permute-done.2.got_ref
  32.3 0.2 fold.1
  32.5 10.8 %all_to_all.21 = bf16[16,40,128]{2,1,0:T(8,128)(2,1)S(1)} all-to-all(bf16[16,40,128]{2,1,0:T(8,128)(2,1)S(1)} %bitcast.21), channel_id=1, replica_groups={{16,17,20,21,24,25,28,29,0,1,4,5,8,9,12,13},{10,11,14,15,18,19,22,23,26..., dimensions={0} | all-to-all | bytes 327680 | tf_op jit(solution)/shard_map/all_to_all | solution.py:541
  43.3 1.7 %back.1 = (f32[256,32]{1,0:T(8,128)S(1)}, bf16[640,128]{1,0:T(8,128)(2,1)}) custom-call(bf16[640,128]{1,0:T(8,128)(2,1)S(1)} %bitcast.22, bf16[256,256]{1,0:T(8,128)(2,1)S(1)} %copy-done.1, bf16[256,256]{1,0:T(8,128)(2,1)S(1)} %copy-done.2, bf16[4,256,256]{2,1,0:T(8,128)(2,1)S(1)} %get-tuple-element.38.weight_ref), custom_call_target="tpu_custom_call" | custom-call | flops 4194304 | bytes 524288 | tf_op jit(solution)/shard_map/back/pallas_call | solution.py:605
  45.0 4.0 %all-to-all-start.3 = ((bf16[16,40,128]{2,1,0:T(8,128)(2,1)}), bf16[16,40,128]{2,1,0:T(8,128)(2,1)S(1)}, u32[]{:S(2)}, u32[]{:S(2)}) async-start(bf16[16,40,128]{2,1,0:T(8,128)(2,1)} %bitcast.12), calls=%async_computation.3 | async-start | bytes 327680 | tf_op jit(solution)/shard_map/all_to_all | solution.py:541
  48.9 3.5 %outer.1 = (f32[16,8,2,32,32]{4,3,2,1,0:T(8,128)}, f32[8,128]{1,0:T(8,128)S(1)}) custom-call(f32[16,16,32]{2,1,0:T(8,128)S(1)} %bitcast.25, f32[16,16,32]{2,1,0:T(8,128)S(1)} %bitcast.26), custom_call_target="tpu_custom_call" | custom-call | flops 4194304 | bytes 5242880 | tf_op jit(solution)/shard_map/outer/pallas_call | solution.py:609
  52.5 2.2 %all-to-all-done.3 = bf16[16,40,128]{2,1,0:T(8,128)(2,1)S(1)} async-done(((bf16[16,40,128]{2,1,0:T(8,128)(2,1)}), bf16[16,40,128]{2,1,0:T(8,128)(2,1)S(1)}, u32[]{:S(2)}, u32[]{:S(2)}) %all-to-all-start.3) | async-done | bytes 163872 | tf_op jit(solution)/shard_map/all_to_all | solution.py:541
  54.7 0.2 part.3
  54.9 2.0 %collective-permute-start.3 = (bf16[96,256]{1,0:T(8,128)(2,1)S(1)}, bf16[96,256]{1,0:T(8,128)(2,1)S(1)}, u32[]{:S(2)}, u32[]{:S(2)}) collective-permute-start(bf16[96,256]{1,0:T(8,128)(2,1)S(1)} %get-tuple-element.58), channel_id=1, source_target_pairs={{0,2},{1,3},{2,0},{3,1},{4,6},{5,7},{6,4},{7,5},{8,10},{9,11},{10,... | collective-permute-start | bytes 147464 | tf_op jit(solution)/shard_map/ppermute | solution.py:528
  56.9 0.2 pointwise.1
  57.1 0.7 %collective-permute-done.3.refs_1_ = bf16[96,256]{1,0:T(8,128)(2,1)S(1)} collective-permute-done((bf16[96,256]{1,0:T(8,128)(2,1)S(1)}, bf16[96,256]{1,0:T(8,128)(2,1)S(1)}, u32[]{:S(2)}, u32[]{:S(2)}) %collective-permute-start.3) | collective-permute-done | bytes 49184 | tf_op jit(solution)/shard_map/ppermute | solution.py:528
  57.7 1.0 %finish.1 = (bf16[256,128]{1,0:T(8,128)(2,1)}, f32[8,128]{1,0:T(8,128)}, f32[32,32]{1,0:T(8,128)}, f32[32,128]{1,0:T(8,128)}) custom-call(f32[32,256]{1,0:T(8,128)S(1)} %get-tuple-element.57.refs_0_, bf16[96,256]{1,0:T(8,128)(2,1)S(1)} %collective-permute-done.3.refs_1_, bf16[32,128]{1,0:T(8,128)(2,1)S(1)} %get-tuple-element.59.refs_2_, ...), custom_call_target="tpu_custom_call" | custom-call | flops 4194304 | bytes 524288 | tf_op jit(solution)/shard_map/finish/pallas_call | solution.py:640
  (1 shorter events, 0.0 us)
Async XLA Ops:
  0.6 15.8 %copy-start.1 = (bf16[256,256]{1,0:T(8,128)(2,1)S(1)}, bf16[256,256]{1,0:T(8,128)(2,1)}, u32[]{:S(2)}) copy-start(bf16[256,256]{1,0:T(8,128)(2,1)} %constant.4.clone.y_forward_ref) | copy-start | bytes 393220
  0.6 15.8 %copy-start.2 = (bf16[256,256]{1,0:T(8,128)(2,1)S(1)}, bf16[256,256]{1,0:T(8,128)(2,1)}, u32[]{:S(2)}) copy-start(bf16[256,256]{1,0:T(8,128)(2,1)} %constant.5.clone.y_inverse_ref) | copy-start | bytes 393220
  0.7 1.5 %collective-permute-start = (bf16[256,128]{1,0:T(8,128)(2,1)}, bf16[256,128]{1,0:T(8,128)(2,1)S(1)}, u32[]{:S(2)}, u32[]{:S(2)}) collective-permute-start(bf16[256,128]{1,0:T(8,128)(2,1)} %bitcast.28), channel_id=1, source_target_pairs={{0,2},{1,3},{2,0},{3,1},{4,6},{5,7},{6,4},{7,5},{8,10},{9,11},{10,... | collective-permute-start | bytes 196616 | tf_op jit(solution)/shard_map/ppermute | solution.py:528
  0.8 0.8 %copy-start.3 = (bf16[1,32,8,128]{3,2,1,0:T(8,128)(2,1)S(1)}, bf16[1,32,8,128]{3,2,1,0:T(8,128)(2,1)}, u32[]{:S(2)}) copy-start(bf16[1,32,8,128]{3,2,1,0:T(8,128)(2,1)} %param.10) | copy-start | bytes 196612
  1.6 27.4 %copy-start.7 = (bf16[128]{0:T(256)(128)(2,1)S(1)}, bf16[128]{0:T(256)(128)(2,1)}, u32[]{:S(2)}) copy-start(bf16[128]{0:T(256)(128)(2,1)} %param.16) | copy-start | bytes 772
  1.6 27.4 %copy-start.9 = (f32[32]{0:T(128)S(1)}, f32[32]{0:T(128)}, u32[]{:S(2)}) copy-start(f32[32]{0:T(128)} %param.13) | copy-start | bytes 388
  1.6 27.5 %copy-start.8 = (f32[128]{0:T(128)S(1)}, f32[128]{0:T(128)}, u32[]{:S(2)}) copy-start(f32[128]{0:T(128)} %param.15) | copy-start | bytes 1540
  1.6 27.8 %copy-start.4 = (bf16[32,128]{1,0:T(8,128)(2,1)S(1)}, bf16[32,128]{1,0:T(8,128)(2,1)}, u32[]{:S(2)}) copy-start(bf16[32,128]{1,0:T(8,128)(2,1)} %refs_4_.1) | copy-start | bytes 24580
  1.6 27.8 %copy-start.5 = (bf16[32,32]{1,0:T(8,128)(2,1)S(1)}, bf16[32,32]{1,0:T(8,128)(2,1)}, u32[]{:S(2)}) copy-start(bf16[32,32]{1,0:T(8,128)(2,1)} %mix_ref.3) | copy-start | bytes 6148
  1.6 28.3 %copy-start.6 = (f32[1,8,128]{2,1,0:T(8,128)S(1)}, f32[1,8,128]{2,1,0:T(8,128)}, u32[]{:S(2)}) copy-start(f32[1,8,128]{2,1,0:T(8,128)} %param.17) | copy-start | bytes 12292
  3.4 13.0 %all-to-all-start = ((bf16[16,16,256]{2,1,0:T(8,128)(2,1)}), bf16[16,16,256]{2,1,0:T(8,128)(2,1)S(1)}, u32[]{:S(2)}, u32[]{:S(2)}) async-start(bf16[16,16,256]{2,1,0:T(8,128)(2,1)} %bitcast.1), calls=%async_computation | async-start | bytes 262144 | tf_op jit(solution)/shard_map/all_to_all | solution.py:541
  11.4 2.2 %copy-start = (f32[16,8,2,32,32]{4,3,2,1,0:T(8,128)S(1)}, f32[16,8,2,32,32]{4,3,2,1,0:T(8,128)}, u32[]{:S(2)}) copy-start(f32[16,8,2,32,32]{4,3,2,1,0:T(8,128)} %weight_ref.1) | copy-start | bytes 3145732
  26.7 3.2 %collective-permute-start.1 = (bf16[32,256]{1,0:T(8,128)(2,1)S(1)}, bf16[32,256]{1,0:T(8,128)(2,1)S(1)}, u32[]{:S(2)}, u32[]{:S(2)}) collective-permute-start(bf16[32,256]{1,0:T(8,128)(2,1)S(1)} %get-tuple-element.42), channel_id=1, source_target_pairs={{0,2},{1,3},{2,0},{3,1},{4,6},{5,7},{6,4},{7,5},{8,10},{9,11},{10,... | collective-permute-start | bytes 49160 | tf_op jit(solution)/shard_map/ppermute | solution.py:528
  31.1 1.2 %collective-permute-start.2 = (bf16[32,256]{1,0:T(8,128)(2,1)S(1)}, bf16[32,256]{1,0:T(8,128)(2,1)S(1)}, u32[]{:S(2)}, u32[]{:S(2)}) collective-permute-start(bf16[32,256]{1,0:T(8,128)(2,1)S(1)} %get-tuple-element.47.own_ref), channel_id=1, source_target_pairs={{0,2},{1,3},{2,0},{3,1},{4,6},{5,7},{6,4},{7,5},{8,10},{9,11},{10,... | collective-permute-start | bytes 49160 | tf_op jit(solution)/shard_map/ppermute | solution.py:528
  45.0 9.8 %all-to-all-start.3 = ((bf16[16,40,128]{2,1,0:T(8,128)(2,1)}), bf16[16,40,128]{2,1,0:T(8,128)(2,1)S(1)}, u32[]{:S(2)}, u32[]{:S(2)}) async-start(bf16[16,40,128]{2,1,0:T(8,128)(2,1)} %bitcast.12), calls=%async_computation.3 | async-start | bytes 327680 | tf_op jit(solution)/shard_map/all_to_all | solution.py:541
  54.9 2.8 %collective-permute-start.3 = (bf16[96,256]{1,0:T(8,128)(2,1)S(1)}, bf16[96,256]{1,0:T(8,128)(2,1)S(1)}, u32[]{:S(2)}, u32[]{:S(2)}) collective-permute-start(bf16[96,256]{1,0:T(8,128)(2,1)S(1)} %get-tuple-element.58), channel_id=1, source_target_pairs={{0,2},{1,3},{2,0},{3,1},{4,6},{5,7},{6,4},{7,5},{8,10},{9,11},{10,... | collective-permute-start | bytes 147464 | tf_op jit(solution)/shard_map/ppermute | solution.py:528

commit v19 on v16

--- a/solution.py
+++ b/solution.py
@@ -12,6 +12,7 @@
 MX = 16
 MY = 16
 MZ = 16
+BLOCK = 32
 F32 = jnp.float32
 BF16 = jnp.bfloat16
 VMEM_LIMIT = 32 * 1024 * 1024
@@ -197,6 +198,12 @@
     return values[:, :width]
 
 
+def diagonal_blocks(count, width, rows):
+    row, lane = grid_of(count, count * width)
+    pattern = jnp.where(row == lane // width, 1.0, 0.0)
+    return jnp.concatenate([pattern] * (rows // count), axis=0)
+
+
 def analysed(place, pieces, y_forward, copies):
     height = 2 * MZ
     turned = sum(
@@ -288,11 +295,10 @@
     kz, channels = place.kz, place.channels
     spectrum = analysed(place, pieces_ref[...], y_forward_ref[...], kz)
     spectrum_ref[...] = spectrum[:, :channels]
-    row, lane = grid_of(*spectrum.shape)
-    blocked = jnp.where(row % kz == lane // channels, spectrum, 0.0)
+    diagonal = diagonal_blocks(kz, channels, 8 * kz)
     mixed = []
     for q in range(place.modes // 4):
-        left = blocked[q * 8 * kz : (q + 1) * 8 * kz].astype(BF16)
+        left = (spectrum[q * 8 * kz : (q + 1) * 8 * kz] * diagonal).astype(BF16)
         product = dot(left, weight_ref[q])
         for j in range(4):
             own = product[j * 2 * kz : (j + 1) * 2 * kz, j * 2 * channels : (j + 1) * 2 * channels]
@@ -346,14 +352,14 @@
 
 def cell_kernel(place, *refs):
     own_ref, got_ref, z_table_ref, pointwise_ref, head_ref, head_turned_ref = refs[:6]
-    head_bias_ref, out_row_ref, out_column_ref, cotangent_ref = refs[6:10]
-    prediction_ref, grad_pre_ref, send_ref, hidden_ref, head_slope_ref = refs[10:]
+    head_bias_ref, out_column_ref, cotangent_ref = refs[6:9]
+    prediction_ref, grad_pre_ref, send_ref, hidden_ref, head_slope_ref = refs[9:]
     rows_y, z_count = place.rows_y, place.z_count
     z_table = z_table_ref[...]
     lines = (own_ref[...] + got_ref[...].astype(F32)).astype(BF16)
     pre_act = side_by_side(dot_tn(lines, z_table), rows_y) + pointwise_ref[...]
     head, head_turned = head_ref[...], head_turned_ref[...]
-    head_bias, out_row, out_column = head_bias_ref[...], out_row_ref[...], out_column_ref[...]
+    head_bias, out_column = head_bias_ref[...], out_column_ref[...]
     width = 2 * z_count
     slopes, head_pre = [], []
     for first in range(0, rows_y * z_count, width):
@@ -367,11 +373,16 @@
         target = jnp.concatenate(
             [cotangent_ref[y : y + 1] for y in range(first, first + 2)], axis=1
         )
-        active, slope = normal(head_pre[index] + head_bias)
-        predicted = dot(out_row, active.astype(BF16))
+        predicted, parts = 0.0, []
+        for top in range(0, head_bias.shape[0], BLOCK):
+            rows = slice(top, top + BLOCK)
+            active, slope = normal(head_pre[index][rows] + head_bias[rows])
+            predicted = predicted + active.astype(BF16).astype(F32) * out_column[rows]
+            parts.append((target * out_column[rows] * slope).astype(BF16))
+        predicted = jnp.sum(predicted, axis=0, keepdims=True)
         prediction_ref[first : first + 1] = predicted[:, :z_count]
         prediction_ref[first + 1 : first + 2] = predicted[:, z_count:]
-        head_slope = (target * out_column * slope).astype(BF16)
+        head_slope = jnp.concatenate(parts, axis=0)
         head_slope_ref[:, first * z_count : first * z_count + width] = head_slope
         gradients.append((dot(head, head_slope) * slopes[index]).astype(BF16))
     gradient = jnp.concatenate(gradients, axis=1)
@@ -413,17 +424,15 @@
         turned += [adjoint[first + kz : first + 2 * kz], -adjoint[first : first + kz]]
     left = jnp.concatenate([adjoint, jnp.concatenate(turned, axis=0)], axis=1)
     left = jnp.concatenate([left] * 4, axis=1)
-    row, lane = grid_of(*left.shape)
-    same = (row // (2 * kz)) % 4 == lane // (2 * channels)
-    left = jnp.where(same, left, 0.0).astype(BF16)
+    row, lane = grid_of(8 * kz, 8 * channels)
+    same = jnp.where(row // (2 * kz) == lane // (2 * channels), 1.0, 0.0)
+    diagonal = diagonal_blocks(kz, channels, 8 * kz)
     block = 8 * kz
-    pulled = [
-        dot_nt(left[q * block : (q + 1) * block], weight_ref[q]) for q in range(place.modes // 4)
-    ]
-    pulled = jnp.concatenate(pulled, axis=0)
-    row, lane = grid_of(*pulled.shape)
-    pulled = jnp.where(row % kz == lane // channels, pulled, 0.0)
-    modes_back = lane_sum(pulled, channels).astype(BF16)
+    pulled = []
+    for q in range(place.modes // 4):
+        own = (left[q * block : (q + 1) * block] * same).astype(BF16)
+        pulled.append(lane_sum(dot_nt(own, weight_ref[q]) * diagonal, channels))
+    modes_back = jnp.concatenate(pulled, axis=0).astype(BF16)
     block = spread_lines(place, modes_back, y_inverse_ref[...])
     if shares is None:
         repeat_rows(send_ref, block)
@@ -587,7 +596,6 @@
         head_weight,
         head_turned,
         head_bias[:, None],
-        out_weight[None],
         out_weight.astype(F32)[:, None],
         cotangent[0],
     )

time: 58.5 us -> 58.4 us (level)
  no operation moved by 1% of the time
where the time goes in v19:
time: 58.4 us; the launch traced here: 57.7 us
  starting transfers between devices  19.3 us (33%)
  blocking collectives  17.6 us (30%)
  Pallas kernels  11.6 us (20%)
  waiting for transfers between devices  5.23 us (9%)
  local copies, waits for them, and re-layouts  3.37 us (6%)
  between operations  0.74 us (1%)
    all_to_all x2, blocking collectives, exchange(): lax.all_to_all(pieces, ('wide', 'narrow'), 0, 0, axis_index_groups=groups...  17.6 us
    all_to_all x2, starting transfers between devices, exchange(): lax.all_to_all(pieces, ('wide', 'narrow'), 0, 0, axis_index_groups=groups...  12.8 us
    ppermute x4, starting transfers between devices, to_twin(): return lax.ppermute(send, ('wide', 'narrow'), pairs)  6.48 us
    all_to_all x2, waiting for transfers between devices, exchange(): lax.all_to_all(pieces, ('wide', 'narrow'), 0, 0, axis_index_groups=groups...  3.57 us
    pallas_call x1, Pallas kernels, body(): pl.pallas_call(outer_kernel, grid=(modes // some,), in_specs=[pl.BlockSpe...  3.55 us
    unnamed x20, local copies, waits for them, and re-layouts  3.06 us
    ppermute x4, waiting for transfers between devices, to_twin(): return lax.ppermute(send, ('wide', 'narrow'), pairs)  1.66 us
    pallas_call x1, Pallas kernels, body(): run(back_kernel, [((mode_lines, channels), F32), shared], 'back')  1.65 us
  transfers between devices with their start and end apart: 6, of which 6 were waited for; matrix products, arithmetic and copies ran while one was open for 1% of the time, Pallas kernels for 9%

profile of v19, /device:TPU:1, one launch (start us, length us, event | category | flops | bytes accessed | tf_op | source)
XLA Modules:
  0.0 57.7 jit_solution(15295316266334397425)
XLA Ops:
  0.6 0.0 copy-start.1
  0.6 0.0 copy-start.2
  0.7 0.1 collective-permute-start
  0.8 0.0 copy-start.3
  0.8 0.8 %copy-done.3 = bf16[1,32,8,128]{3,2,1,0:T(8,128)(2,1)S(1)} copy-done((bf16[1,32,8,128]{3,2,1,0:T(8,128)(2,1)S(1)}, bf16[1,32,8,128]{3,2,1,0:T(8,128)(2,1)}, u32[]{:S(2)}) %copy-start.3) | copy-done | bytes 65560
  1.6 0.0 copy-start.9
  1.6 0.0 copy-start.8
  1.6 0.0 copy-start.7
  1.6 0.0 copy-start.4
  1.6 0.0 copy-start.5
  1.6 0.0 copy-start.6
  1.7 0.3 own.1
  2.0 0.2 collective-permute-done.twin_ref
  2.2 1.2 %start.1 = bf16[256,256]{1,0:T(8,128)(2,1)} custom-call(bf16[32,256]{1,0:T(8,128)(2,1)S(1)} %get-tuple-element.37.spectra_ref, bf16[256,128]{1,0:T(8,128)(2,1)S(1)} %collective-permute-done.twin_ref), custom_call_target="tpu_custom_call" | custom-call | flops 4194304 | bytes 524288 | tf_op jit(solution)/shard_map/start/pallas_call | solution.py:568
  3.4 8.0 %all-to-all-start = ((bf16[16,16,256]{2,1,0:T(8,128)(2,1)}), bf16[16,16,256]{2,1,0:T(8,128)(2,1)S(1)}, u32[]{:S(2)}, u32[]{:S(2)}) async-start(bf16[16,16,256]{2,1,0:T(8,128)(2,1)} %bitcast.1), calls=%async_computation | async-start | bytes 262144 | tf_op jit(solution)/shard_map/all_to_all | solution.py:549
  11.4 0.0 copy-start
  11.4 2.2 %copy-done = f32[16,8,2,32,32]{4,3,2,1,0:T(8,128)S(1)} copy-done((f32[16,8,2,32,32]{4,3,2,1,0:T(8,128)S(1)}, f32[16,8,2,32,32]{4,3,2,1,0:T(8,128)}, u32[]{:S(2)}) %copy-start) | copy-done | bytes 1048600
  13.6 0.5 pack.1
  14.1 2.3 %all-to-all-done = bf16[16,16,256]{2,1,0:T(8,128)(2,1)S(1)} async-done(((bf16[16,16,256]{2,1,0:T(8,128)(2,1)}), bf16[16,16,256]{2,1,0:T(8,128)(2,1)S(1)}, u32[]{:S(2)}, u32[]{:S(2)}) %all-to-all-start) | async-done | bytes 131104 | tf_op jit(solution)/shard_map/all_to_all | solution.py:549
  16.4 0.0 copy-done.1
  16.4 0.0 copy-done.2
  16.4 0.9 %mode.1 = (f32[256,32]{1,0:T(8,128)S(1)}, bf16[256,256]{1,0:T(8,128)(2,1)S(1)}) custom-call(bf16[256,256]{1,0:T(8,128)(2,1)S(1)} %bitcast.22, bf16[256,256]{1,0:T(8,128)(2,1)S(1)} %copy-done.1, bf16[256,256]{1,0:T(8,128)(2,1)S(1)} %copy-done.2, bf16[4,256,256]{2,1,0:T(8,128)(2,1)S(1)} %get-tuple-element.38.weight_ref), custom_call_target="tpu_custom_call" | custom-call | flops 4194304 | bytes 524288 | tf_op jit(solution)/shard_map/mode/pallas_call | solution.py:572
  17.4 8.7 %all_to_all.20 = bf16[16,16,256]{2,1,0:T(8,128)(2,1)S(1)} all-to-all(bf16[16,16,256]{2,1,0:T(8,128)(2,1)S(1)} %bitcast.26), channel_id=1, replica_groups={{16,17,20,21,24,25,28,29,0,1,4,5,8,9,12,13},{18,19,22,23,26,27,30,31,2,..., dimensions={0} | all-to-all | bytes 262144 | tf_op jit(solution)/shard_map/all_to_all | solution.py:549
  26.1 0.1 part.2
  26.2 2.8 %collective-permute-start.1 = (bf16[32,256]{1,0:T(8,128)(2,1)S(1)}, bf16[32,256]{1,0:T(8,128)(2,1)S(1)}, u32[]{:S(2)}, u32[]{:S(2)}) collective-permute-start(bf16[32,256]{1,0:T(8,128)(2,1)S(1)} %get-tuple-element.42), channel_id=1, source_target_pairs={{0,2},{1,3},{2,0},{3,1},{4,6},{5,7},{6,4},{7,5},{8,10},{9,11},{10,... | collective-permute-start | bytes 49160 | tf_op jit(solution)/shard_map/ppermute | solution.py:536
  29.1 0.0 copy-done.9
  29.1 0.0 copy-done.8
  29.1 0.1 copy.15.mix_bias_ref
  29.2 0.0 copy-done.7
  29.2 0.1 copy.16.refs_6_
  29.3 0.1 copy.17.refs_7_
  29.4 0.0 copy-done.4
  29.4 0.0 copy-done.5
  29.4 0.2 ready.1
  29.6 0.3 collective-permute-done.1.refs_1_
  29.9 0.0 copy-done.6
  29.9 1.2 %cell.1 = (f32[8,128]{1,0:T(8,128)S(1)}, bf16[32,1024]{1,0:T(8,128)(2,1)S(1)}, bf16[32,256]{1,0:T(8,128)(2,1)S(1)}, bf16[32,1024]{1,0:T(8,128)(2,1)S(1)}, bf16[128,1024]{1,0:T(8,128)(2,1)S(1)}) custom-call(f32[32,256]{1,0:T(8,128)S(1)} %get-tuple-element.41.refs_0_, bf16[32,256]{1,0:T(8,128)(2,1)S(1)} %collective-permute-done.1.refs_1_, ...), custom_call_target="tpu_custom_call" | custom-call | flops 4194304 | bytes 524288 | tf_op jit(solution)/shard_map/cell/pallas_call | solution.py:581
  31.1 0.4 collective-permute-start.2
  31.5 0.4 sums.1
  31.8 0.5 collective-permute-done.2.got_ref
  32.3 0.2 fold.1
  32.5 8.8 %all_to_all.21 = bf16[16,40,128]{2,1,0:T(8,128)(2,1)S(1)} all-to-all(bf16[16,40,128]{2,1,0:T(8,128)(2,1)S(1)} %bitcast.20), channel_id=1, replica_groups={{16,17,20,21,24,25,28,29,0,1,4,5,8,9,12,13},{18,19,22,23,26,27,30,31,2,..., dimensions={0} | all-to-all | bytes 327680 | tf_op jit(solution)/shard_map/all_to_all | solution.py:549
  41.3 1.6 %back.1 = (f32[256,32]{1,0:T(8,128)S(1)}, bf16[640,128]{1,0:T(8,128)(2,1)}) custom-call(bf16[640,128]{1,0:T(8,128)(2,1)S(1)} %bitcast.21, bf16[256,256]{1,0:T(8,128)(2,1)S(1)} %copy-done.1, bf16[256,256]{1,0:T(8,128)(2,1)S(1)} %copy-done.2, bf16[4,256,256]{2,1,0:T(8,128)(2,1)S(1)} %get-tuple-element.38.weight_ref), custom_call_target="tpu_custom_call" | custom-call | flops 4194304 | bytes 524288 | tf_op jit(solution)/shard_map/back/pallas_call | solution.py:612
  43.0 4.8 %all-to-all-start.3 = ((bf16[16,40,128]{2,1,0:T(8,128)(2,1)}), bf16[16,40,128]{2,1,0:T(8,128)(2,1)S(1)}, u32[]{:S(2)}, u32[]{:S(2)}) async-start(bf16[16,40,128]{2,1,0:T(8,128)(2,1)} %bitcast.11), calls=%async_computation.3 | async-start | bytes 327680 | tf_op jit(solution)/shard_map/all_to_all | solution.py:549
  47.7 3.5 %outer.1 = (f32[16,8,2,32,32]{4,3,2,1,0:T(8,128)}, f32[8,128]{1,0:T(8,128)S(1)}) custom-call(f32[16,16,32]{2,1,0:T(8,128)S(1)} %bitcast.24, f32[16,16,32]{2,1,0:T(8,128)S(1)} %bitcast.25), custom_call_target="tpu_custom_call" | custom-call | flops 4194304 | bytes 5242880 | tf_op jit(solution)/shard_map/outer/pallas_call | solution.py:616
  51.3 1.3 %all-to-all-done.3 = bf16[16,40,128]{2,1,0:T(8,128)(2,1)S(1)} async-done(((bf16[16,40,128]{2,1,0:T(8,128)(2,1)}), bf16[16,40,128]{2,1,0:T(8,128)(2,1)S(1)}, u32[]{:S(2)}, u32[]{:S(2)}) %all-to-all-start.3) | async-done | bytes 163872 | tf_op jit(solution)/shard_map/all_to_all | solution.py:549
  52.5 0.2 part.3
  52.7 3.2 %collective-permute-start.3 = (bf16[96,256]{1,0:T(8,128)(2,1)S(1)}, bf16[96,256]{1,0:T(8,128)(2,1)S(1)}, u32[]{:S(2)}, u32[]{:S(2)}) collective-permute-start(bf16[96,256]{1,0:T(8,128)(2,1)S(1)} %get-tuple-element.58), channel_id=1, source_target_pairs={{0,2},{1,3},{2,0},{3,1},{4,6},{5,7},{6,4},{7,5},{8,10},{9,11},{10,... | collective-permute-start | bytes 147464 | tf_op jit(solution)/shard_map/ppermute | solution.py:536
  55.9 0.2 pointwise.1
  56.1 0.7 %collective-permute-done.3.refs_1_ = bf16[96,256]{1,0:T(8,128)(2,1)S(1)} collective-permute-done((bf16[96,256]{1,0:T(8,128)(2,1)S(1)}, bf16[96,256]{1,0:T(8,128)(2,1)S(1)}, u32[]{:S(2)}, u32[]{:S(2)}) %collective-permute-start.3) | collective-permute-done | bytes 49184 | tf_op jit(solution)/shard_map/ppermute | solution.py:536
  56.7 1.0 %finish.1 = (bf16[256,128]{1,0:T(8,128)(2,1)}, f32[8,128]{1,0:T(8,128)}, f32[32,32]{1,0:T(8,128)}, f32[32,128]{1,0:T(8,128)}) custom-call(f32[32,256]{1,0:T(8,128)S(1)} %get-tuple-element.57.refs_0_, bf16[96,256]{1,0:T(8,128)(2,1)S(1)} %collective-permute-done.3.refs_1_, bf16[32,128]{1,0:T(8,128)(2,1)S(1)} %get-tuple-element.59.refs_2_, ...), custom_call_target="tpu_custom_call" | custom-call | flops 4194304 | bytes 524288 | tf_op jit(solution)/shard_map/finish/pallas_call | solution.py:647
  (1 shorter events, 0.0 us)
Async XLA Ops:
  0.6 15.8 %copy-start.1 = (bf16[256,256]{1,0:T(8,128)(2,1)S(1)}, bf16[256,256]{1,0:T(8,128)(2,1)}, u32[]{:S(2)}) copy-start(bf16[256,256]{1,0:T(8,128)(2,1)} %constant.4.clone.y_forward_ref) | copy-start | bytes 393220
  0.6 15.8 %copy-start.2 = (bf16[256,256]{1,0:T(8,128)(2,1)S(1)}, bf16[256,256]{1,0:T(8,128)(2,1)}, u32[]{:S(2)}) copy-start(bf16[256,256]{1,0:T(8,128)(2,1)} %constant.5.clone.y_inverse_ref) | copy-start | bytes 393220
  0.7 1.5 %collective-permute-start = (bf16[256,128]{1,0:T(8,128)(2,1)}, bf16[256,128]{1,0:T(8,128)(2,1)S(1)}, u32[]{:S(2)}, u32[]{:S(2)}) collective-permute-start(bf16[256,128]{1,0:T(8,128)(2,1)} %bitcast.27), channel_id=1, source_target_pairs={{0,2},{1,3},{2,0},{3,1},{4,6},{5,7},{6,4},{7,5},{8,10},{9,11},{10,... | collective-permute-start | bytes 196616 | tf_op jit(solution)/shard_map/ppermute | solution.py:536
  0.8 0.8 %copy-start.3 = (bf16[1,32,8,128]{3,2,1,0:T(8,128)(2,1)S(1)}, bf16[1,32,8,128]{3,2,1,0:T(8,128)(2,1)}, u32[]{:S(2)}) copy-start(bf16[1,32,8,128]{3,2,1,0:T(8,128)(2,1)} %param.10) | copy-start | bytes 196612
  1.6 27.4 %copy-start.9 = (bf16[128]{0:T(256)(128)(2,1)S(1)}, bf16[128]{0:T(256)(128)(2,1)}, u32[]{:S(2)}) copy-start(bf16[128]{0:T(256)(128)(2,1)} %param.16) | copy-start | bytes 772
  1.6 27.4 %copy-start.8 = (f32[32]{0:T(128)S(1)}, f32[32]{0:T(128)}, u32[]{:S(2)}) copy-start(f32[32]{0:T(128)} %param.13) | copy-start | bytes 388
  1.6 27.5 %copy-start.7 = (f32[128]{0:T(128)S(1)}, f32[128]{0:T(128)}, u32[]{:S(2)}) copy-start(f32[128]{0:T(128)} %param.15) | copy-start | bytes 1540
  1.6 27.8 %copy-start.4 = (bf16[32,128]{1,0:T(8,128)(2,1)S(1)}, bf16[32,128]{1,0:T(8,128)(2,1)}, u32[]{:S(2)}) copy-start(bf16[32,128]{1,0:T(8,128)(2,1)} %refs_4_.1) | copy-start | bytes 24580
  1.6 27.8 %copy-start.5 = (bf16[32,32]{1,0:T(8,128)(2,1)S(1)}, bf16[32,32]{1,0:T(8,128)(2,1)}, u32[]{:S(2)}) copy-start(bf16[32,32]{1,0:T(8,128)(2,1)} %mix_ref.3) | copy-start | bytes 6148
  1.6 28.3 %copy-start.6 = (f32[1,8,128]{2,1,0:T(8,128)S(1)}, f32[1,8,128]{2,1,0:T(8,128)}, u32[]{:S(2)}) copy-start(f32[1,8,128]{2,1,0:T(8,128)} %param.17) | copy-start | bytes 12292
  3.4 13.0 %all-to-all-start = ((bf16[16,16,256]{2,1,0:T(8,128)(2,1)}), bf16[16,16,256]{2,1,0:T(8,128)(2,1)S(1)}, u32[]{:S(2)}, u32[]{:S(2)}) async-start(bf16[16,16,256]{2,1,0:T(8,128)(2,1)} %bitcast.1), calls=%async_computation | async-start | bytes 262144 | tf_op jit(solution)/shard_map/all_to_all | solution.py:549
  11.4 2.2 %copy-start = (f32[16,8,2,32,32]{4,3,2,1,0:T(8,128)S(1)}, f32[16,8,2,32,32]{4,3,2,1,0:T(8,128)}, u32[]{:S(2)}) copy-start(f32[16,8,2,32,32]{4,3,2,1,0:T(8,128)} %weight_ref.1) | copy-start | bytes 3145732
  26.2 3.7 %collective-permute-start.1 = (bf16[32,256]{1,0:T(8,128)(2,1)S(1)}, bf16[32,256]{1,0:T(8,128)(2,1)S(1)}, u32[]{:S(2)}, u32[]{:S(2)}) collective-permute-start(bf16[32,256]{1,0:T(8,128)(2,1)S(1)} %get-tuple-element.42), channel_id=1, source_target_pairs={{0,2},{1,3},{2,0},{3,1},{4,6},{5,7},{6,4},{7,5},{8,10},{9,11},{10,... | collective-permute-start | bytes 49160 | tf_op jit(solution)/shard_map/ppermute | solution.py:536
  31.1 1.2 %collective-permute-start.2 = (bf16[32,256]{1,0:T(8,128)(2,1)S(1)}, bf16[32,256]{1,0:T(8,128)(2,1)S(1)}, u32[]{:S(2)}, u32[]{:S(2)}) collective-permute-start(bf16[32,256]{1,0:T(8,128)(2,1)S(1)} %get-tuple-element.47.own_ref), channel_id=1, source_target_pairs={{0,2},{1,3},{2,0},{3,1},{4,6},{5,7},{6,4},{7,5},{8,10},{9,11},{10,... | collective-permute-start | bytes 49160 | tf_op jit(solution)/shard_map/ppermute | solution.py:536
  43.0 9.6 %all-to-all-start.3 = ((bf16[16,40,128]{2,1,0:T(8,128)(2,1)}), bf16[16,40,128]{2,1,0:T(8,128)(2,1)S(1)}, u32[]{:S(2)}, u32[]{:S(2)}) async-start(bf16[16,40,128]{2,1,0:T(8,128)(2,1)} %bitcast.11), calls=%async_computation.3 | async-start | bytes 327680 | tf_op jit(solution)/shard_map/all_to_all | solution.py:549
  52.7 4.0 %collective-permute-start.3 = (bf16[96,256]{1,0:T(8,128)(2,1)S(1)}, bf16[96,256]{1,0:T(8,128)(2,1)S(1)}, u32[]{:S(2)}, u32[]{:S(2)}) collective-permute-start(bf16[96,256]{1,0:T(8,128)(2,1)S(1)} %get-tuple-element.58), channel_id=1, source_target_pairs={{0,2},{1,3},{2,0},{3,1},{4,6},{5,7},{6,4},{7,5},{8,10},{9,11},{10,... | collective-permute-start | bytes 147464 | tf_op jit(solution)/shard_map/ppermute | solution.py:536

commit v20 on v15

--- a/solution.py
+++ b/solution.py
@@ -12,6 +12,7 @@
 MX = 16
 MY = 16
 MZ = 16
+BLOCK = 32
 F32 = jnp.float32
 BF16 = jnp.bfloat16
 VMEM_LIMIT = 32 * 1024 * 1024
@@ -197,6 +198,26 @@
         blocks.append(jnp.concatenate([left, right], axis=1))
         shares.append(pieces_ref[first + 2 * step : first + height].astype(F32))
     return jnp.concatenate(blocks, axis=0), shares
+
+
+def lane_sum(values, width):
+    while values.shape[1] > 128:
+        half = values.shape[1] // 2
+        values = values[:, :half] + values[:, half:]
+    if values.shape[1] < 128:
+        blocks = range(0, values.shape[1], width)
+        return sum(values[:, first : first + width] for first in blocks)
+    shift = 64
+    while shift >= width:
+        values = values + pltpu.roll(values, shift, 1)
+        shift //= 2
+    return values[:, :width]
+
+
+def diagonal_blocks(count, width, rows):
+    row, lane = grid_of(count, count * width)
+    pattern = jnp.where(row == lane // width, 1.0, 0.0)
+    return jnp.concatenate([pattern] * (rows // count), axis=0)
 
 
 def analysed(place, pieces, y_forward, copies, first):
@@ -265,7 +286,8 @@
     send_ref[...] = dot(tables, jnp.concatenate([values, values], axis=0)).astype(BF16)
 
 
-def pack_kernel(weight_ref, packed_ref):
+def pack_kernel(place, weight_ref, packed_ref, inverse_ref):
+    inverse_ref[...] = place.inverse_x(place.firsts[1])
     modes, kz, _, channels, _ = weight_ref.shape
     for q in range(modes // 4):
         parts = [weight_ref[4 * q + j // 2, :, j % 2] for j in range(8)]
@@ -297,11 +319,10 @@
     kz, channels = place.kz, place.channels
     spectrum = analysed(place, pieces_ref[...], y_forward_ref[...], kz, place.firsts[0])
     spectrum_ref[...] = spectrum[:, :channels]
-    row, lane = grid_of(*spectrum.shape)
-    blocked = jnp.where(row % kz == lane // channels, spectrum, 0.0)
+    diagonal = diagonal_blocks(kz, channels, 8 * kz)
     mixed = []
     for q in range(place.modes // 4):
-        left = blocked[q * 8 * kz : (q + 1) * 8 * kz].astype(BF16)
+        left = (spectrum[q * 8 * kz : (q + 1) * 8 * kz] * diagonal).astype(BF16)
         product = dot(left, weight_ref[q])
         for j in range(4):
             own = product[j * 2 * kz : (j + 1) * 2 * kz, j * 2 * channels : (j + 1) * 2 * channels]
@@ -312,9 +333,9 @@
     repeat_rows(place, send_ref, spread_lines(place, mode, y_inverse_ref[...]), place.firsts[1])
 
 
-def part_kernel(place, first, pieces_ref, *refs):
+def part_kernel(place, pieces_ref, table_ref, *refs):
     pieces, shares = read_pieces(place, pieces_ref)
-    lines = dot(place.inverse_x(first), pieces)
+    lines = dot(table_ref[...], pieces)
     height = 2 * MZ
     if shares is None:
         own_ref, send_ref = refs
@@ -330,7 +351,7 @@
     def chosen(part):
         def condition(row, column):
             owner = place.listed((row % channels) // 2, place.firsts[2])
-            source = place.listed(column // 8, first)
+            source = place.listed(column // 8, place.firsts[3])
             return (
                 (owner[0] == source[0])
                 & (owner[1] == source[1])
@@ -345,8 +366,8 @@
 
 
 def normal(values):
-    scaled = 1.0 / (1.0 + TAIL_SLOPE * jnp.abs(values))
-    decay = jnp.exp(-0.5 * values * values)
+    scaled = pl.reciprocal(1.0 + jnp.abs(TAIL_SLOPE * values), approx=True)
+    decay = jnp.exp2(values * values * (-0.5 / math.log(2.0)))
     tail = TAIL[-1]
     for factor in TAIL[-2::-1]:
         tail = tail * scaled + factor
@@ -357,14 +378,14 @@
 
 def cell_kernel(place, *refs):
     own_ref, got_ref, z_table_ref, pointwise_ref, head_ref, head_turned_ref = refs[:6]
-    head_bias_ref, out_row_ref, out_column_ref, cotangent_ref = refs[6:10]
-    prediction_ref, grad_pre_ref, send_ref, hidden_ref, head_slope_ref = refs[10:]
+    head_bias_ref, out_column_ref, cotangent_ref = refs[6:9]
+    prediction_ref, grad_pre_ref, send_ref, hidden_ref, head_slope_ref = refs[9:]
     rows_y, z_count = place.rows_y, place.z_count
     z_table = z_table_ref[...]
     lines = (own_ref[...] + got_ref[...].astype(F32)).astype(BF16)
     pre_act = side_by_side(dot_tn(lines, z_table), rows_y) + pointwise_ref[...]
     head, head_turned = head_ref[...], head_turned_ref[...]
-    head_bias, out_row, out_column = head_bias_ref[...], out_row_ref[...], out_column_ref[...]
+    head_bias, out_column = head_bias_ref[...], out_column_ref[...]
     width = 2 * z_count
     slopes, head_pre = [], []
     for first in range(0, rows_y * z_count, width):
@@ -378,11 +399,16 @@
         target = jnp.concatenate(
             [cotangent_ref[y : y + 1] for y in range(first, first + 2)], axis=1
         )
-        active, slope = normal(head_pre[index] + head_bias)
-        predicted = dot(out_row, active.astype(BF16))
+        predicted, parts = 0.0, []
+        for top in range(0, head_bias.shape[0], BLOCK):
+            rows = slice(top, top + BLOCK)
+            active, slope = normal(head_pre[index][rows] + head_bias[rows])
+            predicted = predicted + active.astype(BF16).astype(F32) * out_column[rows]
+            parts.append((target * out_column[rows] * slope).astype(BF16))
+        predicted = jnp.sum(predicted, axis=0, keepdims=True)
         prediction_ref[first : first + 1] = predicted[:, :z_count]
         prediction_ref[first + 1 : first + 2] = predicted[:, z_count:]
-        head_slope = (target * out_column * slope).astype(BF16)
+        head_slope = jnp.concatenate(parts, axis=0)
         head_slope_ref[:, first * z_count : first * z_count + width] = head_slope
         gradients.append((dot(head, head_slope) * slopes[index]).astype(BF16))
     gradient = jnp.concatenate(gradients, axis=1)
@@ -424,20 +450,15 @@
         turned += [adjoint[first + kz : first + 2 * kz], -adjoint[first : first + kz]]
     left = jnp.concatenate([adjoint, jnp.concatenate(turned, axis=0)], axis=1)
     left = jnp.concatenate([left] * 4, axis=1)
-    row, lane = grid_of(*left.shape)
-    same = (row // (2 * kz)) % 4 == lane // (2 * channels)
-    left = jnp.where(same, left, 0.0).astype(BF16)
+    row, lane = grid_of(8 * kz, 8 * channels)
+    same = jnp.where(row // (2 * kz) == lane // (2 * channels), 1.0, 0.0)
+    diagonal = diagonal_blocks(kz, channels, 8 * kz)
     block = 8 * kz
-    pulled = [
-        dot_nt(left[q * block : (q + 1) * block], weight_ref[q]) for q in range(place.modes // 4)
-    ]
-    pulled = jnp.concatenate(pulled, axis=0)
-    row, lane = grid_of(*pulled.shape)
-    pulled = jnp.where(row % kz == lane // channels, pulled, 0.0).astype(BF16)
-    gather = selector(
-        kz * channels, channels, lambda row, column: row % channels == column
-    )
-    modes_back = dot(pulled, gather).astype(BF16)
+    pulled = []
+    for q in range(place.modes // 4):
+        own = (left[q * block : (q + 1) * block] * same).astype(BF16)
+        pulled.append(lane_sum(dot_nt(own, weight_ref[q]) * diagonal, channels))
+    modes_back = jnp.concatenate(pulled, axis=0).astype(BF16)
     block = spread_lines(place, modes_back, y_inverse_ref[...])
     if shares is None:
         repeat_rows(place, send_ref, block, place.firsts[3])
@@ -566,12 +587,12 @@
     field, spectra = run(own_kernel, [(across, BF16), twin_plain], "own")(flat_field)
     (send,) = run(start_kernel, [plain], "start")(spectra, twin_field)
     packed_shape = ((modes // 4, kz * channels, 8 * channels), BF16)
-    (weight,) = call(pack_kernel, [packed_shape], "pack")(spectral_weight)
+    inverse_shape = ((2 * height, wide // 2 * height), BF16)
+    weight, inverse = run(pack_kernel, [packed_shape, inverse_shape], "pack")(spectral_weight)
     spectrum, send = run(mode_kernel, [((mode_lines, channels), F32), plain], "mode")(
         exchange(send, 0), y_forward, y_inverse, weight
     )
-    part = functools.partial(part_kernel, place, place.firsts[1])
-    own, send = call(part, [own_lines, twin_plain], "part")(exchange(send, 1))
+    own, send = run(part_kernel, [own_lines, twin_plain], "part")(exchange(send, 1), inverse)
     pointwise, head_turned, z_doubled = run(
         ready_kernel,
         [(across, F32), ((hidden_units, channels), BF16), ((height, z_count), BF16)],
@@ -595,7 +616,6 @@
         head_weight,
         head_turned,
         head_bias[:, None],
-        out_weight[None],
         out_weight.astype(F32)[:, None],
         cotangent[0],
     )
@@ -640,8 +660,7 @@
     )(mix_weight, grad_pre)
     outs = [own_lines, twin_shared] + ([sums_shape] if place.fold else [])
     after = (done,) if place.fold else ()
-    part = functools.partial(part_kernel, place, place.firsts[3])
-    own, send, *sums = call(part, outs, "part")(exchange(send, 3), *after)
+    own, send, *sums = run(part_kernel, outs, "part")(exchange(send, 3), inverse, *after)
     outs = [((cells, z_count), BF16), ((rows_y, z_count), F32)]
     if place.fold:
         outs += [((channels, channels), F32), ((channels, hidden_units), F32)]

time: 59.2 us -> 59 us (level)
  no operation moved by 1% of the time
where the time goes in v20:
time: 59 us; the launch traced here: 58.3 us
  starting transfers between devices  19.4 us (33%)
  blocking collectives  17.1 us (29%)
  Pallas kernels  11.6 us (20%)
  waiting for transfers between devices  5.98 us (10%)
  local copies, waits for them, and re-layouts  3.37 us (6%)
  between operations  0.74 us (1%)
    all_to_all x2, blocking collectives, exchange(): lax.all_to_all(pieces, ('wide', 'narrow'), 0, 0, axis_index_groups=groups...  17.1 us
    all_to_all x2, starting transfers between devices, exchange(): lax.all_to_all(pieces, ('wide', 'narrow'), 0, 0, axis_index_groups=groups...  13.7 us
    ppermute x4, starting transfers between devices, to_twin(): return lax.ppermute(send, ('wide', 'narrow'), pairs)  5.71 us
    all_to_all x2, waiting for transfers between devices, exchange(): lax.all_to_all(pieces, ('wide', 'narrow'), 0, 0, axis_index_groups=groups...  4.34 us
    pallas_call x1, Pallas kernels, body(): pl.pallas_call(outer_kernel, grid=(modes // some,), in_specs=[pl.BlockSpe...  3.55 us
    unnamed x20, local copies, waits for them, and re-layouts  3.06 us
    pallas_call x1, Pallas kernels, body(): run(back_kernel, [((mode_lines, channels), F32), shared], 'back')  1.65 us
    ppermute x4, waiting for transfers between devices, to_twin(): return lax.ppermute(send, ('wide', 'narrow'), pairs)  1.64 us
  transfers between devices with their start and end apart: 6, of which 6 were waited for; matrix products, arithmetic and copies ran while one was open for 1% of the time, Pallas kernels for 9%

profile of v20, /device:TPU:1, one launch (start us, length us, event | category | flops | bytes accessed | tf_op | source)
XLA Modules:
  0.0 58.3 jit_solution(13447676369595287493)
XLA Ops:
  0.6 0.0 copy-start.1
  0.6 0.0 copy-start.2
  0.7 0.1 collective-permute-start
  0.8 0.0 copy-start.3
  0.8 0.8 %copy-done.3 = bf16[1,32,8,128]{3,2,1,0:T(8,128)(2,1)S(1)} copy-done((bf16[1,32,8,128]{3,2,1,0:T(8,128)(2,1)S(1)}, bf16[1,32,8,128]{3,2,1,0:T(8,128)(2,1)}, u32[]{:S(2)}) %copy-start.3) | copy-done | bytes 65560
  1.6 0.0 copy-start.9
  1.6 0.0 copy-start.8
  1.6 0.0 copy-start.7
  1.6 0.0 copy-start.4
  1.6 0.0 copy-start.5
  1.6 0.0 copy-start.6
  1.7 0.3 own.1
  2.0 0.2 collective-permute-done.twin_ref
  2.2 1.2 %start.1 = bf16[256,256]{1,0:T(8,128)(2,1)} custom-call(bf16[32,256]{1,0:T(8,128)(2,1)S(1)} %get-tuple-element.37.spectra_ref, bf16[256,128]{1,0:T(8,128)(2,1)S(1)} %collective-permute-done.twin_ref), custom_call_target="tpu_custom_call" | custom-call | flops 4194304 | bytes 524288 | tf_op jit(solution)/shard_map/start/pallas_call | solution.py:588
  3.4 8.0 %all-to-all-start = ((bf16[16,16,256]{2,1,0:T(8,128)(2,1)}), bf16[16,16,256]{2,1,0:T(8,128)(2,1)S(1)}, u32[]{:S(2)}, u32[]{:S(2)}) async-start(bf16[16,16,256]{2,1,0:T(8,128)(2,1)} %bitcast.1), calls=%async_computation | async-start | bytes 262144 | tf_op jit(solution)/shard_map/all_to_all | solution.py:569
  11.4 0.0 copy-start
  11.4 2.2 %copy-done = f32[16,8,2,32,32]{4,3,2,1,0:T(8,128)S(1)} copy-done((f32[16,8,2,32,32]{4,3,2,1,0:T(8,128)S(1)}, f32[16,8,2,32,32]{4,3,2,1,0:T(8,128)}, u32[]{:S(2)}) %copy-start) | copy-done | bytes 1048600
  13.6 0.5 pack.1
  14.1 3.0 %all-to-all-done = bf16[16,16,256]{2,1,0:T(8,128)(2,1)S(1)} async-done(((bf16[16,16,256]{2,1,0:T(8,128)(2,1)}), bf16[16,16,256]{2,1,0:T(8,128)(2,1)S(1)}, u32[]{:S(2)}, u32[]{:S(2)}) %all-to-all-start) | async-done | bytes 131104 | tf_op jit(solution)/shard_map/all_to_all | solution.py:569
  17.1 0.0 copy-done.1
  17.1 0.0 copy-done.2
  17.1 0.9 %mode.1 = (f32[256,32]{1,0:T(8,128)S(1)}, bf16[256,256]{1,0:T(8,128)(2,1)S(1)}) custom-call(bf16[256,256]{1,0:T(8,128)(2,1)S(1)} %bitcast.22, bf16[256,256]{1,0:T(8,128)(2,1)S(1)} %copy-done.1, bf16[256,256]{1,0:T(8,128)(2,1)S(1)} %copy-done.2, bf16[4,256,256]{2,1,0:T(8,128)(2,1)S(1)} %get-tuple-element.38.weight_ref), custom_call_target="tpu_custom_call" | custom-call | flops 4194304 | bytes 524288 | tf_op jit(solution)/shard_map/mode/pallas_call | solution.py:592
  18.0 8.1 %all_to_all.20 = bf16[16,16,256]{2,1,0:T(8,128)(2,1)S(1)} all-to-all(bf16[16,16,256]{2,1,0:T(8,128)(2,1)S(1)} %bitcast.26), channel_id=1, replica_groups={{16,24,0,8,17,25,1,9,20,28,4,12,21,29,5,13},{18,26,2,10,19,27,3,11,22,3..., dimensions={0} | all-to-all | bytes 262144 | tf_op jit(solution)/shard_map/all_to_all | solution.py:569
  26.2 0.1 part.2
  26.3 2.6 %collective-permute-start.1 = (bf16[32,256]{1,0:T(8,128)(2,1)S(1)}, bf16[32,256]{1,0:T(8,128)(2,1)S(1)}, u32[]{:S(2)}, u32[]{:S(2)}) collective-permute-start(bf16[32,256]{1,0:T(8,128)(2,1)S(1)} %get-tuple-element.42), channel_id=1, source_target_pairs={{0,2},{1,3},{2,0},{3,1},{4,6},{5,7},{6,4},{7,5},{8,10},{9,11},{10,... | collective-permute-start | bytes 49160 | tf_op jit(solution)/shard_map/ppermute | solution.py:562
  28.9 0.0 copy-done.9
  28.9 0.0 copy-done.8
  28.9 0.1 copy.15.mix_bias_ref
  29.0 0.0 copy-done.7
  29.0 0.1 copy.16.refs_6_
  29.1 0.1 copy.17.refs_7_
  29.2 0.0 copy-done.4
  29.2 0.0 copy-done.5
  29.2 0.2 ready.1
  29.4 0.3 collective-permute-done.1.refs_1_
  29.7 0.0 copy-done.6
  29.7 1.2 %cell.1 = (f32[8,128]{1,0:T(8,128)S(1)}, bf16[32,1024]{1,0:T(8,128)(2,1)S(1)}, bf16[32,256]{1,0:T(8,128)(2,1)S(1)}, bf16[32,1024]{1,0:T(8,128)(2,1)S(1)}, bf16[128,1024]{1,0:T(8,128)(2,1)S(1)}) custom-call(f32[32,256]{1,0:T(8,128)S(1)} %get-tuple-element.41.refs_0_, bf16[32,256]{1,0:T(8,128)(2,1)S(1)} %collective-permute-done.1.refs_1_, ...), custom_call_target="tpu_custom_call" | custom-call | flops 4194304 | bytes 524288 | tf_op jit(solution)/shard_map/cell/pallas_call | solution.py:601
  30.9 0.4 collective-permute-start.2
  31.3 0.4 sums.1
  31.7 0.4 collective-permute-done.2.got_ref
  32.1 0.2 fold.1
  32.3 9.0 %all_to_all.21 = bf16[16,40,128]{2,1,0:T(8,128)(2,1)S(1)} all-to-all(bf16[16,40,128]{2,1,0:T(8,128)(2,1)S(1)} %bitcast.20), channel_id=1, replica_groups={{16,24,0,8,17,25,1,9,20,28,4,12,21,29,5,13},{18,26,2,10,19,27,3,11,22,3..., dimensions={0} | all-to-all | bytes 327680 | tf_op jit(solution)/shard_map/all_to_all | solution.py:569
  41.3 1.6 %back.1 = (f32[256,32]{1,0:T(8,128)S(1)}, bf16[640,128]{1,0:T(8,128)(2,1)}) custom-call(bf16[640,128]{1,0:T(8,128)(2,1)S(1)} %bitcast.21, bf16[256,256]{1,0:T(8,128)(2,1)S(1)} %copy-done.1, bf16[256,256]{1,0:T(8,128)(2,1)S(1)} %copy-done.2, bf16[4,256,256]{2,1,0:T(8,128)(2,1)S(1)} %get-tuple-element.38.weight_ref), custom_call_target="tpu_custom_call" | custom-call | flops 4194304 | bytes 524288 | tf_op jit(solution)/shard_map/back/pallas_call | solution.py:632
  43.0 5.7 %all-to-all-start.3 = ((bf16[16,40,128]{2,1,0:T(8,128)(2,1)}), bf16[16,40,128]{2,1,0:T(8,128)(2,1)S(1)}, u32[]{:S(2)}, u32[]{:S(2)}) async-start(bf16[16,40,128]{2,1,0:T(8,128)(2,1)} %bitcast.11), calls=%async_computation.3 | async-start | bytes 327680 | tf_op jit(solution)/shard_map/all_to_all | solution.py:569
  48.6 3.5 %outer.1 = (f32[16,8,2,32,32]{4,3,2,1,0:T(8,128)}, f32[8,128]{1,0:T(8,128)S(1)}) custom-call(f32[16,16,32]{2,1,0:T(8,128)S(1)} %bitcast.24, f32[16,16,32]{2,1,0:T(8,128)S(1)} %bitcast.25), custom_call_target="tpu_custom_call" | custom-call | flops 4194304 | bytes 5242880 | tf_op jit(solution)/shard_map/outer/pallas_call | solution.py:636
  52.2 1.4 %all-to-all-done.3 = bf16[16,40,128]{2,1,0:T(8,128)(2,1)S(1)} async-done(((bf16[16,40,128]{2,1,0:T(8,128)(2,1)}), bf16[16,40,128]{2,1,0:T(8,128)(2,1)S(1)}, u32[]{:S(2)}, u32[]{:S(2)}) %all-to-all-start.3) | async-done | bytes 163872 | tf_op jit(solution)/shard_map/all_to_all | solution.py:569
  53.5 0.2 part.3
  53.7 2.6 %collective-permute-start.3 = (bf16[96,256]{1,0:T(8,128)(2,1)S(1)}, bf16[96,256]{1,0:T(8,128)(2,1)S(1)}, u32[]{:S(2)}, u32[]{:S(2)}) collective-permute-start(bf16[96,256]{1,0:T(8,128)(2,1)S(1)} %get-tuple-element.58), channel_id=1, source_target_pairs={{0,2},{1,3},{2,0},{3,1},{4,6},{5,7},{6,4},{7,5},{8,10},{9,11},{10,... | collective-permute-start | bytes 147464 | tf_op jit(solution)/shard_map/ppermute | solution.py:562
  56.4 0.2 pointwise.1
  56.6 0.7 %collective-permute-done.3.refs_1_ = bf16[96,256]{1,0:T(8,128)(2,1)S(1)} collective-permute-done((bf16[96,256]{1,0:T(8,128)(2,1)S(1)}, bf16[96,256]{1,0:T(8,128)(2,1)S(1)}, u32[]{:S(2)}, u32[]{:S(2)}) %collective-permute-start.3) | collective-permute-done | bytes 49184 | tf_op jit(solution)/shard_map/ppermute | solution.py:562
  57.3 1.0 %finish.1 = (bf16[256,128]{1,0:T(8,128)(2,1)}, f32[8,128]{1,0:T(8,128)}, f32[32,32]{1,0:T(8,128)}, f32[32,128]{1,0:T(8,128)}) custom-call(f32[32,256]{1,0:T(8,128)S(1)} %get-tuple-element.57.refs_0_, bf16[96,256]{1,0:T(8,128)(2,1)S(1)} %collective-permute-done.3.refs_1_, bf16[32,128]{1,0:T(8,128)(2,1)S(1)} %get-tuple-element.59.refs_2_, ...), custom_call_target="tpu_custom_call" | custom-call | flops 4194304 | bytes 524288 | tf_op jit(solution)/shard_map/finish/pallas_call | solution.py:667
  (1 shorter events, 0.0 us)
Async XLA Ops:
  0.6 16.5 %copy-start.1 = (bf16[256,256]{1,0:T(8,128)(2,1)S(1)}, bf16[256,256]{1,0:T(8,128)(2,1)}, u32[]{:S(2)}) copy-start(bf16[256,256]{1,0:T(8,128)(2,1)} %constant.4.clone.y_forward_ref) | copy-start | bytes 393220
  0.6 16.5 %copy-start.2 = (bf16[256,256]{1,0:T(8,128)(2,1)S(1)}, bf16[256,256]{1,0:T(8,128)(2,1)}, u32[]{:S(2)}) copy-start(bf16[256,256]{1,0:T(8,128)(2,1)} %constant.5.clone.y_inverse_ref) | copy-start | bytes 393220
  0.7 1.5 %collective-permute-start = (bf16[256,128]{1,0:T(8,128)(2,1)}, bf16[256,128]{1,0:T(8,128)(2,1)S(1)}, u32[]{:S(2)}, u32[]{:S(2)}) collective-permute-start(bf16[256,128]{1,0:T(8,128)(2,1)} %bitcast.27), channel_id=1, source_target_pairs={{0,2},{1,3},{2,0},{3,1},{4,6},{5,7},{6,4},{7,5},{8,10},{9,11},{10,... | collective-permute-start | bytes 196616 | tf_op jit(solution)/shard_map/ppermute | solution.py:562
  0.8 0.8 %copy-start.3 = (bf16[1,32,8,128]{3,2,1,0:T(8,128)(2,1)S(1)}, bf16[1,32,8,128]{3,2,1,0:T(8,128)(2,1)}, u32[]{:S(2)}) copy-start(bf16[1,32,8,128]{3,2,1,0:T(8,128)(2,1)} %param.10) | copy-start | bytes 196612
  1.6 27.3 %copy-start.9 = (bf16[128]{0:T(256)(128)(2,1)S(1)}, bf16[128]{0:T(256)(128)(2,1)}, u32[]{:S(2)}) copy-start(bf16[128]{0:T(256)(128)(2,1)} %param.16) | copy-start | bytes 772
  1.6 27.3 %copy-start.8 = (f32[32]{0:T(128)S(1)}, f32[32]{0:T(128)}, u32[]{:S(2)}) copy-start(f32[32]{0:T(128)} %param.13) | copy-start | bytes 388
  1.6 27.4 %copy-start.7 = (f32[128]{0:T(128)S(1)}, f32[128]{0:T(128)}, u32[]{:S(2)}) copy-start(f32[128]{0:T(128)} %param.15) | copy-start | bytes 1540
  1.6 27.6 %copy-start.4 = (bf16[32,128]{1,0:T(8,128)(2,1)S(1)}, bf16[32,128]{1,0:T(8,128)(2,1)}, u32[]{:S(2)}) copy-start(bf16[32,128]{1,0:T(8,128)(2,1)} %refs_4_.1) | copy-start | bytes 24580
  1.6 27.6 %copy-start.5 = (bf16[32,32]{1,0:T(8,128)(2,1)S(1)}, bf16[32,32]{1,0:T(8,128)(2,1)}, u32[]{:S(2)}) copy-start(bf16[32,32]{1,0:T(8,128)(2,1)} %mix_ref.3) | copy-start | bytes 6148
  1.6 28.1 %copy-start.6 = (f32[1,8,128]{2,1,0:T(8,128)S(1)}, f32[1,8,128]{2,1,0:T(8,128)}, u32[]{:S(2)}) copy-start(f32[1,8,128]{2,1,0:T(8,128)} %param.17) | copy-start | bytes 12292
  3.4 13.7 %all-to-all-start = ((bf16[16,16,256]{2,1,0:T(8,128)(2,1)}), bf16[16,16,256]{2,1,0:T(8,128)(2,1)S(1)}, u32[]{:S(2)}, u32[]{:S(2)}) async-start(bf16[16,16,256]{2,1,0:T(8,128)(2,1)} %bitcast.1), calls=%async_computation | async-start | bytes 262144 | tf_op jit(solution)/shard_map/all_to_all | solution.py:569
  11.4 2.2 %copy-start = (f32[16,8,2,32,32]{4,3,2,1,0:T(8,128)S(1)}, f32[16,8,2,32,32]{4,3,2,1,0:T(8,128)}, u32[]{:S(2)}) copy-start(f32[16,8,2,32,32]{4,3,2,1,0:T(8,128)} %weight_ref.1) | copy-start | bytes 3145732
  26.3 3.4 %collective-permute-start.1 = (bf16[32,256]{1,0:T(8,128)(2,1)S(1)}, bf16[32,256]{1,0:T(8,128)(2,1)S(1)}, u32[]{:S(2)}, u32[]{:S(2)}) collective-permute-start(bf16[32,256]{1,0:T(8,128)(2,1)S(1)} %get-tuple-element.42), channel_id=1, source_target_pairs={{0,2},{1,3},{2,0},{3,1},{4,6},{5,7},{6,4},{7,5},{8,10},{9,11},{10,... | collective-permute-start | bytes 49160 | tf_op jit(solution)/shard_map/ppermute | solution.py:562
  30.9 1.2 %collective-permute-start.2 = (bf16[32,256]{1,0:T(8,128)(2,1)S(1)}, bf16[32,256]{1,0:T(8,128)(2,1)S(1)}, u32[]{:S(2)}, u32[]{:S(2)}) collective-permute-start(bf16[32,256]{1,0:T(8,128)(2,1)S(1)} %get-tuple-element.47.own_ref), channel_id=1, source_target_pairs={{0,2},{1,3},{2,0},{3,1},{4,6},{5,7},{6,4},{7,5},{8,10},{9,11},{10,... | collective-permute-start | bytes 49160 | tf_op jit(solution)/shard_map/ppermute | solution.py:562
  43.0 10.6 %all-to-all-start.3 = ((bf16[16,40,128]{2,1,0:T(8,128)(2,1)}), bf16[16,40,128]{2,1,0:T(8,128)(2,1)S(1)}, u32[]{:S(2)}, u32[]{:S(2)}) async-start(bf16[16,40,128]{2,1,0:T(8,128)(2,1)} %bitcast.11), calls=%async_computation.3 | async-start | bytes 327680 | tf_op jit(solution)/shard_map/all_to_all | solution.py:569
  53.7 3.5 %collective-permute-start.3 = (bf16[96,256]{1,0:T(8,128)(2,1)S(1)}, bf16[96,256]{1,0:T(8,128)(2,1)S(1)}, u32[]{:S(2)}, u32[]{:S(2)}) collective-permute-start(bf16[96,256]{1,0:T(8,128)(2,1)S(1)} %get-tuple-element.58), channel_id=1, source_target_pairs={{0,2},{1,3},{2,0},{3,1},{4,6},{5,7},{6,4},{7,5},{8,10},{9,11},{10,... | collective-permute-start | bytes 147464 | tf_op jit(solution)/shard_map/ppermute | solution.py:562

commit v21 on v19

--- a/solution.py
+++ b/solution.py
@@ -101,8 +101,8 @@
         self.outer = wide // 2
         self.partners = self.outer * narrow
         self.lanes = rows_y * channels
-        middle, last = self.outer // 4, self.outer // 2 - 1
-        self.firsts = (last, middle, middle, middle)
+        middle = self.outer // 4
+        self.firsts = (middle, middle, middle, middle)
 
     def here(self):
         wide = lax.axis_index("wide")
@@ -248,18 +248,21 @@
     return jnp.concatenate([values[:, y * width : (y + 1) * width] for y in range(count)], axis=0)
 
 
-def own_kernel(place, field_ref, field_out_ref, spectra_ref):
+def own_kernel(place, field_ref, field_out_ref, spectra_ref, z_table_ref, turn_ref, tables_ref):
+    z_table = place.z_table(False)
     turned = dot(turn_matrix(place, False), field_ref[...]).astype(BF16)
     field_out_ref[...] = side_by_side(turned, place.rows_y)
-    spectra_ref[...] = dot_nt(place.z_table(False), turned).astype(BF16)
-
-
-def start_kernel(place, spectra_ref, twin_ref, send_ref):
-    twin = dot_nt(place.z_table(False), twin_ref[...]).astype(BF16)
-    twin = dot(twin, turn_matrix(place, True)).astype(BF16)
+    spectra_ref[...] = dot_nt(z_table, turned).astype(BF16)
+    z_table_ref[...] = z_table
+    turn_ref[...] = turn_matrix(place, True)
+    tables_ref[...] = jnp.concatenate(halves(place.forward_x(place.firsts[0])), axis=1)
+
+
+def start_kernel(place, spectra_ref, twin_ref, z_table_ref, turn_ref, tables_ref, send_ref):
+    twin = dot_nt(z_table_ref[...], twin_ref[...]).astype(BF16)
+    twin = dot(twin, turn_ref[...]).astype(BF16)
     values = jnp.concatenate([spectra_ref[...], twin], axis=0)
-    tables = jnp.concatenate(halves(place.forward_x(place.firsts[0])), axis=1)
-    send_ref[...] = dot(tables, jnp.concatenate([values, values], axis=0)).astype(BF16)
+    send_ref[...] = dot(tables_ref[...], jnp.concatenate([values, values], axis=0)).astype(BF16)
 
 
 def pack_kernel(place, weight_ref, packed_ref, inverse_ref):
@@ -564,8 +567,13 @@
 
     flat_field = lifted_field.reshape(cells, z_count)
     twin_field = to_twin(flat_field)
-    field, spectra = run(own_kernel, [(across, BF16), twin_plain], "own")(flat_field)
-    (send,) = run(start_kernel, [plain], "start")(spectra, twin_field)
+    tables_shape = ((wide // 2 * height, 4 * height), BF16)
+    field, spectra, *tables = run(
+        own_kernel,
+        [(across, BF16), twin_plain, ((height, z_count), BF16), ((cells, cells), BF16), tables_shape],
+        "own",
+    )(flat_field)
+    (send,) = run(start_kernel, [plain], "start")(spectra, twin_field, *tables)
     packed_shape = ((modes // 4, kz * channels, 8 * channels), BF16)
     inverse_shape = ((2 * height, wide // 2 * height), BF16)
     weight, inverse = run(pack_kernel, [packed_shape, inverse_shape], "pack")(spectral_weight)

time: 58.4 us -> 58.4 us (level)
  no operation moved by 1% of the time
where the time goes in v21:
time: 58.4 us; the launch traced here: 57.6 us
  starting transfers between devices  19.3 us (33%)
  blocking collectives  17.9 us (31%)
  Pallas kernels  11.5 us (20%)
  waiting for transfers between devices  4.84 us (8%)
  local copies, waits for them, and re-layouts  3.37 us (6%)
  between operations  0.74 us (1%)
    all_to_all x2, blocking collectives, exchange(): lax.all_to_all(pieces, ('wide', 'narrow'), 0, 0, axis_index_groups=groups...  17.9 us
    all_to_all x2, starting transfers between devices, exchange(): lax.all_to_all(pieces, ('wide', 'narrow'), 0, 0, axis_index_groups=groups...  12.8 us
    ppermute x4, starting transfers between devices, to_twin(): return lax.ppermute(send, ('wide', 'narrow'), pairs)  6.48 us
    pallas_call x1, Pallas kernels, body(): pl.pallas_call(outer_kernel, grid=(modes // some,), in_specs=[pl.BlockSpe...  3.55 us
    all_to_all x2, waiting for transfers between devices, exchange(): lax.all_to_all(pieces, ('wide', 'narrow'), 0, 0, axis_index_groups=groups...  3.21 us
    unnamed x20, local copies, waits for them, and re-layouts  3.06 us
    pallas_call x1, Pallas kernels, body(): run(back_kernel, [((mode_lines, channels), F32), shared], 'back')  1.65 us
    ppermute x4, waiting for transfers between devices, to_twin(): return lax.ppermute(send, ('wide', 'narrow'), pairs)  1.63 us
  transfers between devices with their start and end apart: 6, of which 6 were waited for; matrix products, arithmetic and copies ran while one was open for 1% of the time, Pallas kernels for 9%

profile of v21, /device:TPU:1, one launch (start us, length us, event | category | flops | bytes accessed | tf_op | source)
XLA Modules:
  0.0 57.6 jit_solution(13067001788160219516)
XLA Ops:
  0.6 0.0 copy-start.1
  0.6 0.0 copy-start.2
  0.7 0.1 collective-permute-start
  0.8 0.0 copy-start.3
  0.8 0.8 %copy-done.3 = bf16[1,32,8,128]{3,2,1,0:T(8,128)(2,1)S(1)} copy-done((bf16[1,32,8,128]{3,2,1,0:T(8,128)(2,1)S(1)}, bf16[1,32,8,128]{3,2,1,0:T(8,128)(2,1)}, u32[]{:S(2)}) %copy-start.3) | copy-done | bytes 65560
  1.6 0.0 copy-start.9
  1.6 0.0 copy-start.8
  1.6 0.0 copy-start.7
  1.6 0.0 copy-start.4
  1.6 0.0 copy-start.5
  1.6 0.0 copy-start.6
  1.7 0.3 own.1
  2.0 0.2 collective-permute-done.twin_ref
  2.2 1.1 %start.1 = bf16[256,256]{1,0:T(8,128)(2,1)} custom-call(bf16[32,256]{1,0:T(8,128)(2,1)S(1)} %get-tuple-element.40.spectra_ref, bf16[256,128]{1,0:T(8,128)(2,1)S(1)} %collective-permute-done.twin_ref, bf16[32,128]{1,0:T(8,128)(2,1)S(1)} %get-tuple-element.41.z_table_ref, bf16[256,256]{1,0:T(8,128)(2,1)S(1)} %get-tuple-element.42.turn_ref, ...), custom_call_target="tpu_custom_call" | custom-call | flops 4194304 | bytes 524288 | tf_op jit(solution)/shard_map/start/pallas_call | solution.py:576
  3.3 8.0 %all-to-all-start = ((bf16[16,16,256]{2,1,0:T(8,128)(2,1)}), bf16[16,16,256]{2,1,0:T(8,128)(2,1)S(1)}, u32[]{:S(2)}, u32[]{:S(2)}) async-start(bf16[16,16,256]{2,1,0:T(8,128)(2,1)} %bitcast.1), calls=%async_computation | async-start | bytes 262144 | tf_op jit(solution)/shard_map/all_to_all | solution.py:552
  11.4 0.0 copy-start
  11.4 2.2 %copy-done = f32[16,8,2,32,32]{4,3,2,1,0:T(8,128)S(1)} copy-done((f32[16,8,2,32,32]{4,3,2,1,0:T(8,128)S(1)}, f32[16,8,2,32,32]{4,3,2,1,0:T(8,128)}, u32[]{:S(2)}) %copy-start) | copy-done | bytes 1048600
  13.5 0.5 pack.1
  14.1 1.9 %all-to-all-done = bf16[16,16,256]{2,1,0:T(8,128)(2,1)S(1)} async-done(((bf16[16,16,256]{2,1,0:T(8,128)(2,1)}), bf16[16,16,256]{2,1,0:T(8,128)(2,1)S(1)}, u32[]{:S(2)}, u32[]{:S(2)}) %all-to-all-start) | async-done | bytes 131104 | tf_op jit(solution)/shard_map/all_to_all | solution.py:552
  16.0 0.0 copy-done.1
  16.0 0.0 copy-done.2
  16.0 0.9 %mode.1 = (f32[256,32]{1,0:T(8,128)S(1)}, bf16[256,256]{1,0:T(8,128)(2,1)S(1)}) custom-call(bf16[256,256]{1,0:T(8,128)(2,1)S(1)} %bitcast.22, bf16[256,256]{1,0:T(8,128)(2,1)S(1)} %copy-done.1, bf16[256,256]{1,0:T(8,128)(2,1)S(1)} %copy-done.2, bf16[4,256,256]{2,1,0:T(8,128)(2,1)S(1)} %get-tuple-element.44.weight_ref), custom_call_target="tpu_custom_call" | custom-call | flops 4194304 | bytes 524288 | tf_op jit(solution)/shard_map/mode/pallas_call | solution.py:580
  16.9 9.1 %all_to_all.20 = bf16[16,16,256]{2,1,0:T(8,128)(2,1)S(1)} all-to-all(bf16[16,16,256]{2,1,0:T(8,128)(2,1)S(1)} %bitcast.26), channel_id=1, replica_groups={{16,17,20,21,24,25,28,29,0,1,4,5,8,9,12,13},{18,19,22,23,26,27,30,31,2,..., dimensions={0} | all-to-all | bytes 262144 | tf_op jit(solution)/shard_map/all_to_all | solution.py:552
  26.0 0.1 part.2
  26.1 2.8 %collective-permute-start.1 = (bf16[32,256]{1,0:T(8,128)(2,1)S(1)}, bf16[32,256]{1,0:T(8,128)(2,1)S(1)}, u32[]{:S(2)}, u32[]{:S(2)}) collective-permute-start(bf16[32,256]{1,0:T(8,128)(2,1)S(1)} %get-tuple-element.48), channel_id=1, source_target_pairs={{0,2},{1,3},{2,0},{3,1},{4,6},{5,7},{6,4},{7,5},{8,10},{9,11},{10,... | collective-permute-start | bytes 49160 | tf_op jit(solution)/shard_map/ppermute | solution.py:539
  29.0 0.0 copy-done.9
  29.0 0.0 copy-done.8
  29.0 0.1 copy.15.mix_bias_ref
  29.1 0.0 copy-done.7
  29.1 0.1 copy.16.refs_6_
  29.2 0.1 copy.17.refs_7_
  29.3 0.0 copy-done.4
  29.3 0.0 copy-done.5
  29.3 0.2 ready.1
  29.5 0.3 collective-permute-done.1.refs_1_
  29.8 0.0 copy-done.6
  29.8 1.2 %cell.1 = (f32[8,128]{1,0:T(8,128)S(1)}, bf16[32,1024]{1,0:T(8,128)(2,1)S(1)}, bf16[32,256]{1,0:T(8,128)(2,1)S(1)}, bf16[32,1024]{1,0:T(8,128)(2,1)S(1)}, bf16[128,1024]{1,0:T(8,128)(2,1)S(1)}) custom-call(f32[32,256]{1,0:T(8,128)S(1)} %get-tuple-element.47.refs_0_, bf16[32,256]{1,0:T(8,128)(2,1)S(1)} %collective-permute-done.1.refs_1_, ...), custom_call_target="tpu_custom_call" | custom-call | flops 4194304 | bytes 524288 | tf_op jit(solution)/shard_map/cell/pallas_call | solution.py:589
  31.0 0.4 collective-permute-start.2
  31.4 0.4 sums.1
  31.8 0.5 collective-permute-done.2.got_ref
  32.2 0.2 fold.1
  32.4 8.8 %all_to_all.21 = bf16[16,40,128]{2,1,0:T(8,128)(2,1)S(1)} all-to-all(bf16[16,40,128]{2,1,0:T(8,128)(2,1)S(1)} %bitcast.20), channel_id=1, replica_groups={{16,17,20,21,24,25,28,29,0,1,4,5,8,9,12,13},{18,19,22,23,26,27,30,31,2,..., dimensions={0} | all-to-all | bytes 327680 | tf_op jit(solution)/shard_map/all_to_all | solution.py:552
  41.2 1.6 %back.1 = (f32[256,32]{1,0:T(8,128)S(1)}, bf16[640,128]{1,0:T(8,128)(2,1)}) custom-call(bf16[640,128]{1,0:T(8,128)(2,1)S(1)} %bitcast.21, bf16[256,256]{1,0:T(8,128)(2,1)S(1)} %copy-done.1, bf16[256,256]{1,0:T(8,128)(2,1)S(1)} %copy-done.2, bf16[4,256,256]{2,1,0:T(8,128)(2,1)S(1)} %get-tuple-element.44.weight_ref), custom_call_target="tpu_custom_call" | custom-call | flops 4194304 | bytes 524288 | tf_op jit(solution)/shard_map/back/pallas_call | solution.py:620
  42.9 4.8 %all-to-all-start.3 = ((bf16[16,40,128]{2,1,0:T(8,128)(2,1)}), bf16[16,40,128]{2,1,0:T(8,128)(2,1)S(1)}, u32[]{:S(2)}, u32[]{:S(2)}) async-start(bf16[16,40,128]{2,1,0:T(8,128)(2,1)} %bitcast.11), calls=%async_computation.3 | async-start | bytes 327680 | tf_op jit(solution)/shard_map/all_to_all | solution.py:552
  47.6 3.5 %outer.1 = (f32[16,8,2,32,32]{4,3,2,1,0:T(8,128)}, f32[8,128]{1,0:T(8,128)S(1)}) custom-call(f32[16,16,32]{2,1,0:T(8,128)S(1)} %bitcast.24, f32[16,16,32]{2,1,0:T(8,128)S(1)} %bitcast.25), custom_call_target="tpu_custom_call" | custom-call | flops 4194304 | bytes 5242880 | tf_op jit(solution)/shard_map/outer/pallas_call | solution.py:624
  51.2 1.3 %all-to-all-done.3 = bf16[16,40,128]{2,1,0:T(8,128)(2,1)S(1)} async-done(((bf16[16,40,128]{2,1,0:T(8,128)(2,1)}), bf16[16,40,128]{2,1,0:T(8,128)(2,1)S(1)}, u32[]{:S(2)}, u32[]{:S(2)}) %all-to-all-start.3) | async-done | bytes 163872 | tf_op jit(solution)/shard_map/all_to_all | solution.py:552
  52.5 0.2 part.3
  52.6 3.2 %collective-permute-start.3 = (bf16[96,256]{1,0:T(8,128)(2,1)S(1)}, bf16[96,256]{1,0:T(8,128)(2,1)S(1)}, u32[]{:S(2)}, u32[]{:S(2)}) collective-permute-start(bf16[96,256]{1,0:T(8,128)(2,1)S(1)} %get-tuple-element.64), channel_id=1, source_target_pairs={{0,2},{1,3},{2,0},{3,1},{4,6},{5,7},{6,4},{7,5},{8,10},{9,11},{10,... | collective-permute-start | bytes 147464 | tf_op jit(solution)/shard_map/ppermute | solution.py:539
  55.8 0.2 pointwise.1
  56.0 0.7 %collective-permute-done.3.refs_1_ = bf16[96,256]{1,0:T(8,128)(2,1)S(1)} collective-permute-done((bf16[96,256]{1,0:T(8,128)(2,1)S(1)}, bf16[96,256]{1,0:T(8,128)(2,1)S(1)}, u32[]{:S(2)}, u32[]{:S(2)}) %collective-permute-start.3) | collective-permute-done | bytes 49184 | tf_op jit(solution)/shard_map/ppermute | solution.py:539
  56.7 1.0 %finish.1 = (bf16[256,128]{1,0:T(8,128)(2,1)}, f32[8,128]{1,0:T(8,128)}, f32[32,32]{1,0:T(8,128)}, f32[32,128]{1,0:T(8,128)}) custom-call(f32[32,256]{1,0:T(8,128)S(1)} %get-tuple-element.63.refs_0_, bf16[96,256]{1,0:T(8,128)(2,1)S(1)} %collective-permute-done.3.refs_1_, bf16[32,128]{1,0:T(8,128)(2,1)S(1)} %get-tuple-element.65.refs_2_, ...), custom_call_target="tpu_custom_call" | custom-call | flops 4194304 | bytes 524288 | tf_op jit(solution)/shard_map/finish/pallas_call | solution.py:655
  (1 shorter events, 0.0 us)
Async XLA Ops:
  0.6 15.4 %copy-start.1 = (bf16[256,256]{1,0:T(8,128)(2,1)S(1)}, bf16[256,256]{1,0:T(8,128)(2,1)}, u32[]{:S(2)}) copy-start(bf16[256,256]{1,0:T(8,128)(2,1)} %constant.4.clone.y_forward_ref) | copy-start | bytes 393220
  0.6 15.4 %copy-start.2 = (bf16[256,256]{1,0:T(8,128)(2,1)S(1)}, bf16[256,256]{1,0:T(8,128)(2,1)}, u32[]{:S(2)}) copy-start(bf16[256,256]{1,0:T(8,128)(2,1)} %constant.5.clone.y_inverse_ref) | copy-start | bytes 393220
  0.7 1.5 %collective-permute-start = (bf16[256,128]{1,0:T(8,128)(2,1)}, bf16[256,128]{1,0:T(8,128)(2,1)S(1)}, u32[]{:S(2)}, u32[]{:S(2)}) collective-permute-start(bf16[256,128]{1,0:T(8,128)(2,1)} %bitcast.27), channel_id=1, source_target_pairs={{0,2},{1,3},{2,0},{3,1},{4,6},{5,7},{6,4},{7,5},{8,10},{9,11},{10,... | collective-permute-start | bytes 196616 | tf_op jit(solution)/shard_map/ppermute | solution.py:539
  0.8 0.8 %copy-start.3 = (bf16[1,32,8,128]{3,2,1,0:T(8,128)(2,1)S(1)}, bf16[1,32,8,128]{3,2,1,0:T(8,128)(2,1)}, u32[]{:S(2)}) copy-start(bf16[1,32,8,128]{3,2,1,0:T(8,128)(2,1)} %param.10) | copy-start | bytes 196612
  1.6 27.4 %copy-start.9 = (bf16[128]{0:T(256)(128)(2,1)S(1)}, bf16[128]{0:T(256)(128)(2,1)}, u32[]{:S(2)}) copy-start(bf16[128]{0:T(256)(128)(2,1)} %param.16) | copy-start | bytes 772
  1.6 27.4 %copy-start.8 = (f32[32]{0:T(128)S(1)}, f32[32]{0:T(128)}, u32[]{:S(2)}) copy-start(f32[32]{0:T(128)} %param.13) | copy-start | bytes 388
  1.6 27.5 %copy-start.7 = (f32[128]{0:T(128)S(1)}, f32[128]{0:T(128)}, u32[]{:S(2)}) copy-start(f32[128]{0:T(128)} %param.15) | copy-start | bytes 1540
  1.6 27.7 %copy-start.4 = (bf16[32,128]{1,0:T(8,128)(2,1)S(1)}, bf16[32,128]{1,0:T(8,128)(2,1)}, u32[]{:S(2)}) copy-start(bf16[32,128]{1,0:T(8,128)(2,1)} %refs_4_.1) | copy-start | bytes 24580
  1.6 27.7 %copy-start.5 = (bf16[32,32]{1,0:T(8,128)(2,1)S(1)}, bf16[32,32]{1,0:T(8,128)(2,1)}, u32[]{:S(2)}) copy-start(bf16[32,32]{1,0:T(8,128)(2,1)} %mix_ref.3) | copy-start | bytes 6148
  1.6 28.2 %copy-start.6 = (f32[1,8,128]{2,1,0:T(8,128)S(1)}, f32[1,8,128]{2,1,0:T(8,128)}, u32[]{:S(2)}) copy-start(f32[1,8,128]{2,1,0:T(8,128)} %param.17) | copy-start | bytes 12292
  3.3 12.7 %all-to-all-start = ((bf16[16,16,256]{2,1,0:T(8,128)(2,1)}), bf16[16,16,256]{2,1,0:T(8,128)(2,1)S(1)}, u32[]{:S(2)}, u32[]{:S(2)}) async-start(bf16[16,16,256]{2,1,0:T(8,128)(2,1)} %bitcast.1), calls=%async_computation | async-start | bytes 262144 | tf_op jit(solution)/shard_map/all_to_all | solution.py:552
  11.4 2.2 %copy-start = (f32[16,8,2,32,32]{4,3,2,1,0:T(8,128)S(1)}, f32[16,8,2,32,32]{4,3,2,1,0:T(8,128)}, u32[]{:S(2)}) copy-start(f32[16,8,2,32,32]{4,3,2,1,0:T(8,128)} %weight_ref.1) | copy-start | bytes 3145732
  26.1 3.7 %collective-permute-start.1 = (bf16[32,256]{1,0:T(8,128)(2,1)S(1)}, bf16[32,256]{1,0:T(8,128)(2,1)S(1)}, u32[]{:S(2)}, u32[]{:S(2)}) collective-permute-start(bf16[32,256]{1,0:T(8,128)(2,1)S(1)} %get-tuple-element.48), channel_id=1, source_target_pairs={{0,2},{1,3},{2,0},{3,1},{4,6},{5,7},{6,4},{7,5},{8,10},{9,11},{10,... | collective-permute-start | bytes 49160 | tf_op jit(solution)/shard_map/ppermute | solution.py:539
  31.0 1.2 %collective-permute-start.2 = (bf16[32,256]{1,0:T(8,128)(2,1)S(1)}, bf16[32,256]{1,0:T(8,128)(2,1)S(1)}, u32[]{:S(2)}, u32[]{:S(2)}) collective-permute-start(bf16[32,256]{1,0:T(8,128)(2,1)S(1)} %get-tuple-element.53.own_ref), channel_id=1, source_target_pairs={{0,2},{1,3},{2,0},{3,1},{4,6},{5,7},{6,4},{7,5},{8,10},{9,11},{10,... | collective-permute-start | bytes 49160 | tf_op jit(solution)/shard_map/ppermute | solution.py:539
  42.9 9.6 %all-to-all-start.3 = ((bf16[16,40,128]{2,1,0:T(8,128)(2,1)}), bf16[16,40,128]{2,1,0:T(8,128)(2,1)S(1)}, u32[]{:S(2)}, u32[]{:S(2)}) async-start(bf16[16,40,128]{2,1,0:T(8,128)(2,1)} %bitcast.11), calls=%async_computation.3 | async-start | bytes 327680 | tf_op jit(solution)/shard_map/all_to_all | solution.py:552
  52.6 4.0 %collective-permute-start.3 = (bf16[96,256]{1,0:T(8,128)(2,1)S(1)}, bf16[96,256]{1,0:T(8,128)(2,1)S(1)}, u32[]{:S(2)}, u32[]{:S(2)}) collective-permute-start(bf16[96,256]{1,0:T(8,128)(2,1)S(1)} %get-tuple-element.64), channel_id=1, source_target_pairs={{0,2},{1,3},{2,0},{3,1},{4,6},{5,7},{6,4},{7,5},{8,10},{9,11},{10,... | collective-permute-start | bytes 147464 | tf_op jit(solution)/shard_map/ppermute | solution.py:539

commit v22 on v21

--- a/solution.py
+++ b/solution.py
@@ -108,9 +108,9 @@
         wide = lax.axis_index("wide")
         return wide // 2, wide % 2
 
-    def listed(self, position, first):
+    def listed(self, position, first, inner):
         lines = self.outer // 2
-        return ((first + position // 2) & (lines - 1)) * 2 + position % 2
+        return ((first + (1 - 2 * inner) * (position // 2)) & (lines - 1)) * 2 + position % 2
 
     def frequency(self, wide):
         index = (wide * self.modes) // MY
@@ -137,7 +137,7 @@
         outer, inner = self.here()
         row, column = grid_of(2 * self.outer, 4 * MZ)
         x = 2 * outer + (inner ^ (column // (2 * MZ)))
-        frequency = self.frequency(2 * self.listed(row >> 1, first) + inner)
+        frequency = self.frequency(2 * self.listed(row >> 1, first, inner) + inner)
         quarter = self.wide // 4
         small = cosine_of(x * frequency + quarter * ((row & 1) - (column & 1)), self.wide)
         return self.expanded(small)
@@ -146,7 +146,7 @@
         outer, inner = self.here()
         row, column = grid_of(4, self.outer * 2 * MZ)
         x = 2 * outer + (inner ^ (row >> 1))
-        frequency = self.frequency(2 * self.listed(column // (2 * MZ), first) + inner)
+        frequency = self.frequency(2 * self.listed(column // (2 * MZ), first, inner) + inner)
         quarter = self.wide // 4
         small = cosine_of(x * frequency + quarter * ((column & 1) - (row & 1)), self.wide)
         return self.expanded(small).astype(BF16)
@@ -542,7 +542,7 @@
         first = place.firsts[transform]
         groups = [
             [
-                (2 * place.listed(outer, first) + inner) * narrow + n
+                (2 * place.listed(outer, first, inner) + inner) * narrow + n
                 for outer in range(place.outer)
                 for n in range(narrow)
             ]

time: 58.4 us -> 58.2 us (level)
  starting transfers between devices: 19.3 us -> 18.1 us
  waiting for transfers between devices: 4.84 us -> 5.61 us
    ppermute x4, starting transfers between devices: 6.48 us -> 5.66 us  [to_twin(): return lax.ppermute(send, ('wide', 'narrow'), pairs)]
    all_to_all x2, waiting for transfers between devices: 3.21 us -> 3.98 us  [exchange(): lax.all_to_all(pieces, ('wide', 'narrow'), 0, 0, axis_index_groups=groups...]
where the time goes in v22:
time: 58.2 us; the launch traced here: 57.5 us
  blocking collectives  18.2 us (31%)
  starting transfers between devices  18.1 us (31%)
  Pallas kernels  11.5 us (20%)
  waiting for transfers between devices  5.61 us (10%)
  local copies, waits for them, and re-layouts  3.37 us (6%)
  between operations  0.74 us (1%)
    all_to_all x2, blocking collectives, exchange(): lax.all_to_all(pieces, ('wide', 'narrow'), 0, 0, axis_index_groups=groups...  18.2 us
    all_to_all x2, starting transfers between devices, exchange(): lax.all_to_all(pieces, ('wide', 'narrow'), 0, 0, axis_index_groups=groups...  12.4 us
    ppermute x4, starting transfers between devices, to_twin(): return lax.ppermute(send, ('wide', 'narrow'), pairs)  5.66 us
    all_to_all x2, waiting for transfers between devices, exchange(): lax.all_to_all(pieces, ('wide', 'narrow'), 0, 0, axis_index_groups=groups...  3.98 us
    pallas_call x1, Pallas kernels, body(): pl.pallas_call(outer_kernel, grid=(modes // some,), in_specs=[pl.BlockSpe...  3.55 us
    unnamed x20, local copies, waits for them, and re-layouts  3.06 us
    pallas_call x1, Pallas kernels, body(): run(back_kernel, [((mode_lines, channels), F32), shared], 'back')  1.65 us
    ppermute x4, waiting for transfers between devices, to_twin(): return lax.ppermute(send, ('wide', 'narrow'), pairs)  1.63 us
  transfers between devices with their start and end apart: 6, of which 6 were waited for; matrix products, arithmetic and copies ran while one was open for 1% of the time, Pallas kernels for 9%

profile of v22, /device:TPU:1, one launch (start us, length us, event | category | flops | bytes accessed | tf_op | source)
XLA Modules:
  0.0 57.5 jit_solution(16230634248355964817)
XLA Ops:
  0.6 0.0 copy-start.1
  0.6 0.0 copy-start.2
  0.7 0.1 collective-permute-start
  0.8 0.0 copy-start.3
  0.8 0.8 %copy-done.3 = bf16[1,32,8,128]{3,2,1,0:T(8,128)(2,1)S(1)} copy-done((bf16[1,32,8,128]{3,2,1,0:T(8,128)(2,1)S(1)}, bf16[1,32,8,128]{3,2,1,0:T(8,128)(2,1)}, u32[]{:S(2)}) %copy-start.3) | copy-done | bytes 65560
  1.6 0.0 copy-start.9
  1.6 0.0 copy-start.8
  1.6 0.0 copy-start.7
  1.6 0.0 copy-start.4
  1.6 0.0 copy-start.5
  1.6 0.0 copy-start.6
  1.7 0.3 own.1
  2.0 0.2 collective-permute-done.twin_ref
  2.2 1.1 %start.1 = bf16[256,256]{1,0:T(8,128)(2,1)} custom-call(bf16[32,256]{1,0:T(8,128)(2,1)S(1)} %get-tuple-element.40.spectra_ref, bf16[256,128]{1,0:T(8,128)(2,1)S(1)} %collective-permute-done.twin_ref, bf16[32,128]{1,0:T(8,128)(2,1)S(1)} %get-tuple-element.41.z_table_ref, bf16[256,256]{1,0:T(8,128)(2,1)S(1)} %get-tuple-element.42.turn_ref, ...), custom_call_target="tpu_custom_call" | custom-call | flops 4194304 | bytes 524288 | tf_op jit(solution)/shard_map/start/pallas_call | solution.py:576
  3.3 8.0 %all-to-all-start = ((bf16[16,16,256]{2,1,0:T(8,128)(2,1)}), bf16[16,16,256]{2,1,0:T(8,128)(2,1)S(1)}, u32[]{:S(2)}, u32[]{:S(2)}) async-start(bf16[16,16,256]{2,1,0:T(8,128)(2,1)} %bitcast.1), calls=%async_computation | async-start | bytes 262144 | tf_op jit(solution)/shard_map/all_to_all | solution.py:552
  11.4 0.0 copy-start
  11.4 2.2 %copy-done = f32[16,8,2,32,32]{4,3,2,1,0:T(8,128)S(1)} copy-done((f32[16,8,2,32,32]{4,3,2,1,0:T(8,128)S(1)}, f32[16,8,2,32,32]{4,3,2,1,0:T(8,128)}, u32[]{:S(2)}) %copy-start) | copy-done | bytes 1048600
  13.5 0.5 pack.1
  14.1 2.3 %all-to-all-done = bf16[16,16,256]{2,1,0:T(8,128)(2,1)S(1)} async-done(((bf16[16,16,256]{2,1,0:T(8,128)(2,1)}), bf16[16,16,256]{2,1,0:T(8,128)(2,1)S(1)}, u32[]{:S(2)}, u32[]{:S(2)}) %all-to-all-start) | async-done | bytes 131104 | tf_op jit(solution)/shard_map/all_to_all | solution.py:552
  16.4 0.0 copy-done.1
  16.4 0.0 copy-done.2
  16.4 0.9 %mode.1 = (f32[256,32]{1,0:T(8,128)S(1)}, bf16[256,256]{1,0:T(8,128)(2,1)S(1)}) custom-call(bf16[256,256]{1,0:T(8,128)(2,1)S(1)} %bitcast.22, bf16[256,256]{1,0:T(8,128)(2,1)S(1)} %copy-done.1, bf16[256,256]{1,0:T(8,128)(2,1)S(1)} %copy-done.2, bf16[4,256,256]{2,1,0:T(8,128)(2,1)S(1)} %get-tuple-element.44.weight_ref), custom_call_target="tpu_custom_call" | custom-call | flops 4194304 | bytes 524288 | tf_op jit(solution)/shard_map/mode/pallas_call | solution.py:580
  17.3 9.0 %all_to_all.20 = bf16[16,16,256]{2,1,0:T(8,128)(2,1)S(1)} all-to-all(bf16[16,16,256]{2,1,0:T(8,128)(2,1)S(1)} %bitcast.26), channel_id=1, replica_groups={{16,17,20,21,24,25,28,29,0,1,4,5,8,9,12,13},{18,19,22,23,10,11,14,15,2,..., dimensions={0} | all-to-all | bytes 262144 | tf_op jit(solution)/shard_map/all_to_all | solution.py:552
  26.3 0.1 part.2
  26.4 2.5 %collective-permute-start.1 = (bf16[32,256]{1,0:T(8,128)(2,1)S(1)}, bf16[32,256]{1,0:T(8,128)(2,1)S(1)}, u32[]{:S(2)}, u32[]{:S(2)}) collective-permute-start(bf16[32,256]{1,0:T(8,128)(2,1)S(1)} %get-tuple-element.48), channel_id=1, source_target_pairs={{0,2},{1,3},{2,0},{3,1},{4,6},{5,7},{6,4},{7,5},{8,10},{9,11},{10,... | collective-permute-start | bytes 49160 | tf_op jit(solution)/shard_map/ppermute | solution.py:539
  28.9 0.0 copy-done.9
  28.9 0.0 copy-done.8
  28.9 0.1 copy.15.mix_bias_ref
  29.0 0.0 copy-done.7
  29.0 0.1 copy.16.refs_6_
  29.1 0.1 copy.17.refs_7_
  29.2 0.0 copy-done.4
  29.2 0.0 copy-done.5
  29.2 0.2 ready.1
  29.4 0.3 collective-permute-done.1.refs_1_
  29.7 0.0 copy-done.6
  29.7 1.2 %cell.1 = (f32[8,128]{1,0:T(8,128)S(1)}, bf16[32,1024]{1,0:T(8,128)(2,1)S(1)}, bf16[32,256]{1,0:T(8,128)(2,1)S(1)}, bf16[32,1024]{1,0:T(8,128)(2,1)S(1)}, bf16[128,1024]{1,0:T(8,128)(2,1)S(1)}) custom-call(f32[32,256]{1,0:T(8,128)S(1)} %get-tuple-element.47.refs_0_, bf16[32,256]{1,0:T(8,128)(2,1)S(1)} %collective-permute-done.1.refs_1_, ...), custom_call_target="tpu_custom_call" | custom-call | flops 4194304 | bytes 524288 | tf_op jit(solution)/shard_map/cell/pallas_call | solution.py:589
  30.9 0.4 collective-permute-start.2
  31.3 0.4 sums.1
  31.7 0.5 collective-permute-done.2.got_ref
  32.1 0.2 fold.1
  32.3 9.2 %all_to_all.21 = bf16[16,40,128]{2,1,0:T(8,128)(2,1)S(1)} all-to-all(bf16[16,40,128]{2,1,0:T(8,128)(2,1)S(1)} %bitcast.20), channel_id=1, replica_groups={{16,17,20,21,24,25,28,29,0,1,4,5,8,9,12,13},{18,19,22,23,10,11,14,15,2,..., dimensions={0} | all-to-all | bytes 327680 | tf_op jit(solution)/shard_map/all_to_all | solution.py:552
  41.5 1.7 %back.1 = (f32[256,32]{1,0:T(8,128)S(1)}, bf16[640,128]{1,0:T(8,128)(2,1)}) custom-call(bf16[640,128]{1,0:T(8,128)(2,1)S(1)} %bitcast.21, bf16[256,256]{1,0:T(8,128)(2,1)S(1)} %copy-done.1, bf16[256,256]{1,0:T(8,128)(2,1)S(1)} %copy-done.2, bf16[4,256,256]{2,1,0:T(8,128)(2,1)S(1)} %get-tuple-element.44.weight_ref), custom_call_target="tpu_custom_call" | custom-call | flops 4194304 | bytes 524288 | tf_op jit(solution)/shard_map/back/pallas_call | solution.py:620
  43.2 4.4 %all-to-all-start.3 = ((bf16[16,40,128]{2,1,0:T(8,128)(2,1)}), bf16[16,40,128]{2,1,0:T(8,128)(2,1)S(1)}, u32[]{:S(2)}, u32[]{:S(2)}) async-start(bf16[16,40,128]{2,1,0:T(8,128)(2,1)} %bitcast.11), calls=%async_computation.3 | async-start | bytes 327680 | tf_op jit(solution)/shard_map/all_to_all | solution.py:552
  47.6 3.5 %outer.1 = (f32[16,8,2,32,32]{4,3,2,1,0:T(8,128)}, f32[8,128]{1,0:T(8,128)S(1)}) custom-call(f32[16,16,32]{2,1,0:T(8,128)S(1)} %bitcast.24, f32[16,16,32]{2,1,0:T(8,128)S(1)} %bitcast.25), custom_call_target="tpu_custom_call" | custom-call | flops 4194304 | bytes 5242880 | tf_op jit(solution)/shard_map/outer/pallas_call | solution.py:624
  51.1 1.7 %all-to-all-done.3 = bf16[16,40,128]{2,1,0:T(8,128)(2,1)S(1)} async-done(((bf16[16,40,128]{2,1,0:T(8,128)(2,1)}), bf16[16,40,128]{2,1,0:T(8,128)(2,1)S(1)}, u32[]{:S(2)}, u32[]{:S(2)}) %all-to-all-start.3) | async-done | bytes 163872 | tf_op jit(solution)/shard_map/all_to_all | solution.py:552
  52.8 0.2 part.3
  53.0 2.7 %collective-permute-start.3 = (bf16[96,256]{1,0:T(8,128)(2,1)S(1)}, bf16[96,256]{1,0:T(8,128)(2,1)S(1)}, u32[]{:S(2)}, u32[]{:S(2)}) collective-permute-start(bf16[96,256]{1,0:T(8,128)(2,1)S(1)} %get-tuple-element.64), channel_id=1, source_target_pairs={{0,2},{1,3},{2,0},{3,1},{4,6},{5,7},{6,4},{7,5},{8,10},{9,11},{10,... | collective-permute-start | bytes 147464 | tf_op jit(solution)/shard_map/ppermute | solution.py:539
  55.7 0.2 pointwise.1
  55.9 0.7 %collective-permute-done.3.refs_1_ = bf16[96,256]{1,0:T(8,128)(2,1)S(1)} collective-permute-done((bf16[96,256]{1,0:T(8,128)(2,1)S(1)}, bf16[96,256]{1,0:T(8,128)(2,1)S(1)}, u32[]{:S(2)}, u32[]{:S(2)}) %collective-permute-start.3) | collective-permute-done | bytes 49184 | tf_op jit(solution)/shard_map/ppermute | solution.py:539
  56.5 1.0 %finish.1 = (bf16[256,128]{1,0:T(8,128)(2,1)}, f32[8,128]{1,0:T(8,128)}, f32[32,32]{1,0:T(8,128)}, f32[32,128]{1,0:T(8,128)}) custom-call(f32[32,256]{1,0:T(8,128)S(1)} %get-tuple-element.63.refs_0_, bf16[96,256]{1,0:T(8,128)(2,1)S(1)} %collective-permute-done.3.refs_1_, bf16[32,128]{1,0:T(8,128)(2,1)S(1)} %get-tuple-element.65.refs_2_, ...), custom_call_target="tpu_custom_call" | custom-call | flops 4194304 | bytes 524288 | tf_op jit(solution)/shard_map/finish/pallas_call | solution.py:655
  (1 shorter events, 0.0 us)
Async XLA Ops:
  0.6 15.7 %copy-start.1 = (bf16[256,256]{1,0:T(8,128)(2,1)S(1)}, bf16[256,256]{1,0:T(8,128)(2,1)}, u32[]{:S(2)}) copy-start(bf16[256,256]{1,0:T(8,128)(2,1)} %constant.4.clone.y_forward_ref) | copy-start | bytes 393220
  0.6 15.7 %copy-start.2 = (bf16[256,256]{1,0:T(8,128)(2,1)S(1)}, bf16[256,256]{1,0:T(8,128)(2,1)}, u32[]{:S(2)}) copy-start(bf16[256,256]{1,0:T(8,128)(2,1)} %constant.5.clone.y_inverse_ref) | copy-start | bytes 393220
  0.7 1.5 %collective-permute-start = (bf16[256,128]{1,0:T(8,128)(2,1)}, bf16[256,128]{1,0:T(8,128)(2,1)S(1)}, u32[]{:S(2)}, u32[]{:S(2)}) collective-permute-start(bf16[256,128]{1,0:T(8,128)(2,1)} %bitcast.27), channel_id=1, source_target_pairs={{0,2},{1,3},{2,0},{3,1},{4,6},{5,7},{6,4},{7,5},{8,10},{9,11},{10,... | collective-permute-start | bytes 196616 | tf_op jit(solution)/shard_map/ppermute | solution.py:539
  0.8 0.8 %copy-start.3 = (bf16[1,32,8,128]{3,2,1,0:T(8,128)(2,1)S(1)}, bf16[1,32,8,128]{3,2,1,0:T(8,128)(2,1)}, u32[]{:S(2)}) copy-start(bf16[1,32,8,128]{3,2,1,0:T(8,128)(2,1)} %param.10) | copy-start | bytes 196612
  1.6 27.3 %copy-start.9 = (bf16[128]{0:T(256)(128)(2,1)S(1)}, bf16[128]{0:T(256)(128)(2,1)}, u32[]{:S(2)}) copy-start(bf16[128]{0:T(256)(128)(2,1)} %param.16) | copy-start | bytes 772
  1.6 27.3 %copy-start.8 = (f32[32]{0:T(128)S(1)}, f32[32]{0:T(128)}, u32[]{:S(2)}) copy-start(f32[32]{0:T(128)} %param.13) | copy-start | bytes 388
  1.6 27.4 %copy-start.7 = (f32[128]{0:T(128)S(1)}, f32[128]{0:T(128)}, u32[]{:S(2)}) copy-start(f32[128]{0:T(128)} %param.15) | copy-start | bytes 1540
  1.6 27.6 %copy-start.4 = (bf16[32,128]{1,0:T(8,128)(2,1)S(1)}, bf16[32,128]{1,0:T(8,128)(2,1)}, u32[]{:S(2)}) copy-start(bf16[32,128]{1,0:T(8,128)(2,1)} %refs_4_.1) | copy-start | bytes 24580
  1.6 27.6 %copy-start.5 = (bf16[32,32]{1,0:T(8,128)(2,1)S(1)}, bf16[32,32]{1,0:T(8,128)(2,1)}, u32[]{:S(2)}) copy-start(bf16[32,32]{1,0:T(8,128)(2,1)} %mix_ref.3) | copy-start | bytes 6148
  1.6 28.1 %copy-start.6 = (f32[1,8,128]{2,1,0:T(8,128)S(1)}, f32[1,8,128]{2,1,0:T(8,128)}, u32[]{:S(2)}) copy-start(f32[1,8,128]{2,1,0:T(8,128)} %param.17) | copy-start | bytes 12292
  3.3 13.1 %all-to-all-start = ((bf16[16,16,256]{2,1,0:T(8,128)(2,1)}), bf16[16,16,256]{2,1,0:T(8,128)(2,1)S(1)}, u32[]{:S(2)}, u32[]{:S(2)}) async-start(bf16[16,16,256]{2,1,0:T(8,128)(2,1)} %bitcast.1), calls=%async_computation | async-start | bytes 262144 | tf_op jit(solution)/shard_map/all_to_all | solution.py:552
  11.4 2.2 %copy-start = (f32[16,8,2,32,32]{4,3,2,1,0:T(8,128)S(1)}, f32[16,8,2,32,32]{4,3,2,1,0:T(8,128)}, u32[]{:S(2)}) copy-start(f32[16,8,2,32,32]{4,3,2,1,0:T(8,128)} %weight_ref.1) | copy-start | bytes 3145732
  26.4 3.3 %collective-permute-start.1 = (bf16[32,256]{1,0:T(8,128)(2,1)S(1)}, bf16[32,256]{1,0:T(8,128)(2,1)S(1)}, u32[]{:S(2)}, u32[]{:S(2)}) collective-permute-start(bf16[32,256]{1,0:T(8,128)(2,1)S(1)} %get-tuple-element.48), channel_id=1, source_target_pairs={{0,2},{1,3},{2,0},{3,1},{4,6},{5,7},{6,4},{7,5},{8,10},{9,11},{10,... | collective-permute-start | bytes 49160 | tf_op jit(solution)/shard_map/ppermute | solution.py:539
  30.9 1.2 %collective-permute-start.2 = (bf16[32,256]{1,0:T(8,128)(2,1)S(1)}, bf16[32,256]{1,0:T(8,128)(2,1)S(1)}, u32[]{:S(2)}, u32[]{:S(2)}) collective-permute-start(bf16[32,256]{1,0:T(8,128)(2,1)S(1)} %get-tuple-element.53.own_ref), channel_id=1, source_target_pairs={{0,2},{1,3},{2,0},{3,1},{4,6},{5,7},{6,4},{7,5},{8,10},{9,11},{10,... | collective-permute-start | bytes 49160 | tf_op jit(solution)/shard_map/ppermute | solution.py:539
  43.2 9.6 %all-to-all-start.3 = ((bf16[16,40,128]{2,1,0:T(8,128)(2,1)}), bf16[16,40,128]{2,1,0:T(8,128)(2,1)S(1)}, u32[]{:S(2)}, u32[]{:S(2)}) async-start(bf16[16,40,128]{2,1,0:T(8,128)(2,1)} %bitcast.11), calls=%async_computation.3 | async-start | bytes 327680 | tf_op jit(solution)/shard_map/all_to_all | solution.py:552
  53.0 3.6 %collective-permute-start.3 = (bf16[96,256]{1,0:T(8,128)(2,1)S(1)}, bf16[96,256]{1,0:T(8,128)(2,1)S(1)}, u32[]{:S(2)}, u32[]{:S(2)}) collective-permute-start(bf16[96,256]{1,0:T(8,128)(2,1)S(1)} %get-tuple-element.64), channel_id=1, source_target_pairs={{0,2},{1,3},{2,0},{3,1},{4,6},{5,7},{6,4},{7,5},{8,10},{9,11},{10,... | collective-permute-start | bytes 147464 | tf_op jit(solution)/shard_map/ppermute | solution.py:539

commit v23 on v22

--- a/solution.py
+++ b/solution.py
@@ -110,7 +110,7 @@
 
     def listed(self, position, first, inner):
         lines = self.outer // 2
-        return ((first + (1 - 2 * inner) * (position // 2)) & (lines - 1)) * 2 + position % 2
+        return ((first + (1 - 2 * inner) * (position // 2)) & (lines - 1)) * 2 + (position % 2 ^ inner)
 
     def frequency(self, wide):
         index = (wide * self.modes) // MY

time: 58.2 us -> 59 us (1.014)
  waiting for transfers between devices: 5.61 us -> 4.21 us
  blocking collectives: 18.2 us -> 19.3 us
  starting transfers between devices: 18.1 us -> 19.1 us
    all_to_all x2, waiting for transfers between devices: 3.98 us -> 2.59 us  [exchange(): lax.all_to_all(pieces, ('wide', 'narrow'), 0, 0, axis_index_groups=groups...]
    all_to_all x2, blocking collectives: 18.2 us -> 19.3 us  [exchange(): lax.all_to_all(pieces, ('wide', 'narrow'), 0, 0, axis_index_groups=groups...]
    ppermute x4, starting transfers between devices: 5.66 us -> 6.29 us  [to_twin(): return lax.ppermute(send, ('wide', 'narrow'), pairs)]
where the time goes in v23:
time: 59 us; the launch traced here: 58.3 us
  blocking collectives  19.3 us (33%)
  starting transfers between devices  19.1 us (32%)
  Pallas kernels  11.5 us (19%)
  waiting for transfers between devices  4.21 us (7%)
  local copies, waits for them, and re-layouts  3.37 us (6%)
  between operations  0.74 us (1%)
    all_to_all x2, blocking collectives, exchange(): lax.all_to_all(pieces, ('wide', 'narrow'), 0, 0, axis_index_groups=groups...  19.3 us
    all_to_all x2, starting transfers between devices, exchange(): lax.all_to_all(pieces, ('wide', 'narrow'), 0, 0, axis_index_groups=groups...  12.8 us
    ppermute x4, starting transfers between devices, to_twin(): return lax.ppermute(send, ('wide', 'narrow'), pairs)  6.29 us
    pallas_call x1, Pallas kernels, body(): pl.pallas_call(outer_kernel, grid=(modes // some,), in_specs=[pl.BlockSpe...  3.55 us
    unnamed x20, local copies, waits for them, and re-layouts  3.06 us
    all_to_all x2, waiting for transfers between devices, exchange(): lax.all_to_all(pieces, ('wide', 'narrow'), 0, 0, axis_index_groups=groups...  2.59 us
    pallas_call x1, Pallas kernels, body(): run(back_kernel, [((mode_lines, channels), F32), shared], 'back')  1.65 us
    ppermute x4, waiting for transfers between devices, to_twin(): return lax.ppermute(send, ('wide', 'narrow'), pairs)  1.63 us
  transfers between devices with their start and end apart: 6, of which 6 were waited for; matrix products, arithmetic and copies ran while one was open for 1% of the time, Pallas kernels for 9%

profile of v23, /device:TPU:1, one launch (start us, length us, event | category | flops | bytes accessed | tf_op | source)
XLA Modules:
  0.0 58.3 jit_solution(10530677913344798620)
XLA Ops:
  0.6 0.0 copy-start.1
  0.6 0.0 copy-start.2
  0.7 0.1 collective-permute-start
  0.8 0.0 copy-start.3
  0.8 0.8 %copy-done.3 = bf16[1,32,8,128]{3,2,1,0:T(8,128)(2,1)S(1)} copy-done((bf16[1,32,8,128]{3,2,1,0:T(8,128)(2,1)S(1)}, bf16[1,32,8,128]{3,2,1,0:T(8,128)(2,1)}, u32[]{:S(2)}) %copy-start.3) | copy-done | bytes 65560
  1.6 0.0 copy-start.9
  1.6 0.0 copy-start.8
  1.6 0.0 copy-start.7
  1.6 0.0 copy-start.4
  1.6 0.0 copy-start.5
  1.6 0.0 copy-start.6
  1.7 0.3 own.1
  2.0 0.2 collective-permute-done.twin_ref
  2.2 1.1 %start.1 = bf16[256,256]{1,0:T(8,128)(2,1)} custom-call(bf16[32,256]{1,0:T(8,128)(2,1)S(1)} %get-tuple-element.40.spectra_ref, bf16[256,128]{1,0:T(8,128)(2,1)S(1)} %collective-permute-done.twin_ref, bf16[32,128]{1,0:T(8,128)(2,1)S(1)} %get-tuple-element.41.z_table_ref, bf16[256,256]{1,0:T(8,128)(2,1)S(1)} %get-tuple-element.42.turn_ref, ...), custom_call_target="tpu_custom_call" | custom-call | flops 4194304 | bytes 524288 | tf_op jit(solution)/shard_map/start/pallas_call | solution.py:576
  3.3 8.0 %all-to-all-start = ((bf16[16,16,256]{2,1,0:T(8,128)(2,1)}), bf16[16,16,256]{2,1,0:T(8,128)(2,1)S(1)}, u32[]{:S(2)}, u32[]{:S(2)}) async-start(bf16[16,16,256]{2,1,0:T(8,128)(2,1)} %bitcast.1), calls=%async_computation | async-start | bytes 262144 | tf_op jit(solution)/shard_map/all_to_all | solution.py:552
  11.4 0.0 copy-start
  11.4 2.2 %copy-done = f32[16,8,2,32,32]{4,3,2,1,0:T(8,128)S(1)} copy-done((f32[16,8,2,32,32]{4,3,2,1,0:T(8,128)S(1)}, f32[16,8,2,32,32]{4,3,2,1,0:T(8,128)}, u32[]{:S(2)}) %copy-start) | copy-done | bytes 1048600
  13.5 0.5 pack.1
  14.1 1.6 %all-to-all-done = bf16[16,16,256]{2,1,0:T(8,128)(2,1)S(1)} async-done(((bf16[16,16,256]{2,1,0:T(8,128)(2,1)}), bf16[16,16,256]{2,1,0:T(8,128)(2,1)S(1)}, u32[]{:S(2)}, u32[]{:S(2)}) %all-to-all-start) | async-done | bytes 131104 | tf_op jit(solution)/shard_map/all_to_all | solution.py:552
  15.7 0.0 copy-done.1
  15.7 0.0 copy-done.2
  15.7 0.9 %mode.1 = (f32[256,32]{1,0:T(8,128)S(1)}, bf16[256,256]{1,0:T(8,128)(2,1)S(1)}) custom-call(bf16[256,256]{1,0:T(8,128)(2,1)S(1)} %bitcast.22, bf16[256,256]{1,0:T(8,128)(2,1)S(1)} %copy-done.1, bf16[256,256]{1,0:T(8,128)(2,1)S(1)} %copy-done.2, bf16[4,256,256]{2,1,0:T(8,128)(2,1)S(1)} %get-tuple-element.44.weight_ref), custom_call_target="tpu_custom_call" | custom-call | flops 4194304 | bytes 524288 | tf_op jit(solution)/shard_map/mode/pallas_call | solution.py:580
  16.6 8.7 %all_to_all.20 = bf16[16,16,256]{2,1,0:T(8,128)(2,1)S(1)} all-to-all(bf16[16,16,256]{2,1,0:T(8,128)(2,1)S(1)} %bitcast.26), channel_id=1, replica_groups={{16,17,20,21,24,25,28,29,0,1,4,5,8,9,12,13},{22,23,18,19,14,15,10,11,6,..., dimensions={0} | all-to-all | bytes 262144 | tf_op jit(solution)/shard_map/all_to_all | solution.py:552
  25.3 0.1 part.2
  25.4 3.5 %collective-permute-start.1 = (bf16[32,256]{1,0:T(8,128)(2,1)S(1)}, bf16[32,256]{1,0:T(8,128)(2,1)S(1)}, u32[]{:S(2)}, u32[]{:S(2)}) collective-permute-start(bf16[32,256]{1,0:T(8,128)(2,1)S(1)} %get-tuple-element.48), channel_id=1, source_target_pairs={{0,2},{1,3},{2,0},{3,1},{4,6},{5,7},{6,4},{7,5},{8,10},{9,11},{10,... | collective-permute-start | bytes 49160 | tf_op jit(solution)/shard_map/ppermute | solution.py:539
  28.9 0.0 copy-done.9
  28.9 0.0 copy-done.8
  28.9 0.1 copy.15.mix_bias_ref
  29.0 0.0 copy-done.7
  29.0 0.1 copy.16.refs_6_
  29.1 0.1 copy.17.refs_7_
  29.2 0.0 copy-done.4
  29.2 0.0 copy-done.5
  29.2 0.2 ready.1
  29.4 0.3 collective-permute-done.1.refs_1_
  29.7 0.0 copy-done.6
  29.7 1.2 %cell.1 = (f32[8,128]{1,0:T(8,128)S(1)}, bf16[32,1024]{1,0:T(8,128)(2,1)S(1)}, bf16[32,256]{1,0:T(8,128)(2,1)S(1)}, bf16[32,1024]{1,0:T(8,128)(2,1)S(1)}, bf16[128,1024]{1,0:T(8,128)(2,1)S(1)}) custom-call(f32[32,256]{1,0:T(8,128)S(1)} %get-tuple-element.47.refs_0_, bf16[32,256]{1,0:T(8,128)(2,1)S(1)} %collective-permute-done.1.refs_1_, ...), custom_call_target="tpu_custom_call" | custom-call | flops 4194304 | bytes 524288 | tf_op jit(solution)/shard_map/cell/pallas_call | solution.py:589
  30.9 0.4 collective-permute-start.2
  31.3 0.4 sums.1
  31.7 0.5 collective-permute-done.2.got_ref
  32.1 0.2 fold.1
  32.3 10.6 %all_to_all.21 = bf16[16,40,128]{2,1,0:T(8,128)(2,1)S(1)} all-to-all(bf16[16,40,128]{2,1,0:T(8,128)(2,1)S(1)} %bitcast.20), channel_id=1, replica_groups={{16,17,20,21,24,25,28,29,0,1,4,5,8,9,12,13},{22,23,18,19,14,15,10,11,6,..., dimensions={0} | all-to-all | bytes 327680 | tf_op jit(solution)/shard_map/all_to_all | solution.py:552
  42.9 1.6 %back.1 = (f32[256,32]{1,0:T(8,128)S(1)}, bf16[640,128]{1,0:T(8,128)(2,1)}) custom-call(bf16[640,128]{1,0:T(8,128)(2,1)S(1)} %bitcast.21, bf16[256,256]{1,0:T(8,128)(2,1)S(1)} %copy-done.1, bf16[256,256]{1,0:T(8,128)(2,1)S(1)} %copy-done.2, bf16[4,256,256]{2,1,0:T(8,128)(2,1)S(1)} %get-tuple-element.44.weight_ref), custom_call_target="tpu_custom_call" | custom-call | flops 4194304 | bytes 524288 | tf_op jit(solution)/shard_map/back/pallas_call | solution.py:620
  44.6 4.8 %all-to-all-start.3 = ((bf16[16,40,128]{2,1,0:T(8,128)(2,1)}), bf16[16,40,128]{2,1,0:T(8,128)(2,1)S(1)}, u32[]{:S(2)}, u32[]{:S(2)}) async-start(bf16[16,40,128]{2,1,0:T(8,128)(2,1)} %bitcast.11), calls=%async_computation.3 | async-start | bytes 327680 | tf_op jit(solution)/shard_map/all_to_all | solution.py:552
  49.4 3.5 %outer.1 = (f32[16,8,2,32,32]{4,3,2,1,0:T(8,128)}, f32[8,128]{1,0:T(8,128)S(1)}) custom-call(f32[16,16,32]{2,1,0:T(8,128)S(1)} %bitcast.24, f32[16,16,32]{2,1,0:T(8,128)S(1)} %bitcast.25), custom_call_target="tpu_custom_call" | custom-call | flops 4194304 | bytes 5242880 | tf_op jit(solution)/shard_map/outer/pallas_call | solution.py:624
  52.9 1.0 %all-to-all-done.3 = bf16[16,40,128]{2,1,0:T(8,128)(2,1)S(1)} async-done(((bf16[16,40,128]{2,1,0:T(8,128)(2,1)}), bf16[16,40,128]{2,1,0:T(8,128)(2,1)S(1)}, u32[]{:S(2)}, u32[]{:S(2)}) %all-to-all-start.3) | async-done | bytes 163872 | tf_op jit(solution)/shard_map/all_to_all | solution.py:552
  53.9 0.2 part.3
  54.1 2.3 %collective-permute-start.3 = (bf16[96,256]{1,0:T(8,128)(2,1)S(1)}, bf16[96,256]{1,0:T(8,128)(2,1)S(1)}, u32[]{:S(2)}, u32[]{:S(2)}) collective-permute-start(bf16[96,256]{1,0:T(8,128)(2,1)S(1)} %get-tuple-element.64), channel_id=1, source_target_pairs={{0,2},{1,3},{2,0},{3,1},{4,6},{5,7},{6,4},{7,5},{8,10},{9,11},{10,... | collective-permute-start | bytes 147464 | tf_op jit(solution)/shard_map/ppermute | solution.py:539
  56.4 0.2 pointwise.1
  56.6 0.7 %collective-permute-done.3.refs_1_ = bf16[96,256]{1,0:T(8,128)(2,1)S(1)} collective-permute-done((bf16[96,256]{1,0:T(8,128)(2,1)S(1)}, bf16[96,256]{1,0:T(8,128)(2,1)S(1)}, u32[]{:S(2)}, u32[]{:S(2)}) %collective-permute-start.3) | collective-permute-done | bytes 49184 | tf_op jit(solution)/shard_map/ppermute | solution.py:539
  57.3 1.0 %finish.1 = (bf16[256,128]{1,0:T(8,128)(2,1)}, f32[8,128]{1,0:T(8,128)}, f32[32,32]{1,0:T(8,128)}, f32[32,128]{1,0:T(8,128)}) custom-call(f32[32,256]{1,0:T(8,128)S(1)} %get-tuple-element.63.refs_0_, bf16[96,256]{1,0:T(8,128)(2,1)S(1)} %collective-permute-done.3.refs_1_, bf16[32,128]{1,0:T(8,128)(2,1)S(1)} %get-tuple-element.65.refs_2_, ...), custom_call_target="tpu_custom_call" | custom-call | flops 4194304 | bytes 524288 | tf_op jit(solution)/shard_map/finish/pallas_call | solution.py:655
  (1 shorter events, 0.0 us)
Async XLA Ops:
  0.6 15.0 %copy-start.1 = (bf16[256,256]{1,0:T(8,128)(2,1)S(1)}, bf16[256,256]{1,0:T(8,128)(2,1)}, u32[]{:S(2)}) copy-start(bf16[256,256]{1,0:T(8,128)(2,1)} %constant.4.clone.y_forward_ref) | copy-start | bytes 393220
  0.6 15.0 %copy-start.2 = (bf16[256,256]{1,0:T(8,128)(2,1)S(1)}, bf16[256,256]{1,0:T(8,128)(2,1)}, u32[]{:S(2)}) copy-start(bf16[256,256]{1,0:T(8,128)(2,1)} %constant.5.clone.y_inverse_ref) | copy-start | bytes 393220
  0.7 1.5 %collective-permute-start = (bf16[256,128]{1,0:T(8,128)(2,1)}, bf16[256,128]{1,0:T(8,128)(2,1)S(1)}, u32[]{:S(2)}, u32[]{:S(2)}) collective-permute-start(bf16[256,128]{1,0:T(8,128)(2,1)} %bitcast.27), channel_id=1, source_target_pairs={{0,2},{1,3},{2,0},{3,1},{4,6},{5,7},{6,4},{7,5},{8,10},{9,11},{10,... | collective-permute-start | bytes 196616 | tf_op jit(solution)/shard_map/ppermute | solution.py:539
  0.8 0.8 %copy-start.3 = (bf16[1,32,8,128]{3,2,1,0:T(8,128)(2,1)S(1)}, bf16[1,32,8,128]{3,2,1,0:T(8,128)(2,1)}, u32[]{:S(2)}) copy-start(bf16[1,32,8,128]{3,2,1,0:T(8,128)(2,1)} %param.10) | copy-start | bytes 196612
  1.6 27.3 %copy-start.9 = (bf16[128]{0:T(256)(128)(2,1)S(1)}, bf16[128]{0:T(256)(128)(2,1)}, u32[]{:S(2)}) copy-start(bf16[128]{0:T(256)(128)(2,1)} %param.16) | copy-start | bytes 772
  1.6 27.3 %copy-start.8 = (f32[32]{0:T(128)S(1)}, f32[32]{0:T(128)}, u32[]{:S(2)}) copy-start(f32[32]{0:T(128)} %param.13) | copy-start | bytes 388
  1.6 27.4 %copy-start.7 = (f32[128]{0:T(128)S(1)}, f32[128]{0:T(128)}, u32[]{:S(2)}) copy-start(f32[128]{0:T(128)} %param.15) | copy-start | bytes 1540
  1.6 27.6 %copy-start.4 = (bf16[32,128]{1,0:T(8,128)(2,1)S(1)}, bf16[32,128]{1,0:T(8,128)(2,1)}, u32[]{:S(2)}) copy-start(bf16[32,128]{1,0:T(8,128)(2,1)} %refs_4_.1) | copy-start | bytes 24580
  1.6 27.6 %copy-start.5 = (bf16[32,32]{1,0:T(8,128)(2,1)S(1)}, bf16[32,32]{1,0:T(8,128)(2,1)}, u32[]{:S(2)}) copy-start(bf16[32,32]{1,0:T(8,128)(2,1)} %mix_ref.3) | copy-start | bytes 6148
  1.6 28.1 %copy-start.6 = (f32[1,8,128]{2,1,0:T(8,128)S(1)}, f32[1,8,128]{2,1,0:T(8,128)}, u32[]{:S(2)}) copy-start(f32[1,8,128]{2,1,0:T(8,128)} %param.17) | copy-start | bytes 12292
  3.3 12.3 %all-to-all-start = ((bf16[16,16,256]{2,1,0:T(8,128)(2,1)}), bf16[16,16,256]{2,1,0:T(8,128)(2,1)S(1)}, u32[]{:S(2)}, u32[]{:S(2)}) async-start(bf16[16,16,256]{2,1,0:T(8,128)(2,1)} %bitcast.1), calls=%async_computation | async-start | bytes 262144 | tf_op jit(solution)/shard_map/all_to_all | solution.py:552
  11.4 2.2 %copy-start = (f32[16,8,2,32,32]{4,3,2,1,0:T(8,128)S(1)}, f32[16,8,2,32,32]{4,3,2,1,0:T(8,128)}, u32[]{:S(2)}) copy-start(f32[16,8,2,32,32]{4,3,2,1,0:T(8,128)} %weight_ref.1) | copy-start | bytes 3145732
  25.4 4.3 %collective-permute-start.1 = (bf16[32,256]{1,0:T(8,128)(2,1)S(1)}, bf16[32,256]{1,0:T(8,128)(2,1)S(1)}, u32[]{:S(2)}, u32[]{:S(2)}) collective-permute-start(bf16[32,256]{1,0:T(8,128)(2,1)S(1)} %get-tuple-element.48), channel_id=1, source_target_pairs={{0,2},{1,3},{2,0},{3,1},{4,6},{5,7},{6,4},{7,5},{8,10},{9,11},{10,... | collective-permute-start | bytes 49160 | tf_op jit(solution)/shard_map/ppermute | solution.py:539
  30.9 1.2 %collective-permute-start.2 = (bf16[32,256]{1,0:T(8,128)(2,1)S(1)}, bf16[32,256]{1,0:T(8,128)(2,1)S(1)}, u32[]{:S(2)}, u32[]{:S(2)}) collective-permute-start(bf16[32,256]{1,0:T(8,128)(2,1)S(1)} %get-tuple-element.53.own_ref), channel_id=1, source_target_pairs={{0,2},{1,3},{2,0},{3,1},{4,6},{5,7},{6,4},{7,5},{8,10},{9,11},{10,... | collective-permute-start | bytes 49160 | tf_op jit(solution)/shard_map/ppermute | solution.py:539
  44.6 9.3 %all-to-all-start.3 = ((bf16[16,40,128]{2,1,0:T(8,128)(2,1)}), bf16[16,40,128]{2,1,0:T(8,128)(2,1)S(1)}, u32[]{:S(2)}, u32[]{:S(2)}) async-start(bf16[16,40,128]{2,1,0:T(8,128)(2,1)} %bitcast.11), calls=%async_computation.3 | async-start | bytes 327680 | tf_op jit(solution)/shard_map/all_to_all | solution.py:552
  54.1 3.2 %collective-permute-start.3 = (bf16[96,256]{1,0:T(8,128)(2,1)S(1)}, bf16[96,256]{1,0:T(8,128)(2,1)S(1)}, u32[]{:S(2)}, u32[]{:S(2)}) collective-permute-start(bf16[96,256]{1,0:T(8,128)(2,1)S(1)} %get-tuple-element.64), channel_id=1, source_target_pairs={{0,2},{1,3},{2,0},{3,1},{4,6},{5,7},{6,4},{7,5},{8,10},{9,11},{10,... | collective-permute-start | bytes 147464 | tf_op jit(solution)/shard_map/ppermute | solution.py:539

commit v24 on v23

--- a/solution.py
+++ b/solution.py
@@ -110,7 +110,7 @@
 
     def listed(self, position, first, inner):
         lines = self.outer // 2
-        return ((first + (1 - 2 * inner) * (position // 2)) & (lines - 1)) * 2 + (position % 2 ^ inner)
+        return ((first + (2 * inner - 1) * (position // 2)) & (lines - 1)) * 2 + position % 2
 
     def frequency(self, wide):
         index = (wide * self.modes) // MY

time: 59 us -> 59.1 us (level)
  blocking collectives: 19.3 us -> 17.5 us
  starting transfers between devices: 19.1 us -> 20.4 us
  waiting for transfers between devices: 4.21 us -> 4.88 us
    all_to_all x2, blocking collectives: 19.3 us -> 17.5 us  [exchange(): lax.all_to_all(pieces, ('wide', 'narrow'), 0, 0, axis_index_groups=groups...]
    ppermute x4, starting transfers between devices: 6.29 us -> 7.57 us  [to_twin(): return lax.ppermute(send, ('wide', 'narrow'), pairs)]
    all_to_all x2, waiting for transfers between devices: 2.59 us -> 3.25 us  [exchange(): lax.all_to_all(pieces, ('wide', 'narrow'), 0, 0, axis_index_groups=groups...]
where the time goes in v24:
time: 59.1 us; the launch traced here: 58.4 us
  starting transfers between devices  20.4 us (35%)
  blocking collectives  17.5 us (30%)
  Pallas kernels  11.5 us (19%)
  waiting for transfers between devices  4.88 us (8%)
  local copies, waits for them, and re-layouts  3.37 us (6%)
  between operations  0.74 us (1%)
    all_to_all x2, blocking collectives, exchange(): lax.all_to_all(pieces, ('wide', 'narrow'), 0, 0, axis_index_groups=groups...  17.5 us
    all_to_all x2, starting transfers between devices, exchange(): lax.all_to_all(pieces, ('wide', 'narrow'), 0, 0, axis_index_groups=groups...  12.8 us
    ppermute x4, starting transfers between devices, to_twin(): return lax.ppermute(send, ('wide', 'narrow'), pairs)  7.57 us
    pallas_call x1, Pallas kernels, body(): pl.pallas_call(outer_kernel, grid=(modes // some,), in_specs=[pl.BlockSpe...  3.55 us
    all_to_all x2, waiting for transfers between devices, exchange(): lax.all_to_all(pieces, ('wide', 'narrow'), 0, 0, axis_index_groups=groups...  3.25 us
    unnamed x20, local copies, waits for them, and re-layouts  3.06 us
    pallas_call x1, Pallas kernels, body(): run(back_kernel, [((mode_lines, channels), F32), shared], 'back')  1.65 us
    ppermute x4, waiting for transfers between devices, to_twin(): return lax.ppermute(send, ('wide', 'narrow'), pairs)  1.63 us
  transfers between devices with their start and end apart: 6, of which 6 were waited for; matrix products, arithmetic and copies ran while one was open for 1% of the time, Pallas kernels for 9%

profile of v24, /device:TPU:1, one launch (start us, length us, event | category | flops | bytes accessed | tf_op | source)
XLA Modules:
  0.0 58.4 jit_solution(3544945185272067363)
XLA Ops:
  0.6 0.0 copy-start.1
  0.6 0.0 copy-start.2
  0.7 0.1 collective-permute-start
  0.8 0.0 copy-start.3
  0.8 0.8 %copy-done.3 = bf16[1,32,8,128]{3,2,1,0:T(8,128)(2,1)S(1)} copy-done((bf16[1,32,8,128]{3,2,1,0:T(8,128)(2,1)S(1)}, bf16[1,32,8,128]{3,2,1,0:T(8,128)(2,1)}, u32[]{:S(2)}) %copy-start.3) | copy-done | bytes 65560
  1.6 0.0 copy-start.9
  1.6 0.0 copy-start.8
  1.6 0.0 copy-start.7
  1.6 0.0 copy-start.4
  1.6 0.0 copy-start.5
  1.6 0.0 copy-start.6
  1.7 0.3 own.1
  2.0 0.2 collective-permute-done.twin_ref
  2.2 1.1 %start.1 = bf16[256,256]{1,0:T(8,128)(2,1)} custom-call(bf16[32,256]{1,0:T(8,128)(2,1)S(1)} %get-tuple-element.40.spectra_ref, bf16[256,128]{1,0:T(8,128)(2,1)S(1)} %collective-permute-done.twin_ref, bf16[32,128]{1,0:T(8,128)(2,1)S(1)} %get-tuple-element.41.z_table_ref, bf16[256,256]{1,0:T(8,128)(2,1)S(1)} %get-tuple-element.42.turn_ref, ...), custom_call_target="tpu_custom_call" | custom-call | flops 4194304 | bytes 524288 | tf_op jit(solution)/shard_map/start/pallas_call | solution.py:576
  3.3 8.0 %all-to-all-start = ((bf16[16,16,256]{2,1,0:T(8,128)(2,1)}), bf16[16,16,256]{2,1,0:T(8,128)(2,1)S(1)}, u32[]{:S(2)}, u32[]{:S(2)}) async-start(bf16[16,16,256]{2,1,0:T(8,128)(2,1)} %bitcast.1), calls=%async_computation | async-start | bytes 262144 | tf_op jit(solution)/shard_map/all_to_all | solution.py:552
  11.4 0.0 copy-start
  11.4 2.2 %copy-done = f32[16,8,2,32,32]{4,3,2,1,0:T(8,128)S(1)} copy-done((f32[16,8,2,32,32]{4,3,2,1,0:T(8,128)S(1)}, f32[16,8,2,32,32]{4,3,2,1,0:T(8,128)}, u32[]{:S(2)}) %copy-start) | copy-done | bytes 1048600
  13.5 0.5 pack.1
  14.1 2.0 %all-to-all-done = bf16[16,16,256]{2,1,0:T(8,128)(2,1)S(1)} async-done(((bf16[16,16,256]{2,1,0:T(8,128)(2,1)}), bf16[16,16,256]{2,1,0:T(8,128)(2,1)S(1)}, u32[]{:S(2)}, u32[]{:S(2)}) %all-to-all-start) | async-done | bytes 131104 | tf_op jit(solution)/shard_map/all_to_all | solution.py:552
  16.1 0.0 copy-done.1
  16.1 0.0 copy-done.2
  16.1 0.9 %mode.1 = (f32[256,32]{1,0:T(8,128)S(1)}, bf16[256,256]{1,0:T(8,128)(2,1)S(1)}) custom-call(bf16[256,256]{1,0:T(8,128)(2,1)S(1)} %bitcast.22, bf16[256,256]{1,0:T(8,128)(2,1)S(1)} %copy-done.1, bf16[256,256]{1,0:T(8,128)(2,1)S(1)} %copy-done.2, bf16[4,256,256]{2,1,0:T(8,128)(2,1)S(1)} %get-tuple-element.44.weight_ref), custom_call_target="tpu_custom_call" | custom-call | flops 4194304 | bytes 524288 | tf_op jit(solution)/shard_map/mode/pallas_call | solution.py:580
  17.0 9.0 %all_to_all.20 = bf16[16,16,256]{2,1,0:T(8,128)(2,1)S(1)} all-to-all(bf16[16,16,256]{2,1,0:T(8,128)(2,1)S(1)} %bitcast.26), channel_id=1, replica_groups={{16,17,20,21,8,9,12,13,0,1,4,5,24,25,28,29},{18,19,22,23,26,27,30,31,2,..., dimensions={0} | all-to-all | bytes 262144 | tf_op jit(solution)/shard_map/all_to_all | solution.py:552
  26.0 0.1 part.2
  26.1 3.1 %collective-permute-start.1 = (bf16[32,256]{1,0:T(8,128)(2,1)S(1)}, bf16[32,256]{1,0:T(8,128)(2,1)S(1)}, u32[]{:S(2)}, u32[]{:S(2)}) collective-permute-start(bf16[32,256]{1,0:T(8,128)(2,1)S(1)} %get-tuple-element.48), channel_id=1, source_target_pairs={{0,2},{1,3},{2,0},{3,1},{4,6},{5,7},{6,4},{7,5},{8,10},{9,11},{10,... | collective-permute-start | bytes 49160 | tf_op jit(solution)/shard_map/ppermute | solution.py:539
  29.3 0.0 copy-done.9
  29.3 0.0 copy-done.8
  29.3 0.1 copy.15.mix_bias_ref
  29.4 0.0 copy-done.7
  29.4 0.1 copy.16.refs_6_
  29.5 0.1 copy.17.refs_7_
  29.6 0.0 copy-done.4
  29.6 0.0 copy-done.5
  29.6 0.2 ready.1
  29.8 0.3 collective-permute-done.1.refs_1_
  30.1 0.0 copy-done.6
  30.1 1.2 %cell.1 = (f32[8,128]{1,0:T(8,128)S(1)}, bf16[32,1024]{1,0:T(8,128)(2,1)S(1)}, bf16[32,256]{1,0:T(8,128)(2,1)S(1)}, bf16[32,1024]{1,0:T(8,128)(2,1)S(1)}, bf16[128,1024]{1,0:T(8,128)(2,1)S(1)}) custom-call(f32[32,256]{1,0:T(8,128)S(1)} %get-tuple-element.47.refs_0_, bf16[32,256]{1,0:T(8,128)(2,1)S(1)} %collective-permute-done.1.refs_1_, ...), custom_call_target="tpu_custom_call" | custom-call | flops 4194304 | bytes 524288 | tf_op jit(solution)/shard_map/cell/pallas_call | solution.py:589
  31.3 0.4 collective-permute-start.2
  31.7 0.4 sums.1
  32.0 0.5 collective-permute-done.2.got_ref
  32.5 0.2 fold.1
  32.7 8.5 %all_to_all.21 = bf16[16,40,128]{2,1,0:T(8,128)(2,1)S(1)} all-to-all(bf16[16,40,128]{2,1,0:T(8,128)(2,1)S(1)} %bitcast.20), channel_id=1, replica_groups={{16,17,20,21,8,9,12,13,0,1,4,5,24,25,28,29},{18,19,22,23,26,27,30,31,2,..., dimensions={0} | all-to-all | bytes 327680 | tf_op jit(solution)/shard_map/all_to_all | solution.py:552
  41.2 1.6 %back.1 = (f32[256,32]{1,0:T(8,128)S(1)}, bf16[640,128]{1,0:T(8,128)(2,1)}) custom-call(bf16[640,128]{1,0:T(8,128)(2,1)S(1)} %bitcast.21, bf16[256,256]{1,0:T(8,128)(2,1)S(1)} %copy-done.1, bf16[256,256]{1,0:T(8,128)(2,1)S(1)} %copy-done.2, bf16[4,256,256]{2,1,0:T(8,128)(2,1)S(1)} %get-tuple-element.44.weight_ref), custom_call_target="tpu_custom_call" | custom-call | flops 4194304 | bytes 524288 | tf_op jit(solution)/shard_map/back/pallas_call | solution.py:620
  42.8 4.8 %all-to-all-start.3 = ((bf16[16,40,128]{2,1,0:T(8,128)(2,1)}), bf16[16,40,128]{2,1,0:T(8,128)(2,1)S(1)}, u32[]{:S(2)}, u32[]{:S(2)}) async-start(bf16[16,40,128]{2,1,0:T(8,128)(2,1)} %bitcast.11), calls=%async_computation.3 | async-start | bytes 327680 | tf_op jit(solution)/shard_map/all_to_all | solution.py:552
  47.6 3.5 %outer.1 = (f32[16,8,2,32,32]{4,3,2,1,0:T(8,128)}, f32[8,128]{1,0:T(8,128)S(1)}) custom-call(f32[16,16,32]{2,1,0:T(8,128)S(1)} %bitcast.24, f32[16,16,32]{2,1,0:T(8,128)S(1)} %bitcast.25), custom_call_target="tpu_custom_call" | custom-call | flops 4194304 | bytes 5242880 | tf_op jit(solution)/shard_map/outer/pallas_call | solution.py:624
  51.1 1.2 %all-to-all-done.3 = bf16[16,40,128]{2,1,0:T(8,128)(2,1)S(1)} async-done(((bf16[16,40,128]{2,1,0:T(8,128)(2,1)}), bf16[16,40,128]{2,1,0:T(8,128)(2,1)S(1)}, u32[]{:S(2)}, u32[]{:S(2)}) %all-to-all-start.3) | async-done | bytes 163872 | tf_op jit(solution)/shard_map/all_to_all | solution.py:552
  52.4 0.2 part.3
  52.5 4.0 %collective-permute-start.3 = (bf16[96,256]{1,0:T(8,128)(2,1)S(1)}, bf16[96,256]{1,0:T(8,128)(2,1)S(1)}, u32[]{:S(2)}, u32[]{:S(2)}) collective-permute-start(bf16[96,256]{1,0:T(8,128)(2,1)S(1)} %get-tuple-element.64), channel_id=1, source_target_pairs={{0,2},{1,3},{2,0},{3,1},{4,6},{5,7},{6,4},{7,5},{8,10},{9,11},{10,... | collective-permute-start | bytes 147464 | tf_op jit(solution)/shard_map/ppermute | solution.py:539
  56.5 0.2 pointwise.1
  56.7 0.7 %collective-permute-done.3.refs_1_ = bf16[96,256]{1,0:T(8,128)(2,1)S(1)} collective-permute-done((bf16[96,256]{1,0:T(8,128)(2,1)S(1)}, bf16[96,256]{1,0:T(8,128)(2,1)S(1)}, u32[]{:S(2)}, u32[]{:S(2)}) %collective-permute-start.3) | collective-permute-done | bytes 49184 | tf_op jit(solution)/shard_map/ppermute | solution.py:539
  57.4 1.0 %finish.1 = (bf16[256,128]{1,0:T(8,128)(2,1)}, f32[8,128]{1,0:T(8,128)}, f32[32,32]{1,0:T(8,128)}, f32[32,128]{1,0:T(8,128)}) custom-call(f32[32,256]{1,0:T(8,128)S(1)} %get-tuple-element.63.refs_0_, bf16[96,256]{1,0:T(8,128)(2,1)S(1)} %collective-permute-done.3.refs_1_, bf16[32,128]{1,0:T(8,128)(2,1)S(1)} %get-tuple-element.65.refs_2_, ...), custom_call_target="tpu_custom_call" | custom-call | flops 4194304 | bytes 524288 | tf_op jit(solution)/shard_map/finish/pallas_call | solution.py:655
  (1 shorter events, 0.0 us)
Async XLA Ops:
  0.6 15.5 %copy-start.1 = (bf16[256,256]{1,0:T(8,128)(2,1)S(1)}, bf16[256,256]{1,0:T(8,128)(2,1)}, u32[]{:S(2)}) copy-start(bf16[256,256]{1,0:T(8,128)(2,1)} %constant.4.clone.y_forward_ref) | copy-start | bytes 393220
  0.6 15.4 %copy-start.2 = (bf16[256,256]{1,0:T(8,128)(2,1)S(1)}, bf16[256,256]{1,0:T(8,128)(2,1)}, u32[]{:S(2)}) copy-start(bf16[256,256]{1,0:T(8,128)(2,1)} %constant.5.clone.y_inverse_ref) | copy-start | bytes 393220
  0.7 1.5 %collective-permute-start = (bf16[256,128]{1,0:T(8,128)(2,1)}, bf16[256,128]{1,0:T(8,128)(2,1)S(1)}, u32[]{:S(2)}, u32[]{:S(2)}) collective-permute-start(bf16[256,128]{1,0:T(8,128)(2,1)} %bitcast.27), channel_id=1, source_target_pairs={{0,2},{1,3},{2,0},{3,1},{4,6},{5,7},{6,4},{7,5},{8,10},{9,11},{10,... | collective-permute-start | bytes 196616 | tf_op jit(solution)/shard_map/ppermute | solution.py:539
  0.8 0.8 %copy-start.3 = (bf16[1,32,8,128]{3,2,1,0:T(8,128)(2,1)S(1)}, bf16[1,32,8,128]{3,2,1,0:T(8,128)(2,1)}, u32[]{:S(2)}) copy-start(bf16[1,32,8,128]{3,2,1,0:T(8,128)(2,1)} %param.10) | copy-start | bytes 196612
  1.6 27.6 %copy-start.9 = (bf16[128]{0:T(256)(128)(2,1)S(1)}, bf16[128]{0:T(256)(128)(2,1)}, u32[]{:S(2)}) copy-start(bf16[128]{0:T(256)(128)(2,1)} %param.16) | copy-start | bytes 772
  1.6 27.6 %copy-start.8 = (f32[32]{0:T(128)S(1)}, f32[32]{0:T(128)}, u32[]{:S(2)}) copy-start(f32[32]{0:T(128)} %param.13) | copy-start | bytes 388
  1.6 27.7 %copy-start.7 = (f32[128]{0:T(128)S(1)}, f32[128]{0:T(128)}, u32[]{:S(2)}) copy-start(f32[128]{0:T(128)} %param.15) | copy-start | bytes 1540
  1.6 28.0 %copy-start.4 = (bf16[32,128]{1,0:T(8,128)(2,1)S(1)}, bf16[32,128]{1,0:T(8,128)(2,1)}, u32[]{:S(2)}) copy-start(bf16[32,128]{1,0:T(8,128)(2,1)} %refs_4_.1) | copy-start | bytes 24580
  1.6 28.0 %copy-start.5 = (bf16[32,32]{1,0:T(8,128)(2,1)S(1)}, bf16[32,32]{1,0:T(8,128)(2,1)}, u32[]{:S(2)}) copy-start(bf16[32,32]{1,0:T(8,128)(2,1)} %mix_ref.3) | copy-start | bytes 6148
  1.6 28.5 %copy-start.6 = (f32[1,8,128]{2,1,0:T(8,128)S(1)}, f32[1,8,128]{2,1,0:T(8,128)}, u32[]{:S(2)}) copy-start(f32[1,8,128]{2,1,0:T(8,128)} %param.17) | copy-start | bytes 12292
  3.3 12.8 %all-to-all-start = ((bf16[16,16,256]{2,1,0:T(8,128)(2,1)}), bf16[16,16,256]{2,1,0:T(8,128)(2,1)S(1)}, u32[]{:S(2)}, u32[]{:S(2)}) async-start(bf16[16,16,256]{2,1,0:T(8,128)(2,1)} %bitcast.1), calls=%async_computation | async-start | bytes 262144 | tf_op jit(solution)/shard_map/all_to_all | solution.py:552
  11.4 2.2 %copy-start = (f32[16,8,2,32,32]{4,3,2,1,0:T(8,128)S(1)}, f32[16,8,2,32,32]{4,3,2,1,0:T(8,128)}, u32[]{:S(2)}) copy-start(f32[16,8,2,32,32]{4,3,2,1,0:T(8,128)} %weight_ref.1) | copy-start | bytes 3145732
  26.1 4.0 %collective-permute-start.1 = (bf16[32,256]{1,0:T(8,128)(2,1)S(1)}, bf16[32,256]{1,0:T(8,128)(2,1)S(1)}, u32[]{:S(2)}, u32[]{:S(2)}) collective-permute-start(bf16[32,256]{1,0:T(8,128)(2,1)S(1)} %get-tuple-element.48), channel_id=1, source_target_pairs={{0,2},{1,3},{2,0},{3,1},{4,6},{5,7},{6,4},{7,5},{8,10},{9,11},{10,... | collective-permute-start | bytes 49160 | tf_op jit(solution)/shard_map/ppermute | solution.py:539
  31.3 1.2 %collective-permute-start.2 = (bf16[32,256]{1,0:T(8,128)(2,1)S(1)}, bf16[32,256]{1,0:T(8,128)(2,1)S(1)}, u32[]{:S(2)}, u32[]{:S(2)}) collective-permute-start(bf16[32,256]{1,0:T(8,128)(2,1)S(1)} %get-tuple-element.53.own_ref), channel_id=1, source_target_pairs={{0,2},{1,3},{2,0},{3,1},{4,6},{5,7},{6,4},{7,5},{8,10},{9,11},{10,... | collective-permute-start | bytes 49160 | tf_op jit(solution)/shard_map/ppermute | solution.py:539
  42.8 9.5 %all-to-all-start.3 = ((bf16[16,40,128]{2,1,0:T(8,128)(2,1)}), bf16[16,40,128]{2,1,0:T(8,128)(2,1)S(1)}, u32[]{:S(2)}, u32[]{:S(2)}) async-start(bf16[16,40,128]{2,1,0:T(8,128)(2,1)} %bitcast.11), calls=%async_computation.3 | async-start | bytes 327680 | tf_op jit(solution)/shard_map/all_to_all | solution.py:552
  52.5 4.9 %collective-permute-start.3 = (bf16[96,256]{1,0:T(8,128)(2,1)S(1)}, bf16[96,256]{1,0:T(8,128)(2,1)S(1)}, u32[]{:S(2)}, u32[]{:S(2)}) collective-permute-start(bf16[96,256]{1,0:T(8,128)(2,1)S(1)} %get-tuple-element.64), channel_id=1, source_target_pairs={{0,2},{1,3},{2,0},{3,1},{4,6},{5,7},{6,4},{7,5},{8,10},{9,11},{10,... | collective-permute-start | bytes 147464 | tf_op jit(solution)/shard_map/ppermute | solution.py:539

commit v25 on v22

--- a/solution.py
+++ b/solution.py
@@ -102,7 +102,7 @@
         self.partners = self.outer * narrow
         self.lanes = rows_y * channels
         middle = self.outer // 4
-        self.firsts = (middle, middle, middle, middle)
+        self.firsts = (self.outer // 2 - 1, middle, middle, middle)
 
     def here(self):
         wide = lax.axis_index("wide")

time: 58.2 us -> 58.2 us (level)
  starting transfers between devices: 18.1 us -> 17.5 us
    ppermute x4, starting transfers between devices: 5.66 us -> 5.03 us  [to_twin(): return lax.ppermute(send, ('wide', 'narrow'), pairs)]
where the time goes in v25:
time: 58.2 us; the launch traced here: 57.5 us
  blocking collectives  18.4 us (32%)
  starting transfers between devices  17.5 us (30%)
  Pallas kernels  11.5 us (20%)
  waiting for transfers between devices  6.01 us (10%)
  local copies, waits for them, and re-layouts  3.37 us (6%)
  between operations  0.74 us (1%)
    all_to_all x2, blocking collectives, exchange(): lax.all_to_all(pieces, ('wide', 'narrow'), 0, 0, axis_index_groups=groups...  18.4 us
    all_to_all x2, starting transfers between devices, exchange(): lax.all_to_all(pieces, ('wide', 'narrow'), 0, 0, axis_index_groups=groups...  12.4 us
    ppermute x4, starting transfers between devices, to_twin(): return lax.ppermute(send, ('wide', 'narrow'), pairs)  5.03 us
    all_to_all x2, waiting for transfers between devices, exchange(): lax.all_to_all(pieces, ('wide', 'narrow'), 0, 0, axis_index_groups=groups...  4.38 us
    pallas_call x1, Pallas kernels, body(): pl.pallas_call(outer_kernel, grid=(modes // some,), in_specs=[pl.BlockSpe...  3.55 us
    unnamed x20, local copies, waits for them, and re-layouts  3.06 us
    pallas_call x1, Pallas kernels, body(): run(back_kernel, [((mode_lines, channels), F32), shared], 'back')  1.65 us
    ppermute x4, waiting for transfers between devices, to_twin(): return lax.ppermute(send, ('wide', 'narrow'), pairs)  1.63 us
  transfers between devices with their start and end apart: 6, of which 6 were waited for; matrix products, arithmetic and copies ran while one was open for 1% of the time, Pallas kernels for 9%

profile of v25, /device:TPU:1, one launch (start us, length us, event | category | flops | bytes accessed | tf_op | source)
XLA Modules:
  0.0 57.5 jit_solution(15374331644359392737)
XLA Ops:
  0.6 0.0 copy-start.1
  0.6 0.0 copy-start.2
  0.7 0.1 collective-permute-start
  0.8 0.0 copy-start.3
  0.8 0.8 %copy-done.3 = bf16[1,32,8,128]{3,2,1,0:T(8,128)(2,1)S(1)} copy-done((bf16[1,32,8,128]{3,2,1,0:T(8,128)(2,1)S(1)}, bf16[1,32,8,128]{3,2,1,0:T(8,128)(2,1)}, u32[]{:S(2)}) %copy-start.3) | copy-done | bytes 65560
  1.6 0.0 copy-start.9
  1.6 0.0 copy-start.8
  1.6 0.0 copy-start.7
  1.6 0.0 copy-start.4
  1.6 0.0 copy-start.5
  1.6 0.0 copy-start.6
  1.7 0.3 own.1
  2.0 0.2 collective-permute-done.twin_ref
  2.2 1.1 %start.1 = bf16[256,256]{1,0:T(8,128)(2,1)} custom-call(bf16[32,256]{1,0:T(8,128)(2,1)S(1)} %get-tuple-element.40.spectra_ref, bf16[256,128]{1,0:T(8,128)(2,1)S(1)} %collective-permute-done.twin_ref, bf16[32,128]{1,0:T(8,128)(2,1)S(1)} %get-tuple-element.41.z_table_ref, bf16[256,256]{1,0:T(8,128)(2,1)S(1)} %get-tuple-element.42.turn_ref, ...), custom_call_target="tpu_custom_call" | custom-call | flops 4194304 | bytes 524288 | tf_op jit(solution)/shard_map/start/pallas_call | solution.py:576
  3.3 8.1 %all-to-all-start = ((bf16[16,16,256]{2,1,0:T(8,128)(2,1)}), bf16[16,16,256]{2,1,0:T(8,128)(2,1)S(1)}, u32[]{:S(2)}, u32[]{:S(2)}) async-start(bf16[16,16,256]{2,1,0:T(8,128)(2,1)} %bitcast.1), calls=%async_computation | async-start | bytes 262144 | tf_op jit(solution)/shard_map/all_to_all | solution.py:552
  11.4 0.0 copy-start
  11.4 2.2 %copy-done = f32[16,8,2,32,32]{4,3,2,1,0:T(8,128)S(1)} copy-done((f32[16,8,2,32,32]{4,3,2,1,0:T(8,128)S(1)}, f32[16,8,2,32,32]{4,3,2,1,0:T(8,128)}, u32[]{:S(2)}) %copy-start) | copy-done | bytes 1048600
  13.5 0.5 pack.1
  14.1 2.7 %all-to-all-done = bf16[16,16,256]{2,1,0:T(8,128)(2,1)S(1)} async-done(((bf16[16,16,256]{2,1,0:T(8,128)(2,1)}), bf16[16,16,256]{2,1,0:T(8,128)(2,1)S(1)}, u32[]{:S(2)}, u32[]{:S(2)}) %all-to-all-start) | async-done | bytes 131104 | tf_op jit(solution)/shard_map/all_to_all | solution.py:552
  16.8 0.0 copy-done.1
  16.8 0.0 copy-done.2
  16.8 0.9 %mode.1 = (f32[256,32]{1,0:T(8,128)S(1)}, bf16[256,256]{1,0:T(8,128)(2,1)S(1)}) custom-call(bf16[256,256]{1,0:T(8,128)(2,1)S(1)} %bitcast.22, bf16[256,256]{1,0:T(8,128)(2,1)S(1)} %copy-done.1, bf16[256,256]{1,0:T(8,128)(2,1)S(1)} %copy-done.2, bf16[4,256,256]{2,1,0:T(8,128)(2,1)S(1)} %get-tuple-element.44.weight_ref), custom_call_target="tpu_custom_call" | custom-call | flops 4194304 | bytes 524288 | tf_op jit(solution)/shard_map/mode/pallas_call | solution.py:580
  17.7 9.2 %all_to_all.20 = bf16[16,16,256]{2,1,0:T(8,128)(2,1)S(1)} all-to-all(bf16[16,16,256]{2,1,0:T(8,128)(2,1)S(1)} %bitcast.26), channel_id=1, replica_groups={{16,17,20,21,24,25,28,29,0,1,4,5,8,9,12,13},{18,19,22,23,10,11,14,15,2,..., dimensions={0} | all-to-all | bytes 262144 | tf_op jit(solution)/shard_map/all_to_all | solution.py:552
  26.9 0.1 part.2
  27.0 1.9 %collective-permute-start.1 = (bf16[32,256]{1,0:T(8,128)(2,1)S(1)}, bf16[32,256]{1,0:T(8,128)(2,1)S(1)}, u32[]{:S(2)}, u32[]{:S(2)}) collective-permute-start(bf16[32,256]{1,0:T(8,128)(2,1)S(1)} %get-tuple-element.48), channel_id=1, source_target_pairs={{0,2},{1,3},{2,0},{3,1},{4,6},{5,7},{6,4},{7,5},{8,10},{9,11},{10,... | collective-permute-start | bytes 49160 | tf_op jit(solution)/shard_map/ppermute | solution.py:539
  28.9 0.0 copy-done.9
  28.9 0.0 copy-done.8
  28.9 0.1 copy.15.mix_bias_ref
  29.0 0.0 copy-done.7
  29.0 0.1 copy.16.refs_6_
  29.1 0.1 copy.17.refs_7_
  29.2 0.0 copy-done.4
  29.2 0.0 copy-done.5
  29.2 0.2 ready.1
  29.4 0.3 collective-permute-done.1.refs_1_
  29.7 0.0 copy-done.6
  29.7 1.2 %cell.1 = (f32[8,128]{1,0:T(8,128)S(1)}, bf16[32,1024]{1,0:T(8,128)(2,1)S(1)}, bf16[32,256]{1,0:T(8,128)(2,1)S(1)}, bf16[32,1024]{1,0:T(8,128)(2,1)S(1)}, bf16[128,1024]{1,0:T(8,128)(2,1)S(1)}) custom-call(f32[32,256]{1,0:T(8,128)S(1)} %get-tuple-element.47.refs_0_, bf16[32,256]{1,0:T(8,128)(2,1)S(1)} %collective-permute-done.1.refs_1_, ...), custom_call_target="tpu_custom_call" | custom-call | flops 4194304 | bytes 524288 | tf_op jit(solution)/shard_map/cell/pallas_call | solution.py:589
  30.9 0.4 collective-permute-start.2
  31.3 0.4 sums.1
  31.7 0.5 collective-permute-done.2.got_ref
  32.1 0.2 fold.1
  32.3 9.2 %all_to_all.21 = bf16[16,40,128]{2,1,0:T(8,128)(2,1)S(1)} all-to-all(bf16[16,40,128]{2,1,0:T(8,128)(2,1)S(1)} %bitcast.20), channel_id=1, replica_groups={{16,17,20,21,24,25,28,29,0,1,4,5,8,9,12,13},{18,19,22,23,10,11,14,15,2,..., dimensions={0} | all-to-all | bytes 327680 | tf_op jit(solution)/shard_map/all_to_all | solution.py:552
  41.5 1.6 %back.1 = (f32[256,32]{1,0:T(8,128)S(1)}, bf16[640,128]{1,0:T(8,128)(2,1)}) custom-call(bf16[640,128]{1,0:T(8,128)(2,1)S(1)} %bitcast.21, bf16[256,256]{1,0:T(8,128)(2,1)S(1)} %copy-done.1, bf16[256,256]{1,0:T(8,128)(2,1)S(1)} %copy-done.2, bf16[4,256,256]{2,1,0:T(8,128)(2,1)S(1)} %get-tuple-element.44.weight_ref), custom_call_target="tpu_custom_call" | custom-call | flops 4194304 | bytes 524288 | tf_op jit(solution)/shard_map/back/pallas_call | solution.py:620
  43.2 4.4 %all-to-all-start.3 = ((bf16[16,40,128]{2,1,0:T(8,128)(2,1)}), bf16[16,40,128]{2,1,0:T(8,128)(2,1)S(1)}, u32[]{:S(2)}, u32[]{:S(2)}) async-start(bf16[16,40,128]{2,1,0:T(8,128)(2,1)} %bitcast.11), calls=%async_computation.3 | async-start | bytes 327680 | tf_op jit(solution)/shard_map/all_to_all | solution.py:552
  47.6 3.5 %outer.1 = (f32[16,8,2,32,32]{4,3,2,1,0:T(8,128)}, f32[8,128]{1,0:T(8,128)S(1)}) custom-call(f32[16,16,32]{2,1,0:T(8,128)S(1)} %bitcast.24, f32[16,16,32]{2,1,0:T(8,128)S(1)} %bitcast.25), custom_call_target="tpu_custom_call" | custom-call | flops 4194304 | bytes 5242880 | tf_op jit(solution)/shard_map/outer/pallas_call | solution.py:624
  51.1 1.7 %all-to-all-done.3 = bf16[16,40,128]{2,1,0:T(8,128)(2,1)S(1)} async-done(((bf16[16,40,128]{2,1,0:T(8,128)(2,1)}), bf16[16,40,128]{2,1,0:T(8,128)(2,1)S(1)}, u32[]{:S(2)}, u32[]{:S(2)}) %all-to-all-start.3) | async-done | bytes 163872 | tf_op jit(solution)/shard_map/all_to_all | solution.py:552
  52.8 0.2 part.3
  53.0 2.7 %collective-permute-start.3 = (bf16[96,256]{1,0:T(8,128)(2,1)S(1)}, bf16[96,256]{1,0:T(8,128)(2,1)S(1)}, u32[]{:S(2)}, u32[]{:S(2)}) collective-permute-start(bf16[96,256]{1,0:T(8,128)(2,1)S(1)} %get-tuple-element.64), channel_id=1, source_target_pairs={{0,2},{1,3},{2,0},{3,1},{4,6},{5,7},{6,4},{7,5},{8,10},{9,11},{10,... | collective-permute-start | bytes 147464 | tf_op jit(solution)/shard_map/ppermute | solution.py:539
  55.7 0.2 pointwise.1
  55.9 0.7 %collective-permute-done.3.refs_1_ = bf16[96,256]{1,0:T(8,128)(2,1)S(1)} collective-permute-done((bf16[96,256]{1,0:T(8,128)(2,1)S(1)}, bf16[96,256]{1,0:T(8,128)(2,1)S(1)}, u32[]{:S(2)}, u32[]{:S(2)}) %collective-permute-start.3) | collective-permute-done | bytes 49184 | tf_op jit(solution)/shard_map/ppermute | solution.py:539
  56.5 1.0 %finish.1 = (bf16[256,128]{1,0:T(8,128)(2,1)}, f32[8,128]{1,0:T(8,128)}, f32[32,32]{1,0:T(8,128)}, f32[32,128]{1,0:T(8,128)}) custom-call(f32[32,256]{1,0:T(8,128)S(1)} %get-tuple-element.63.refs_0_, bf16[96,256]{1,0:T(8,128)(2,1)S(1)} %collective-permute-done.3.refs_1_, bf16[32,128]{1,0:T(8,128)(2,1)S(1)} %get-tuple-element.65.refs_2_, ...), custom_call_target="tpu_custom_call" | custom-call | flops 4194304 | bytes 524288 | tf_op jit(solution)/shard_map/finish/pallas_call | solution.py:655
  (1 shorter events, 0.0 us)
Async XLA Ops:
  0.6 16.1 %copy-start.1 = (bf16[256,256]{1,0:T(8,128)(2,1)S(1)}, bf16[256,256]{1,0:T(8,128)(2,1)}, u32[]{:S(2)}) copy-start(bf16[256,256]{1,0:T(8,128)(2,1)} %constant.4.clone.y_forward_ref) | copy-start | bytes 393220
  0.6 16.1 %copy-start.2 = (bf16[256,256]{1,0:T(8,128)(2,1)S(1)}, bf16[256,256]{1,0:T(8,128)(2,1)}, u32[]{:S(2)}) copy-start(bf16[256,256]{1,0:T(8,128)(2,1)} %constant.5.clone.y_inverse_ref) | copy-start | bytes 393220
  0.7 1.5 %collective-permute-start = (bf16[256,128]{1,0:T(8,128)(2,1)}, bf16[256,128]{1,0:T(8,128)(2,1)S(1)}, u32[]{:S(2)}, u32[]{:S(2)}) collective-permute-start(bf16[256,128]{1,0:T(8,128)(2,1)} %bitcast.27), channel_id=1, source_target_pairs={{0,2},{1,3},{2,0},{3,1},{4,6},{5,7},{6,4},{7,5},{8,10},{9,11},{10,... | collective-permute-start | bytes 196616 | tf_op jit(solution)/shard_map/ppermute | solution.py:539
  0.8 0.8 %copy-start.3 = (bf16[1,32,8,128]{3,2,1,0:T(8,128)(2,1)S(1)}, bf16[1,32,8,128]{3,2,1,0:T(8,128)(2,1)}, u32[]{:S(2)}) copy-start(bf16[1,32,8,128]{3,2,1,0:T(8,128)(2,1)} %param.10) | copy-start | bytes 196612
  1.6 27.3 %copy-start.9 = (bf16[128]{0:T(256)(128)(2,1)S(1)}, bf16[128]{0:T(256)(128)(2,1)}, u32[]{:S(2)}) copy-start(bf16[128]{0:T(256)(128)(2,1)} %param.16) | copy-start | bytes 772
  1.6 27.3 %copy-start.8 = (f32[32]{0:T(128)S(1)}, f32[32]{0:T(128)}, u32[]{:S(2)}) copy-start(f32[32]{0:T(128)} %param.13) | copy-start | bytes 388
  1.6 27.4 %copy-start.7 = (f32[128]{0:T(128)S(1)}, f32[128]{0:T(128)}, u32[]{:S(2)}) copy-start(f32[128]{0:T(128)} %param.15) | copy-start | bytes 1540
  1.6 27.6 %copy-start.4 = (bf16[32,128]{1,0:T(8,128)(2,1)S(1)}, bf16[32,128]{1,0:T(8,128)(2,1)}, u32[]{:S(2)}) copy-start(bf16[32,128]{1,0:T(8,128)(2,1)} %refs_4_.1) | copy-start | bytes 24580
  1.6 27.6 %copy-start.5 = (bf16[32,32]{1,0:T(8,128)(2,1)S(1)}, bf16[32,32]{1,0:T(8,128)(2,1)}, u32[]{:S(2)}) copy-start(bf16[32,32]{1,0:T(8,128)(2,1)} %mix_ref.3) | copy-start | bytes 6148
  1.6 28.1 %copy-start.6 = (f32[1,8,128]{2,1,0:T(8,128)S(1)}, f32[1,8,128]{2,1,0:T(8,128)}, u32[]{:S(2)}) copy-start(f32[1,8,128]{2,1,0:T(8,128)} %param.17) | copy-start | bytes 12292
  3.3 13.5 %all-to-all-start = ((bf16[16,16,256]{2,1,0:T(8,128)(2,1)}), bf16[16,16,256]{2,1,0:T(8,128)(2,1)S(1)}, u32[]{:S(2)}, u32[]{:S(2)}) async-start(bf16[16,16,256]{2,1,0:T(8,128)(2,1)} %bitcast.1), calls=%async_computation | async-start | bytes 262144 | tf_op jit(solution)/shard_map/all_to_all | solution.py:552
  11.4 2.2 %copy-start = (f32[16,8,2,32,32]{4,3,2,1,0:T(8,128)S(1)}, f32[16,8,2,32,32]{4,3,2,1,0:T(8,128)}, u32[]{:S(2)}) copy-start(f32[16,8,2,32,32]{4,3,2,1,0:T(8,128)} %weight_ref.1) | copy-start | bytes 3145732
  27.0 2.7 %collective-permute-start.1 = (bf16[32,256]{1,0:T(8,128)(2,1)S(1)}, bf16[32,256]{1,0:T(8,128)(2,1)S(1)}, u32[]{:S(2)}, u32[]{:S(2)}) collective-permute-start(bf16[32,256]{1,0:T(8,128)(2,1)S(1)} %get-tuple-element.48), channel_id=1, source_target_pairs={{0,2},{1,3},{2,0},{3,1},{4,6},{5,7},{6,4},{7,5},{8,10},{9,11},{10,... | collective-permute-start | bytes 49160 | tf_op jit(solution)/shard_map/ppermute | solution.py:539
  30.9 1.2 %collective-permute-start.2 = (bf16[32,256]{1,0:T(8,128)(2,1)S(1)}, bf16[32,256]{1,0:T(8,128)(2,1)S(1)}, u32[]{:S(2)}, u32[]{:S(2)}) collective-permute-start(bf16[32,256]{1,0:T(8,128)(2,1)S(1)} %get-tuple-element.53.own_ref), channel_id=1, source_target_pairs={{0,2},{1,3},{2,0},{3,1},{4,6},{5,7},{6,4},{7,5},{8,10},{9,11},{10,... | collective-permute-start | bytes 49160 | tf_op jit(solution)/shard_map/ppermute | solution.py:539
  43.2 9.6 %all-to-all-start.3 = ((bf16[16,40,128]{2,1,0:T(8,128)(2,1)}), bf16[16,40,128]{2,1,0:T(8,128)(2,1)S(1)}, u32[]{:S(2)}, u32[]{:S(2)}) async-start(bf16[16,40,128]{2,1,0:T(8,128)(2,1)} %bitcast.11), calls=%async_computation.3 | async-start | bytes 327680 | tf_op jit(solution)/shard_map/all_to_all | solution.py:552
  53.0 3.6 %collective-permute-start.3 = (bf16[96,256]{1,0:T(8,128)(2,1)S(1)}, bf16[96,256]{1,0:T(8,128)(2,1)S(1)}, u32[]{:S(2)}, u32[]{:S(2)}) collective-permute-start(bf16[96,256]{1,0:T(8,128)(2,1)S(1)} %get-tuple-element.64), channel_id=1, source_target_pairs={{0,2},{1,3},{2,0},{3,1},{4,6},{5,7},{6,4},{7,5},{8,10},{9,11},{10,... | collective-permute-start | bytes 147464 | tf_op jit(solution)/shard_map/ppermute | solution.py:539
